TPU v7x, 32 devices: a whole 2x2x4 slice. The times are simulated.
32 devices in a mesh: rev: 4 (over y, x), cust: 4 (over z), prod: 2 (over core).
Axes of the slice: x: 2, y: 2, z: 4, core: 2. Of those that a mesh axis runs over, the one named last changes fastest.
Arguments:
- review_cols: bfloat16 [16384, 2048], P(('rev', 'cust', 'prod')), may hold values from -24 to 24
- cust_state: bfloat16 [8192, 512], P(('rev', 'cust')), may hold values from -6 to 6
- prod_state: bfloat16 [4096, 512], P(('cust', 'prod')), may hold values from -6 to 6
- w_qkv: bfloat16 [512, 1536], replicated, may hold values from -0.25 to 0.25
- w_out: bfloat16 [512, 512], replicated, may hold values from -0.25 to 0.25
- w_msg: bfloat16 [512, 1024], replicated, may hold values from -0.25 to 0.25
- w_cust_up: bfloat16 [512, 512], replicated, may hold values from -0.25 to 0.25
- w_prod_up: bfloat16 [512, 512], replicated, may hold values from -0.25 to 0.25
- w_back: bfloat16 [1024, 512], replicated, may hold values from -0.1875 to 0.1875
- cust_slot: int32 [16384], P(('rev', 'cust', 'prod')), may hold values from 0 to 511
- prod_slot: int32 [16384], P(('rev', 'cust', 'prod')), may hold values from 0 to 511
- prod_pos: int32 [32, 512], P(('rev', 'cust', 'prod')), may hold values from 0 to 511, each once within a row
- live_count: int32 [32, 16], P(('rev', 'cust', 'prod')), may hold values from 1 to 32, 264 in all within a row
Outputs:
- review_out: bfloat16 [16384, 512], P(('rev', 'cust', 'prod'))
- new_cust: bfloat16 [8192, 512], P(('rev', 'cust'))
- new_prod: bfloat16 [4096, 512], P(('cust', 'prod'))
Inputs may be any that keep to these rules, and one draw needn't show every extreme that they name: `prod_pos`: each device's row is a permutation of 0 to 511. `live_count`: each device's counts sum to 264, and some block holds 32 live reviews.
All inputs are finite; a program needn't handle non-finite values.
Results may differ from a plain program's by a relative error of at most 0.011.
Values may be sent and summed in bfloat16 or wider, within the bound.
No kernel may reach another device: no remote copies, remote signals or barrier semaphores. Data moves between devices by JAX's collectives and lax.ppermute only.
A program may use at most 128 MiB of HBM per device.

v0:
```python
import math

import jax
import jax.numpy as jnp
from jax import lax
from jax.sharding import PartitionSpec as P

H = 512
HEADS = 8
NCOL = 4
HD = 64


def rms_norm(vector):
    return vector * lax.rsqrt(jnp.mean(vector * vector, axis=-1, keepdims=True) + 1e-06)


def encode(columns, w_qkv, w_out):
    count_rows = columns.shape[0]
    column_tok = columns.reshape(count_rows * NCOL, H)
    qkv_rows = jnp.dot(column_tok, w_qkv, preferred_element_type=jnp.float32).astype(jnp.bfloat16)
    qkv_rows = qkv_rows.reshape(count_rows, NCOL, 3, HEADS, HD)
    queries = qkv_rows[:, :, 0]
    key_part = qkv_rows[:, :, 1]
    val_part = qkv_rows[:, :, 2]
    scores = jnp.einsum(
        "rihd,rjhd->rhij", queries, key_part, preferred_element_type=jnp.float32
    ) * (1.0 / math.sqrt(HD))
    scores = scores - jnp.max(scores, axis=-1, keepdims=True)
    expon = jnp.exp(scores)
    att_weight = (expon / jnp.sum(expon, axis=-1, keepdims=True)).astype(jnp.bfloat16)
    attended = jnp.einsum(
        "rhij,rjhd->rihd", att_weight, val_part, preferred_element_type=jnp.float32
    ).astype(jnp.bfloat16)
    attended = attended.reshape(count_rows * NCOL, H)
    mixed_tok = column_tok.astype(jnp.float32) + jnp.dot(
        attended, w_out, preferred_element_type=jnp.float32
    )
    pooled = jnp.mean(mixed_tok.reshape(count_rows, NCOL, H), axis=1)
    return rms_norm(pooled).astype(jnp.bfloat16)


def refresh(totals, counts, states, weight):
    normed_sum = (totals / jnp.sqrt(jnp.maximum(counts, 1.0))[:, None]).astype(jnp.bfloat16)
    update = jax.nn.silu(jnp.dot(normed_sum, weight, preferred_element_type=jnp.float32))
    return rms_norm(states.astype(jnp.float32) + update).astype(jnp.bfloat16)


def pick_back(picker, states):
    return lax.dot_general(
        picker, states, (((0,), (0,)), ((), ())), preferred_element_type=jnp.float32
    ).astype(jnp.bfloat16)


def on_device(
    review_cols,
    cust_state,
    prod_state,
    w_qkv,
    w_out,
    w_msg,
    w_cust_up,
    w_prod_up,
    w_back,
    cust_slot,
    prod_slot,
    prod_pos,
    live_count,
):
    review_rows = review_cols.shape[0]
    rev_size = lax.axis_size("rev")
    cust_size = lax.axis_size("cust")
    prod_size = lax.axis_size("prod")
    cust_owners = rev_size * cust_size
    cust_slots = review_rows // cust_owners
    prod_owners = cust_size * prod_size
    prod_slots = review_rows // prod_owners
    cust_rows = cust_state.shape[0]
    prod_rows = prod_state.shape[0]
    review_h = encode(review_cols, w_qkv, w_out)
    message = jnp.dot(review_h, w_msg, preferred_element_type=jnp.float32).astype(jnp.bfloat16)
    to_cust = message[:, :H]
    to_prod = message[:, H:]
    filled = jnp.arange(cust_slots, dtype=jnp.int32)[None, :] < live_count.reshape(cust_owners, 1)
    cust_ids = jnp.where(filled, cust_slot.reshape(cust_owners, cust_slots), -1)
    position = prod_pos.reshape(review_rows)
    prod_ids = (
        jnp.zeros((review_rows,), jnp.int32)
        .at[position]
        .set(jnp.where(filled.reshape(review_rows), prod_slot, -1))
    )
    prod_msgs = jnp.zeros((review_rows, H), jnp.bfloat16).at[position].set(to_prod)
    got_rows, got_ids = (
        lax.all_to_all(
            to_cust.reshape(cust_owners, cust_slots, H),
            ("rev", "cust"),
            split_axis=0,
            concat_axis=0,
            tiled=True,
        ),
        lax.all_to_all(cust_ids, ("rev", "cust"), split_axis=0, concat_axis=0, tiled=True),
    )
    cust_pick = (
        got_ids.reshape(1, review_rows) == jnp.arange(cust_rows, dtype=jnp.int32)[:, None]
    ).astype(jnp.bfloat16)
    cust_part = jnp.dot(
        cust_pick, got_rows.reshape(review_rows, H), preferred_element_type=jnp.float32
    )
    cust_counts = jnp.sum(cust_pick, axis=1, dtype=jnp.float32)
    cust_sum, cust_total = lax.psum((cust_part, cust_counts), "prod")
    new_cust = refresh(cust_sum, cust_total, cust_state, w_cust_up)
    cust_reply = pick_back(cust_pick, new_cust)
    ret_cust = lax.all_to_all(
        cust_reply.reshape(cust_owners, cust_slots, H),
        ("rev", "cust"),
        split_axis=0,
        concat_axis=0,
        tiled=True,
    )
    ret_cust = ret_cust.reshape(review_rows, H)
    prod_got, prod_got_ids = (
        lax.all_to_all(
            prod_msgs.reshape(prod_owners, prod_slots, H),
            ("cust", "prod"),
            split_axis=0,
            concat_axis=0,
            tiled=True,
        ),
        lax.all_to_all(
            prod_ids.reshape(prod_owners, prod_slots),
            ("cust", "prod"),
            split_axis=0,
            concat_axis=0,
            tiled=True,
        ),
    )
    prod_pick = (
        prod_got_ids.reshape(1, review_rows) == jnp.arange(prod_rows, dtype=jnp.int32)[:, None]
    ).astype(jnp.bfloat16)
    prod_part = jnp.dot(
        prod_pick, prod_got.reshape(review_rows, H), preferred_element_type=jnp.float32
    )
    prod_counts = jnp.sum(prod_pick, axis=1, dtype=jnp.float32)
    whole_sum, whole_count = (
        lax.psum(prod_part.astype(jnp.bfloat16), "rev").astype(jnp.float32),
        lax.psum(prod_counts.astype(jnp.bfloat16), "rev").astype(jnp.float32),
    )
    new_prod = refresh(whole_sum, whole_count, prod_state, w_prod_up)
    prod_reply = pick_back(prod_pick, new_prod)
    ret_sorted = lax.all_to_all(
        prod_reply.reshape(prod_owners, prod_slots, H),
        ("cust", "prod"),
        split_axis=0,
        concat_axis=0,
        tiled=True,
    )
    ret_prod = jnp.take(ret_sorted.reshape(review_rows, H), position, axis=0)
    back_proj = jnp.dot(
        jnp.concatenate([ret_cust, ret_prod], axis=1), w_back, preferred_element_type=jnp.float32
    )
    review_out = rms_norm(review_h.astype(jnp.float32) + back_proj).astype(jnp.bfloat16)
    return (review_out, new_cust, new_prod)


def solution(mesh):
    in_specs = (
        P(("rev", "cust", "prod"), None),
        P(("rev", "cust"), None),
        P(("cust", "prod"), None),
        P(),
        P(),
        P(),
        P(),
        P(),
        P(),
        P(("rev", "cust", "prod")),
        P(("rev", "cust", "prod")),
        P(("rev", "cust", "prod"), None),
        P(("rev", "cust", "prod"), None),
    )
    out_specs = (
        P(("rev", "cust", "prod"), None),
        P(("rev", "cust"), None),
        P(("cust", "prod"), None),
    )
    return jax.shard_map(
        on_device, mesh=mesh, in_specs=in_specs, out_specs=out_specs, check_vma=False
    )
```

profile of v0, /device:TPU:0, one launch (start us, length us, event | category | flops | bytes accessed | tf_op | source)
XLA Modules:
  0.0 267.1 jit_solution(38328643463401300)
XLA Ops:
  7.2 0.8 compare_select_fusion.1
  8.0 0.7 iota_compare_fusion.4
  8.7 0.1 lt.66
  8.8 0.7 broadcast_select_fusion.1
  9.5 2.4 scatter_custom_fusion
  11.9 0.7 all_to_all.25
  12.6 6.3 %all-to-all-start.3 = ((s32[8,1,64]{2,1,0:T(1,128)}), s32[8,1,64]{2,1,0:T(1,128)S(1)}, u32[]{:S(2)}, u32[]{:S(2)}) async-start(s32[8,1,64]{2,1,0:T(1,128)} %all_to_all.25), calls=%async_computation.3 | async-start | bytes 8192 | tf_op jit(solution)/shard_map/all_to_all | solution.py:129
  18.9 4.4 %reshape.185 = bf16[2048,512]{1,0:T(8,128)(2,1)} reshape(bf16[512,2048]{1,0:T(8,128)(2,1)} %param.13) | data formatting | bytes 4194304 | tf_op jit(solution)/shard_map/reshape | solution.py:20
  23.3 7.0 %convolution_convert_fusion = bf16[2048,1536]{1,0:T(8,128)(2,1)} fusion(bf16[2048,512]{1,0:T(8,128)(2,1)} %reshape.185, bf16[512,1536]{1,0:T(8,128)(2,1)S(1)} %copy-done), kind=kOutput, calls=%fused_computation.6 | convolution fusion | flops 3224371200 | bytes 9961472 | tf_op jit(solution)/shard_map/dot_general | solution.py:21
  30.3 16.2 %reshape.186 = bf16[512,4,3,8,64]{4,3,2,1,0:T(8,128)(2,1)} reshape(bf16[2048,1536]{1,0:T(8,128)(2,1)} %convolution_convert_fusion) | data formatting | bytes 12582912 | tf_op jit(solution)/shard_map/reshape | solution.py:22
  46.6 8.8 %fusion.29 = (bf16[512,4,1,8,64]{4,3,2,1,0:T(8,128)(2,1)}, bf16[512,4,1,8,64]{4,3,2,1,0:T(8,128)(2,1)}, bf16[512,4,1,8,64]{4,3,2,1,0:T(8,128)(2,1)}) fusion(bf16[512,4,3,8,64]{4,3,2,1,0:T(8,128)(2,1)} %reshape.186), kind=kLoop, calls=%fused_computation.73 | loop fusion | bytes 12582912 | tf_op jit(solution)/shard_map/slice | solution.py:25
  55.3 18.4 %fusion.30 = (f32[512,8,4]{2,1,0:T(8,128)}, f32[512,8,4,4]{2,3,1,0:T(4,128)}) fusion(bf16[512,4,1,8,64]{4,3,2,1,0:T(8,128)(2,1)} %get-tuple-element.17, bf16[512,4,1,8,64]{4,3,2,1,0:T(8,128)(2,1)} %get-tuple-element.16), kind=kOutput, calls=%fused_computation.74 | convolution fusion | flops 8585219 | bytes 4521984 | tf_op jit(solution)/shard_map/sub | solution.py:29
  73.8 8.4 %fusion.4 = bf16[512,4,8,64]{3,1,2,0:T(4,128)(2,1)S(1)} fusion(f32[512,8,4,4]{2,3,1,0:T(4,128)} %get-tuple-element.19, f32[512,8,4]{2,1,0:T(8,128)} %get-tuple-element.18, bf16[512,4,1,8,64]{4,3,2,1,0:T(8,128)(2,1)} %get-tuple-element.15), kind=kOutput, calls=%fused_computation.16 | convolution fusion | flops 9568256 | bytes 4521984 | tf_op jit(solution)/shard_map/rhij,rjhd->rihd/dot_general | solution.py:32
  82.2 2.6 copy.50
  84.8 6.5 %reshape.187 = bf16[2048,512]{1,0:T(8,128)(2,1)} reshape(bf16[512,4,8,64]{3,2,1,0:T(8,128)(2,1)} %copy.50) | data formatting | bytes 4194304 | tf_op jit(solution)/shard_map/reshape | solution.py:35
  91.4 5.4 %convert_add_fusion = f32[2048,512]{1,0:T(8,128)} fusion(bf16[2048,512]{1,0:T(8,128)(2,1)} %reshape.185, bf16[2048,512]{1,0:T(8,128)(2,1)} %reshape.187, bf16[512,512]{1,0:T(8,128)(2,1)S(1)} %copy-done.2), kind=kOutput, calls=%fused_computation.15 | convolution fusion | flops 1075838976 | bytes 8912896 | tf_op jit(solution)/shard_map/dot_general | solution.py:36
  96.8 5.2 %reshape.188 = f32[512,4,512]{2,1,0:T(4,128)} reshape(f32[2048,512]{1,0:T(8,128)} %convert_add_fusion) | data formatting | bytes 8388608 | tf_op jit(solution)/shard_map/reshape | solution.py:39
  101.9 4.7 %reduce_sum.76 = f32[512,512]{1,0:T(8,128)S(1)} reduce(f32[512,4,512]{2,1,0:T(4,128)} %reshape.188, f32[]{:T(128)} %constant.17.clone.1), dimensions={1}, to_apply=%region_2.0 | reduce | flops 786432 | bytes 5242884 | tf_op jit(solution)/shard_map/reduce_sum | solution.py:39
  106.6 0.2 multiply_reduce_fusion.4
  106.8 0.1 reshape.189
  106.9 0.7 compare_select_fusion
  107.6 0.3 copy.51
  107.9 7.2 %all-to-all-start = ((s32[16,1,32]{2,1,0:T(1,128)}), s32[16,1,32]{2,1,0:T(1,128)S(1)}, u32[]{:S(2)}, u32[]{:S(2)}) async-start(s32[16,1,32]{2,1,0:T(1,128)} %compare_select_fusion), calls=%async_computation | async-start | bytes 16384 | tf_op jit(solution)/shard_map/all_to_all | solution.py:101
  115.2 2.0 convolution_convert_fusion.2
  117.2 3.2 %scatter_custom_fusion.1 = bf16[512,512]{1,0:T(8,128)(2,1)} fusion(s32[512]{0:T(512)S(1)} %bitcast.52, bf16[512,1024]{1,0:T(8,128)(2,1)S(1)} %convolution_convert_fusion.2, bf16[]{:T(256)} %constant.43.clone.1), kind=kCustom, calls=%fused_computation.46 | custom fusion | bytes 1048578 | tf_op jit(solution)/shard_map/scatter | solution.py:92
  120.3 2.0 all-to-all-done
  122.4 3.5 %all-to-all-start.4 = ((bf16[8,64,512]{2,1,0:T(8,128)(2,1)}), bf16[8,64,512]{2,1,0:T(8,128)(2,1)S(1)}, u32[]{:S(2)}, u32[]{:S(2)}) async-start(bf16[8,64,512]{2,1,0:T(8,128)(2,1)} %bitcast.12), calls=%async_computation.4 | async-start | bytes 1048576 | tf_op jit(solution)/shard_map/all_to_all | solution.py:122
  125.9 0.8 slice.25
  126.7 14.4 %all-to-all-done.4 = bf16[8,64,512]{2,1,0:T(8,128)(2,1)S(1)} async-done(((bf16[8,64,512]{2,1,0:T(8,128)(2,1)}), bf16[8,64,512]{2,1,0:T(8,128)(2,1)S(1)}, u32[]{:S(2)}, u32[]{:S(2)}) %all-to-all-start.4) | async-done | bytes 524320 | tf_op jit(solution)/shard_map/all_to_all | solution.py:122
  141.2 0.8 copy-done.4
  142.0 4.0 %all-to-all-start.1 = ((bf16[16,32,512]{2,1,0:T(8,128)(2,1)}), bf16[16,32,512]{2,1,0:T(8,128)(2,1)S(1)}, u32[]{:S(2)}, u32[]{:S(2)}) async-start(bf16[16,32,512]{2,1,0:T(8,128)(2,1)} %bitcast.5), calls=%async_computation.1 | async-start | bytes 1048576 | tf_op jit(solution)/shard_map/all_to_all | solution.py:94
  145.9 0.0 all-reduce.5.cloned.1.call-start
  146.0 0.2 copy.53
  146.2 2.1 copy.52
  148.3 0.5 broadcast.138
  148.8 0.7 reduce.7
  149.5 0.1 eq.34
  149.5 0.2 fusion.12
  149.7 10.3 %psum.31 = bf16[512]{0:T(512)(128)(2,1)S(1)} all-reduce(bf16[512]{0:T(512)(128)(2,1)S(1)} %fusion.12), channel_id=1, replica_groups=mesh['rev'=4,'cust'=4,'prod'=2] {'rev'}, use_global_device_ids=true, to_apply=%region_12.13 | all-reduce | flops 512 | bytes 2048 | tf_op jit(solution)/shard_map/psum | solution.py:146
  160.0 0.7 reduce.8
  160.7 0.1 eq.30
  160.8 2.3 convolution_convert_fusion.5
  163.1 0.0 all-reduce.3.cloned.1.call-start
  163.1 0.2 convert_reduce_fusion
  163.3 2.5 psum.29
  165.8 1.5 fusion.10
  167.3 40.3 %all-reduce.5.cloned.1.call-done = bf16[512,512]{1,0:T(8,128)(2,1)} async-done(((bf16[512,512]{1,0:T(8,128)(2,1)}), bf16[512,512]{1,0:T(8,128)(2,1)}) %all-reduce.5.cloned.1.call-update) | async-done | bytes 524304 | tf_op jit(solution)/shard_map/psum | solution.py:145
  207.6 2.0 multiply_reduce_fusion.2
  209.6 0.1 multiply_convert_fusion.1
  209.8 1.3 convolution_convert_fusion.3
  211.1 4.6 %all-to-all-start.5 = ((bf16[8,64,512]{2,1,0:T(8,128)(2,1)}), bf16[8,64,512]{2,1,0:T(8,128)(2,1)S(1)}, u32[]{:S(2)}, u32[]{:S(2)}) async-start(bf16[8,64,512]{2,1,0:T(8,128)(2,1)} %bitcast.14), calls=%async_computation.5 | async-start | bytes 1048576 | tf_op jit(solution)/shard_map/all_to_all | solution.py:150
  215.7 13.9 %all-reduce.3.cloned.1.call-done = f32[512,512]{1,0:T(8,128)} async-done(((f32[512,512]{1,0:T(8,128)}), f32[512,512]{1,0:T(8,128)}) %all-reduce.3.cloned.1.call-update) | async-done | bytes 1048592 | tf_op jit(solution)/shard_map/psum | solution.py:110
  229.6 2.3 multiply_reduce_fusion.3
  231.9 0.1 multiply_convert_fusion.2
  232.0 1.3 convolution_convert_fusion.4
  233.3 6.8 %all-to-all-start.2 = ((bf16[16,32,512]{2,1,0:T(8,128)(2,1)}), bf16[16,32,512]{2,1,0:T(8,128)(2,1)}, u32[]{:S(2)}, u32[]{:S(2)}) async-start(bf16[16,32,512]{2,1,0:T(8,128)(2,1)} %bitcast.7), calls=%async_computation.2 | async-start | bytes 1048576 | tf_op jit(solution)/shard_map/all_to_all | solution.py:113
  240.2 1.0 copy.56
  241.2 1.0 copy.55
  242.2 2.6 gather_fusion
  244.9 1.2 broadcast_select_fusion
  246.1 10.8 %all-to-all-done.2 = bf16[16,32,512]{2,1,0:T(8,128)(2,1)} async-done(((bf16[16,32,512]{2,1,0:T(8,128)(2,1)}), bf16[16,32,512]{2,1,0:T(8,128)(2,1)}, u32[]{:S(2)}, u32[]{:S(2)}) %all-to-all-start.2) | async-done | bytes 524320 | tf_op jit(solution)/shard_map/all_to_all | solution.py:113
  256.9 2.2 multiply_reduce_fusion.1
  259.1 0.1 multiply_convert_fusion
  259.2 1.0 copy.54
  (28 shorter events, 0.1 us)
Async XLA Ops:
  7.2 16.2 %copy-start = (bf16[512,1536]{1,0:T(8,128)(2,1)S(1)}, bf16[512,1536]{1,0:T(8,128)(2,1)}, u32[]{:S(2)}) copy-start(bf16[512,1536]{1,0:T(8,128)(2,1)} %param.16) | copy-start | bytes 4718596
  12.6 95.3 %all-to-all-start.3 = ((s32[8,1,64]{2,1,0:T(1,128)}), s32[8,1,64]{2,1,0:T(1,128)S(1)}, u32[]{:S(2)}, u32[]{:S(2)}) async-start(s32[8,1,64]{2,1,0:T(1,128)} %all_to_all.25), calls=%async_computation.3 | async-start | bytes 8192 | tf_op jit(solution)/shard_map/all_to_all | solution.py:129
  84.8 6.5 %copy-start.2 = (bf16[512,512]{1,0:T(8,128)(2,1)S(1)}, bf16[512,512]{1,0:T(8,128)(2,1)}, u32[]{:S(2)}) copy-start(bf16[512,512]{1,0:T(8,128)(2,1)} %param.17) | copy-start | bytes 1572868
  101.9 4.9 %copy-start.6 = (s32[512]{0:T(512)S(1)}, s32[512]{0:T(512)}, u32[]{:S(2)}) copy-start(s32[512]{0:T(512)} %param.22) | copy-start | bytes 6148
  101.9 5.0 %copy-start.7 = (s32[1,16]{1,0:T(1,128)S(1)}, s32[1,16]{1,0:T(1,128)}, u32[]{:S(2)}) copy-start(s32[1,16]{1,0:T(1,128)} %param.25) | copy-start | bytes 196
  107.9 38.1 %copy-start.3 = (bf16[512,512]{1,0:T(8,128)(2,1)S(1)}, bf16[512,512]{1,0:T(8,128)(2,1)}, u32[]{:S(2)}) copy-start(bf16[512,512]{1,0:T(8,128)(2,1)} %param.15) | copy-start | bytes 1572868
  107.9 14.4 %all-to-all-start = ((s32[16,1,32]{2,1,0:T(1,128)}), s32[16,1,32]{2,1,0:T(1,128)S(1)}, u32[]{:S(2)}, u32[]{:S(2)}) async-start(s32[16,1,32]{2,1,0:T(1,128)} %compare_select_fusion), calls=%async_computation | async-start | bytes 16384 | tf_op jit(solution)/shard_map/all_to_all | solution.py:101
  122.4 18.8 %all-to-all-start.4 = ((bf16[8,64,512]{2,1,0:T(8,128)(2,1)}), bf16[8,64,512]{2,1,0:T(8,128)(2,1)S(1)}, u32[]{:S(2)}, u32[]{:S(2)}) async-start(bf16[8,64,512]{2,1,0:T(8,128)(2,1)} %bitcast.12), calls=%async_computation.4 | async-start | bytes 1048576 | tf_op jit(solution)/shard_map/all_to_all | solution.py:122
  141.2 0.8 copy-start.4
  142.0 23.8 %all-to-all-start.1 = ((bf16[16,32,512]{2,1,0:T(8,128)(2,1)}), bf16[16,32,512]{2,1,0:T(8,128)(2,1)S(1)}, u32[]{:S(2)}, u32[]{:S(2)}) async-start(bf16[16,32,512]{2,1,0:T(8,128)(2,1)} %bitcast.5), calls=%async_computation.1 | async-start | bytes 1048576 | tf_op jit(solution)/shard_map/all_to_all | solution.py:94
  145.9 61.7 %all-reduce.5.cloned.1.call-start = ((), (), s32[]{:S(2)}) async-start(), calls=%async_computation.7 | async-start | bytes 1048576 | tf_op jit(solution)/shard_map/psum | solution.py:145
  163.1 66.5 %all-reduce.3.cloned.1.call-start = ((), (), s32[]{:S(2)}) async-start(), calls=%async_computation.6 | async-start | bytes 2097152 | tf_op jit(solution)/shard_map/psum | solution.py:110
  211.1 22.3 %all-to-all-start.5 = ((bf16[8,64,512]{2,1,0:T(8,128)(2,1)}), bf16[8,64,512]{2,1,0:T(8,128)(2,1)S(1)}, u32[]{:S(2)}, u32[]{:S(2)}) async-start(bf16[8,64,512]{2,1,0:T(8,128)(2,1)} %bitcast.14), calls=%async_computation.5 | async-start | bytes 1048576 | tf_op jit(solution)/shard_map/all_to_all | solution.py:150
  215.7 24.6 %copy-start.5 = (s32[1,512]{1,0:T(1,128)S(1)}, s32[1,512]{1,0:T(1,128)}, u32[]{:S(2)}) copy-start(s32[1,512]{1,0:T(1,128)} %param.24) | copy-start | bytes 6148
  233.3 23.6 %all-to-all-start.2 = ((bf16[16,32,512]{2,1,0:T(8,128)(2,1)}), bf16[16,32,512]{2,1,0:T(8,128)(2,1)}, u32[]{:S(2)}, u32[]{:S(2)}) async-start(bf16[16,32,512]{2,1,0:T(8,128)(2,1)} %bitcast.7), calls=%async_computation.2 | async-start | bytes 1048576 | tf_op jit(solution)/shard_map/all_to_all | solution.py:113
  242.2 18.0 %copy-start.1 = (bf16[512,1536]{1,0:T(8,128)(2,1)S(1)}, bf16[512,1536]{1,0:T(8,128)(2,1)}, u32[]{:S(2)}) copy-start(bf16[512,1536]{1,0:T(8,128)(2,1)} %param.16) | copy-start | bytes 4718596
Sparse Core Ops, SparseCore 0:
  163.2 44.3 all-reduce.4
  209.9 19.5 all-reduce.2
where the time goes:
time: 269 us; the launch traced here: 267 us
  waiting for transfers between devices  81.6 us (30%)
  local copies, waits for them, and re-layouts  60.7 us (23%)
  matrix products  54.1 us (20%)
  starting transfers between devices  32.6 us (12%)
  between operations  14.3 us (5%)
  blocking collectives  12.8 us (5%)
  other arithmetic  11.1 us (4%)
    psum x1, waiting for transfers between devices, on_device(): lax.psum(prod_part.astype(jnp.bfloat16), 'rev').astype(jnp.float32)  40.3 us
    sub x1, matrix products, encode(): scores = scores - jnp.max(scores, axis=-1, keepdims=True)  18.4 us
    reshape x1, local copies, waits for them, and re-layouts, encode(): qkv_rows = qkv_rows.reshape(count_rows, NCOL, 3, HEADS, HD)  16.2 us
    all_to_all x1, waiting for transfers between devices, on_device(): lax.all_to_all(prod_msgs.reshape(prod_owners, prod_slots, H), ('cust', 'p...  14.4 us
    psum x1, waiting for transfers between devices, on_device(): cust_sum, cust_total = lax.psum((cust_part, cust_counts), 'prod')  13.9 us
    all_to_all x1, waiting for transfers between devices, on_device(): lax.all_to_all(cust_reply.reshape(cust_owners, cust_slots, H), ('rev', 'c...  10.8 us
    psum x1, blocking collectives, on_device(): lax.psum(prod_counts.astype(jnp.bfloat16), 'rev').astype(jnp.float32)  10.3 us
    slice x1, local copies, waits for them, and re-layouts, encode(): val_part = qkv_rows[:, :, 2]  8.76 us
  transfers between devices with their start and end apart: 8, of which 5 were waited for; matrix products, arithmetic and copies ran while one was open for 44% of the time, Pallas kernels for 0%

commit v1 on v0

v1 whole, which is shorter than its diff:
```python
import functools
import math

import jax
import jax.numpy as jnp
from jax import lax
from jax.experimental import pallas as pl
from jax.experimental.pallas import tpu as pltpu
from jax.sharding import PartitionSpec as P

H = 512
HEADS = 8
NCOL = 4
HD = 64
EPS = 1e-06
BF = jnp.bfloat16
F32 = jnp.float32
VMEM = pl.BlockSpec(memory_space=pltpu.VMEM)
SMEM = pl.BlockSpec(memory_space=pltpu.SMEM)
PARAMS = pltpu.CompilerParams(vmem_limit_bytes=48 * 1024 * 1024)


def rms_norm(vector):
    return vector * lax.rsqrt(jnp.mean(vector * vector, axis=-1, keepdims=True) + EPS)


def dot(left, right):
    return jnp.dot(left, right, preferred_element_type=F32)


def dot_t(left, right):
    return lax.dot_general(left, right, (((0,), (0,)), ((), ())), preferred_element_type=F32)


def one_hot(rows, first, ids):
    row = lax.broadcasted_iota(jnp.int32, (rows, ids.shape[1]), 0) + first
    return jnp.where(row == ids, 1.0, 0.0).astype(BF)


def iota(shape, dim):
    return lax.broadcasted_iota(jnp.int32, shape, dim)


def encode_rows(tokens, w_qkv, w_out, pair_sum, spread):
    rows = tokens[0].shape[0]
    stacked = jnp.concatenate(tokens, axis=0)
    qkv = dot(stacked, w_qkv).astype(BF)
    part = lambda c, which: qkv[c * rows:(c + 1) * rows, which * H:(which + 1) * H]
    lane = iota((rows, 128), 1)
    scores = jnp.zeros((rows, 128), F32)
    for j in range(NCOL):
        for i in range(NCOL):
            both = dot(part(i, 0) * part(j, 1), pair_sum)
            scores = jnp.where(lane // HEADS == j * NCOL + i, both, scores)
    scores = scores * (1.0 / math.sqrt(HD))
    top = jnp.maximum(scores, pltpu.roll(scores, 64, 1))
    top = jnp.maximum(top, pltpu.roll(top, 32, 1))
    expon = jnp.exp(scores - top)
    total = expon + pltpu.roll(expon, 64, 1)
    total = total + pltpu.roll(total, 32, 1)
    weight = (expon / total).astype(BF)
    weights = dot(weight, spread)
    attended = jnp.zeros((rows, H), F32)
    pooled = jnp.zeros((rows, H), F32)
    for j in range(NCOL):
        attended = attended + weights[:, j * H:(j + 1) * H] * part(j, 2).astype(F32)
        pooled = pooled + tokens[j].astype(F32)
    pooled = pooled + dot((attended * (1.0 / NCOL)).astype(BF), w_out) * NCOL
    return rms_norm(pooled * (1.0 / NCOL)).astype(BF)


def encode_kernel(parts, cols_ref, w_qkv_ref, w_out_ref, w_msg_ref, order_ref, h_ref, *rest):
    cust_refs, prod_refs = rest[:parts], rest[parts:2 * parts]
    held, pair_sum, spread = rest[2 * parts:]
    step = pl.program_id(0)
    rows = cols_ref.shape[0]

    @pl.when(step == 0)
    def _():
        pair_sum[...] = jnp.where(
            iota((H, 128), 0) // HD == iota((H, 128), 1) % HEADS, 1.0, 0.0
        ).astype(BF)
        lane, wide = iota((128, NCOL * H), 0), iota((128, NCOL * H), 1)
        spread[...] = jnp.where(
            (lane // (NCOL * HEADS) == wide // H) & (lane % HEADS == wide % H // HD), 1.0, 0.0
        ).astype(BF)

    tokens = [cols_ref[:, c * H:(c + 1) * H] for c in range(NCOL)]
    review_h = encode_rows(tokens, w_qkv_ref[...], w_out_ref[...], pair_sum[...], spread[...])
    h_ref[...] = review_h
    held[pl.ds(pl.multiple_of(step * rows, rows), rows), :] = review_h

    @pl.when(step == pl.num_programs(0) - 1)
    def _():
        message = dot(held[...], w_msg_ref[...]).astype(BF)
        for refs, which in ((cust_refs, 0), (prod_refs, 1)):
            for s, ref in enumerate(refs):
                size = ref.shape[0]
                pick = one_hot(size, s * size, order_ref[which:which + 1, :])
                ref[...] = dot(pick, message[:, which * H:(which + 1) * H]).astype(BF)


def encode(review_cols, w_qkv, w_out, w_msg, order, parts):
    count = review_cols.shape[0]
    rows = min(count, 128)
    piece = jax.ShapeDtypeStruct((count // parts, H), BF)
    fixed = lambda a: pl.BlockSpec(a.shape, lambda i: (0, 0))
    out = pl.pallas_call(
        functools.partial(encode_kernel, parts),
        grid=(count // rows,),
        in_specs=[pl.BlockSpec((rows, NCOL * H), lambda i: (i, 0))]
        + [fixed(a) for a in (w_qkv, w_out, w_msg, order)],
        out_specs=[pl.BlockSpec((rows, H), lambda i: (i, 0))] + [fixed(piece)] * (2 * parts),
        out_shape=[jax.ShapeDtypeStruct((count, H), BF)] + [piece] * (2 * parts),
        scratch_shapes=[
            pltpu.VMEM((count, H), BF),
            pltpu.VMEM((H, 128), BF),
            pltpu.VMEM((128, NCOL * H), BF),
        ],
        compiler_params=PARAMS,
        name="encode",
    )(review_cols, w_qkv, w_out, w_msg, order)
    return out[0], out[1:1 + parts], out[1 + parts:]


def refresh(totals, counts, states, weight):
    average = (totals / jnp.sqrt(jnp.maximum(counts, 1.0))).astype(BF)
    update = dot(average, weight)
    update = update * (1.0 / (1.0 + jnp.exp(-update)))
    return rms_norm(states.astype(F32) + update).astype(BF)


def count_of(pick):
    return jnp.sum(pick.astype(F32), axis=1, keepdims=True)


def cust_kernel(own_ref, peer_ref, ids_ref, state_ref, w_ref, new_ref, reply_ref):
    size = state_ref.shape[0]
    own = one_hot(size, 0, ids_ref[0:1, :])
    peer = one_hot(size, 0, ids_ref[1:2, :])
    totals = dot(own, own_ref[...]) + dot(peer, peer_ref[...])
    new = refresh(totals, count_of(own) + count_of(peer), state_ref[...], w_ref[...])
    new_ref[...] = new
    reply_ref[...] = dot_t(own, new).astype(BF)


def update_cust(own, peer, ids, state, weight):
    return pl.pallas_call(
        cust_kernel,
        in_specs=[VMEM] * 5,
        out_specs=[VMEM] * 2,
        out_shape=[jax.ShapeDtypeStruct(state.shape, BF), jax.ShapeDtypeStruct(own.shape, BF)],
        compiler_params=PARAMS,
        name="update_cust",
    )(own, peer, ids, state, weight)


def prod_sum_kernel(slabs, me_ref, own_ref, peer_ref, ids_ref, first_ref, *rest):
    size = first_ref.shape[0]
    rows = jnp.concatenate([own_ref[...], peer_ref[...]], axis=0)
    for t, ref in enumerate((first_ref,) + rest):
        owner = lax.rem(me_ref[0] - t + slabs, slabs)
        part = dot(one_hot(size, owner * size, ids_ref[...]), rows)
        ref[...] = part.astype(ref.dtype)


def sum_prod(me, own, peer, ids, size, slabs):
    piece = lambda kind: jax.ShapeDtypeStruct((size // slabs, H), kind)
    return pl.pallas_call(
        functools.partial(prod_sum_kernel, slabs),
        in_specs=[SMEM] + [VMEM] * 3,
        out_specs=[VMEM] * slabs,
        out_shape=[piece(F32)] + [piece(BF)] * (slabs - 1),
        compiler_params=PARAMS,
        name="sum_prod",
    )(me, own, peer, ids)


def prod_update_kernel(slabs, me_ref, ids_ref, state_ref, w_ref, *rest):
    new_ref = rest[slabs]
    size = new_ref.shape[0]
    first = pl.multiple_of(me_ref[0] * size, size)
    totals = rest[0][...]
    for ref in rest[1:slabs]:
        totals = totals + ref[...].astype(F32)
    counts = jnp.zeros((size, 1), F32)
    for r in range(ids_ref.shape[0]):
        row = iota((size, ids_ref.shape[1]), 0) + first
        counts = counts + jnp.sum(
            jnp.where(row == ids_ref[r:r + 1, :], 1.0, 0.0), axis=1, keepdims=True
        )
    new_ref[...] = refresh(totals, counts, state_ref[pl.ds(first, size), :], w_ref[...])


def update_prod(me, ids, state, weight, pieces):
    slabs = len(pieces)
    return pl.pallas_call(
        functools.partial(prod_update_kernel, slabs),
        in_specs=[SMEM] + [VMEM] * (3 + slabs),
        out_specs=VMEM,
        out_shape=jax.ShapeDtypeStruct(pieces[0].shape, BF),
        compiler_params=PARAMS,
        name="update_prod",
    )(me, ids, state, weight, *pieces)


def prod_reply_kernel(slabs, me_ref, ids_ref, *rest):
    pieces, (new_ref, own_ref, peer_ref) = rest[:slabs], rest[slabs:]
    size = pieces[0].shape[0]
    reply = None
    for t, ref in enumerate(pieces):
        first = pl.multiple_of(lax.rem(me_ref[0] + t, slabs) * size, size)
        new_ref[pl.ds(first, size), :] = ref[...]
        term = dot_t(one_hot(size, first, ids_ref[...]), ref[...])
        reply = term if reply is None else reply + term
    half = own_ref.shape[0]
    own_ref[...] = reply[:half].astype(BF)
    peer_ref[...] = reply[half:].astype(BF)


def reply_prod(me, ids, pieces):
    slabs = len(pieces)
    size, rows = pieces[0].shape[0] * slabs, ids.shape[1]
    return pl.pallas_call(
        functools.partial(prod_reply_kernel, slabs),
        in_specs=[SMEM] + [VMEM] * (1 + slabs),
        out_specs=[VMEM] * 3,
        out_shape=[jax.ShapeDtypeStruct((size, H), BF)]
        + [jax.ShapeDtypeStruct((rows // 2, H), BF)] * 2,
        compiler_params=PARAMS,
        name="reply_prod",
    )(me, ids, *pieces)


def finish_kernel(parts, order_ref, h_ref, w_ref, *rest):
    out_ref = rest[2 * parts]
    total = h_ref[...].astype(F32)
    for which in range(2):
        rows = jnp.concatenate([ref[...] for ref in rest[which * parts:(which + 1) * parts]], axis=0)
        pick = one_hot(rows.shape[0], 0, order_ref[which:which + 1, :])
        back = dot_t(pick, rows).astype(BF)
        total = total + dot(back, w_ref[which * H:(which + 1) * H, :])
    out_ref[...] = rms_norm(total).astype(BF)


def finish(order, review_h, w_back, cust_back, prod_back):
    parts = len(cust_back)
    return pl.pallas_call(
        functools.partial(finish_kernel, parts),
        in_specs=[VMEM] * (3 + 2 * parts),
        out_specs=VMEM,
        out_shape=jax.ShapeDtypeStruct(review_h.shape, BF),
        compiler_params=PARAMS,
        name="finish",
    )(order, review_h, w_back, *cust_back, *prod_back)


def shift(value, axis, by):
    size = lax.axis_size(axis)
    if by % size == 0:
        return value
    return lax.ppermute(value, axis, [(i, (i + by) % size) for i in range(size)])


def turn(array, by, axis):
    twice = jnp.concatenate([array, array], axis=axis)
    return lax.dynamic_slice_in_dim(twice, by, array.shape[axis], axis=axis)


def on_device(
    review_cols,
    cust_state,
    prod_state,
    w_qkv,
    w_out,
    w_msg,
    w_cust_up,
    w_prod_up,
    w_back,
    cust_slot,
    prod_slot,
    prod_pos,
    live_count,
):
    rows = review_cols.shape[0]
    nr, nz, nc = lax.axis_size("rev"), lax.axis_size("cust"), lax.axis_size("prod")
    mr, mz, mc = lax.axis_index("rev"), lax.axis_index("cust"), lax.axis_index("prod")
    cs = rows // (nr * nz)
    ps = rows // (nz * nc)
    me = mr.reshape(1)

    slot = jnp.arange(rows, dtype=jnp.int32)
    block = slot // cs
    position = prod_pos.reshape(rows)
    pblock = position // ps
    cust_order = (
        (mz - block % nz) % nz * (nr * cs) + (mr - block // nz) % nr * cs + slot % cs
    )
    prod_order = (
        (mz - pblock // nc) % nz * (nc * ps) + (mc - pblock % nc) % nc * ps + position % ps
    )
    order = jnp.stack([cust_order, prod_order])

    live = (slot % cs) < jnp.repeat(live_count.reshape(nr * nz), cs)
    cust_ids = jnp.where(live, cust_slot, -1)
    prod_ids = jnp.where(live, prod_slot, -1)
    prod_ids = jnp.sum(
        jnp.where(position[None, :] == slot[:, None], prod_ids[None, :], 0), axis=1
    )
    ids = lax.all_gather(jnp.stack([cust_ids, prod_ids]), ("rev", "cust", "prod"))
    ids = ids.reshape(nr, nz, nc, 2, rows)
    cust_in = lax.dynamic_slice_in_dim(ids[:, :, :, 0], (mr * nz + mz) * cs, cs, axis=3)
    cust_in = turn(turn(turn(cust_in, mr, 0), mz, 1), mc, 2)
    cust_in = cust_in.transpose(2, 0, 1, 3).reshape(nc, rows)
    prod_in = lax.dynamic_slice_in_dim(ids[:, :, :, 1], (mz * nc + mc) * ps, ps, axis=3)
    prod_all = prod_in.reshape(nr, rows)
    prod_in = lax.dynamic_index_in_dim(prod_in, mr, 0, keepdims=False)
    prod_in = turn(turn(prod_in, mz, 0), mc, 1).transpose(1, 0, 2).reshape(1, rows)

    review_h, cust_parts, prod_parts = encode(review_cols, w_qkv, w_out, w_msg, order, nz)

    prod_got = [shift(prod_parts[s], "cust", -s) for s in range(nz)]
    own = jnp.concatenate([p[:ps] for p in prod_got], axis=0)
    peer = shift(jnp.concatenate([p[ps:] for p in prod_got], axis=0), "prod", -1)
    pieces = sum_prod(me, own, peer, prod_in, prod_state.shape[0], nr)
    pieces = [shift(pieces[t], "rev", -t) for t in range(nr)]
    new_piece = update_prod(me, prod_all, prod_state, w_prod_up, pieces)
    new_pieces = [shift(new_piece, "rev", -t) for t in range(nr)]
    new_prod, own_reply, peer_reply = reply_prod(me, prod_in, new_pieces)
    peer_reply = shift(peer_reply, "prod", 1)
    prod_back = [
        shift(
            jnp.concatenate([own_reply[s * ps:(s + 1) * ps], peer_reply[s * ps:(s + 1) * ps]]),
            "cust",
            s,
        )
        for s in range(nz)
    ]

    cust_got = [shift(cust_parts[s], "cust", -s) for s in range(nz)]
    cust_got = [
        shift(jnp.concatenate([p[t * cs:(t + 1) * cs] for p in cust_got], axis=0), "rev", -t)
        for t in range(nr)
    ]
    own = jnp.concatenate(cust_got, axis=0)
    new_cust, reply = update_cust(own, shift(own, "prod", -1), cust_in, cust_state, w_cust_up)
    size = nz * cs
    reply = [shift(reply[t * size:(t + 1) * size], "rev", t) for t in range(nr)]
    cust_back = [
        shift(jnp.concatenate([p[s * cs:(s + 1) * cs] for p in reply], axis=0), "cust", s)
        for s in range(nz)
    ]

    review_out = finish(order, review_h, w_back, cust_back, prod_back)
    return (review_out, new_cust, new_prod)


def solution(mesh):
    every = P(("rev", "cust", "prod"))
    in_specs = (
        P(("rev", "cust", "prod"), None),
        P(("rev", "cust"), None),
        P(("cust", "prod"), None),
        P(),
        P(),
        P(),
        P(),
        P(),
        P(),
        every,
        every,
        P(("rev", "cust", "prod"), None),
        P(("rev", "cust", "prod"), None),
    )
    out_specs = (
        P(("rev", "cust", "prod"), None),
        P(("rev", "cust"), None),
        P(("cust", "prod"), None),
    )
    return jax.shard_map(
        on_device, mesh=mesh, in_specs=in_specs, out_specs=out_specs, check_vma=False
    )
```

time: 269 us -> 141 us (0.52)
  local copies, waits for them, and re-layouts: 60.7 us -> 4.76 us
  matrix products: 54.1 us -> 0 us
  waiting for transfers between devices: 81.6 us -> 35.4 us
  blocking collectives: 12.8 us -> 46.8 us
  Pallas kernels: 0 us -> 18.9 us
  between operations: 14.3 us -> 1.13 us
  other arithmetic: 11.1 us -> 1.28 us
    psum x2 -> x0, waiting for transfers between devices: 54.2 us -> none  [the longest x1 40.3 us: on_device(): lax.psum(prod_part.astype(jnp.bfloat16), 'rev').astype(jnp.float32)]
    all_gather x0 -> x1, blocking collectives: none -> 46.8 us  [on_device(): lax.all_gather(jnp.stack([cust_ids, prod_ids]), ('rev', 'cust', 'prod'))]
    dot_general x11 -> x0, matrix products: 35.6 us -> none  [the longest x1 8.41 us: encode(): jnp.einsum('rhij,rjhd->rihd', att_weight, val_part, preferred_element_typ...]
    ppermute x0 -> x27, waiting for transfers between devices: none -> 35.4 us  [shift(): lax.ppermute(value, axis, [(i, (i + by) % size) for i in range(size)])]
    all_to_all x6 -> x0, starting transfers between devices: 32.5 us -> none  [the longest x1 7.24 us: on_device(): lax.all_to_all(cust_ids, ('rev', 'cust'), split_axis=0, concat_axis=0, ti...]
    reshape x5 -> x4, local copies, waits for them, and re-layouts: 32.4 us -> 0.34 us  [the longest x1 0.09 us: on_device(): prod_all = prod_in.reshape(nr, rows)]
    ppermute x0 -> x27, starting transfers between devices: none -> 31.7 us  [shift(): lax.ppermute(value, axis, [(i, (i + by) % size) for i in range(size)])]
    all_to_all x6 -> x0, waiting for transfers between devices: 27.3 us -> none  [the longest x1 14.4 us: on_device(): lax.all_to_all(prod_msgs.reshape(prod_owners, prod_slots, H), ('cust', 'p...]
  transfers between devices with their start and end apart: 8 -> 27, of which waited for: 5 -> 13; matrix products, arithmetic and copies ran while one was open for 44% -> 1% of each run, Pallas kernels for 0% -> 3%
where the time goes in v1:
time: 141 us; the launch traced here: 140 us
  blocking collectives  46.8 us (33%)
  waiting for transfers between devices  35.4 us (25%)
  starting transfers between devices  31.7 us (22%)
  Pallas kernels  18.9 us (13%)
  local copies, waits for them, and re-layouts  4.76 us (3%)
    all_gather x1, blocking collectives, on_device(): lax.all_gather(jnp.stack([cust_ids, prod_ids]), ('rev', 'cust', 'prod'))  46.8 us
    ppermute x27, waiting for transfers between devices, shift(): lax.ppermute(value, axis, [(i, (i + by) % size) for i in range(size)])  35.4 us
    ppermute x27, starting transfers between devices, shift(): lax.ppermute(value, axis, [(i, (i + by) % size) for i in range(size)])  31.7 us
    pallas_call x1, Pallas kernels, encode(): pl.pallas_call(functools.partial(encode_kernel, parts), grid=(count // ro...  11.9 us
    unnamed x26, local copies, waits for them, and re-layouts  3.73 us
  transfers between devices with their start and end apart: 27, of which 13 were waited for; matrix products, arithmetic and copies ran while one was open for 1% of the time, Pallas kernels for 3%

profile of v1, /device:TPU:0, one launch (start us, length us, event | category | flops | bytes accessed | tf_op | source)
XLA Modules:
  0.0 139.9 jit_solution(9233132577583667408)
XLA Ops:
  0.6 0.8 fusion.7
  1.4 0.0 copy-start
  1.4 1.4 copy-done
  2.8 1.2 copy-done.2
  4.1 1.0 copy-done.3
  5.1 11.9 %encode.1 = (bf16[512,512]{1,0:T(8,128)(2,1)S(1)}, bf16[128,512]{1,0:T(8,128)(2,1)S(1)}, bf16[128,512]{1,0:T(8,128)(2,1)S(1)}, bf16[128,512]{1,0:T(8,128)(2,1)S(...) custom-call(bf16[512,2048]{1,0:T(8,128)(2,1)} %cols_ref.1, ...), custom_call_target="tpu_custom_call" | custom-call | tf_op jit(solution)/shard_map/encode/pallas_call | solution.py:108
  17.0 3.1 %collective-permute-start.2 = (bf16[128,512]{1,0:T(8,128)(2,1)S(1)}, bf16[128,512]{1,0:T(8,128)(2,1)S(1)}, u32[]{:S(2)}, u32[]{:S(2)}) collective-permute-start(bf16[128,512]{1,0:T(8,128)(2,1)S(1)} %get-tuple-element.25), channel_id=1, source_target_pairs={{0,2},{2,4},{4,6},{6,0},{1,3},{3,5},{5,7},{7,1},{8,10},{10,12},{12... | collective-permute-start | bytes 393224 | tf_op jit(solution)/shard_map/ppermute | solution.py:262
  20.1 2.6 %collective-permute-start.1 = (bf16[128,512]{1,0:T(8,128)(2,1)S(1)}, bf16[128,512]{1,0:T(8,128)(2,1)S(1)}, u32[]{:S(2)}, u32[]{:S(2)}) collective-permute-start(bf16[128,512]{1,0:T(8,128)(2,1)S(1)} %get-tuple-element.24), channel_id=1, source_target_pairs={{0,4},{2,6},{4,0},{6,2},{1,5},{3,7},{5,1},{7,3},{8,12},{10,14},{12... | collective-permute-start | bytes 393224 | tf_op jit(solution)/shard_map/ppermute | solution.py:262
  22.7 1.3 collective-permute-start
  24.0 0.7 collective-permute-start.15
  24.7 0.3 collective-permute-start.14
  25.1 0.1 broadcast_in_dim.22
  25.1 0.1 reshape.232
  25.2 0.2 select_reduce_fusion
  25.4 46.8 %all-gather.1 = s32[32,2,512]{2,1,0:T(2,128)S(1)} all-gather(s32[1,2,512]{2,1,0:T(2,128)S(1)} %add_bitcast_fusion), channel_id=2, replica_groups=mesh['rev'=4,'cust'=4,'prod'=2] {'rev','cust','prod'}, dimensions={0}, use_global_device_ids=true | all-gather | bytes 135168 | tf_op jit(solution)/shard_map/all_gather | solution.py:310
  72.2 0.1 fusion.33
  72.3 0.1 constant_dynamic-slice_fusion
  72.5 0.1 reshape.236.ids_ref
  72.6 0.1 dynamic-slice_reduce_fusion
  72.7 0.1 reshape.237.ids_ref
  72.8 0.1 constant_dynamic-slice_fusion.1
  72.9 0.1 collective-permute-start.13
  73.0 0.0 copy-start.4
  73.1 0.0 copy-start.5
  73.1 0.5 collective-permute-start.3
  73.7 1.1 collective-permute-start.4
  74.8 2.1 %collective-permute-start.5 = (bf16[128,512]{1,0:T(8,128)(2,1)S(1)}, bf16[128,512]{1,0:T(8,128)(2,1)S(1)}, u32[]{:S(2)}, u32[]{:S(2)}) collective-permute-start(bf16[128,512]{1,0:T(8,128)(2,1)S(1)} %pad_maximum_fusion.4), channel_id=1, source_target_pairs={{0,8},{8,16},{16,24},{24,0},{1,9},{9,17},{17,25},{25,1},{2,10},{10... | collective-permute-start | bytes 393224 | tf_op jit(solution)/shard_map/ppermute | solution.py:262
  76.9 1.8 %collective-permute-done.13 = bf16[128,512]{1,0:T(8,128)(2,1)S(1)} collective-permute-done((bf16[128,512]{1,0:T(8,128)(2,1)S(1)}, bf16[128,512]{1,0:T(8,128)(2,1)S(1)}, u32[]{:S(2)}, u32[]{:S(2)}) %collective-permute-start.13) | collective-permute-done | bytes 131104 | tf_op jit(solution)/shard_map/ppermute | solution.py:262
  78.8 0.1 collective-permute-start.16
  78.9 0.6 collective-permute-done.3
  79.5 0.0 copy-start.6
  79.5 0.8 collective-permute-done.16.peer_ref
  80.4 0.5 sum_prod.1
  80.8 2.6 %collective-permute-start.17 = (bf16[128,512]{1,0:T(8,128)(2,1)S(1)}, bf16[128,512]{1,0:T(8,128)(2,1)S(1)}, u32[]{:S(2)}, u32[]{:S(2)}) collective-permute-start(bf16[128,512]{1,0:T(8,128)(2,1)S(1)} %get-tuple-element.32), channel_id=1, source_target_pairs={{0,24},{8,0},{16,8},{24,16},{1,25},{9,1},{17,9},{25,17},{2,26},{10... | collective-permute-start | bytes 393224 | tf_op jit(solution)/shard_map/ppermute | solution.py:262
  83.4 1.5 %collective-permute-start.18 = (bf16[128,512]{1,0:T(8,128)(2,1)S(1)}, bf16[128,512]{1,0:T(8,128)(2,1)S(1)}, u32[]{:S(2)}, u32[]{:S(2)}) collective-permute-start(bf16[128,512]{1,0:T(8,128)(2,1)S(1)} %get-tuple-element.33), channel_id=1, source_target_pairs={{0,16},{8,24},{16,0},{24,8},{1,17},{9,25},{17,1},{25,9},{2,18},{10... | collective-permute-start | bytes 393224 | tf_op jit(solution)/shard_map/ppermute | solution.py:262
  85.0 0.9 collective-permute-start.19
  85.9 0.1 collective-permute-start.6
  86.0 1.3 collective-permute-done.17.rest_1_
  87.4 4.0 %collective-permute-done.18.rest_2_ = bf16[128,512]{1,0:T(8,128)(2,1)S(1)} collective-permute-done((bf16[128,512]{1,0:T(8,128)(2,1)S(1)}, bf16[128,512]{1,0:T(8,128)(2,1)S(1)}, u32[]{:S(2)}, u32[]{:S(2)}) %collective-permute-start.18) | collective-permute-done | bytes 131104 | tf_op jit(solution)/shard_map/ppermute | solution.py:262
  91.4 0.5 update_prod.1.rest_0_
  91.9 1.3 collective-permute-start.20
  93.3 0.6 collective-permute-start.21
  93.9 1.7 %collective-permute-start.22 = (bf16[128,512]{1,0:T(8,128)(2,1)S(1)}, bf16[128,512]{1,0:T(8,128)(2,1)S(1)}, u32[]{:S(2)}, u32[]{:S(2)}) collective-permute-start(bf16[128,512]{1,0:T(8,128)(2,1)S(1)} %update_prod.1.rest_0_), channel_id=1, source_target_pairs={{0,8},{8,16},{16,24},{24,0},{1,9},{9,17},{17,25},{25,1},{2,10},{10... | collective-permute-start | bytes 393224 | tf_op jit(solution)/shard_map/ppermute | solution.py:262
  95.6 0.1 reshape.234.ids_ref
  95.7 2.3 %collective-permute-done.20.rest_1_ = bf16[128,512]{1,0:T(8,128)(2,1)S(1)} collective-permute-done((bf16[128,512]{1,0:T(8,128)(2,1)S(1)}, bf16[128,512]{1,0:T(8,128)(2,1)S(1)}, u32[]{:S(2)}, u32[]{:S(2)}) %collective-permute-start.20) | collective-permute-done | bytes 131104 | tf_op jit(solution)/shard_map/ppermute | solution.py:262
  98.1 2.3 %collective-permute-done.21.rest_2_ = bf16[128,512]{1,0:T(8,128)(2,1)S(1)} collective-permute-done((bf16[128,512]{1,0:T(8,128)(2,1)S(1)}, bf16[128,512]{1,0:T(8,128)(2,1)S(1)}, u32[]{:S(2)}, u32[]{:S(2)}) %collective-permute-start.21) | collective-permute-done | bytes 131104 | tf_op jit(solution)/shard_map/ppermute | solution.py:262
  100.4 1.5 %reply_prod.1 = (bf16[512,512]{1,0:T(8,128)(2,1)}, bf16[256,512]{1,0:T(8,128)(2,1)S(1)}, bf16[256,512]{1,0:T(8,128)(2,1)S(1)}) custom-call(s32[1]{0:T(128)} %bitcast.8.me_ref, s32[1,512]{1,0:T(1,128)S(1)} %reshape.236.ids_ref, bf16[128,512]{1,0:T(8,128)(2,1)S(1)} %update_prod.1.rest_0_, bf16[128,512]{1,0:T(8,128)(2,1)S(1)} %collective-permute-done.20.rest_1_, ...), custom_call_target="tpu_custom_call" | custom-call | tf_op jit(solution)/shard_map/reply_prod/pallas_call | solution.py:224
  101.9 2.3 %update_cust.1 = (bf16[512,512]{1,0:T(8,128)(2,1)}, bf16[512,512]{1,0:T(8,128)(2,1)S(1)}) custom-call(bf16[512,512]{1,0:T(8,128)(2,1)S(1)} %constant_dynamic-update-slice_fusion.own_ref, bf16[512,512]{1,0:T(8,128)(2,1)S(1)} %collective-permute-done.6.peer_ref, s32[2,512]{1,0:T(2,128)S(1)} %reshape.234.ids_ref, bf16[512,512]{1,0:T(8,128)(2,1)S(1)} %copy-done.6, ...), custom_call_target="tpu_custom_call" | custom-call | tf_op jit(solution)/shard_map/update_cust/pallas_call | solution.py:148
  104.3 1.2 collective-permute-start.9
  105.5 0.6 collective-permute-start.8
  106.0 1.5 %collective-permute-start.7 = (bf16[128,512]{1,0:T(8,128)(2,1)S(1)}, bf16[128,512]{1,0:T(8,128)(2,1)S(1)}, u32[]{:S(2)}, u32[]{:S(2)}) collective-permute-start(bf16[128,512]{1,0:T(8,128)(2,1)S(1)} %get-tuple-element.43), channel_id=1, source_target_pairs={{0,8},{8,16},{16,24},{24,0},{1,9},{9,17},{17,25},{25,1},{2,10},{10... | collective-permute-start | bytes 393224 | tf_op jit(solution)/shard_map/ppermute | solution.py:262
  107.6 3.0 %collective-permute-done.9 = bf16[128,512]{1,0:T(8,128)(2,1)S(1)} collective-permute-done((bf16[128,512]{1,0:T(8,128)(2,1)S(1)}, bf16[128,512]{1,0:T(8,128)(2,1)S(1)}, u32[]{:S(2)}, u32[]{:S(2)}) %collective-permute-start.9) | collective-permute-done | bytes 131104 | tf_op jit(solution)/shard_map/ppermute | solution.py:262
  110.6 3.3 %collective-permute-done.8 = bf16[128,512]{1,0:T(8,128)(2,1)S(1)} collective-permute-done((bf16[128,512]{1,0:T(8,128)(2,1)S(1)}, bf16[128,512]{1,0:T(8,128)(2,1)S(1)}, u32[]{:S(2)}, u32[]{:S(2)}) %collective-permute-start.8) | collective-permute-done | bytes 131104 | tf_op jit(solution)/shard_map/ppermute | solution.py:262
  114.0 1.7 %collective-permute-start.10 = (bf16[128,512]{1,0:T(8,128)(2,1)S(1)}, bf16[128,512]{1,0:T(8,128)(2,1)S(1)}, u32[]{:S(2)}, u32[]{:S(2)}) collective-permute-start(bf16[128,512]{1,0:T(8,128)(2,1)S(1)} %pad_maximum_fusion.6), channel_id=1, source_target_pairs={{0,2},{2,4},{4,6},{6,0},{1,3},{3,5},{5,7},{7,1},{8,10},{10,12},{12... | collective-permute-start | bytes 393224 | tf_op jit(solution)/shard_map/ppermute | solution.py:262
  115.7 0.1 collective-permute-start.11
  115.8 2.4 %collective-permute-start.12 = (bf16[128,512]{1,0:T(8,128)(2,1)S(1)}, bf16[128,512]{1,0:T(8,128)(2,1)S(1)}, u32[]{:S(2)}, u32[]{:S(2)}) collective-permute-start(bf16[128,512]{1,0:T(8,128)(2,1)S(1)} %pad_maximum_fusion.8), channel_id=1, source_target_pairs={{0,6},{2,0},{4,2},{6,4},{1,7},{3,1},{5,3},{7,5},{8,14},{10,8},{12,... | collective-permute-start | bytes 393224 | tf_op jit(solution)/shard_map/ppermute | solution.py:262
  118.3 0.4 collective-permute-start.24
  118.7 2.3 %collective-permute-start.25 = (bf16[128,512]{1,0:T(8,128)(2,1)S(1)}, bf16[128,512]{1,0:T(8,128)(2,1)S(1)}, u32[]{:S(2)}, u32[]{:S(2)}) collective-permute-start(bf16[128,512]{1,0:T(8,128)(2,1)S(1)} %pad_maximum_fusion.11), channel_id=1, source_target_pairs={{0,4},{2,6},{4,0},{6,2},{1,5},{3,7},{5,1},{7,3},{8,12},{10,14},{12... | collective-permute-start | bytes 393224 | tf_op jit(solution)/shard_map/ppermute | solution.py:262
  121.0 1.3 collective-permute-done.10.rest_1_
  122.3 0.9 collective-permute-start.26
  123.2 7.4 %collective-permute-done.11.rest_2_ = bf16[128,512]{1,0:T(8,128)(2,1)S(1)} collective-permute-done((bf16[128,512]{1,0:T(8,128)(2,1)S(1)}, bf16[128,512]{1,0:T(8,128)(2,1)S(1)}, u32[]{:S(2)}, u32[]{:S(2)}) %collective-permute-start.11) | collective-permute-done | bytes 131104 | tf_op jit(solution)/shard_map/ppermute | solution.py:262
  130.6 0.1 collective-permute-done.24.rest_5_
  130.7 7.0 %collective-permute-done.25.rest_6_ = bf16[128,512]{1,0:T(8,128)(2,1)S(1)} collective-permute-done((bf16[128,512]{1,0:T(8,128)(2,1)S(1)}, bf16[128,512]{1,0:T(8,128)(2,1)S(1)}, u32[]{:S(2)}, u32[]{:S(2)}) %collective-permute-start.25) | collective-permute-done | bytes 131104 | tf_op jit(solution)/shard_map/ppermute | solution.py:262
  137.7 2.2 %finish.1 = bf16[512,512]{1,0:T(8,128)(2,1)} custom-call(s32[2,512]{1,0:T(2,128)S(1)} %pad_add_fusion.order_ref, bf16[512,512]{1,0:T(8,128)(2,1)S(1)} %get-tuple-element.21.h_ref, bf16[1024,512]{1,0:T(8,128)(2,1)S(1)} %copy-done.1, bf16[128,512]{1,0:T(8,128)(2,1)S(1)} %pad_maximum_fusion.5.rest_0_, bf16[128,512]{1,0:T(8,128)(2,1)S(1)} %collective-permute-done.10.rest_1_, ...), custom_call_target="tpu_custom_call" | custom-call | tf_op jit(solution)/shard_map/finish/pallas_call | solution.py:248
  (73 shorter events, 0.6 us)
Async XLA Ops:
  1.4 1.4 %copy-start = (bf16[512,1536]{1,0:T(8,128)(2,1)S(1)}, bf16[512,1536]{1,0:T(8,128)(2,1)}, u32[]{:S(2)}) copy-start(bf16[512,1536]{1,0:T(8,128)(2,1)} %w_qkv_ref.1) | copy-start | bytes 4718596
  2.8 1.2 copy-start.2
  4.0 1.0 copy-start.3
  5.1 20.0 %copy-start.11 = (s32[1,16]{1,0:T(1,128)S(1)}, s32[1,16]{1,0:T(1,128)}, u32[]{:S(2)}) copy-start(s32[1,16]{1,0:T(1,128)} %param.25) | copy-start | bytes 196
  5.1 20.1 %copy-start.9 = (s32[512]{0:T(512)S(1)}, s32[512]{0:T(512)}, u32[]{:S(2)}) copy-start(s32[512]{0:T(512)} %param.22) | copy-start | bytes 6148
  5.1 20.1 %copy-start.10 = (s32[512]{0:T(512)S(1)}, s32[512]{0:T(512)}, u32[]{:S(2)}) copy-start(s32[512]{0:T(512)} %param.23) | copy-start | bytes 6148
  5.1 20.1 %copy-start.8 = (s32[1,512]{1,0:T(1,128)S(1)}, s32[1,512]{1,0:T(1,128)}, u32[]{:S(2)}) copy-start(s32[1,512]{1,0:T(1,128)} %param.24) | copy-start | bytes 6148
  17.0 56.0 %collective-permute-start.2 = (bf16[128,512]{1,0:T(8,128)(2,1)S(1)}, bf16[128,512]{1,0:T(8,128)(2,1)S(1)}, u32[]{:S(2)}, u32[]{:S(2)}) collective-permute-start(bf16[128,512]{1,0:T(8,128)(2,1)S(1)} %get-tuple-element.25), channel_id=1, source_target_pairs={{0,2},{2,4},{4,6},{6,0},{1,3},{3,5},{5,7},{7,1},{8,10},{10,12},{12... | collective-permute-start | bytes 393224 | tf_op jit(solution)/shard_map/ppermute | solution.py:262
  20.1 52.9 %collective-permute-start.1 = (bf16[128,512]{1,0:T(8,128)(2,1)S(1)}, bf16[128,512]{1,0:T(8,128)(2,1)S(1)}, u32[]{:S(2)}, u32[]{:S(2)}) collective-permute-start(bf16[128,512]{1,0:T(8,128)(2,1)S(1)} %get-tuple-element.24), channel_id=1, source_target_pairs={{0,4},{2,6},{4,0},{6,2},{1,5},{3,7},{5,1},{7,3},{8,12},{10,14},{12... | collective-permute-start | bytes 393224 | tf_op jit(solution)/shard_map/ppermute | solution.py:262
  22.7 50.2 %collective-permute-start = (bf16[128,512]{1,0:T(8,128)(2,1)S(1)}, bf16[128,512]{1,0:T(8,128)(2,1)S(1)}, u32[]{:S(2)}, u32[]{:S(2)}) collective-permute-start(bf16[128,512]{1,0:T(8,128)(2,1)S(1)} %get-tuple-element.23), channel_id=1, source_target_pairs={{0,6},{2,0},{4,2},{6,4},{1,7},{3,1},{5,3},{7,5},{8,14},{10,8},{12,... | collective-permute-start | bytes 393224 | tf_op jit(solution)/shard_map/ppermute | solution.py:262
  24.0 50.8 %collective-permute-start.15 = (bf16[128,512]{1,0:T(8,128)(2,1)S(1)}, bf16[128,512]{1,0:T(8,128)(2,1)S(1)}, u32[]{:S(2)}, u32[]{:S(2)}) collective-permute-start(bf16[128,512]{1,0:T(8,128)(2,1)S(1)} %get-tuple-element.30), channel_id=1, source_target_pairs={{0,2},{2,4},{4,6},{6,0},{1,3},{3,5},{5,7},{7,1},{8,10},{10,12},{12... | collective-permute-start | bytes 393224 | tf_op jit(solution)/shard_map/ppermute | solution.py:262
  24.7 52.2 %collective-permute-start.14 = (bf16[128,512]{1,0:T(8,128)(2,1)S(1)}, bf16[128,512]{1,0:T(8,128)(2,1)S(1)}, u32[]{:S(2)}, u32[]{:S(2)}) collective-permute-start(bf16[128,512]{1,0:T(8,128)(2,1)S(1)} %get-tuple-element.29), channel_id=1, source_target_pairs={{0,4},{2,6},{4,0},{6,2},{1,5},{3,7},{5,1},{7,3},{8,12},{10,14},{12... | collective-permute-start | bytes 393224 | tf_op jit(solution)/shard_map/ppermute | solution.py:262
  72.9 5.8 %collective-permute-start.13 = (bf16[128,512]{1,0:T(8,128)(2,1)S(1)}, bf16[128,512]{1,0:T(8,128)(2,1)S(1)}, u32[]{:S(2)}, u32[]{:S(2)}) collective-permute-start(bf16[128,512]{1,0:T(8,128)(2,1)S(1)} %get-tuple-element.28), channel_id=1, source_target_pairs={{0,6},{2,0},{4,2},{6,4},{1,7},{3,1},{5,3},{7,5},{8,14},{10,8},{12,... | collective-permute-start | bytes 393224 | tf_op jit(solution)/shard_map/ppermute | solution.py:262
  73.0 18.4 %copy-start.4 = (bf16[512,512]{1,0:T(8,128)(2,1)S(1)}, bf16[512,512]{1,0:T(8,128)(2,1)}, u32[]{:S(2)}) copy-start(bf16[512,512]{1,0:T(8,128)(2,1)} %state_ref.3) | copy-start | bytes 1572868
  73.1 18.4 %copy-start.5 = (bf16[512,512]{1,0:T(8,128)(2,1)S(1)}, bf16[512,512]{1,0:T(8,128)(2,1)}, u32[]{:S(2)}) copy-start(bf16[512,512]{1,0:T(8,128)(2,1)} %w_ref.4) | copy-start | bytes 1572868
  73.1 6.4 %collective-permute-start.3 = (bf16[128,512]{1,0:T(8,128)(2,1)S(1)}, bf16[128,512]{1,0:T(8,128)(2,1)S(1)}, u32[]{:S(2)}, u32[]{:S(2)}) collective-permute-start(bf16[128,512]{1,0:T(8,128)(2,1)S(1)} %pad_maximum_fusion.2), channel_id=1, source_target_pairs={{0,24},{8,0},{16,8},{24,16},{1,25},{9,1},{17,9},{25,17},{2,26},{10... | collective-permute-start | bytes 393224 | tf_op jit(solution)/shard_map/ppermute | solution.py:262
  73.7 5.9 %collective-permute-start.4 = (bf16[128,512]{1,0:T(8,128)(2,1)S(1)}, bf16[128,512]{1,0:T(8,128)(2,1)S(1)}, u32[]{:S(2)}, u32[]{:S(2)}) collective-permute-start(bf16[128,512]{1,0:T(8,128)(2,1)S(1)} %pad_maximum_fusion.3), channel_id=1, source_target_pairs={{0,16},{8,24},{16,0},{24,8},{1,17},{9,25},{17,1},{25,9},{2,18},{10... | collective-permute-start | bytes 393224 | tf_op jit(solution)/shard_map/ppermute | solution.py:262
  74.8 11.1 %collective-permute-start.5 = (bf16[128,512]{1,0:T(8,128)(2,1)S(1)}, bf16[128,512]{1,0:T(8,128)(2,1)S(1)}, u32[]{:S(2)}, u32[]{:S(2)}) collective-permute-start(bf16[128,512]{1,0:T(8,128)(2,1)S(1)} %pad_maximum_fusion.4), channel_id=1, source_target_pairs={{0,8},{8,16},{16,24},{24,0},{1,9},{9,17},{17,25},{25,1},{2,10},{10... | collective-permute-start | bytes 393224 | tf_op jit(solution)/shard_map/ppermute | solution.py:262
  78.8 1.6 %collective-permute-start.16 = (bf16[256,512]{1,0:T(8,128)(2,1)S(1)}, bf16[256,512]{1,0:T(8,128)(2,1)S(1)}, u32[]{:S(2)}, u32[]{:S(2)}) collective-permute-start(bf16[256,512]{1,0:T(8,128)(2,1)S(1)} %pad_maximum_fusion.1), channel_id=1, source_target_pairs={{0,1},{1,0},{2,3},{3,2},{4,5},{5,4},{6,7},{7,6},{8,9},{9,8},{10,11... | collective-permute-start | bytes 786440 | tf_op jit(solution)/shard_map/ppermute | solution.py:262
  79.5 22.4 %copy-start.6 = (bf16[512,512]{1,0:T(8,128)(2,1)S(1)}, bf16[512,512]{1,0:T(8,128)(2,1)}, u32[]{:S(2)}) copy-start(bf16[512,512]{1,0:T(8,128)(2,1)} %state_ref.2) | copy-start | bytes 1572868
  79.5 22.4 %copy-start.7 = (bf16[512,512]{1,0:T(8,128)(2,1)S(1)}, bf16[512,512]{1,0:T(8,128)(2,1)}, u32[]{:S(2)}) copy-start(bf16[512,512]{1,0:T(8,128)(2,1)} %w_ref.3) | copy-start | bytes 1572868
  80.8 6.5 %collective-permute-start.17 = (bf16[128,512]{1,0:T(8,128)(2,1)S(1)}, bf16[128,512]{1,0:T(8,128)(2,1)S(1)}, u32[]{:S(2)}, u32[]{:S(2)}) collective-permute-start(bf16[128,512]{1,0:T(8,128)(2,1)S(1)} %get-tuple-element.32), channel_id=1, source_target_pairs={{0,24},{8,0},{16,8},{24,16},{1,25},{9,1},{17,9},{25,17},{2,26},{10... | collective-permute-start | bytes 393224 | tf_op jit(solution)/shard_map/ppermute | solution.py:262
  83.4 8.0 %collective-permute-start.18 = (bf16[128,512]{1,0:T(8,128)(2,1)S(1)}, bf16[128,512]{1,0:T(8,128)(2,1)S(1)}, u32[]{:S(2)}, u32[]{:S(2)}) collective-permute-start(bf16[128,512]{1,0:T(8,128)(2,1)S(1)} %get-tuple-element.33), channel_id=1, source_target_pairs={{0,16},{8,24},{16,0},{24,8},{1,17},{9,25},{17,1},{25,9},{2,18},{10... | collective-permute-start | bytes 393224 | tf_op jit(solution)/shard_map/ppermute | solution.py:262
  85.0 6.4 %collective-permute-start.19 = (bf16[128,512]{1,0:T(8,128)(2,1)S(1)}, bf16[128,512]{1,0:T(8,128)(2,1)S(1)}, u32[]{:S(2)}, u32[]{:S(2)}) collective-permute-start(bf16[128,512]{1,0:T(8,128)(2,1)S(1)} %get-tuple-element.34), channel_id=1, source_target_pairs={{0,8},{8,16},{16,24},{24,0},{1,9},{9,17},{17,25},{25,1},{2,10},{10... | collective-permute-start | bytes 393224 | tf_op jit(solution)/shard_map/ppermute | solution.py:262
  85.9 16.0 %collective-permute-start.6 = (bf16[512,512]{1,0:T(8,128)(2,1)S(1)}, bf16[512,512]{1,0:T(8,128)(2,1)S(1)}, u32[]{:S(2)}, u32[]{:S(2)}) collective-permute-start(bf16[512,512]{1,0:T(8,128)(2,1)S(1)} %constant_dynamic-update-slice_fusion.own_ref), channel_id=1, source_target_pairs={{0,1},{1,0},{2,3},{3,2},{4,5},{5,4},{6,7},{7,6},{8,9},{9,8},{10,11... | collective-permute-start | bytes 1572872 | tf_op jit(solution)/shard_map/ppermute | solution.py:262
  91.9 6.1 %collective-permute-start.20 = (bf16[128,512]{1,0:T(8,128)(2,1)S(1)}, bf16[128,512]{1,0:T(8,128)(2,1)S(1)}, u32[]{:S(2)}, u32[]{:S(2)}) collective-permute-start(bf16[128,512]{1,0:T(8,128)(2,1)S(1)} %update_prod.1.rest_0_), channel_id=1, source_target_pairs={{0,24},{8,0},{16,8},{24,16},{1,25},{9,1},{17,9},{25,17},{2,26},{10... | collective-permute-start | bytes 393224 | tf_op jit(solution)/shard_map/ppermute | solution.py:262
  93.3 7.1 %collective-permute-start.21 = (bf16[128,512]{1,0:T(8,128)(2,1)S(1)}, bf16[128,512]{1,0:T(8,128)(2,1)S(1)}, u32[]{:S(2)}, u32[]{:S(2)}) collective-permute-start(bf16[128,512]{1,0:T(8,128)(2,1)S(1)} %update_prod.1.rest_0_), channel_id=1, source_target_pairs={{0,16},{8,24},{16,0},{24,8},{1,17},{9,25},{17,1},{25,9},{2,18},{10... | collective-permute-start | bytes 393224 | tf_op jit(solution)/shard_map/ppermute | solution.py:262
  93.9 6.5 %collective-permute-start.22 = (bf16[128,512]{1,0:T(8,128)(2,1)S(1)}, bf16[128,512]{1,0:T(8,128)(2,1)S(1)}, u32[]{:S(2)}, u32[]{:S(2)}) collective-permute-start(bf16[128,512]{1,0:T(8,128)(2,1)S(1)} %update_prod.1.rest_0_), channel_id=1, source_target_pairs={{0,8},{8,16},{16,24},{24,0},{1,9},{9,17},{17,25},{25,1},{2,10},{10... | collective-permute-start | bytes 393224 | tf_op jit(solution)/shard_map/ppermute | solution.py:262
  101.9 16.4 %collective-permute-start.23 = (bf16[256,512]{1,0:T(8,128)(2,1)S(1)}, bf16[256,512]{1,0:T(8,128)(2,1)S(1)}, u32[]{:S(2)}, u32[]{:S(2)}) collective-permute-start(bf16[256,512]{1,0:T(8,128)(2,1)S(1)} %get-tuple-element.36), channel_id=1, source_target_pairs={{0,1},{1,0},{2,3},{3,2},{4,5},{5,4},{6,7},{7,6},{8,9},{9,8},{10,11... | collective-permute-start | bytes 786440 | tf_op jit(solution)/shard_map/ppermute | solution.py:262
  104.2 33.5 %copy-start.1 = (bf16[1024,512]{1,0:T(8,128)(2,1)S(1)}, bf16[1024,512]{1,0:T(8,128)(2,1)}, u32[]{:S(2)}) copy-start(bf16[1024,512]{1,0:T(8,128)(2,1)} %w_ref.5) | copy-start | bytes 3145732
  104.3 6.3 %collective-permute-start.9 = (bf16[128,512]{1,0:T(8,128)(2,1)S(1)}, bf16[128,512]{1,0:T(8,128)(2,1)S(1)}, u32[]{:S(2)}, u32[]{:S(2)}) collective-permute-start(bf16[128,512]{1,0:T(8,128)(2,1)S(1)} %get-tuple-element.44), channel_id=1, source_target_pairs={{0,24},{8,0},{16,8},{24,16},{1,25},{9,1},{17,9},{25,17},{2,26},{10... | collective-permute-start | bytes 393224 | tf_op jit(solution)/shard_map/ppermute | solution.py:262
  105.5 8.4 %collective-permute-start.8 = (bf16[128,512]{1,0:T(8,128)(2,1)S(1)}, bf16[128,512]{1,0:T(8,128)(2,1)S(1)}, u32[]{:S(2)}, u32[]{:S(2)}) collective-permute-start(bf16[128,512]{1,0:T(8,128)(2,1)S(1)} %get-tuple-element.45), channel_id=1, source_target_pairs={{0,16},{8,24},{16,0},{24,8},{1,17},{9,25},{17,1},{25,9},{2,18},{10... | collective-permute-start | bytes 393224 | tf_op jit(solution)/shard_map/ppermute | solution.py:262
  106.0 7.9 %collective-permute-start.7 = (bf16[128,512]{1,0:T(8,128)(2,1)S(1)}, bf16[128,512]{1,0:T(8,128)(2,1)S(1)}, u32[]{:S(2)}, u32[]{:S(2)}) collective-permute-start(bf16[128,512]{1,0:T(8,128)(2,1)S(1)} %get-tuple-element.43), channel_id=1, source_target_pairs={{0,8},{8,16},{16,24},{24,0},{1,9},{9,17},{17,25},{25,1},{2,10},{10... | collective-permute-start | bytes 393224 | tf_op jit(solution)/shard_map/ppermute | solution.py:262
  114.0 8.3 %collective-permute-start.10 = (bf16[128,512]{1,0:T(8,128)(2,1)S(1)}, bf16[128,512]{1,0:T(8,128)(2,1)S(1)}, u32[]{:S(2)}, u32[]{:S(2)}) collective-permute-start(bf16[128,512]{1,0:T(8,128)(2,1)S(1)} %pad_maximum_fusion.6), channel_id=1, source_target_pairs={{0,2},{2,4},{4,6},{6,0},{1,3},{3,5},{5,7},{7,1},{8,10},{10,12},{12... | collective-permute-start | bytes 393224 | tf_op jit(solution)/shard_map/ppermute | solution.py:262
  115.7 14.9 %collective-permute-start.11 = (bf16[128,512]{1,0:T(8,128)(2,1)S(1)}, bf16[128,512]{1,0:T(8,128)(2,1)S(1)}, u32[]{:S(2)}, u32[]{:S(2)}) collective-permute-start(bf16[128,512]{1,0:T(8,128)(2,1)S(1)} %pad_maximum_fusion.7), channel_id=1, source_target_pairs={{0,4},{2,6},{4,0},{6,2},{1,5},{3,7},{5,1},{7,3},{8,12},{10,14},{12... | collective-permute-start | bytes 393224 | tf_op jit(solution)/shard_map/ppermute | solution.py:262
  115.8 14.8 %collective-permute-start.12 = (bf16[128,512]{1,0:T(8,128)(2,1)S(1)}, bf16[128,512]{1,0:T(8,128)(2,1)S(1)}, u32[]{:S(2)}, u32[]{:S(2)}) collective-permute-start(bf16[128,512]{1,0:T(8,128)(2,1)S(1)} %pad_maximum_fusion.8), channel_id=1, source_target_pairs={{0,6},{2,0},{4,2},{6,4},{1,7},{3,1},{5,3},{7,5},{8,14},{10,8},{12,... | collective-permute-start | bytes 393224 | tf_op jit(solution)/shard_map/ppermute | solution.py:262
  118.3 12.4 %collective-permute-start.24 = (bf16[128,512]{1,0:T(8,128)(2,1)S(1)}, bf16[128,512]{1,0:T(8,128)(2,1)S(1)}, u32[]{:S(2)}, u32[]{:S(2)}) collective-permute-start(bf16[128,512]{1,0:T(8,128)(2,1)S(1)} %pad_maximum_fusion.10), channel_id=1, source_target_pairs={{0,2},{2,4},{4,6},{6,0},{1,3},{3,5},{5,7},{7,1},{8,10},{10,12},{12... | collective-permute-start | bytes 393224 | tf_op jit(solution)/shard_map/ppermute | solution.py:262
  118.7 19.0 %collective-permute-start.25 = (bf16[128,512]{1,0:T(8,128)(2,1)S(1)}, bf16[128,512]{1,0:T(8,128)(2,1)S(1)}, u32[]{:S(2)}, u32[]{:S(2)}) collective-permute-start(bf16[128,512]{1,0:T(8,128)(2,1)S(1)} %pad_maximum_fusion.11), channel_id=1, source_target_pairs={{0,4},{2,6},{4,0},{6,2},{1,5},{3,7},{5,1},{7,3},{8,12},{10,14},{12... | collective-permute-start | bytes 393224 | tf_op jit(solution)/shard_map/ppermute | solution.py:262
  122.3 15.4 %collective-permute-start.26 = (bf16[128,512]{1,0:T(8,128)(2,1)S(1)}, bf16[128,512]{1,0:T(8,128)(2,1)S(1)}, u32[]{:S(2)}, u32[]{:S(2)}) collective-permute-start(bf16[128,512]{1,0:T(8,128)(2,1)S(1)} %pad_maximum_fusion.12), channel_id=1, source_target_pairs={{0,6},{2,0},{4,2},{6,4},{1,7},{3,1},{5,3},{7,5},{8,14},{10,8},{12,... | collective-permute-start | bytes 393224 | tf_op jit(solution)/shard_map/ppermute | solution.py:262

commit v2 on v1

v2 whole, which is shorter than its diff:
```python
import functools
import math

import jax
import jax.numpy as jnp
from jax import lax
from jax.experimental import pallas as pl
from jax.experimental.pallas import tpu as pltpu
from jax.sharding import PartitionSpec as P

H = 512
HEADS = 8
NCOL = 4
HD = 64
EPS = 1e-06
BF = jnp.bfloat16
F32 = jnp.float32
ID_ROWS = 16
VMEM = pl.BlockSpec(memory_space=pltpu.VMEM)
HBM = pl.BlockSpec(memory_space=pl.ANY)
SMEM = pl.BlockSpec(memory_space=pltpu.SMEM)
PARAMS = pltpu.CompilerParams(vmem_limit_bytes=48 * 1024 * 1024)


def rms_norm(vector):
    return vector * lax.rsqrt(jnp.mean(vector * vector, axis=-1, keepdims=True) + EPS)


def dot(left, right):
    return jnp.dot(left, right, preferred_element_type=F32)


def dot_t(left, right):
    return lax.dot_general(left, right, (((0,), (0,)), ((), ())), preferred_element_type=F32)


def dot_nt(left, right):
    return lax.dot_general(left, right, (((1,), (1,)), ((), ())), preferred_element_type=F32)


def one_hot(rows, first, ids):
    row = lax.broadcasted_iota(jnp.int32, (rows, ids.shape[1]), 0) + first
    return jnp.where(row == ids, 1.0, 0.0).astype(BF)


def iota(shape, dim):
    return lax.broadcasted_iota(jnp.int32, shape, dim)


def encode_rows(tokens, w_qkv, w_out, pair_sum, spread, before):
    rows = tokens[0].shape[0]
    stacked = jnp.concatenate(tokens, axis=0)
    part = []
    for which in range(3):
        before(which)
        made = dot(stacked, w_qkv[:, which * H:(which + 1) * H]).astype(BF)
        part.append([made[c * rows:(c + 1) * rows] for c in range(NCOL)])
    query, key, value = part
    lane = iota((rows, 128), 1)
    scores = jnp.zeros((rows, 128), F32)
    for j in range(NCOL):
        both = dot(jnp.concatenate([query[i] * key[j] for i in range(NCOL)], axis=0), pair_sum)
        for i in range(NCOL):
            scores = jnp.where(lane >> 3 == j * NCOL + i, both[i * rows:(i + 1) * rows], scores)
    scores = scores * (1.0 / math.sqrt(HD))
    top = jnp.maximum(scores, pltpu.roll(scores, 64, 1))
    top = jnp.maximum(top, pltpu.roll(top, 32, 1))
    expon = jnp.exp(scores - top)
    total = expon + pltpu.roll(expon, 64, 1)
    total = total + pltpu.roll(total, 32, 1)
    weight = (expon / total).astype(BF).astype(F32)
    attended = jnp.zeros((rows, H), F32)
    pooled = jnp.zeros((rows, H), F32)
    for j in range(NCOL):
        turned = pltpu.roll(weight, (128 - NCOL * HEADS * j) % 128, 1).astype(BF)
        attended = attended + dot(turned, spread) * value[j].astype(F32)
        pooled = pooled + tokens[j].astype(F32)
    before(3)
    mixed = dot((attended * (1.0 / NCOL)).astype(BF), w_out[...])
    return rms_norm(pooled * (1.0 / NCOL) + mixed).astype(BF)


def split_ids(ids):
    row = iota((ID_ROWS, ids.shape[1]), 0)
    halves = jnp.where(row == 0, ids >> 5, jnp.where(row == 1, ids & 31, 0))
    return halves.astype(F32).astype(BF)


def encode_kernel(parts, rows, x_hbm, w_qkv_hbm, w_out_hbm, w_msg_hbm, order_ref, h_ref, *rest):
    cust_refs, prod_refs = rest[:parts], rest[parts:2 * parts]
    x_ref, w_qkv, w_out, w_msg, sem = rest[2 * parts:]
    chunks = x_hbm.shape[0] // rows
    copy = pltpu.make_async_copy
    x_copies = [
        copy(x_hbm.at[pl.ds(c * rows, rows)], x_ref.at[pl.ds(c * rows, rows)], sem.at[c])
        for c in range(chunks)
    ]
    w_copies = [
        copy(w_qkv_hbm.at[:, pl.ds(k * H, H)], w_qkv.at[:, pl.ds(k * H, H)], sem.at[chunks + k])
        for k in range(3)
    ]
    w_copies.append(copy(w_out_hbm, w_out, sem.at[chunks + 3]))
    last = copy(w_msg_hbm, w_msg, sem.at[chunks + 4])
    x_copies[0].start()
    w_copies[0].start()
    w_copies[1].start()
    pair_sum = jnp.where(iota((H, 128), 0) >> 6 == (iota((H, 128), 1) & 7), 1.0, 0.0).astype(BF)
    spread = jnp.where(
        (iota((128, H), 0) < NCOL * HEADS) & ((iota((128, H), 0) & 7) == iota((128, H), 1) >> 6),
        1.0,
        0.0,
    ).astype(BF)

    def first_before(which):
        w_copies[which].wait()
        if which == 0:
            w_copies[2].start()
            for x_copy in x_copies[1:]:
                x_copy.start()
        if which == 1:
            w_copies[3].start()
            last.start()

    for c in range(chunks):
        x_copies[c].wait()
        at = slice(c * rows, (c + 1) * rows)
        tokens = [x_ref[at, k * H:(k + 1) * H] for k in range(NCOL)]
        before = first_before if c == 0 else lambda which: None
        h_ref[at, :] = encode_rows(tokens, w_qkv, w_out, pair_sum, spread, before)
    last.wait()
    message = dot(h_ref[...], w_msg[...]).astype(BF)
    for refs, which in ((cust_refs, 0), (prod_refs, 1)):
        ids = split_ids(order_ref[2 + which:3 + which, :])
        for s, ref in enumerate(refs):
            size = ref.shape[0] - ID_ROWS
            pick = one_hot(size, s * size, order_ref[which:which + 1, :])
            ref[:size, :] = dot(pick, message[:, which * H:(which + 1) * H]).astype(BF)
            ref[size:, :] = jnp.zeros((ID_ROWS, H), BF)
            ref[size:, :size] = dot_nt(ids, pick).astype(BF)


def encode(review_cols, w_qkv, w_out, w_msg, order, parts):
    count = review_cols.shape[0]
    rows = min(count, 256)
    piece = jax.ShapeDtypeStruct((count // parts + ID_ROWS, H), BF)
    out = pl.pallas_call(
        functools.partial(encode_kernel, parts, rows),
        in_specs=[HBM] * 4 + [VMEM],
        out_specs=[VMEM] * (1 + 2 * parts),
        out_shape=[jax.ShapeDtypeStruct((count, H), BF)] + [piece] * (2 * parts),
        scratch_shapes=[pltpu.VMEM(a.shape, BF) for a in (review_cols, w_qkv, w_out, w_msg)]
        + [pltpu.SemaphoreType.DMA((count // rows + 5,))],
        compiler_params=PARAMS,
        name="encode",
    )(review_cols, w_qkv, w_out, w_msg, order)
    return out[0], out[1:1 + parts], out[1 + parts:]


def refresh(totals, counts, states, weight):
    average = (totals / jnp.sqrt(jnp.maximum(counts, 1.0))).astype(BF)
    update = dot(average, weight)
    update = update * (1.0 / (1.0 + jnp.exp(-update)))
    return rms_norm(states.astype(F32) + update).astype(BF)


def count_of(pick):
    return jnp.sum(pick.astype(F32), axis=1, keepdims=True)


def cust_kernel(groups, own_ref, peer_ref, ids_ref, state_ref, w_ref, new_ref, reply_ref):
    size = state_ref.shape[0]
    held = own_ref.shape[0] // groups
    totals, counts = jnp.zeros((size, H), F32), jnp.zeros((size, 1), F32)
    for which, ref in ((1, peer_ref), (0, own_ref)):
        rows = jnp.concatenate(
            [ref[t * held:(t + 1) * held - ID_ROWS, :] for t in range(groups)], axis=0
        )
        pick = one_hot(size, 0, ids_ref[which:which + 1, :])
        totals = totals + dot(pick, rows)
        counts = counts + count_of(pick)
    new = refresh(totals, counts, state_ref[...], w_ref[...])
    new_ref[...] = new
    reply_ref[...] = dot_t(pick, new).astype(BF)


def update_cust(groups, own, peer, ids, state, weight):
    return pl.pallas_call(
        functools.partial(cust_kernel, groups),
        in_specs=[VMEM] * 5,
        out_specs=[VMEM] * 2,
        out_shape=[
            jax.ShapeDtypeStruct(state.shape, BF),
            jax.ShapeDtypeStruct((ids.shape[1], H), BF),
        ],
        compiler_params=PARAMS,
        name="update_cust",
    )(own, peer, ids, state, weight)


def prod_sum_kernel(slabs, me_ref, own_ref, peer_ref, ids_ref, *pieces):
    size = pieces[0].shape[0] - ID_ROWS
    rows = jnp.concatenate([own_ref[...], peer_ref[:own_ref.shape[0], :]], axis=0)
    ones = jnp.ones((ID_ROWS, rows.shape[0]), BF)
    row = iota((ID_ROWS, size), 0)
    for t, ref in enumerate(pieces):
        owner = lax.rem(me_ref[0] - t + slabs, slabs)
        pick = one_hot(size, owner * size, ids_ref[...])
        counts = dot_nt(ones, pick).astype(jnp.int32)
        halves = jnp.where(row == 0, counts >> 5, jnp.where(row == 1, counts & 31, 0))
        ref[:size, :] = dot(pick, rows).astype(ref.dtype)
        ref[size:, :] = jnp.zeros((ID_ROWS, H), ref.dtype)
        ref[size:, :size] = halves.astype(F32).astype(ref.dtype)


def sum_prod(me, own, peer, ids, size, slabs):
    piece = lambda kind: jax.ShapeDtypeStruct((size // slabs + ID_ROWS, H), kind)
    return pl.pallas_call(
        functools.partial(prod_sum_kernel, slabs),
        in_specs=[SMEM] + [VMEM] * 3,
        out_specs=[VMEM] * slabs,
        out_shape=[piece(F32)] + [piece(BF)] * (slabs - 1),
        compiler_params=PARAMS,
        name="sum_prod",
    )(me, own, peer, ids)


def prod_update_kernel(slabs, me_ref, state_ref, w_ref, *rest):
    new_ref = rest[slabs]
    size = new_ref.shape[0]
    first = pl.multiple_of(me_ref[0] * size, size)
    totals = sum(ref[:size, :].astype(F32) for ref in rest[:slabs])
    halves = sum(ref[size:, :size].astype(F32) for ref in rest[:slabs])
    count_row = halves[0:1, :] * 32.0 + halves[1:2, :]
    diagonal = iota((size, size), 0) == iota((size, size), 1)
    counts = jnp.sum(jnp.where(diagonal, count_row, 0.0), axis=1, keepdims=True)
    new_ref[...] = refresh(totals, counts, state_ref[pl.ds(first, size), :], w_ref[...])


def update_prod(me, state, weight, pieces):
    slabs = len(pieces)
    return pl.pallas_call(
        functools.partial(prod_update_kernel, slabs),
        in_specs=[SMEM] + [VMEM] * (2 + slabs),
        out_specs=VMEM,
        out_shape=jax.ShapeDtypeStruct((state.shape[0] // slabs, H), BF),
        compiler_params=PARAMS,
        name="update_prod",
    )(me, state, weight, *pieces)


def prod_reply_kernel(slabs, me_ref, ids_ref, *rest):
    pieces, (new_ref, own_ref, peer_ref) = rest[:slabs], rest[slabs:]
    size = pieces[0].shape[0]
    reply = None
    for t, ref in enumerate(pieces):
        first = pl.multiple_of(lax.rem(me_ref[0] + t, slabs) * size, size)
        new_ref[pl.ds(first, size), :] = ref[...]
        term = dot_t(one_hot(size, first, ids_ref[...]), ref[...])
        reply = term if reply is None else reply + term
    half = own_ref.shape[0]
    own_ref[...] = reply[:half].astype(BF)
    peer_ref[...] = reply[half:].astype(BF)


def reply_prod(me, ids, pieces):
    slabs = len(pieces)
    size, rows = pieces[0].shape[0] * slabs, ids.shape[1]
    return pl.pallas_call(
        functools.partial(prod_reply_kernel, slabs),
        in_specs=[SMEM] + [VMEM] * (1 + slabs),
        out_specs=[VMEM] * 3,
        out_shape=[jax.ShapeDtypeStruct((size, H), BF)]
        + [jax.ShapeDtypeStruct((rows // 2, H), BF)] * 2,
        compiler_params=PARAMS,
        name="reply_prod",
    )(me, ids, *pieces)


def finish_kernel(parts, order_ref, h_ref, w_ref, *rest):
    out_ref = rest[2 * parts]
    total = h_ref[...].astype(F32)
    for which in range(2):
        rows = jnp.concatenate([ref[...] for ref in rest[which * parts:(which + 1) * parts]], axis=0)
        pick = one_hot(rows.shape[0], 0, order_ref[which:which + 1, :])
        back = dot_t(pick, rows).astype(BF)
        total = total + dot(back, w_ref[which * H:(which + 1) * H, :])
    out_ref[...] = rms_norm(total).astype(BF)


def finish(order, review_h, w_back, cust_back, prod_back):
    parts = len(cust_back)
    return pl.pallas_call(
        functools.partial(finish_kernel, parts),
        in_specs=[VMEM] * (3 + 2 * parts),
        out_specs=VMEM,
        out_shape=jax.ShapeDtypeStruct(review_h.shape, BF),
        compiler_params=PARAMS,
        name="finish",
    )(order, review_h, w_back, *cust_back, *prod_back)


def shift(value, axis, by):
    size = lax.axis_size(axis)
    if by % size == 0:
        return value
    return lax.ppermute(value, axis, [(i, (i + by) % size) for i in range(size)])


def read_ids(rows):
    rows = rows[:2].astype(F32)
    return (rows[0:1] * 32.0 + rows[1:2]).astype(jnp.int32) - 1


def with_ids(rows, ids):
    return jnp.concatenate([rows, jnp.pad(ids, ((0, 0), (0, H - ids.shape[1])))], axis=0)


def on_device(
    review_cols,
    cust_state,
    prod_state,
    w_qkv,
    w_out,
    w_msg,
    w_cust_up,
    w_prod_up,
    w_back,
    cust_slot,
    prod_slot,
    prod_pos,
    live_count,
):
    rows = review_cols.shape[0]
    nr, nz, nc = lax.axis_size("rev"), lax.axis_size("cust"), lax.axis_size("prod")
    mr, mz, mc = lax.axis_index("rev"), lax.axis_index("cust"), lax.axis_index("prod")
    cs = rows // (nr * nz)
    ps = rows // (nz * nc)
    me = mr.reshape(1)

    slot = jnp.arange(rows, dtype=jnp.int32)
    block = slot // cs
    position = prod_pos.reshape(rows)
    pblock = position // ps
    cust_order = (
        (mz - block % nz) % nz * (nr * cs) + (mr - block // nz) % nr * cs + slot % cs
    )
    prod_order = (
        (mz - pblock // nc) % nz * (nc * ps) + (mc - pblock % nc) % nc * ps + position % ps
    )
    live = (slot % cs) < jnp.repeat(live_count.reshape(nr * nz), cs)
    order = jnp.stack(
        [
            cust_order,
            prod_order,
            jnp.where(live, cust_slot + 1, 0),
            jnp.where(live, prod_slot + 1, 0),
        ]
    )
    review_h, cust_parts, prod_parts = encode(review_cols, w_qkv, w_out, w_msg, order, nz)

    got = [shift(prod_parts[s], "cust", -s) for s in range(nz)]
    half = lambda u: jnp.concatenate([p[u * ps:(u + 1) * ps] for p in got], axis=0)
    half_ids = lambda u: jnp.concatenate(
        [p[nc * ps:, u * ps:(u + 1) * ps] for p in got], axis=1
    )
    own, peer = half(0), shift(with_ids(half(1), half_ids(1)), "prod", -1)
    prod_in = jnp.concatenate(
        [read_ids(half_ids(0)), read_ids(peer[nz * ps:, :nz * ps])], axis=1
    )
    pieces = sum_prod(me, own, peer, prod_in, prod_state.shape[0], nr)
    pieces = [shift(pieces[t], "rev", -t) for t in range(nr)]
    new_piece = update_prod(me, prod_state, w_prod_up, pieces)
    new_pieces = [shift(new_piece, "rev", -t) for t in range(nr)]
    new_prod, own_reply, peer_reply = reply_prod(me, prod_in, new_pieces)
    peer_reply = shift(peer_reply, "prod", 1)
    prod_back = [
        shift(
            jnp.concatenate([own_reply[s * ps:(s + 1) * ps], peer_reply[s * ps:(s + 1) * ps]]),
            "cust",
            s,
        )
        for s in range(nz)
    ]

    got = [shift(cust_parts[s], "cust", -s) for s in range(nz)]
    group = lambda t: jnp.concatenate([p[t * cs:(t + 1) * cs] for p in got], axis=0)
    group_ids = lambda t: jnp.concatenate(
        [p[nr * cs:, t * cs:(t + 1) * cs] for p in got], axis=1
    )
    got_groups = [shift(with_ids(group(t), group_ids(t)), "rev", -t) for t in range(nr)]
    own = jnp.concatenate(got_groups, axis=0)
    peer = shift(own, "prod", -1)
    size = nz * cs
    held = size + ID_ROWS
    cust_in = jnp.concatenate(
        [
            jnp.concatenate(
                [read_ids(a[t * held + size:(t + 1) * held, :size]) for t in range(nr)], axis=1
            )
            for a in (own, peer)
        ],
        axis=0,
    )
    new_cust, reply = update_cust(nr, own, peer, cust_in, cust_state, w_cust_up)
    reply = [shift(reply[t * size:(t + 1) * size], "rev", t) for t in range(nr)]
    cust_back = [
        shift(jnp.concatenate([p[s * cs:(s + 1) * cs] for p in reply], axis=0), "cust", s)
        for s in range(nz)
    ]

    review_out = finish(order, review_h, w_back, cust_back, prod_back)
    return (review_out, new_cust, new_prod)


def solution(mesh):
    every = P(("rev", "cust", "prod"))
    in_specs = (
        P(("rev", "cust", "prod"), None),
        P(("rev", "cust"), None),
        P(("cust", "prod"), None),
        P(),
        P(),
        P(),
        P(),
        P(),
        P(),
        every,
        every,
        P(("rev", "cust", "prod"), None),
        P(("rev", "cust", "prod"), None),
    )
    out_specs = (
        P(("rev", "cust", "prod"), None),
        P(("rev", "cust"), None),
        P(("cust", "prod"), None),
    )
    return jax.shard_map(
        on_device, mesh=mesh, in_specs=in_specs, out_specs=out_specs, check_vma=False
    )
```

time: 141 us -> 108 us (0.77)
  blocking collectives: 46.8 us -> 0 us
  waiting for transfers between devices: 35.4 us -> 43.2 us
  starting transfers between devices: 31.7 us -> 36.6 us
    all_gather x1 -> x0, blocking collectives: 46.8 us -> none  [on_device(): lax.all_gather(jnp.stack([cust_ids, prod_ids]), ('rev', 'cust', 'prod'))]
    ppermute x27, waiting for transfers between devices: 35.4 us -> 43.2 us  [shift(): lax.ppermute(value, axis, [(i, (i + by) % size) for i in range(size)])]
    ppermute x27, starting transfers between devices: 31.7 us -> 36.6 us  [shift(): lax.ppermute(value, axis, [(i, (i + by) % size) for i in range(size)])]
    unnamed x26 -> x23, local copies, waits for them, and re-layouts: 3.73 us -> 3.76 us
  transfers between devices with their start and end apart: 27 -> 27, of which waited for: 13 -> 13; matrix products, arithmetic and copies ran while one was open for 1% -> 1% of each run, Pallas kernels for 3% -> 5%
where the time goes in v2:
time: 108 us; the launch traced here: 107 us
  waiting for transfers between devices  43.2 us (40%)
  starting transfers between devices  36.6 us (34%)
  Pallas kernels  18.6 us (17%)
  local copies, waits for them, and re-layouts  5.33 us (5%)
  other arithmetic  2.18 us (2%)
  between operations  1.08 us (1%)
    ppermute x27, waiting for transfers between devices, shift(): lax.ppermute(value, axis, [(i, (i + by) % size) for i in range(size)])  43.2 us
    ppermute x27, starting transfers between devices, shift(): lax.ppermute(value, axis, [(i, (i + by) % size) for i in range(size)])  36.6 us
    pallas_call x1, Pallas kernels, encode(): pl.pallas_call(functools.partial(encode_kernel, parts, rows), in_specs=[H...  11.5 us
    unnamed x23, local copies, waits for them, and re-layouts  3.76 us
    pallas_call x1, Pallas kernels, update_cust(): pl.pallas_call(functools.partial(cust_kernel, groups), in_specs=[VMEM] *...  2.32 us
    pallas_call x1, Pallas kernels, finish(): pl.pallas_call(functools.partial(finish_kernel, parts), in_specs=[VMEM] *...  2.21 us
  transfers between devices with their start and end apart: 27, of which 13 were waited for; matrix products, arithmetic and copies ran while one was open for 1% of the time, Pallas kernels for 5%

profile of v2, /device:TPU:0, one launch (start us, length us, event | category | flops | bytes accessed | tf_op | source)
XLA Modules:
  0.0 106.9 jit_solution(3772292573636188056)
XLA Ops:
  0.6 0.7 broadcast_in_dim.6
  1.4 0.1 reshape.214
  1.4 0.7 add_select_fusion.2
  2.1 0.8 fusion.28
  2.9 1.4 %copy-done = bf16[512,1536]{1,0:T(8,128)(2,1)S(1)} copy-done((bf16[512,1536]{1,0:T(8,128)(2,1)S(1)}, bf16[512,1536]{1,0:T(8,128)(2,1)}, u32[]{:S(2)}) %copy-start) | copy-done | bytes 1572888
  4.3 1.2 %copy-done.1 = bf16[512,1024]{1,0:T(8,128)(2,1)S(1)} copy-done((bf16[512,1024]{1,0:T(8,128)(2,1)S(1)}, bf16[512,1024]{1,0:T(8,128)(2,1)}, u32[]{:S(2)}) %copy-start.1) | copy-done | bytes 1048600
  5.6 1.0 copy-done.3
  6.6 11.5 %encode.1 = (bf16[512,512]{1,0:T(8,128)(2,1)S(1)}, bf16[144,512]{1,0:T(8,128)(2,1)S(1)}, bf16[144,512]{1,0:T(8,128)(2,1)S(1)}, bf16[144,512]{1,0:T(8,128)(2,1)S(...) custom-call(bf16[512,2048]{1,0:T(8,128)(2,1)} %x_hbm.1, ...), custom_call_target="tpu_custom_call" | custom-call | tf_op jit(solution)/shard_map/encode/pallas_call | solution.py:146
  18.1 5.1 %collective-permute-start = (bf16[144,512]{1,0:T(8,128)(2,1)S(1)}, bf16[144,512]{1,0:T(8,128)(2,1)S(1)}, u32[]{:S(2)}, u32[]{:S(2)}) collective-permute-start(bf16[144,512]{1,0:T(8,128)(2,1)S(1)} %get-tuple-element.23), channel_id=1, source_target_pairs={{0,6},{2,0},{4,2},{6,4},{1,7},{3,1},{5,3},{7,5},{8,14},{10,8},{12,... | collective-permute-start | bytes 442376 | tf_op jit(solution)/shard_map/ppermute | solution.py:306
  23.3 1.0 collective-permute-start.2
  24.3 2.5 %collective-permute-start.15 = (bf16[144,512]{1,0:T(8,128)(2,1)S(1)}, bf16[144,512]{1,0:T(8,128)(2,1)S(1)}, u32[]{:S(2)}, u32[]{:S(2)}) collective-permute-start(bf16[144,512]{1,0:T(8,128)(2,1)S(1)} %get-tuple-element.30), channel_id=1, source_target_pairs={{0,2},{2,4},{4,6},{6,0},{1,3},{3,5},{5,7},{7,1},{8,10},{10,12},{12... | collective-permute-start | bytes 442376 | tf_op jit(solution)/shard_map/ppermute | solution.py:306
  26.7 0.9 collective-permute-start.14
  27.7 0.1 fusion.63
  27.8 0.1 fusion.59
  27.8 7.0 %collective-permute-done.2 = bf16[144,512]{1,0:T(8,128)(2,1)S(1)} collective-permute-done((bf16[144,512]{1,0:T(8,128)(2,1)S(1)}, bf16[144,512]{1,0:T(8,128)(2,1)S(1)}, u32[]{:S(2)}, u32[]{:S(2)}) %collective-permute-start.2) | collective-permute-done | bytes 147488 | tf_op jit(solution)/shard_map/ppermute | solution.py:306
  34.8 0.2 collective-permute-start.13
  35.1 0.1 fusion.66
  35.1 7.7 %collective-permute-done.1 = bf16[144,512]{1,0:T(8,128)(2,1)S(1)} collective-permute-done((bf16[144,512]{1,0:T(8,128)(2,1)S(1)}, bf16[144,512]{1,0:T(8,128)(2,1)S(1)}, u32[]{:S(2)}, u32[]{:S(2)}) %collective-permute-start.1) | collective-permute-done | bytes 147488 | tf_op jit(solution)/shard_map/ppermute | solution.py:306
  42.9 0.1 fusion.65
  42.9 0.1 fusion.64
  43.1 0.1 constant_dynamic-update-slice_fusion
  43.2 2.4 %collective-permute-start.3 = (bf16[144,512]{1,0:T(8,128)(2,1)S(1)}, bf16[144,512]{1,0:T(8,128)(2,1)S(1)}, u32[]{:S(2)}, u32[]{:S(2)}) collective-permute-start(bf16[144,512]{1,0:T(8,128)(2,1)S(1)} %constant_dynamic-update-slice_fusion), channel_id=1, source_target_pairs={{0,24},{8,0},{16,8},{24,16},{1,25},{9,1},{17,9},{25,17},{2,26},{10... | collective-permute-start | bytes 442376 | tf_op jit(solution)/shard_map/ppermute | solution.py:306
  45.6 0.1 constant_dynamic-update-slice_fusion.5
  45.7 0.5 collective-permute-start.4
  46.2 0.1 pad_maximum_fusion.9
  46.3 0.1 constant_dynamic-update-slice_fusion.10
  46.4 0.2 collective-permute-done.13
  46.5 1.5 %collective-permute-start.5 = (bf16[144,512]{1,0:T(8,128)(2,1)S(1)}, bf16[144,512]{1,0:T(8,128)(2,1)S(1)}, u32[]{:S(2)}, u32[]{:S(2)}) collective-permute-start(bf16[144,512]{1,0:T(8,128)(2,1)S(1)} %constant_dynamic-update-slice_fusion.10), channel_id=1, source_target_pairs={{0,8},{8,16},{16,24},{24,0},{1,9},{9,17},{17,25},{25,1},{2,10},{10... | collective-permute-start | bytes 442376 | tf_op jit(solution)/shard_map/ppermute | solution.py:306
  48.0 0.1 fusion.60
  48.1 0.1 fusion.61
  48.2 0.1 fusion.62
  48.3 0.1 constant_dynamic-update-slice_fusion.23
  48.4 0.1 fusion.50
  48.6 0.6 collective-permute-done.3
  49.2 4.2 %collective-permute-done.4 = bf16[144,512]{1,0:T(8,128)(2,1)S(1)} collective-permute-done((bf16[144,512]{1,0:T(8,128)(2,1)S(1)}, bf16[144,512]{1,0:T(8,128)(2,1)S(1)}, u32[]{:S(2)}, u32[]{:S(2)}) %collective-permute-start.4) | collective-permute-done | bytes 147488 | tf_op jit(solution)/shard_map/ppermute | solution.py:306
  53.4 0.1 collective-permute-start.6
  53.6 0.6 sum_prod.1
  54.1 0.8 collective-permute-start.17
  55.0 0.5 collective-permute-start.18
  55.5 1.8 %collective-permute-start.19 = (bf16[144,512]{1,0:T(8,128)(2,1)S(1)}, bf16[144,512]{1,0:T(8,128)(2,1)S(1)}, u32[]{:S(2)}, u32[]{:S(2)}) collective-permute-start(bf16[144,512]{1,0:T(8,128)(2,1)S(1)} %get-tuple-element.34), channel_id=1, source_target_pairs={{0,8},{8,16},{16,24},{24,0},{1,9},{9,17},{17,25},{25,1},{2,10},{10... | collective-permute-start | bytes 442376 | tf_op jit(solution)/shard_map/ppermute | solution.py:306
  57.3 3.6 %collective-permute-done.17.rest_1_ = bf16[144,512]{1,0:T(8,128)(2,1)S(1)} collective-permute-done((bf16[144,512]{1,0:T(8,128)(2,1)S(1)}, bf16[144,512]{1,0:T(8,128)(2,1)S(1)}, u32[]{:S(2)}, u32[]{:S(2)}) %collective-permute-start.17) | collective-permute-done | bytes 147488 | tf_op jit(solution)/shard_map/ppermute | solution.py:306
  60.8 0.5 collective-permute-done.18.rest_2_
  61.3 2.7 %collective-permute-done.19.rest_3_ = bf16[144,512]{1,0:T(8,128)(2,1)S(1)} collective-permute-done((bf16[144,512]{1,0:T(8,128)(2,1)S(1)}, bf16[144,512]{1,0:T(8,128)(2,1)S(1)}, u32[]{:S(2)}, u32[]{:S(2)}) %collective-permute-start.19) | collective-permute-done | bytes 147488 | tf_op jit(solution)/shard_map/ppermute | solution.py:306
  64.1 0.5 update_prod.1.rest_0_
  64.5 1.2 %collective-permute-start.20 = (bf16[128,512]{1,0:T(8,128)(2,1)S(1)}, bf16[128,512]{1,0:T(8,128)(2,1)S(1)}, u32[]{:S(2)}, u32[]{:S(2)}) collective-permute-start(bf16[128,512]{1,0:T(8,128)(2,1)S(1)} %update_prod.1.rest_0_), channel_id=1, source_target_pairs={{0,24},{8,0},{16,8},{24,16},{1,25},{9,1},{17,9},{25,17},{2,26},{10... | collective-permute-start | bytes 393224 | tf_op jit(solution)/shard_map/ppermute | solution.py:306
  65.8 0.6 collective-permute-start.21
  66.4 1.2 %collective-permute-start.22 = (bf16[128,512]{1,0:T(8,128)(2,1)S(1)}, bf16[128,512]{1,0:T(8,128)(2,1)S(1)}, u32[]{:S(2)}, u32[]{:S(2)}) collective-permute-start(bf16[128,512]{1,0:T(8,128)(2,1)S(1)} %update_prod.1.rest_0_), channel_id=1, source_target_pairs={{0,8},{8,16},{16,24},{24,0},{1,9},{9,17},{17,25},{25,1},{2,10},{10... | collective-permute-start | bytes 393224 | tf_op jit(solution)/shard_map/ppermute | solution.py:306
  67.6 2.4 %collective-permute-done.20.rest_1_ = bf16[128,512]{1,0:T(8,128)(2,1)S(1)} collective-permute-done((bf16[128,512]{1,0:T(8,128)(2,1)S(1)}, bf16[128,512]{1,0:T(8,128)(2,1)S(1)}, u32[]{:S(2)}, u32[]{:S(2)}) %collective-permute-start.20) | collective-permute-done | bytes 131104 | tf_op jit(solution)/shard_map/ppermute | solution.py:306
  70.0 3.8 %collective-permute-done.21.rest_2_ = bf16[128,512]{1,0:T(8,128)(2,1)S(1)} collective-permute-done((bf16[128,512]{1,0:T(8,128)(2,1)S(1)}, bf16[128,512]{1,0:T(8,128)(2,1)S(1)}, u32[]{:S(2)}, u32[]{:S(2)}) %collective-permute-start.21) | collective-permute-done | bytes 131104 | tf_op jit(solution)/shard_map/ppermute | solution.py:306
  73.7 1.5 %reply_prod.1 = (bf16[512,512]{1,0:T(8,128)(2,1)}, bf16[256,512]{1,0:T(8,128)(2,1)S(1)}, bf16[256,512]{1,0:T(8,128)(2,1)S(1)}) custom-call(s32[1]{0:T(128)} %bitcast.3.me_ref, s32[1,512]{1,0:T(1,128)S(1)} %pad_add_fusion.1.ids_ref, bf16[128,512]{1,0:T(8,128)(2,1)S(1)} %update_prod.1.rest_0_, bf16[128,512]{1,0:T(8,128)(2,1)S(1)} %collective-permute-done.20.rest_1_, ...), custom_call_target="tpu_custom_call" | custom-call | tf_op jit(solution)/shard_map/reply_prod/pallas_call | solution.py:268
  75.4 2.3 %update_cust.1 = (bf16[512,512]{1,0:T(8,128)(2,1)}, bf16[512,512]{1,0:T(8,128)(2,1)S(1)}) custom-call(bf16[576,512]{1,0:T(8,128)(2,1)S(1)} %constant_dynamic-update-slice_fusion.15.own_ref, bf16[576,512]{1,0:T(8,128)(2,1)S(1)} %collective-permute-done.6.peer_ref, s32[2,512]{1,0:T(2,128)S(1)} %add_add_fusion.ids_ref, bf16[512,512]{1,0:T(8,128)(2,1)S(1)} %copy-done.4, ...), custom_call_target="tpu_custom_call" | custom-call | tf_op jit(solution)/shard_map/update_cust/pallas_call | solution.py:187
  77.7 0.9 collective-permute-start.9
  78.7 0.9 collective-permute-start.8
  79.6 0.8 collective-permute-start.7
  80.4 2.9 %collective-permute-start.24 = (bf16[128,512]{1,0:T(8,128)(2,1)S(1)}, bf16[128,512]{1,0:T(8,128)(2,1)S(1)}, u32[]{:S(2)}, u32[]{:S(2)}) collective-permute-start(bf16[128,512]{1,0:T(8,128)(2,1)S(1)} %pad_maximum_fusion.6), channel_id=1, source_target_pairs={{0,2},{2,4},{4,6},{6,0},{1,3},{3,5},{5,7},{7,1},{8,10},{10,12},{12... | collective-permute-start | bytes 393224 | tf_op jit(solution)/shard_map/ppermute | solution.py:306
  83.3 1.7 %collective-permute-start.25 = (bf16[128,512]{1,0:T(8,128)(2,1)S(1)}, bf16[128,512]{1,0:T(8,128)(2,1)S(1)}, u32[]{:S(2)}, u32[]{:S(2)}) collective-permute-start(bf16[128,512]{1,0:T(8,128)(2,1)S(1)} %pad_maximum_fusion.7), channel_id=1, source_target_pairs={{0,4},{2,6},{4,0},{6,2},{1,5},{3,7},{5,1},{7,3},{8,12},{10,14},{12... | collective-permute-start | bytes 393224 | tf_op jit(solution)/shard_map/ppermute | solution.py:306
  85.1 2.7 %collective-permute-start.26 = (bf16[128,512]{1,0:T(8,128)(2,1)S(1)}, bf16[128,512]{1,0:T(8,128)(2,1)S(1)}, u32[]{:S(2)}, u32[]{:S(2)}) collective-permute-start(bf16[128,512]{1,0:T(8,128)(2,1)S(1)} %pad_maximum_fusion.8), channel_id=1, source_target_pairs={{0,6},{2,0},{4,2},{6,4},{1,7},{3,1},{5,3},{7,5},{8,14},{10,8},{12,... | collective-permute-start | bytes 393224 | tf_op jit(solution)/shard_map/ppermute | solution.py:306
  87.9 1.6 %collective-permute-start.10 = (bf16[128,512]{1,0:T(8,128)(2,1)S(1)}, bf16[128,512]{1,0:T(8,128)(2,1)S(1)}, u32[]{:S(2)}, u32[]{:S(2)}) collective-permute-start(bf16[128,512]{1,0:T(8,128)(2,1)S(1)} %pad_maximum_fusion.2), channel_id=1, source_target_pairs={{0,2},{2,4},{4,6},{6,0},{1,3},{3,5},{5,7},{7,1},{8,10},{10,12},{12... | collective-permute-start | bytes 393224 | tf_op jit(solution)/shard_map/ppermute | solution.py:306
  89.6 1.8 %collective-permute-start.11 = (bf16[128,512]{1,0:T(8,128)(2,1)S(1)}, bf16[128,512]{1,0:T(8,128)(2,1)S(1)}, u32[]{:S(2)}, u32[]{:S(2)}) collective-permute-start(bf16[128,512]{1,0:T(8,128)(2,1)S(1)} %pad_maximum_fusion.3), channel_id=1, source_target_pairs={{0,4},{2,6},{4,0},{6,2},{1,5},{3,7},{5,1},{7,3},{8,12},{10,14},{12... | collective-permute-start | bytes 393224 | tf_op jit(solution)/shard_map/ppermute | solution.py:306
  91.4 2.7 %collective-permute-start.12 = (bf16[128,512]{1,0:T(8,128)(2,1)S(1)}, bf16[128,512]{1,0:T(8,128)(2,1)S(1)}, u32[]{:S(2)}, u32[]{:S(2)}) collective-permute-start(bf16[128,512]{1,0:T(8,128)(2,1)S(1)} %pad_maximum_fusion.4), channel_id=1, source_target_pairs={{0,6},{2,0},{4,2},{6,4},{1,7},{3,1},{5,3},{7,5},{8,14},{10,8},{12,... | collective-permute-start | bytes 393224 | tf_op jit(solution)/shard_map/ppermute | solution.py:306
  94.1 0.3 collective-permute-done.25.rest_6_
  94.4 3.0 %collective-permute-done.10.rest_1_ = bf16[128,512]{1,0:T(8,128)(2,1)S(1)} collective-permute-done((bf16[128,512]{1,0:T(8,128)(2,1)S(1)}, bf16[128,512]{1,0:T(8,128)(2,1)S(1)}, u32[]{:S(2)}, u32[]{:S(2)}) %collective-permute-start.10) | collective-permute-done | bytes 131104 | tf_op jit(solution)/shard_map/ppermute | solution.py:306
  97.4 7.3 %collective-permute-done.11.rest_2_ = bf16[128,512]{1,0:T(8,128)(2,1)S(1)} collective-permute-done((bf16[128,512]{1,0:T(8,128)(2,1)S(1)}, bf16[128,512]{1,0:T(8,128)(2,1)S(1)}, u32[]{:S(2)}, u32[]{:S(2)}) %collective-permute-start.11) | collective-permute-done | bytes 131104 | tf_op jit(solution)/shard_map/ppermute | solution.py:306
  104.7 2.2 %finish.1 = bf16[512,512]{1,0:T(8,128)(2,1)} custom-call(s32[4,512]{1,0:T(4,128)S(1)} %pad_add_fusion.order_ref, bf16[512,512]{1,0:T(8,128)(2,1)S(1)} %get-tuple-element.21.h_ref, bf16[1024,512]{1,0:T(8,128)(2,1)S(1)} %copy-done.2, bf16[128,512]{1,0:T(8,128)(2,1)S(1)} %pad_maximum_fusion.1.rest_0_, bf16[128,512]{1,0:T(8,128)(2,1)S(1)} %collective-permute-done.10.rest_1_, ...), custom_call_target="tpu_custom_call" | custom-call | tf_op jit(solution)/shard_map/finish/pallas_call | solution.py:292
  (77 shorter events, 0.6 us)
Async XLA Ops:
  2.9 1.4 %copy-start = (bf16[512,1536]{1,0:T(8,128)(2,1)S(1)}, bf16[512,1536]{1,0:T(8,128)(2,1)}, u32[]{:S(2)}) copy-start(bf16[512,1536]{1,0:T(8,128)(2,1)} %w_qkv_hbm.1) | copy-start | bytes 4718596
  4.3 1.2 %copy-start.1 = (bf16[512,1024]{1,0:T(8,128)(2,1)S(1)}, bf16[512,1024]{1,0:T(8,128)(2,1)}, u32[]{:S(2)}) copy-start(bf16[512,1024]{1,0:T(8,128)(2,1)} %w_msg_hbm.1) | copy-start | bytes 3145732
  5.6 1.0 copy-start.3
  18.1 24.8 %collective-permute-start = (bf16[144,512]{1,0:T(8,128)(2,1)S(1)}, bf16[144,512]{1,0:T(8,128)(2,1)S(1)}, u32[]{:S(2)}, u32[]{:S(2)}) collective-permute-start(bf16[144,512]{1,0:T(8,128)(2,1)S(1)} %get-tuple-element.23), channel_id=1, source_target_pairs={{0,6},{2,0},{4,2},{6,4},{1,7},{3,1},{5,3},{7,5},{8,14},{10,8},{12,... | collective-permute-start | bytes 442376 | tf_op jit(solution)/shard_map/ppermute | solution.py:306
  23.3 19.6 %collective-permute-start.1 = (bf16[144,512]{1,0:T(8,128)(2,1)S(1)}, bf16[144,512]{1,0:T(8,128)(2,1)S(1)}, u32[]{:S(2)}, u32[]{:S(2)}) collective-permute-start(bf16[144,512]{1,0:T(8,128)(2,1)S(1)} %get-tuple-element.24), channel_id=1, source_target_pairs={{0,4},{2,6},{4,0},{6,2},{1,5},{3,7},{5,1},{7,3},{8,12},{10,14},{12... | collective-permute-start | bytes 442376 | tf_op jit(solution)/shard_map/ppermute | solution.py:306
  23.3 11.6 %collective-permute-start.2 = (bf16[144,512]{1,0:T(8,128)(2,1)S(1)}, bf16[144,512]{1,0:T(8,128)(2,1)S(1)}, u32[]{:S(2)}, u32[]{:S(2)}) collective-permute-start(bf16[144,512]{1,0:T(8,128)(2,1)S(1)} %get-tuple-element.25), channel_id=1, source_target_pairs={{0,2},{2,4},{4,6},{6,0},{1,3},{3,5},{5,7},{7,1},{8,10},{10,12},{12... | collective-permute-start | bytes 442376 | tf_op jit(solution)/shard_map/ppermute | solution.py:306
  24.3 24.0 %collective-permute-start.15 = (bf16[144,512]{1,0:T(8,128)(2,1)S(1)}, bf16[144,512]{1,0:T(8,128)(2,1)S(1)}, u32[]{:S(2)}, u32[]{:S(2)}) collective-permute-start(bf16[144,512]{1,0:T(8,128)(2,1)S(1)} %get-tuple-element.30), channel_id=1, source_target_pairs={{0,2},{2,4},{4,6},{6,0},{1,3},{3,5},{5,7},{7,1},{8,10},{10,12},{12... | collective-permute-start | bytes 442376 | tf_op jit(solution)/shard_map/ppermute | solution.py:306
  26.7 21.4 %collective-permute-start.14 = (bf16[144,512]{1,0:T(8,128)(2,1)S(1)}, bf16[144,512]{1,0:T(8,128)(2,1)S(1)}, u32[]{:S(2)}, u32[]{:S(2)}) collective-permute-start(bf16[144,512]{1,0:T(8,128)(2,1)S(1)} %get-tuple-element.29), channel_id=1, source_target_pairs={{0,4},{2,6},{4,0},{6,2},{1,5},{3,7},{5,1},{7,3},{8,12},{10,14},{12... | collective-permute-start | bytes 442376 | tf_op jit(solution)/shard_map/ppermute | solution.py:306
  27.7 36.3 %copy-start.6 = (bf16[512,512]{1,0:T(8,128)(2,1)S(1)}, bf16[512,512]{1,0:T(8,128)(2,1)}, u32[]{:S(2)}) copy-start(bf16[512,512]{1,0:T(8,128)(2,1)} %state_ref.3) | copy-start | bytes 1572868
  27.7 36.3 %copy-start.7 = (bf16[512,512]{1,0:T(8,128)(2,1)S(1)}, bf16[512,512]{1,0:T(8,128)(2,1)}, u32[]{:S(2)}) copy-start(bf16[512,512]{1,0:T(8,128)(2,1)} %w_ref.4) | copy-start | bytes 1572868
  34.8 11.7 %collective-permute-start.13 = (bf16[144,512]{1,0:T(8,128)(2,1)S(1)}, bf16[144,512]{1,0:T(8,128)(2,1)S(1)}, u32[]{:S(2)}, u32[]{:S(2)}) collective-permute-start(bf16[144,512]{1,0:T(8,128)(2,1)S(1)} %get-tuple-element.28), channel_id=1, source_target_pairs={{0,6},{2,0},{4,2},{6,4},{1,7},{3,1},{5,3},{7,5},{8,14},{10,8},{12,... | collective-permute-start | bytes 442376 | tf_op jit(solution)/shard_map/ppermute | solution.py:306
  43.2 6.0 %collective-permute-start.3 = (bf16[144,512]{1,0:T(8,128)(2,1)S(1)}, bf16[144,512]{1,0:T(8,128)(2,1)S(1)}, u32[]{:S(2)}, u32[]{:S(2)}) collective-permute-start(bf16[144,512]{1,0:T(8,128)(2,1)S(1)} %constant_dynamic-update-slice_fusion), channel_id=1, source_target_pairs={{0,24},{8,0},{16,8},{24,16},{1,25},{9,1},{17,9},{25,17},{2,26},{10... | collective-permute-start | bytes 442376 | tf_op jit(solution)/shard_map/ppermute | solution.py:306
  45.7 7.6 %collective-permute-start.4 = (bf16[144,512]{1,0:T(8,128)(2,1)S(1)}, bf16[144,512]{1,0:T(8,128)(2,1)S(1)}, u32[]{:S(2)}, u32[]{:S(2)}) collective-permute-start(bf16[144,512]{1,0:T(8,128)(2,1)S(1)} %constant_dynamic-update-slice_fusion.5), channel_id=1, source_target_pairs={{0,16},{8,24},{16,0},{24,8},{1,17},{9,25},{17,1},{25,9},{2,18},{10... | collective-permute-start | bytes 442376 | tf_op jit(solution)/shard_map/ppermute | solution.py:306
  46.5 6.8 %collective-permute-start.5 = (bf16[144,512]{1,0:T(8,128)(2,1)S(1)}, bf16[144,512]{1,0:T(8,128)(2,1)S(1)}, u32[]{:S(2)}, u32[]{:S(2)}) collective-permute-start(bf16[144,512]{1,0:T(8,128)(2,1)S(1)} %constant_dynamic-update-slice_fusion.10), channel_id=1, source_target_pairs={{0,8},{8,16},{16,24},{24,0},{1,9},{9,17},{17,25},{25,1},{2,10},{10... | collective-permute-start | bytes 442376 | tf_op jit(solution)/shard_map/ppermute | solution.py:306
  48.4 5.1 %collective-permute-start.16 = (bf16[272,512]{1,0:T(8,128)(2,1)S(1)}, bf16[272,512]{1,0:T(8,128)(2,1)S(1)}, u32[]{:S(2)}, u32[]{:S(2)}) collective-permute-start(bf16[272,512]{1,0:T(8,128)(2,1)S(1)} %constant_dynamic-update-slice_fusion.23), channel_id=1, source_target_pairs={{0,1},{1,0},{2,3},{3,2},{4,5},{5,4},{6,7},{7,6},{8,9},{9,8},{10,11... | collective-permute-start | bytes 835592 | tf_op jit(solution)/shard_map/ppermute | solution.py:306
  49.1 26.2 %copy-start.4 = (bf16[512,512]{1,0:T(8,128)(2,1)S(1)}, bf16[512,512]{1,0:T(8,128)(2,1)}, u32[]{:S(2)}) copy-start(bf16[512,512]{1,0:T(8,128)(2,1)} %state_ref.2) | copy-start | bytes 1572868
  49.2 26.2 %copy-start.5 = (bf16[512,512]{1,0:T(8,128)(2,1)S(1)}, bf16[512,512]{1,0:T(8,128)(2,1)}, u32[]{:S(2)}) copy-start(bf16[512,512]{1,0:T(8,128)(2,1)} %w_ref.3) | copy-start | bytes 1572868
  53.4 21.9 %collective-permute-start.6 = (bf16[576,512]{1,0:T(8,128)(2,1)S(1)}, bf16[576,512]{1,0:T(8,128)(2,1)S(1)}, u32[]{:S(2)}, u32[]{:S(2)}) collective-permute-start(bf16[576,512]{1,0:T(8,128)(2,1)S(1)} %constant_dynamic-update-slice_fusion.15.own_ref), channel_id=1, source_target_pairs={{0,1},{1,0},{2,3},{3,2},{4,5},{5,4},{6,7},{7,6},{8,9},{9,8},{10,11... | collective-permute-start | bytes 1769480 | tf_op jit(solution)/shard_map/ppermute | solution.py:306
  54.1 6.7 %collective-permute-start.17 = (bf16[144,512]{1,0:T(8,128)(2,1)S(1)}, bf16[144,512]{1,0:T(8,128)(2,1)S(1)}, u32[]{:S(2)}, u32[]{:S(2)}) collective-permute-start(bf16[144,512]{1,0:T(8,128)(2,1)S(1)} %get-tuple-element.32), channel_id=1, source_target_pairs={{0,24},{8,0},{16,8},{24,16},{1,25},{9,1},{17,9},{25,17},{2,26},{10... | collective-permute-start | bytes 442376 | tf_op jit(solution)/shard_map/ppermute | solution.py:306
  55.0 6.4 %collective-permute-start.18 = (bf16[144,512]{1,0:T(8,128)(2,1)S(1)}, bf16[144,512]{1,0:T(8,128)(2,1)S(1)}, u32[]{:S(2)}, u32[]{:S(2)}) collective-permute-start(bf16[144,512]{1,0:T(8,128)(2,1)S(1)} %get-tuple-element.33), channel_id=1, source_target_pairs={{0,16},{8,24},{16,0},{24,8},{1,17},{9,25},{17,1},{25,9},{2,18},{10... | collective-permute-start | bytes 442376 | tf_op jit(solution)/shard_map/ppermute | solution.py:306
  55.5 8.6 %collective-permute-start.19 = (bf16[144,512]{1,0:T(8,128)(2,1)S(1)}, bf16[144,512]{1,0:T(8,128)(2,1)S(1)}, u32[]{:S(2)}, u32[]{:S(2)}) collective-permute-start(bf16[144,512]{1,0:T(8,128)(2,1)S(1)} %get-tuple-element.34), channel_id=1, source_target_pairs={{0,8},{8,16},{16,24},{24,0},{1,9},{9,17},{17,25},{25,1},{2,10},{10... | collective-permute-start | bytes 442376 | tf_op jit(solution)/shard_map/ppermute | solution.py:306
  64.5 5.5 %collective-permute-start.20 = (bf16[128,512]{1,0:T(8,128)(2,1)S(1)}, bf16[128,512]{1,0:T(8,128)(2,1)S(1)}, u32[]{:S(2)}, u32[]{:S(2)}) collective-permute-start(bf16[128,512]{1,0:T(8,128)(2,1)S(1)} %update_prod.1.rest_0_), channel_id=1, source_target_pairs={{0,24},{8,0},{16,8},{24,16},{1,25},{9,1},{17,9},{25,17},{2,26},{10... | collective-permute-start | bytes 393224 | tf_op jit(solution)/shard_map/ppermute | solution.py:306
  65.8 8.0 %collective-permute-start.21 = (bf16[128,512]{1,0:T(8,128)(2,1)S(1)}, bf16[128,512]{1,0:T(8,128)(2,1)S(1)}, u32[]{:S(2)}, u32[]{:S(2)}) collective-permute-start(bf16[128,512]{1,0:T(8,128)(2,1)S(1)} %update_prod.1.rest_0_), channel_id=1, source_target_pairs={{0,16},{8,24},{16,0},{24,8},{1,17},{9,25},{17,1},{25,9},{2,18},{10... | collective-permute-start | bytes 393224 | tf_op jit(solution)/shard_map/ppermute | solution.py:306
  66.4 7.4 %collective-permute-start.22 = (bf16[128,512]{1,0:T(8,128)(2,1)S(1)}, bf16[128,512]{1,0:T(8,128)(2,1)S(1)}, u32[]{:S(2)}, u32[]{:S(2)}) collective-permute-start(bf16[128,512]{1,0:T(8,128)(2,1)S(1)} %update_prod.1.rest_0_), channel_id=1, source_target_pairs={{0,8},{8,16},{16,24},{24,0},{1,9},{9,17},{17,25},{25,1},{2,10},{10... | collective-permute-start | bytes 393224 | tf_op jit(solution)/shard_map/ppermute | solution.py:306
  75.2 5.1 %collective-permute-start.23 = (bf16[256,512]{1,0:T(8,128)(2,1)S(1)}, bf16[256,512]{1,0:T(8,128)(2,1)S(1)}, u32[]{:S(2)}, u32[]{:S(2)}) collective-permute-start(bf16[256,512]{1,0:T(8,128)(2,1)S(1)} %get-tuple-element.36), channel_id=1, source_target_pairs={{0,1},{1,0},{2,3},{3,2},{4,5},{5,4},{6,7},{7,6},{8,9},{9,8},{10,11... | collective-permute-start | bytes 786440 | tf_op jit(solution)/shard_map/ppermute | solution.py:306
  77.7 27.0 %copy-start.2 = (bf16[1024,512]{1,0:T(8,128)(2,1)S(1)}, bf16[1024,512]{1,0:T(8,128)(2,1)}, u32[]{:S(2)}) copy-start(bf16[1024,512]{1,0:T(8,128)(2,1)} %w_ref.5) | copy-start | bytes 3145732
  77.7 7.4 %collective-permute-start.9 = (bf16[128,512]{1,0:T(8,128)(2,1)S(1)}, bf16[128,512]{1,0:T(8,128)(2,1)S(1)}, u32[]{:S(2)}, u32[]{:S(2)}) collective-permute-start(bf16[128,512]{1,0:T(8,128)(2,1)S(1)} %get-tuple-element.48), channel_id=1, source_target_pairs={{0,24},{8,0},{16,8},{24,16},{1,25},{9,1},{17,9},{25,17},{2,26},{10... | collective-permute-start | bytes 393224 | tf_op jit(solution)/shard_map/ppermute | solution.py:306
  78.7 9.2 %collective-permute-start.8 = (bf16[128,512]{1,0:T(8,128)(2,1)S(1)}, bf16[128,512]{1,0:T(8,128)(2,1)S(1)}, u32[]{:S(2)}, u32[]{:S(2)}) collective-permute-start(bf16[128,512]{1,0:T(8,128)(2,1)S(1)} %get-tuple-element.49), channel_id=1, source_target_pairs={{0,16},{8,24},{16,0},{24,8},{1,17},{9,25},{17,1},{25,9},{2,18},{10... | collective-permute-start | bytes 393224 | tf_op jit(solution)/shard_map/ppermute | solution.py:306
  79.6 8.3 %collective-permute-start.7 = (bf16[128,512]{1,0:T(8,128)(2,1)S(1)}, bf16[128,512]{1,0:T(8,128)(2,1)S(1)}, u32[]{:S(2)}, u32[]{:S(2)}) collective-permute-start(bf16[128,512]{1,0:T(8,128)(2,1)S(1)} %get-tuple-element.47), channel_id=1, source_target_pairs={{0,8},{8,16},{16,24},{24,0},{1,9},{9,17},{17,25},{25,1},{2,10},{10... | collective-permute-start | bytes 393224 | tf_op jit(solution)/shard_map/ppermute | solution.py:306
  80.4 11.0 %collective-permute-start.24 = (bf16[128,512]{1,0:T(8,128)(2,1)S(1)}, bf16[128,512]{1,0:T(8,128)(2,1)S(1)}, u32[]{:S(2)}, u32[]{:S(2)}) collective-permute-start(bf16[128,512]{1,0:T(8,128)(2,1)S(1)} %pad_maximum_fusion.6), channel_id=1, source_target_pairs={{0,2},{2,4},{4,6},{6,0},{1,3},{3,5},{5,7},{7,1},{8,10},{10,12},{12... | collective-permute-start | bytes 393224 | tf_op jit(solution)/shard_map/ppermute | solution.py:306
  83.3 11.1 %collective-permute-start.25 = (bf16[128,512]{1,0:T(8,128)(2,1)S(1)}, bf16[128,512]{1,0:T(8,128)(2,1)S(1)}, u32[]{:S(2)}, u32[]{:S(2)}) collective-permute-start(bf16[128,512]{1,0:T(8,128)(2,1)S(1)} %pad_maximum_fusion.7), channel_id=1, source_target_pairs={{0,4},{2,6},{4,0},{6,2},{1,5},{3,7},{5,1},{7,3},{8,12},{10,14},{12... | collective-permute-start | bytes 393224 | tf_op jit(solution)/shard_map/ppermute | solution.py:306
  85.1 9.3 %collective-permute-start.26 = (bf16[128,512]{1,0:T(8,128)(2,1)S(1)}, bf16[128,512]{1,0:T(8,128)(2,1)S(1)}, u32[]{:S(2)}, u32[]{:S(2)}) collective-permute-start(bf16[128,512]{1,0:T(8,128)(2,1)S(1)} %pad_maximum_fusion.8), channel_id=1, source_target_pairs={{0,6},{2,0},{4,2},{6,4},{1,7},{3,1},{5,3},{7,5},{8,14},{10,8},{12,... | collective-permute-start | bytes 393224 | tf_op jit(solution)/shard_map/ppermute | solution.py:306
  87.9 9.5 %collective-permute-start.10 = (bf16[128,512]{1,0:T(8,128)(2,1)S(1)}, bf16[128,512]{1,0:T(8,128)(2,1)S(1)}, u32[]{:S(2)}, u32[]{:S(2)}) collective-permute-start(bf16[128,512]{1,0:T(8,128)(2,1)S(1)} %pad_maximum_fusion.2), channel_id=1, source_target_pairs={{0,2},{2,4},{4,6},{6,0},{1,3},{3,5},{5,7},{7,1},{8,10},{10,12},{12... | collective-permute-start | bytes 393224 | tf_op jit(solution)/shard_map/ppermute | solution.py:306
  89.6 15.1 %collective-permute-start.11 = (bf16[128,512]{1,0:T(8,128)(2,1)S(1)}, bf16[128,512]{1,0:T(8,128)(2,1)S(1)}, u32[]{:S(2)}, u32[]{:S(2)}) collective-permute-start(bf16[128,512]{1,0:T(8,128)(2,1)S(1)} %pad_maximum_fusion.3), channel_id=1, source_target_pairs={{0,4},{2,6},{4,0},{6,2},{1,5},{3,7},{5,1},{7,3},{8,12},{10,14},{12... | collective-permute-start | bytes 393224 | tf_op jit(solution)/shard_map/ppermute | solution.py:306
  91.4 13.3 %collective-permute-start.12 = (bf16[128,512]{1,0:T(8,128)(2,1)S(1)}, bf16[128,512]{1,0:T(8,128)(2,1)S(1)}, u32[]{:S(2)}, u32[]{:S(2)}) collective-permute-start(bf16[128,512]{1,0:T(8,128)(2,1)S(1)} %pad_maximum_fusion.4), channel_id=1, source_target_pairs={{0,6},{2,0},{4,2},{6,4},{1,7},{3,1},{5,3},{7,5},{8,14},{10,8},{12,... | collective-permute-start | bytes 393224 | tf_op jit(solution)/shard_map/ppermute | solution.py:306

commit v3 on v2

v3 whole, which is shorter than its diff:
```python
import functools
import math

import jax
import jax.numpy as jnp
from jax import lax
from jax.experimental import pallas as pl
from jax.experimental.pallas import tpu as pltpu
from jax.sharding import PartitionSpec as P

H = 512
HEADS = 8
NCOL = 4
HD = 64
EPS = 1e-06
BF = jnp.bfloat16
F32 = jnp.float32
ID_ROWS = 16
VMEM = pl.BlockSpec(memory_space=pltpu.VMEM)
HBM = pl.BlockSpec(memory_space=pltpu.HBM)
ANY = pl.BlockSpec(memory_space=pl.ANY)
SMEM = pl.BlockSpec(memory_space=pltpu.SMEM)
PARAMS = pltpu.CompilerParams(vmem_limit_bytes=16 * 1024 * 1024)
ENCODE_PARAMS = pltpu.CompilerParams(vmem_limit_bytes=60 * 1024 * 1024)


def rms_norm(vector):
    return vector * lax.rsqrt(jnp.mean(vector * vector, axis=-1, keepdims=True) + EPS)


def dot(left, right):
    return jnp.dot(left, right, preferred_element_type=F32)


def dot_t(left, right):
    return lax.dot_general(left, right, (((0,), (0,)), ((), ())), preferred_element_type=F32)


def dot_nt(left, right):
    return lax.dot_general(left, right, (((1,), (1,)), ((), ())), preferred_element_type=F32)


def one_hot(rows, first, ids):
    row = lax.broadcasted_iota(jnp.int32, (rows, ids.shape[1]), 0) + first
    return jnp.where(row == ids, 1.0, 0.0).astype(BF)


def iota(shape, dim):
    return lax.broadcasted_iota(jnp.int32, shape, dim)


def encode_rows(tokens, w_qkv, w_out, pair_sum, spread, before):
    rows = tokens[0].shape[0]
    stacked = jnp.concatenate(tokens, axis=0)
    part = []
    for which in range(3):
        before(which)
        made = dot(stacked, w_qkv[:, which * H:(which + 1) * H]).astype(BF)
        part.append([made[c * rows:(c + 1) * rows] for c in range(NCOL)])
    query, key, value = part
    lane = iota((rows, 128), 1)
    scores = jnp.zeros((rows, 128), F32)
    for j in range(NCOL):
        both = dot(jnp.concatenate([query[i] * key[j] for i in range(NCOL)], axis=0), pair_sum)
        for i in range(NCOL):
            scores = jnp.where(lane >> 3 == j * NCOL + i, both[i * rows:(i + 1) * rows], scores)
    scores = scores * (1.0 / math.sqrt(HD))
    top = jnp.maximum(scores, pltpu.roll(scores, 64, 1))
    top = jnp.maximum(top, pltpu.roll(top, 32, 1))
    expon = jnp.exp(scores - top)
    total = expon + pltpu.roll(expon, 64, 1)
    total = total + pltpu.roll(total, 32, 1)
    weight = (expon / total).astype(BF).astype(F32)
    attended = jnp.zeros((rows, H), F32)
    pooled = jnp.zeros((rows, H), F32)
    for j in range(NCOL):
        turned = pltpu.roll(weight, (128 - NCOL * HEADS * j) % 128, 1).astype(BF)
        attended = attended + dot(turned, spread) * value[j].astype(F32)
        pooled = pooled + tokens[j].astype(F32)
    before(3)
    mixed = dot((attended * (1.0 / NCOL)).astype(BF), w_out[...])
    return rms_norm(pooled * (1.0 / NCOL) + mixed).astype(BF)


def halves_at(ids, place, count):
    row = iota((count, ids.shape[1]), 0)
    halves = jnp.where((row & 1) == 0, ids >> 5, ids & 31)
    return jnp.where(row >> 1 == place, halves, 0).astype(F32).astype(BF)


def id_rows(count):
    return -(-2 * count // ID_ROWS) * ID_ROWS


def split(index, size):
    if size & (size - 1) == 0:
        return index >> (size.bit_length() - 1), index & (size - 1)
    return lax.div(index, size), lax.rem(index, size)


def send_orders(sizes, me_ref, pos, cust_slot, prod_slot, live_ref):
    nr, nz, nc = sizes
    rows = pos.shape[1]
    cs, ps = rows // (nr * nz), rows // (nz * nc)
    mr, mz, mc = me_ref[0], me_ref[1], me_ref[2]
    block, k = split(iota((1, rows), 1), cs)
    r, z = split(block, nz)
    live = jnp.zeros((1, rows), jnp.int32)
    for b in range(nr * nz):
        live = jnp.where(block == b, live_ref[0, b], live)
    cust = mz ^ z, mr ^ r, k, jnp.where(k < live, cust_slot + 1, 0)
    prod_id = jnp.where(k < live, prod_slot + 1, 0)
    block, k = split(pos, ps)
    z, c = split(block, nc)
    return cust, (mz ^ z, mc ^ c, k, prod_id)


def encode_kernel(sizes, rows, *refs):
    x_hbm, w_qkv_hbm, w_out_hbm, w_msg_hbm, me_ref = refs[:5]
    index_hbm, (h_ref, order_ref) = refs[5:9], refs[9:11]
    x_ref, w_qkv, w_out, w_msg, pos_ref, cust_slot_ref, prod_slot_ref, live_ref, sem = refs[-9:]
    nr, nz, nc = sizes
    cust_refs, prod_refs = refs[11:11 + nz], refs[11 + nz:-9]
    chunks = x_hbm.shape[0] // rows
    copy = pltpu.make_async_copy
    x_copies = [
        copy(x_hbm.at[pl.ds(c * rows, rows)], x_ref.at[pl.ds(c * rows, rows)], sem.at[c])
        for c in range(chunks)
    ]
    w_copies = [
        copy(w_qkv_hbm.at[:, pl.ds(k * H, H)], w_qkv.at[:, pl.ds(k * H, H)], sem.at[chunks + k])
        for k in range(3)
    ]
    w_copies.append(copy(w_out_hbm, w_out, sem.at[chunks + 3]))
    last = copy(w_msg_hbm, w_msg, sem.at[chunks + 4])
    index_refs = (pos_ref, cust_slot_ref, prod_slot_ref, live_ref)
    index_copies = [
        copy(source, ref, sem.at[chunks + 5 + n])
        for n, (source, ref) in enumerate(zip(index_hbm, index_refs))
    ]
    x_copies[0].start()
    w_copies[0].start()
    w_copies[1].start()
    for index_copy in index_copies:
        index_copy.start()
    pair_sum = jnp.where(iota((H, 128), 0) >> 6 == (iota((H, 128), 1) & 7), 1.0, 0.0).astype(BF)
    spread = jnp.where(
        (iota((128, H), 0) < NCOL * HEADS) & ((iota((128, H), 0) & 7) == iota((128, H), 1) >> 6),
        1.0,
        0.0,
    ).astype(BF)

    def first_before(which):
        w_copies[which].wait()
        if which == 0:
            w_copies[2].start()
            for x_copy in x_copies[1:]:
                x_copy.start()
        if which == 1:
            w_copies[3].start()
            last.start()

    for c in range(chunks):
        x_copies[c].wait()
        at = slice(c * rows, (c + 1) * rows)
        tokens = [x_ref[at, k * H:(k + 1) * H] for k in range(NCOL)]
        before = first_before if c == 0 else lambda which: None
        h_ref[at, :] = encode_rows(tokens, w_qkv, w_out, pair_sum, spread, before)
    for index_copy in index_copies:
        index_copy.wait()
    (s_of, t_of, k, ids), (ps_of, u_of, pk, prod_ids) = send_orders(
        sizes, me_ref, pos_ref[...], cust_slot_ref[...], prod_slot_ref[...], live_ref
    )
    count = h_ref.shape[0]
    cs, ps = count // (nr * nz), count // (nz * nc)
    cust_sent, prod_sent = (s_of * nr + t_of) * cs + k, (u_of * nz + ps_of) * ps + pk
    order_ref[0:1, :] = (t_of * nz + s_of) * cs + k
    order_ref[1:2, :] = prod_sent
    lanes = one_hot(nz * cs, 0, s_of * cs + k)
    halves = halves_at(ids, t_of, id_rows(nr))
    cust_ids = [
        dot_nt(jnp.where(s_of == s, halves, jnp.zeros_like(halves)), lanes) for s in range(nz)
    ]
    lanes = one_hot(nc * ps, 0, u_of * ps + pk)
    halves = halves_at(prod_ids, ps_of * (ID_ROWS // 2), nz * ID_ROWS)
    prod_ids = [
        dot_nt(jnp.where(u_of == u, halves, jnp.zeros_like(halves)), lanes) for u in range(nc)
    ]
    last.wait()
    message = dot(h_ref[...], w_msg[...]).astype(BF)
    for sent, made, refs, which in (
        (cust_sent, cust_ids, cust_refs, 0),
        (prod_sent, prod_ids, prod_refs, 1),
    ):
        size = count // len(refs)
        for s, ref in enumerate(refs):
            pick = one_hot(size, s * size, sent)
            ref[:size, :] = dot(pick, message[:, which * H:(which + 1) * H]).astype(BF)
            ref[size:, :] = jnp.zeros((ref.shape[0] - size, H), BF)
            ref[size:, :made[s].shape[1]] = made[s].astype(BF)


def encode(sizes, me, review_cols, w_qkv, w_out, w_msg, *index):
    count = review_cols.shape[0]
    nr, nz, nc = sizes
    rows = min(count, 256)
    cust_block = jax.ShapeDtypeStruct((count // nz + id_rows(nr), H), BF)
    prod_block = jax.ShapeDtypeStruct((count // nc + nz * ID_ROWS, H), BF)
    out = pl.pallas_call(
        functools.partial(encode_kernel, sizes, rows),
        in_specs=[HBM] * 4 + [SMEM] + [HBM] * 4,
        out_specs=[VMEM] * (2 + nz + nc),
        out_shape=[
            jax.ShapeDtypeStruct((count, H), BF),
            jax.ShapeDtypeStruct((2, count), jnp.int32),
        ]
        + [cust_block] * nz
        + [prod_block] * nc,
        scratch_shapes=[pltpu.VMEM(a.shape, BF) for a in (review_cols, w_qkv, w_out, w_msg)]
        + [pltpu.VMEM(a.shape, jnp.int32) for a in index[:3]]
        + [pltpu.SMEM(index[3].shape, jnp.int32)]
        + [pltpu.SemaphoreType.DMA((count // rows + 9,))],
        compiler_params=ENCODE_PARAMS,
        name="encode",
    )(review_cols, w_qkv, w_out, w_msg, me, *index)
    return out[0], out[1], out[2:2 + nz], out[2 + nz:]


def pair_kernel(parts, own_ref, peer_ref, *refs):
    part = (own_ref.shape[0] - parts * ID_ROWS) // parts
    for s, ref in enumerate(refs[-parts:]):
        at = parts * part + s * ID_ROWS
        ref[:part, :] = own_ref[s * part:(s + 1) * part, :]
        ref[part:2 * part, :] = peer_ref[s * part:(s + 1) * part, :]
        ref[2 * part:, :] = own_ref[at:at + ID_ROWS, :] + peer_ref[at:at + ID_ROWS, :]


def pair(parts, own, peer, after):
    part = (own.shape[0] - parts * ID_ROWS) // parts
    return pl.pallas_call(
        functools.partial(pair_kernel, parts),
        in_specs=[VMEM] * 2 + [ANY] * len(after),
        out_specs=[VMEM] * parts,
        out_shape=[jax.ShapeDtypeStruct((2 * part + ID_ROWS, H), BF)] * parts,
        compiler_params=PARAMS,
        name="pair_product_blocks",
    )(own, peer, *after)


def regroup_kernel(size, parts, groups, *refs):
    held = groups * size
    for t, ref in enumerate(refs[-groups:]):
        for s in range(parts):
            ref[s * size:(s + 1) * size, :] = refs[s][t * size:(t + 1) * size, :]
        ref[parts * size:, :] = sum(refs[s][held:, :] for s in range(parts))


def regroup(size, groups, got, after):
    parts, ids = len(got), got[0].shape[0] - groups * size
    if size % 16:
        tail = sum(p[groups * size:] for p in got)
        return [
            jnp.concatenate([p[t * size:(t + 1) * size] for p in got] + [tail], axis=0)
            for t in range(groups)
        ]
    return pl.pallas_call(
        functools.partial(regroup_kernel, size, parts, groups),
        in_specs=[VMEM] * parts + [ANY] * len(after),
        out_specs=[VMEM] * groups,
        out_shape=[jax.ShapeDtypeStruct((parts * size + ids, H), BF)] * groups,
        compiler_params=PARAMS,
        name="regroup_customer_blocks",
    )(*got, *after)


def join_kernel(count, *refs):
    at = 0
    for ref in refs[:count]:
        refs[-1][at:at + ref.shape[0], :] = ref[...]
        at += ref.shape[0]


def join(parts, after):
    rows = sum(part.shape[0] for part in parts)
    return pl.pallas_call(
        functools.partial(join_kernel, len(parts)),
        in_specs=[VMEM] * len(parts) + [ANY] * len(after),
        out_specs=VMEM,
        out_shape=jax.ShapeDtypeStruct((rows, H), BF),
        compiler_params=PARAMS,
        name="join",
    )(*parts, *after)


def refresh(totals, counts, states, weight):
    average = (totals / jnp.sqrt(jnp.maximum(counts, 1.0))).astype(BF)
    update = dot(average, weight)
    update = update * (1.0 / (1.0 + jnp.exp(-update)))
    return rms_norm(states.astype(F32) + update).astype(BF)


def count_of(pick):
    return jnp.sum(pick.astype(F32), axis=1, keepdims=True)


def ids_in(rows):
    rows = rows.astype(F32)
    return (rows[0:1, :] * 32.0 + rows[1:2, :]).astype(jnp.int32) - 1


def cust_kernel(groups, own_ref, peer_ref, state_ref, w_ref, *refs):
    new_ref, reply_ref = refs[-2:]
    size = state_ref.shape[0]
    held = own_ref.shape[0] // groups
    rows = held - id_rows(groups)
    totals, counts = jnp.zeros((size, H), F32), jnp.zeros((size, 1), F32)
    for ref in (peer_ref, own_ref):
        ids = [
            ids_in(ref[t * held + rows:(t + 1) * held, :rows][2 * t:2 * t + 2, :])
            for t in range(groups)
        ]
        pick = one_hot(size, 0, jnp.concatenate(ids, axis=1))
        messages = [ref[t * held:t * held + rows, :] for t in range(groups)]
        totals = totals + dot(pick, jnp.concatenate(messages, axis=0))
        counts = counts + count_of(pick)
    new = refresh(totals, counts, state_ref[...], w_ref[...])
    new_ref[...] = new
    reply_ref[...] = dot_t(pick, new).astype(BF)


def update_cust(groups, own, peer, state, weight, after):
    rows = own.shape[0] - groups * id_rows(groups)
    return pl.pallas_call(
        functools.partial(cust_kernel, groups),
        in_specs=[VMEM] * 4 + [ANY] * len(after),
        out_specs=[VMEM] * 2,
        out_shape=[
            jax.ShapeDtypeStruct(state.shape, BF),
            jax.ShapeDtypeStruct((rows, H), BF),
        ],
        compiler_params=PARAMS,
        name="update_cust",
    )(own, peer, state, weight, *after)


def prod_sum_kernel(slabs, parts, me_ref, ids_ref, *refs):
    blocks, pieces = refs[:parts], refs[-slabs:]
    size = pieces[0].shape[0] - ID_ROWS
    rows = jnp.concatenate([ref[:ref.shape[0] - ID_ROWS, :] for ref in blocks], axis=0)
    ones = jnp.ones((ID_ROWS, rows.shape[0]), BF)
    row = iota((ID_ROWS, size), 0)
    for t, ref in enumerate(pieces):
        owner = me_ref[0] ^ t
        pick = one_hot(size, owner * size, ids_ref[...])
        counts = dot_nt(ones, pick).astype(jnp.int32)
        halves = jnp.where(row == 0, counts >> 5, jnp.where(row == 1, counts & 31, 0))
        ref[:size, :] = dot(pick, rows).astype(ref.dtype)
        ref[size:, :] = jnp.zeros((ID_ROWS, H), ref.dtype)
        ref[size:, :size] = halves.astype(F32).astype(ref.dtype)


def sum_prod(me, ids, blocks, size, slabs, after):
    piece = lambda kind: jax.ShapeDtypeStruct((size // slabs + ID_ROWS, H), kind)
    return pl.pallas_call(
        functools.partial(prod_sum_kernel, slabs, len(blocks)),
        in_specs=[SMEM] + [VMEM] * (1 + len(blocks)) + [ANY] * len(after),
        out_specs=[VMEM] * slabs,
        out_shape=[piece(F32)] + [piece(BF)] * (slabs - 1),
        compiler_params=PARAMS,
        name="sum_prod",
    )(me, ids, *blocks, *after)


def prod_update_kernel(slabs, me_ref, state_ref, w_ref, *rest):
    new_ref = rest[-1]
    size = new_ref.shape[0]
    first = pl.multiple_of(me_ref[0] * size, size)
    totals = sum(ref[:size, :].astype(F32) for ref in rest[:slabs])
    halves = sum(ref[size:, :size].astype(F32) for ref in rest[:slabs])
    count_row = halves[0:1, :] * 32.0 + halves[1:2, :]
    diagonal = iota((size, size), 0) == iota((size, size), 1)
    counts = jnp.sum(jnp.where(diagonal, count_row, 0.0), axis=1, keepdims=True)
    new_ref[...] = refresh(totals, counts, state_ref[pl.ds(first, size), :], w_ref[...])


def update_prod(me, state, weight, pieces, after):
    slabs = len(pieces)
    return pl.pallas_call(
        functools.partial(prod_update_kernel, slabs),
        in_specs=[SMEM] + [VMEM] * (2 + slabs) + [ANY] * len(after),
        out_specs=VMEM,
        out_shape=jax.ShapeDtypeStruct((state.shape[0] // slabs, H), BF),
        compiler_params=PARAMS,
        name="update_prod",
    )(me, state, weight, *pieces, *after)


def prod_reply_kernel(slabs, parts, me_ref, ids_ref, *rest):
    pieces, new_ref, reply_refs = rest[:slabs], rest[-1 - parts], rest[-parts:]
    size = pieces[0].shape[0]
    reply = None
    for t, ref in enumerate(pieces):
        first = pl.multiple_of((me_ref[0] ^ t) * size, size)
        new_ref[pl.ds(first, size), :] = ref[...]
        term = dot_t(one_hot(size, first, ids_ref[...]), ref[...])
        reply = term if reply is None else reply + term
    rows = reply_refs[0].shape[0]
    for s, ref in enumerate(reply_refs):
        ref[...] = reply[s * rows:(s + 1) * rows].astype(BF)


def reply_prod(me, ids, pieces, parts, after):
    slabs = len(pieces)
    size, rows = pieces[0].shape[0] * slabs, ids.shape[1]
    out = pl.pallas_call(
        functools.partial(prod_reply_kernel, slabs, parts),
        in_specs=[SMEM] + [VMEM] * (1 + slabs) + [ANY] * len(after),
        out_specs=[VMEM] * (1 + parts),
        out_shape=[jax.ShapeDtypeStruct((size, H), BF)]
        + [jax.ShapeDtypeStruct((rows // parts, H), BF)] * parts,
        compiler_params=PARAMS,
        name="reply_prod",
    )(me, ids, *pieces, *after)
    return out[0], out[1:]


def pick_rows(order, refs):
    rows = jnp.concatenate([ref[...] for ref in refs], axis=0)
    return dot_t(one_hot(rows.shape[0], 0, order), rows).astype(BF)


def finish_cust_kernel(order_ref, h_ref, w_ref, *rest):
    back = pick_rows(order_ref[0:1, :], rest[:-1])
    rest[-1][...] = h_ref[...].astype(F32) + dot(back, w_ref[:H, :])


def finish_cust(order, review_h, w_back, cust_back):
    return pl.pallas_call(
        finish_cust_kernel,
        in_specs=[VMEM] * (3 + len(cust_back)),
        out_specs=VMEM,
        out_shape=jax.ShapeDtypeStruct(review_h.shape, F32),
        compiler_params=PARAMS,
        name="finish_cust",
    )(order, review_h, w_back, *cust_back)


def finish_kernel(order_ref, part_ref, w_ref, *rest):
    back = pick_rows(order_ref[1:2, :], rest[:-1])
    rest[-1][...] = rms_norm(part_ref[...] + dot(back, w_ref[H:, :])).astype(BF)


def finish(order, part, w_back, prod_back):
    return pl.pallas_call(
        finish_kernel,
        in_specs=[VMEM] * (3 + len(prod_back)),
        out_specs=VMEM,
        out_shape=jax.ShapeDtypeStruct(part.shape, BF),
        compiler_params=PARAMS,
        name="finish",
    )(order, part, w_back, *prod_back)


def halve_kernel(parts, *refs):
    half = refs[0].shape[0] // 2
    for u, ref in enumerate(refs[-2:]):
        for s in range(parts):
            ref[s * half:(s + 1) * half, :] = refs[s][u * half:(u + 1) * half, :]


def halve(parts, after):
    rows = sum(part.shape[0] for part in parts) // 2
    return pl.pallas_call(
        functools.partial(halve_kernel, len(parts)),
        in_specs=[VMEM] * len(parts) + [ANY] * len(after),
        out_specs=[VMEM] * 2,
        out_shape=[jax.ShapeDtypeStruct((rows, H), BF)] * 2,
        compiler_params=PARAMS,
        name="halve_product_replies",
    )(*parts, *after)


def swap(value, axis, by):
    if by == 0:
        return value
    return lax.ppermute(value, axis, [(i, i ^ by) for i in range(lax.axis_size(axis))])


def rows_of(parts, start, size):
    return jnp.concatenate([part[start:start + size] for part in parts], axis=0)


def on_device(
    review_cols,
    cust_state,
    prod_state,
    w_qkv,
    w_out,
    w_msg,
    w_cust_up,
    w_prod_up,
    w_back,
    cust_slot,
    prod_slot,
    prod_pos,
    live_count,
):
    rows = review_cols.shape[0]
    nr, nz, nc = lax.axis_size("rev"), lax.axis_size("cust"), lax.axis_size("prod")
    mr, mz, mc = lax.axis_index("rev"), lax.axis_index("cust"), lax.axis_index("prod")
    cs = rows // (nr * nz)
    ps = rows // (nz * nc)
    wide = rows // nz
    me = jnp.stack([mr, mz, mc])
    flat = lambda ids: ids.reshape(1, rows)
    review_h, order, cust_blocks, prod_blocks = encode(
        (nr, nz, nc),
        me,
        review_cols,
        w_qkv,
        w_out,
        w_msg,
        flat(prod_pos),
        flat(cust_slot),
        flat(prod_slot),
        live_count,
    )

    prod_peer = swap(prod_blocks[1], "prod", 1)
    got = [swap(cust_blocks[s], "cust", s) for s in range(nz)]
    prod_blocks = pair(nz, prod_blocks[0], prod_peer, got[1:])
    prod_got = [swap(prod_blocks[s], "cust", s) for s in range(nz)]

    groups = regroup(cs, nr, got, prod_blocks[1:])
    groups = [swap(groups[t], "rev", t) for t in range(nr)]
    own = join(groups, prod_got[1:3])
    peer = swap(own, "prod", 1)

    prod_in = jnp.concatenate([ids_in(block[wide:, :wide]) for block in prod_got], axis=1)
    pieces = sum_prod(me, prod_in, prod_got, prod_state.shape[0], nr, [])
    new_cust, reply = update_cust(nr, own, peer, cust_state, w_cust_up, [])
    pieces = [swap(pieces[t], "rev", t) for t in range(nr)]
    blocks = reply.reshape(nr, nz, cs, H)
    cust_got = [swap(blocks[:, s].reshape(wide, H), "cust", s) for s in range(nz)]

    cust_back = [swap(rows_of(cust_got, t * cs, cs), "rev", t) for t in range(nr)]

    new_piece = update_prod(me, prod_state, w_prod_up, pieces, cust_got[1:3])
    new_pieces = [swap(new_piece, "rev", t) for t in range(nr)]
    new_prod, replies = reply_prod(me, prod_in, new_pieces, nz, cust_got[3:])
    replies = [swap(replies[s], "cust", s) for s in range(nz)]
    part = finish_cust(order, review_h, w_back, cust_back)
    own_replies, peer_replies = halve(replies, [part])
    prod_back = [own_replies, swap(peer_replies, "prod", 1)]

    review_out = finish(order, part, w_back, prod_back)
    return (review_out, new_cust, new_prod)


def solution(mesh):
    every = P(("rev", "cust", "prod"))
    in_specs = (
        P(("rev", "cust", "prod"), None),
        P(("rev", "cust"), None),
        P(("cust", "prod"), None),
        P(),
        P(),
        P(),
        P(),
        P(),
        P(),
        every,
        every,
        P(("rev", "cust", "prod"), None),
        P(("rev", "cust", "prod"), None),
    )
    out_specs = (
        P(("rev", "cust", "prod"), None),
        P(("rev", "cust"), None),
        P(("cust", "prod"), None),
    )
    return jax.shard_map(
        on_device, mesh=mesh, in_specs=in_specs, out_specs=out_specs, check_vma=False
    )
```

time: 108 us -> 94.8 us (0.88)
  waiting for transfers between devices: 43.2 us -> 32.6 us
  Pallas kernels: 18.6 us -> 22.2 us
  local copies, waits for them, and re-layouts: 5.33 us -> 1.99 us
  other arithmetic: 2.18 us -> 0.65 us
    ppermute x27, waiting for transfers between devices: 43.2 us -> 32.6 us  [swap(): lax.ppermute(value, axis, [(i, i ^ by) for i in range(lax.axis_size(axis))])]
    pallas_call x4 -> x9, Pallas kernels: 15.8 us -> 18.9 us  [the longest x1 13.2 us: encode(): pl.pallas_call(functools.partial(encode_kernel, sizes, rows), in_specs=[H...]
    unnamed x23 -> x20, local copies, waits for them, and re-layouts: 3.76 us -> 1.92 us
  transfers between devices with their start and end apart: 27 -> 27, of which waited for: 13 -> 12; matrix products, arithmetic and copies ran while one was open for 1% -> 0% of each run, Pallas kernels for 5% -> 8%
where the time goes in v3:
time: 94.8 us; the launch traced here: 94.6 us
  starting transfers between devices  36.2 us (38%)
  waiting for transfers between devices  32.6 us (34%)
  Pallas kernels  22.2 us (23%)
  local copies, waits for them, and re-layouts  1.99 us (2%)
    ppermute x27, starting transfers between devices, swap(): lax.ppermute(value, axis, [(i, i ^ by) for i in range(lax.axis_size(axis))])  36.2 us
    ppermute x27, waiting for transfers between devices, swap(): lax.ppermute(value, axis, [(i, i ^ by) for i in range(lax.axis_size(axis))])  32.6 us
    pallas_call x1, Pallas kernels, encode(): pl.pallas_call(functools.partial(encode_kernel, sizes, rows), in_specs=[H...  13.2 us
    pallas_call x1, Pallas kernels, update_cust(): pl.pallas_call(functools.partial(cust_kernel, groups), in_specs=[VMEM] *...  2.3 us
    pallas_call x1, Pallas kernels, reply_prod(): pl.pallas_call(functools.partial(prod_reply_kernel, slabs, parts), in_spe...  2.02 us
    unnamed x20, local copies, waits for them, and re-layouts  1.92 us
  transfers between devices with their start and end apart: 27, of which 12 were waited for; matrix products, arithmetic and copies ran while one was open for 0% of the time, Pallas kernels for 8%

profile of v3, /device:TPU:0, one launch (start us, length us, event | category | flops | bytes accessed | tf_op | source)
XLA Modules:
  0.0 94.6 jit_solution(11250078186502244615)
XLA Ops:
  0.6 0.6 pad_add_fusion.1.refs_4_.me_ref
  1.2 13.2 %encode.1 = (bf16[512,512]{1,0:T(8,128)(2,1)}, s32[2,512]{1,0:T(2,128)}, bf16[144,512]{1,0:T(8,128)(2,1)}, bf16[144,512]{1,0:T(8,128)(2,1)}, bf16[144,512]{1,0:T...) custom-call(bf16[512,2048]{1,0:T(8,128)(2,1)} %refs_0_.1, ...), custom_call_target="tpu_custom_call" | custom-call | tf_op jit(solution)/shard_map/encode/pallas_call | solution.py:209
  14.4 0.5 collective-permute-start.3
  14.9 2.6 %collective-permute-start = (bf16[144,512]{1,0:T(8,128)(2,1)}, bf16[144,512]{1,0:T(8,128)(2,1)S(1)}, u32[]{:S(2)}, u32[]{:S(2)}) collective-permute-start(bf16[144,512]{1,0:T(8,128)(2,1)} %get-tuple-element.35), channel_id=1, source_target_pairs={{0,2},{2,0},{4,6},{6,4},{1,3},{3,1},{5,7},{7,5},{8,10},{10,8},{12,... | collective-permute-start | bytes 442376 | tf_op jit(solution)/shard_map/ppermute | solution.py:486
  17.6 2.6 %collective-permute-start.1 = (bf16[144,512]{1,0:T(8,128)(2,1)}, bf16[144,512]{1,0:T(8,128)(2,1)S(1)}, u32[]{:S(2)}, u32[]{:S(2)}) collective-permute-start(bf16[144,512]{1,0:T(8,128)(2,1)} %get-tuple-element.36), channel_id=1, source_target_pairs={{0,4},{2,6},{4,0},{6,2},{1,5},{3,7},{5,1},{7,3},{8,12},{10,14},{12... | collective-permute-start | bytes 442376 | tf_op jit(solution)/shard_map/ppermute | solution.py:486
  20.2 0.0 collective-permute-start.2
  20.2 4.7 %collective-permute-done.refs_0_.refs_1_ = bf16[144,512]{1,0:T(8,128)(2,1)S(1)} collective-permute-done((bf16[144,512]{1,0:T(8,128)(2,1)}, bf16[144,512]{1,0:T(8,128)(2,1)S(1)}, u32[]{:S(2)}, u32[]{:S(2)}) %collective-permute-start) | collective-permute-done | bytes 147488 | tf_op jit(solution)/shard_map/ppermute | solution.py:486
  24.9 6.9 %collective-permute-done.1.refs_1_.refs_2_ = bf16[144,512]{1,0:T(8,128)(2,1)S(1)} collective-permute-done((bf16[144,512]{1,0:T(8,128)(2,1)}, bf16[144,512]{1,0:T(8,128)(2,1)S(1)}, u32[]{:S(2)}, u32[]{:S(2)}) %collective-permute-start.1) | collective-permute-done | bytes 147488 | tf_op jit(solution)/shard_map/ppermute | solution.py:486
  31.7 0.0 collective-permute-done.2.refs_2_.refs_3_
  31.7 0.0 collective-permute-done.3.peer_ref
  31.7 1.0 %copy-done.6 = bf16[320,512]{1,0:T(8,128)(2,1)S(1)} copy-done((bf16[320,512]{1,0:T(8,128)(2,1)S(1)}, bf16[320,512]{1,0:T(8,128)(2,1)}, u32[]{:S(2)}) %copy-start.6) | copy-done | bytes 327704
  32.8 3.0 %collective-permute-start.7 = (bf16[144,512]{1,0:T(8,128)(2,1)S(1)}, bf16[144,512]{1,0:T(8,128)(2,1)S(1)}, u32[]{:S(2)}, u32[]{:S(2)}) collective-permute-start(bf16[144,512]{1,0:T(8,128)(2,1)S(1)} %get-tuple-element.40.refs_4_), channel_id=1, source_target_pairs={{0,2},{2,0},{4,6},{6,4},{1,3},{3,1},{5,7},{7,5},{8,10},{10,8},{12,... | collective-permute-start | bytes 442376 | tf_op jit(solution)/shard_map/ppermute | solution.py:486
  35.8 1.1 %collective-permute-start.8 = (bf16[144,512]{1,0:T(8,128)(2,1)S(1)}, bf16[144,512]{1,0:T(8,128)(2,1)S(1)}, u32[]{:S(2)}, u32[]{:S(2)}) collective-permute-start(bf16[144,512]{1,0:T(8,128)(2,1)S(1)} %get-tuple-element.41.refs_5_), channel_id=1, source_target_pairs={{0,4},{2,6},{4,0},{6,2},{1,5},{3,7},{5,1},{7,3},{8,12},{10,14},{12... | collective-permute-start | bytes 442376 | tf_op jit(solution)/shard_map/ppermute | solution.py:486
  36.9 1.4 %collective-permute-start.16 = (bf16[144,512]{1,0:T(8,128)(2,1)S(1)}, bf16[144,512]{1,0:T(8,128)(2,1)S(1)}, u32[]{:S(2)}, u32[]{:S(2)}) collective-permute-start(bf16[144,512]{1,0:T(8,128)(2,1)S(1)} %get-tuple-element.42.refs_6_), channel_id=1, source_target_pairs={{0,6},{2,4},{4,2},{6,0},{1,7},{3,5},{5,3},{7,1},{8,14},{10,12},{12... | collective-permute-start | bytes 442376 | tf_op jit(solution)/shard_map/ppermute | solution.py:486
  38.3 0.9 copy-done.7
  39.2 1.6 %collective-permute-start.4 = (bf16[144,512]{1,0:T(8,128)(2,1)S(1)}, bf16[144,512]{1,0:T(8,128)(2,1)S(1)}, u32[]{:S(2)}, u32[]{:S(2)}) collective-permute-start(bf16[144,512]{1,0:T(8,128)(2,1)S(1)} %get-tuple-element.44), channel_id=1, source_target_pairs={{0,8},{8,0},{16,24},{24,16},{1,9},{9,1},{17,25},{25,17},{2,10},{10... | collective-permute-start | bytes 442376 | tf_op jit(solution)/shard_map/ppermute | solution.py:486
  40.8 1.5 %collective-permute-start.5 = (bf16[144,512]{1,0:T(8,128)(2,1)S(1)}, bf16[144,512]{1,0:T(8,128)(2,1)S(1)}, u32[]{:S(2)}, u32[]{:S(2)}) collective-permute-start(bf16[144,512]{1,0:T(8,128)(2,1)S(1)} %get-tuple-element.45), channel_id=1, source_target_pairs={{0,16},{8,24},{16,0},{24,8},{1,17},{9,25},{17,1},{25,9},{2,18},{10... | collective-permute-start | bytes 442376 | tf_op jit(solution)/shard_map/ppermute | solution.py:486
  42.3 0.0 collective-permute-done.7.refs_4_.refs_1_
  42.3 1.0 %collective-permute-start.6 = (bf16[144,512]{1,0:T(8,128)(2,1)S(1)}, bf16[144,512]{1,0:T(8,128)(2,1)S(1)}, u32[]{:S(2)}, u32[]{:S(2)}) collective-permute-start(bf16[144,512]{1,0:T(8,128)(2,1)S(1)} %get-tuple-element.46), channel_id=1, source_target_pairs={{0,24},{8,16},{16,8},{24,0},{1,25},{9,17},{17,9},{25,1},{2,26},{10... | collective-permute-start | bytes 442376 | tf_op jit(solution)/shard_map/ppermute | solution.py:486
  43.3 2.4 %collective-permute-done.4.refs_1_ = bf16[144,512]{1,0:T(8,128)(2,1)S(1)} collective-permute-done((bf16[144,512]{1,0:T(8,128)(2,1)S(1)}, bf16[144,512]{1,0:T(8,128)(2,1)S(1)}, u32[]{:S(2)}, u32[]{:S(2)}) %collective-permute-start.4) | collective-permute-done | bytes 147488 | tf_op jit(solution)/shard_map/ppermute | solution.py:486
  45.7 3.2 %collective-permute-done.5.refs_2_ = bf16[144,512]{1,0:T(8,128)(2,1)S(1)} collective-permute-done((bf16[144,512]{1,0:T(8,128)(2,1)S(1)}, bf16[144,512]{1,0:T(8,128)(2,1)S(1)}, u32[]{:S(2)}, u32[]{:S(2)}) %collective-permute-start.5) | collective-permute-done | bytes 147488 | tf_op jit(solution)/shard_map/ppermute | solution.py:486
  49.0 0.0 collective-permute-done.6.refs_3_
  49.0 0.5 collective-permute-done.8.refs_5_.refs_2_
  49.5 0.0 copy-start.3
  49.5 0.0 copy-start.4
  49.5 0.1 collective-permute-start.9
  49.6 0.0 collective-permute-done.16.refs_3_
  49.7 1.1 %sum_prod.1 = (f32[144,512]{1,0:T(8,128)S(1)}, bf16[144,512]{1,0:T(8,128)(2,1)S(1)}, bf16[144,512]{1,0:T(8,128)(2,1)S(1)}, bf16[144,512]{1,0:T(8,128)(2,1)S(1)}) custom-call(s32[3]{0:T(128)S(1)} %copy-done.9, s32[1,512]{1,0:T(1,128)S(1)} %pad_add_fusion.ids_ref, bf16[144,512]{1,0:T(8,128)(2,1)S(1)} %get-tuple-element.48.refs_0_, ...), custom_call_target="tpu_custom_call" | custom-call | tf_op jit(solution)/shard_map/sum_prod/pallas_call | solution.py:364
  50.8 1.6 %collective-permute-start.17 = (bf16[144,512]{1,0:T(8,128)(2,1)S(1)}, bf16[144,512]{1,0:T(8,128)(2,1)S(1)}, u32[]{:S(2)}, u32[]{:S(2)}) collective-permute-start(bf16[144,512]{1,0:T(8,128)(2,1)S(1)} %get-tuple-element.50), channel_id=1, source_target_pairs={{0,8},{8,0},{16,24},{24,16},{1,9},{9,1},{17,25},{25,17},{2,10},{10... | collective-permute-start | bytes 442376 | tf_op jit(solution)/shard_map/ppermute | solution.py:486
  52.4 1.5 %collective-permute-start.18 = (bf16[144,512]{1,0:T(8,128)(2,1)S(1)}, bf16[144,512]{1,0:T(8,128)(2,1)S(1)}, u32[]{:S(2)}, u32[]{:S(2)}) collective-permute-start(bf16[144,512]{1,0:T(8,128)(2,1)S(1)} %get-tuple-element.51), channel_id=1, source_target_pairs={{0,16},{8,24},{16,0},{24,8},{1,17},{9,25},{17,1},{25,9},{2,18},{10... | collective-permute-start | bytes 442376 | tf_op jit(solution)/shard_map/ppermute | solution.py:486
  53.9 0.5 collective-permute-start.19
  54.4 0.0 collective-permute-done.9.peer_ref
  54.4 2.3 %update_cust.1 = (bf16[512,512]{1,0:T(8,128)(2,1)}, bf16[512,512]{1,0:T(8,128)(2,1)S(1)}) custom-call(bf16[576,512]{1,0:T(8,128)(2,1)S(1)} %join.1.own_ref, bf16[576,512]{1,0:T(8,128)(2,1)S(1)} %collective-permute-done.9.peer_ref, bf16[512,512]{1,0:T(8,128)(2,1)S(1)} %copy-done.1, bf16[512,512]{1,0:T(8,128)(2,1)S(1)} %copy-done.2), custom_call_target="tpu_custom_call" | custom-call | tf_op jit(solution)/shard_map/update_cust/pallas_call | solution.py:333
  56.7 2.0 %collective-permute-start.10 = (bf16[128,512]{1,0:T(8,128)(2,1)S(1)}, bf16[128,512]{1,0:T(8,128)(2,1)S(1)}, u32[]{:S(2)}, u32[]{:S(2)}) collective-permute-start(bf16[128,512]{1,0:T(8,128)(2,1)S(1)} %bitcast.21), channel_id=1, source_target_pairs={{0,2},{2,0},{4,6},{6,4},{1,3},{3,1},{5,7},{7,5},{8,10},{10,8},{12,... | collective-permute-start | bytes 393224 | tf_op jit(solution)/shard_map/ppermute | solution.py:486
  58.7 1.0 %collective-permute-start.11 = (bf16[128,512]{1,0:T(8,128)(2,1)S(1)}, bf16[128,512]{1,0:T(8,128)(2,1)S(1)}, u32[]{:S(2)}, u32[]{:S(2)}) collective-permute-start(bf16[128,512]{1,0:T(8,128)(2,1)S(1)} %bitcast.20), channel_id=1, source_target_pairs={{0,4},{2,6},{4,0},{6,2},{1,5},{3,7},{5,1},{7,3},{8,12},{10,14},{12... | collective-permute-start | bytes 393224 | tf_op jit(solution)/shard_map/ppermute | solution.py:486
  59.8 0.0 collective-permute-done.17.rest_1_
  59.8 1.5 %collective-permute-start.12 = (bf16[128,512]{1,0:T(8,128)(2,1)S(1)}, bf16[128,512]{1,0:T(8,128)(2,1)S(1)}, u32[]{:S(2)}, u32[]{:S(2)}) collective-permute-start(bf16[128,512]{1,0:T(8,128)(2,1)S(1)} %bitcast.19), channel_id=1, source_target_pairs={{0,6},{2,4},{4,2},{6,0},{1,7},{3,5},{5,3},{7,1},{8,14},{10,12},{12... | collective-permute-start | bytes 393224 | tf_op jit(solution)/shard_map/ppermute | solution.py:486
  61.2 0.2 collective-permute-done.18.rest_2_
  61.5 0.0 collective-permute-done.19.rest_3_
  61.5 2.3 %collective-permute-done.10.rest_4_ = bf16[128,512]{1,0:T(8,128)(2,1)S(1)} collective-permute-done((bf16[128,512]{1,0:T(8,128)(2,1)S(1)}, bf16[128,512]{1,0:T(8,128)(2,1)S(1)}, u32[]{:S(2)}, u32[]{:S(2)}) %collective-permute-start.10) | collective-permute-done | bytes 131104 | tf_op jit(solution)/shard_map/ppermute | solution.py:486
  63.8 6.1 %collective-permute-done.11.rest_5_ = bf16[128,512]{1,0:T(8,128)(2,1)S(1)} collective-permute-done((bf16[128,512]{1,0:T(8,128)(2,1)S(1)}, bf16[128,512]{1,0:T(8,128)(2,1)S(1)}, u32[]{:S(2)}, u32[]{:S(2)}) %collective-permute-start.11) | collective-permute-done | bytes 131104 | tf_op jit(solution)/shard_map/ppermute | solution.py:486
  69.9 1.0 %update_prod.1.rest_0_ = bf16[128,512]{1,0:T(8,128)(2,1)S(1)} custom-call(s32[3]{0:T(128)S(1)} %copy-done.9, bf16[512,512]{1,0:T(8,128)(2,1)S(1)} %copy-done.3, bf16[512,512]{1,0:T(8,128)(2,1)S(1)} %copy-done.4, f32[144,512]{1,0:T(8,128)S(1)} %get-tuple-element.49.rest_0_, bf16[144,512]{1,0:T(8,128)(2,1)S(1)} %collective-permute-done.17.rest_1_, ...), custom_call_target="tpu_custom_call" | custom-call | tf_op jit(solution)/shard_map/update_prod/pallas_call | solution.py:388
  70.9 2.5 %collective-permute-start.22 = (bf16[128,512]{1,0:T(8,128)(2,1)S(1)}, bf16[128,512]{1,0:T(8,128)(2,1)S(1)}, u32[]{:S(2)}, u32[]{:S(2)}) collective-permute-start(bf16[128,512]{1,0:T(8,128)(2,1)S(1)} %update_prod.1.rest_0_), channel_id=1, source_target_pairs={{0,24},{8,16},{16,8},{24,0},{1,25},{9,17},{17,9},{25,1},{2,26},{10... | collective-permute-start | bytes 393224 | tf_op jit(solution)/shard_map/ppermute | solution.py:486
  73.4 0.5 collective-permute-start.21
  73.9 0.6 collective-permute-start.20
  74.5 0.0 collective-permute-done.12.rest_4_
  74.5 1.5 %collective-permute-start.13 = (bf16[128,512]{1,0:T(8,128)(2,1)S(1)}, bf16[128,512]{1,0:T(8,128)(2,1)S(1)}, u32[]{:S(2)}, u32[]{:S(2)}) collective-permute-start(bf16[128,512]{1,0:T(8,128)(2,1)S(1)} %pad_maximum_fusion.1), channel_id=1, source_target_pairs={{0,8},{8,0},{16,24},{24,16},{1,9},{9,1},{17,25},{25,17},{2,10},{10... | collective-permute-start | bytes 393224 | tf_op jit(solution)/shard_map/ppermute | solution.py:486
  76.1 1.6 %collective-permute-start.14 = (bf16[128,512]{1,0:T(8,128)(2,1)S(1)}, bf16[128,512]{1,0:T(8,128)(2,1)S(1)}, u32[]{:S(2)}, u32[]{:S(2)}) collective-permute-start(bf16[128,512]{1,0:T(8,128)(2,1)S(1)} %pad_maximum_fusion.2), channel_id=1, source_target_pairs={{0,16},{8,24},{16,0},{24,8},{1,17},{9,25},{17,1},{25,9},{2,18},{10... | collective-permute-start | bytes 393224 | tf_op jit(solution)/shard_map/ppermute | solution.py:486
  77.7 0.0 collective-permute-done.22.rest_3_
  77.7 1.7 %collective-permute-start.15 = (bf16[128,512]{1,0:T(8,128)(2,1)S(1)}, bf16[128,512]{1,0:T(8,128)(2,1)S(1)}, u32[]{:S(2)}, u32[]{:S(2)}) collective-permute-start(bf16[128,512]{1,0:T(8,128)(2,1)S(1)} %pad_maximum_fusion.3), channel_id=1, source_target_pairs={{0,24},{8,16},{16,8},{24,0},{1,25},{9,17},{17,9},{25,1},{2,26},{10... | collective-permute-start | bytes 393224 | tf_op jit(solution)/shard_map/ppermute | solution.py:486
  79.4 0.0 collective-permute-done.21.rest_2_
  79.4 2.0 %reply_prod.1 = (bf16[512,512]{1,0:T(8,128)(2,1)}, bf16[128,512]{1,0:T(8,128)(2,1)S(1)}, bf16[128,512]{1,0:T(8,128)(2,1)S(1)}, bf16[128,512]{1,0:T(8,128)(2,1)S(1)}, bf16[128,512]{1,0:T(8,128)(2,1)S(1)}) custom-call(s32[3]{0:T(128)S(1)} %copy-done.9, s32[1,512]{1,0:T(1,128)S(1)} %pad_add_fusion.ids_ref, bf16[128,512]{1,0:T(8,128)(2,1)S(1)} %update_prod.1.rest_0_, ...), custom_call_target="tpu_custom_call" | custom-call | tf_op jit(solution)/shard_map/reply_prod/pallas_call | solution.py:415
  81.4 0.3 collective-permute-start.23
  81.7 2.7 %collective-permute-start.24 = (bf16[128,512]{1,0:T(8,128)(2,1)S(1)}, bf16[128,512]{1,0:T(8,128)(2,1)S(1)}, u32[]{:S(2)}, u32[]{:S(2)}) collective-permute-start(bf16[128,512]{1,0:T(8,128)(2,1)S(1)} %get-tuple-element.55), channel_id=1, source_target_pairs={{0,4},{2,6},{4,0},{6,2},{1,5},{3,7},{5,1},{7,3},{8,12},{10,14},{12... | collective-permute-start | bytes 393224 | tf_op jit(solution)/shard_map/ppermute | solution.py:486
  84.4 0.0 collective-permute-done.13.rest_1_
  84.4 1.4 %collective-permute-start.25 = (bf16[128,512]{1,0:T(8,128)(2,1)S(1)}, bf16[128,512]{1,0:T(8,128)(2,1)S(1)}, u32[]{:S(2)}, u32[]{:S(2)}) collective-permute-start(bf16[128,512]{1,0:T(8,128)(2,1)S(1)} %get-tuple-element.56), channel_id=1, source_target_pairs={{0,6},{2,4},{4,2},{6,0},{1,7},{3,5},{5,3},{7,1},{8,14},{10,12},{12... | collective-permute-start | bytes 393224 | tf_op jit(solution)/shard_map/ppermute | solution.py:486
  85.8 0.0 collective-permute-done.14.rest_2_
  85.9 0.7 finish_cust.1.refs_4_.part_ref
  86.6 1.0 %collective-permute-done.23.refs_1_ = bf16[128,512]{1,0:T(8,128)(2,1)S(1)} collective-permute-done((bf16[128,512]{1,0:T(8,128)(2,1)S(1)}, bf16[128,512]{1,0:T(8,128)(2,1)S(1)}, u32[]{:S(2)}, u32[]{:S(2)}) %collective-permute-start.23) | collective-permute-done | bytes 131104 | tf_op jit(solution)/shard_map/ppermute | solution.py:486
  87.6 1.4 %collective-permute-done.24.refs_2_ = bf16[128,512]{1,0:T(8,128)(2,1)S(1)} collective-permute-done((bf16[128,512]{1,0:T(8,128)(2,1)S(1)}, bf16[128,512]{1,0:T(8,128)(2,1)S(1)}, u32[]{:S(2)}, u32[]{:S(2)}) %collective-permute-start.24) | collective-permute-done | bytes 131104 | tf_op jit(solution)/shard_map/ppermute | solution.py:486
  89.0 2.3 %collective-permute-done.25.refs_3_ = bf16[128,512]{1,0:T(8,128)(2,1)S(1)} collective-permute-done((bf16[128,512]{1,0:T(8,128)(2,1)S(1)}, bf16[128,512]{1,0:T(8,128)(2,1)S(1)}, u32[]{:S(2)}, u32[]{:S(2)}) %collective-permute-start.25) | collective-permute-done | bytes 131104 | tf_op jit(solution)/shard_map/ppermute | solution.py:486
  91.3 0.1 collective-permute-start.26
  91.4 1.5 %collective-permute-done.26.rest_1_ = bf16[256,512]{1,0:T(8,128)(2,1)S(1)} collective-permute-done((bf16[256,512]{1,0:T(8,128)(2,1)S(1)}, bf16[256,512]{1,0:T(8,128)(2,1)S(1)}, u32[]{:S(2)}, u32[]{:S(2)}) %collective-permute-start.26) | collective-permute-done | bytes 262176 | tf_op jit(solution)/shard_map/ppermute | solution.py:486
  92.9 1.6 %finish.1 = bf16[512,512]{1,0:T(8,128)(2,1)} custom-call(s32[2,512]{1,0:T(2,128)S(1)} %copy-done.8, f32[512,512]{1,0:T(8,128)S(1)} %finish_cust.1.refs_4_.part_ref, bf16[1024,512]{1,0:T(8,128)(2,1)S(1)} %copy-done, bf16[256,512]{1,0:T(8,128)(2,1)S(1)} %get-tuple-element.57.rest_0_, bf16[256,512]{1,0:T(8,128)(2,1)S(1)} %collective-permute-done.26.rest_1_), custom_call_target="tpu_custom_call" | custom-call | tf_op jit(solution)/shard_map/finish/pallas_call | solution.py:454
  (40 shorter events, 0.4 us)
Async XLA Ops:
  14.4 35.3 %copy-start.9 = (s32[3]{0:T(128)S(1)}, s32[3]{0:T(128)}, u32[]{:S(2)}) copy-start(s32[3]{0:T(128)} %pad_add_fusion.1.refs_4_.me_ref) | copy-start | bytes 40
  14.4 17.3 %collective-permute-start.3 = (bf16[320,512]{1,0:T(8,128)(2,1)}, bf16[320,512]{1,0:T(8,128)(2,1)S(1)}, u32[]{:S(2)}, u32[]{:S(2)}) collective-permute-start(bf16[320,512]{1,0:T(8,128)(2,1)} %get-tuple-element.39), channel_id=1, source_target_pairs={{0,1},{1,0},{2,3},{3,2},{4,5},{5,4},{6,7},{7,6},{8,9},{9,8},{10,11... | collective-permute-start | bytes 983048 | tf_op jit(solution)/shard_map/ppermute | solution.py:486
  14.9 10.0 %collective-permute-start = (bf16[144,512]{1,0:T(8,128)(2,1)}, bf16[144,512]{1,0:T(8,128)(2,1)S(1)}, u32[]{:S(2)}, u32[]{:S(2)}) collective-permute-start(bf16[144,512]{1,0:T(8,128)(2,1)} %get-tuple-element.35), channel_id=1, source_target_pairs={{0,2},{2,0},{4,6},{6,4},{1,3},{3,1},{5,7},{7,5},{8,10},{10,8},{12,... | collective-permute-start | bytes 442376 | tf_op jit(solution)/shard_map/ppermute | solution.py:486
  17.6 14.2 %collective-permute-start.1 = (bf16[144,512]{1,0:T(8,128)(2,1)}, bf16[144,512]{1,0:T(8,128)(2,1)S(1)}, u32[]{:S(2)}, u32[]{:S(2)}) collective-permute-start(bf16[144,512]{1,0:T(8,128)(2,1)} %get-tuple-element.36), channel_id=1, source_target_pairs={{0,4},{2,6},{4,0},{6,2},{1,5},{3,7},{5,1},{7,3},{8,12},{10,14},{12... | collective-permute-start | bytes 442376 | tf_op jit(solution)/shard_map/ppermute | solution.py:486
  20.2 11.6 %collective-permute-start.2 = (bf16[144,512]{1,0:T(8,128)(2,1)}, bf16[144,512]{1,0:T(8,128)(2,1)S(1)}, u32[]{:S(2)}, u32[]{:S(2)}) collective-permute-start(bf16[144,512]{1,0:T(8,128)(2,1)} %get-tuple-element.37), channel_id=1, source_target_pairs={{0,6},{2,4},{4,2},{6,0},{1,7},{3,5},{5,3},{7,1},{8,14},{10,12},{12... | collective-permute-start | bytes 442376 | tf_op jit(solution)/shard_map/ppermute | solution.py:486
  31.7 1.0 %copy-start.6 = (bf16[320,512]{1,0:T(8,128)(2,1)S(1)}, bf16[320,512]{1,0:T(8,128)(2,1)}, u32[]{:S(2)}) copy-start(bf16[320,512]{1,0:T(8,128)(2,1)} %get-tuple-element.38.own_ref) | copy-start | bytes 983044
  32.7 21.6 %copy-start.1 = (bf16[512,512]{1,0:T(8,128)(2,1)S(1)}, bf16[512,512]{1,0:T(8,128)(2,1)}, u32[]{:S(2)}) copy-start(bf16[512,512]{1,0:T(8,128)(2,1)} %state_ref.2) | copy-start | bytes 1572868
  32.7 21.6 %copy-start.2 = (bf16[512,512]{1,0:T(8,128)(2,1)S(1)}, bf16[512,512]{1,0:T(8,128)(2,1)}, u32[]{:S(2)}) copy-start(bf16[512,512]{1,0:T(8,128)(2,1)} %w_ref.4) | copy-start | bytes 1572868
  32.8 9.5 %collective-permute-start.7 = (bf16[144,512]{1,0:T(8,128)(2,1)S(1)}, bf16[144,512]{1,0:T(8,128)(2,1)S(1)}, u32[]{:S(2)}, u32[]{:S(2)}) collective-permute-start(bf16[144,512]{1,0:T(8,128)(2,1)S(1)} %get-tuple-element.40.refs_4_), channel_id=1, source_target_pairs={{0,2},{2,0},{4,6},{6,4},{1,3},{3,1},{5,7},{7,5},{8,10},{10,8},{12,... | collective-permute-start | bytes 442376 | tf_op jit(solution)/shard_map/ppermute | solution.py:486
  35.8 13.7 %collective-permute-start.8 = (bf16[144,512]{1,0:T(8,128)(2,1)S(1)}, bf16[144,512]{1,0:T(8,128)(2,1)S(1)}, u32[]{:S(2)}, u32[]{:S(2)}) collective-permute-start(bf16[144,512]{1,0:T(8,128)(2,1)S(1)} %get-tuple-element.41.refs_5_), channel_id=1, source_target_pairs={{0,4},{2,6},{4,0},{6,2},{1,5},{3,7},{5,1},{7,3},{8,12},{10,14},{12... | collective-permute-start | bytes 442376 | tf_op jit(solution)/shard_map/ppermute | solution.py:486
  36.9 12.7 %collective-permute-start.16 = (bf16[144,512]{1,0:T(8,128)(2,1)S(1)}, bf16[144,512]{1,0:T(8,128)(2,1)S(1)}, u32[]{:S(2)}, u32[]{:S(2)}) collective-permute-start(bf16[144,512]{1,0:T(8,128)(2,1)S(1)} %get-tuple-element.42.refs_6_), channel_id=1, source_target_pairs={{0,6},{2,4},{4,2},{6,0},{1,7},{3,5},{5,3},{7,1},{8,14},{10,12},{12... | collective-permute-start | bytes 442376 | tf_op jit(solution)/shard_map/ppermute | solution.py:486
  38.3 0.9 copy-start.7
  39.2 6.5 %collective-permute-start.4 = (bf16[144,512]{1,0:T(8,128)(2,1)S(1)}, bf16[144,512]{1,0:T(8,128)(2,1)S(1)}, u32[]{:S(2)}, u32[]{:S(2)}) collective-permute-start(bf16[144,512]{1,0:T(8,128)(2,1)S(1)} %get-tuple-element.44), channel_id=1, source_target_pairs={{0,8},{8,0},{16,24},{24,16},{1,9},{9,1},{17,25},{25,17},{2,10},{10... | collective-permute-start | bytes 442376 | tf_op jit(solution)/shard_map/ppermute | solution.py:486
  40.8 8.2 %collective-permute-start.5 = (bf16[144,512]{1,0:T(8,128)(2,1)S(1)}, bf16[144,512]{1,0:T(8,128)(2,1)S(1)}, u32[]{:S(2)}, u32[]{:S(2)}) collective-permute-start(bf16[144,512]{1,0:T(8,128)(2,1)S(1)} %get-tuple-element.45), channel_id=1, source_target_pairs={{0,16},{8,24},{16,0},{24,8},{1,17},{9,25},{17,1},{25,9},{2,18},{10... | collective-permute-start | bytes 442376 | tf_op jit(solution)/shard_map/ppermute | solution.py:486
  42.3 6.6 %collective-permute-start.6 = (bf16[144,512]{1,0:T(8,128)(2,1)S(1)}, bf16[144,512]{1,0:T(8,128)(2,1)S(1)}, u32[]{:S(2)}, u32[]{:S(2)}) collective-permute-start(bf16[144,512]{1,0:T(8,128)(2,1)S(1)} %get-tuple-element.46), channel_id=1, source_target_pairs={{0,24},{8,16},{16,8},{24,0},{1,25},{9,17},{17,9},{25,1},{2,26},{10... | collective-permute-start | bytes 442376 | tf_op jit(solution)/shard_map/ppermute | solution.py:486
  49.5 20.4 %copy-start.3 = (bf16[512,512]{1,0:T(8,128)(2,1)S(1)}, bf16[512,512]{1,0:T(8,128)(2,1)}, u32[]{:S(2)}) copy-start(bf16[512,512]{1,0:T(8,128)(2,1)} %state_ref.3) | copy-start | bytes 1572868
  49.5 20.4 %copy-start.4 = (bf16[512,512]{1,0:T(8,128)(2,1)S(1)}, bf16[512,512]{1,0:T(8,128)(2,1)}, u32[]{:S(2)}) copy-start(bf16[512,512]{1,0:T(8,128)(2,1)} %w_ref.6) | copy-start | bytes 1572868
  49.5 4.8 %collective-permute-start.9 = (bf16[576,512]{1,0:T(8,128)(2,1)S(1)}, bf16[576,512]{1,0:T(8,128)(2,1)S(1)}, u32[]{:S(2)}, u32[]{:S(2)}) collective-permute-start(bf16[576,512]{1,0:T(8,128)(2,1)S(1)} %join.1.own_ref), channel_id=1, source_target_pairs={{0,1},{1,0},{2,3},{3,2},{4,5},{5,4},{6,7},{7,6},{8,9},{9,8},{10,11... | collective-permute-start | bytes 1769480 | tf_op jit(solution)/shard_map/ppermute | solution.py:486
  50.8 9.0 %collective-permute-start.17 = (bf16[144,512]{1,0:T(8,128)(2,1)S(1)}, bf16[144,512]{1,0:T(8,128)(2,1)S(1)}, u32[]{:S(2)}, u32[]{:S(2)}) collective-permute-start(bf16[144,512]{1,0:T(8,128)(2,1)S(1)} %get-tuple-element.50), channel_id=1, source_target_pairs={{0,8},{8,0},{16,24},{24,16},{1,9},{9,1},{17,25},{25,17},{2,10},{10... | collective-permute-start | bytes 442376 | tf_op jit(solution)/shard_map/ppermute | solution.py:486
  52.4 9.1 %collective-permute-start.18 = (bf16[144,512]{1,0:T(8,128)(2,1)S(1)}, bf16[144,512]{1,0:T(8,128)(2,1)S(1)}, u32[]{:S(2)}, u32[]{:S(2)}) collective-permute-start(bf16[144,512]{1,0:T(8,128)(2,1)S(1)} %get-tuple-element.51), channel_id=1, source_target_pairs={{0,16},{8,24},{16,0},{24,8},{1,17},{9,25},{17,1},{25,9},{2,18},{10... | collective-permute-start | bytes 442376 | tf_op jit(solution)/shard_map/ppermute | solution.py:486
  53.9 7.6 %collective-permute-start.19 = (bf16[144,512]{1,0:T(8,128)(2,1)S(1)}, bf16[144,512]{1,0:T(8,128)(2,1)S(1)}, u32[]{:S(2)}, u32[]{:S(2)}) collective-permute-start(bf16[144,512]{1,0:T(8,128)(2,1)S(1)} %get-tuple-element.52), channel_id=1, source_target_pairs={{0,24},{8,16},{16,8},{24,0},{1,25},{9,17},{17,9},{25,1},{2,26},{10... | collective-permute-start | bytes 442376 | tf_op jit(solution)/shard_map/ppermute | solution.py:486
  56.7 7.1 %collective-permute-start.10 = (bf16[128,512]{1,0:T(8,128)(2,1)S(1)}, bf16[128,512]{1,0:T(8,128)(2,1)S(1)}, u32[]{:S(2)}, u32[]{:S(2)}) collective-permute-start(bf16[128,512]{1,0:T(8,128)(2,1)S(1)} %bitcast.21), channel_id=1, source_target_pairs={{0,2},{2,0},{4,6},{6,4},{1,3},{3,1},{5,7},{7,5},{8,10},{10,8},{12,... | collective-permute-start | bytes 393224 | tf_op jit(solution)/shard_map/ppermute | solution.py:486
  58.7 11.2 %collective-permute-start.11 = (bf16[128,512]{1,0:T(8,128)(2,1)S(1)}, bf16[128,512]{1,0:T(8,128)(2,1)S(1)}, u32[]{:S(2)}, u32[]{:S(2)}) collective-permute-start(bf16[128,512]{1,0:T(8,128)(2,1)S(1)} %bitcast.20), channel_id=1, source_target_pairs={{0,4},{2,6},{4,0},{6,2},{1,5},{3,7},{5,1},{7,3},{8,12},{10,14},{12... | collective-permute-start | bytes 393224 | tf_op jit(solution)/shard_map/ppermute | solution.py:486
  59.8 14.7 %collective-permute-start.12 = (bf16[128,512]{1,0:T(8,128)(2,1)S(1)}, bf16[128,512]{1,0:T(8,128)(2,1)S(1)}, u32[]{:S(2)}, u32[]{:S(2)}) collective-permute-start(bf16[128,512]{1,0:T(8,128)(2,1)S(1)} %bitcast.19), channel_id=1, source_target_pairs={{0,6},{2,4},{4,2},{6,0},{1,7},{3,5},{5,3},{7,1},{8,14},{10,12},{12... | collective-permute-start | bytes 393224 | tf_op jit(solution)/shard_map/ppermute | solution.py:486
  69.9 15.9 %copy-start = (bf16[1024,512]{1,0:T(8,128)(2,1)S(1)}, bf16[1024,512]{1,0:T(8,128)(2,1)}, u32[]{:S(2)}) copy-start(bf16[1024,512]{1,0:T(8,128)(2,1)} %w_ref.7) | copy-start | bytes 3145732
  69.9 15.9 %copy-start.5 = (bf16[512,512]{1,0:T(8,128)(2,1)S(1)}, bf16[512,512]{1,0:T(8,128)(2,1)}, u32[]{:S(2)}) copy-start(bf16[512,512]{1,0:T(8,128)(2,1)} %get-tuple-element.33.h_ref) | copy-start | bytes 1572868
  69.9 15.9 %copy-start.8 = (s32[2,512]{1,0:T(2,128)S(1)}, s32[2,512]{1,0:T(2,128)}, u32[]{:S(2)}) copy-start(s32[2,512]{1,0:T(2,128)} %get-tuple-element.32.order_ref) | copy-start | bytes 12292
  70.9 6.8 %collective-permute-start.22 = (bf16[128,512]{1,0:T(8,128)(2,1)S(1)}, bf16[128,512]{1,0:T(8,128)(2,1)S(1)}, u32[]{:S(2)}, u32[]{:S(2)}) collective-permute-start(bf16[128,512]{1,0:T(8,128)(2,1)S(1)} %update_prod.1.rest_0_), channel_id=1, source_target_pairs={{0,24},{8,16},{16,8},{24,0},{1,25},{9,17},{17,9},{25,1},{2,26},{10... | collective-permute-start | bytes 393224 | tf_op jit(solution)/shard_map/ppermute | solution.py:486
  73.4 6.0 %collective-permute-start.21 = (bf16[128,512]{1,0:T(8,128)(2,1)S(1)}, bf16[128,512]{1,0:T(8,128)(2,1)S(1)}, u32[]{:S(2)}, u32[]{:S(2)}) collective-permute-start(bf16[128,512]{1,0:T(8,128)(2,1)S(1)} %update_prod.1.rest_0_), channel_id=1, source_target_pairs={{0,16},{8,24},{16,0},{24,8},{1,17},{9,25},{17,1},{25,9},{2,18},{10... | collective-permute-start | bytes 393224 | tf_op jit(solution)/shard_map/ppermute | solution.py:486
  73.9 5.5 %collective-permute-start.20 = (bf16[128,512]{1,0:T(8,128)(2,1)S(1)}, bf16[128,512]{1,0:T(8,128)(2,1)S(1)}, u32[]{:S(2)}, u32[]{:S(2)}) collective-permute-start(bf16[128,512]{1,0:T(8,128)(2,1)S(1)} %update_prod.1.rest_0_), channel_id=1, source_target_pairs={{0,8},{8,0},{16,24},{24,16},{1,9},{9,1},{17,25},{25,17},{2,10},{10... | collective-permute-start | bytes 393224 | tf_op jit(solution)/shard_map/ppermute | solution.py:486
  74.5 9.9 %collective-permute-start.13 = (bf16[128,512]{1,0:T(8,128)(2,1)S(1)}, bf16[128,512]{1,0:T(8,128)(2,1)S(1)}, u32[]{:S(2)}, u32[]{:S(2)}) collective-permute-start(bf16[128,512]{1,0:T(8,128)(2,1)S(1)} %pad_maximum_fusion.1), channel_id=1, source_target_pairs={{0,8},{8,0},{16,24},{24,16},{1,9},{9,1},{17,25},{25,17},{2,10},{10... | collective-permute-start | bytes 393224 | tf_op jit(solution)/shard_map/ppermute | solution.py:486
  76.1 9.7 %collective-permute-start.14 = (bf16[128,512]{1,0:T(8,128)(2,1)S(1)}, bf16[128,512]{1,0:T(8,128)(2,1)S(1)}, u32[]{:S(2)}, u32[]{:S(2)}) collective-permute-start(bf16[128,512]{1,0:T(8,128)(2,1)S(1)} %pad_maximum_fusion.2), channel_id=1, source_target_pairs={{0,16},{8,24},{16,0},{24,8},{1,17},{9,25},{17,1},{25,9},{2,18},{10... | collective-permute-start | bytes 393224 | tf_op jit(solution)/shard_map/ppermute | solution.py:486
  77.7 8.1 %collective-permute-start.15 = (bf16[128,512]{1,0:T(8,128)(2,1)S(1)}, bf16[128,512]{1,0:T(8,128)(2,1)S(1)}, u32[]{:S(2)}, u32[]{:S(2)}) collective-permute-start(bf16[128,512]{1,0:T(8,128)(2,1)S(1)} %pad_maximum_fusion.3), channel_id=1, source_target_pairs={{0,24},{8,16},{16,8},{24,0},{1,25},{9,17},{17,9},{25,1},{2,26},{10... | collective-permute-start | bytes 393224 | tf_op jit(solution)/shard_map/ppermute | solution.py:486
  81.4 6.2 %collective-permute-start.23 = (bf16[128,512]{1,0:T(8,128)(2,1)S(1)}, bf16[128,512]{1,0:T(8,128)(2,1)S(1)}, u32[]{:S(2)}, u32[]{:S(2)}) collective-permute-start(bf16[128,512]{1,0:T(8,128)(2,1)S(1)} %get-tuple-element.54), channel_id=1, source_target_pairs={{0,2},{2,0},{4,6},{6,4},{1,3},{3,1},{5,7},{7,5},{8,10},{10,8},{12,... | collective-permute-start | bytes 393224 | tf_op jit(solution)/shard_map/ppermute | solution.py:486
  81.7 7.3 %collective-permute-start.24 = (bf16[128,512]{1,0:T(8,128)(2,1)S(1)}, bf16[128,512]{1,0:T(8,128)(2,1)S(1)}, u32[]{:S(2)}, u32[]{:S(2)}) collective-permute-start(bf16[128,512]{1,0:T(8,128)(2,1)S(1)} %get-tuple-element.55), channel_id=1, source_target_pairs={{0,4},{2,6},{4,0},{6,2},{1,5},{3,7},{5,1},{7,3},{8,12},{10,14},{12... | collective-permute-start | bytes 393224 | tf_op jit(solution)/shard_map/ppermute | solution.py:486
  84.4 6.9 %collective-permute-start.25 = (bf16[128,512]{1,0:T(8,128)(2,1)S(1)}, bf16[128,512]{1,0:T(8,128)(2,1)S(1)}, u32[]{:S(2)}, u32[]{:S(2)}) collective-permute-start(bf16[128,512]{1,0:T(8,128)(2,1)S(1)} %get-tuple-element.56), channel_id=1, source_target_pairs={{0,6},{2,4},{4,2},{6,0},{1,7},{3,5},{5,3},{7,1},{8,14},{10,12},{12... | collective-permute-start | bytes 393224 | tf_op jit(solution)/shard_map/ppermute | solution.py:486
  91.3 1.6 %collective-permute-start.26 = (bf16[256,512]{1,0:T(8,128)(2,1)S(1)}, bf16[256,512]{1,0:T(8,128)(2,1)S(1)}, u32[]{:S(2)}, u32[]{:S(2)}) collective-permute-start(bf16[256,512]{1,0:T(8,128)(2,1)S(1)} %get-tuple-element.58), channel_id=1, source_target_pairs={{0,1},{1,0},{2,3},{3,2},{4,5},{5,4},{6,7},{7,6},{8,9},{9,8},{10,11... | collective-permute-start | bytes 786440 | tf_op jit(solution)/shard_map/ppermute | solution.py:486

commit v4 on v3

--- a/solution.py
+++ b/solution.py
@@ -16,12 +16,12 @@
 BF = jnp.bfloat16
 F32 = jnp.float32
 ID_ROWS = 16
+LANES = 128
 VMEM = pl.BlockSpec(memory_space=pltpu.VMEM)
 HBM = pl.BlockSpec(memory_space=pltpu.HBM)
 ANY = pl.BlockSpec(memory_space=pl.ANY)
-SMEM = pl.BlockSpec(memory_space=pltpu.SMEM)
 PARAMS = pltpu.CompilerParams(vmem_limit_bytes=16 * 1024 * 1024)
-ENCODE_PARAMS = pltpu.CompilerParams(vmem_limit_bytes=60 * 1024 * 1024)
+ENCODE_PARAMS = pltpu.CompilerParams(vmem_limit_bytes=52 * 1024 * 1024)
 
 
 def rms_norm(vector):
@@ -98,16 +98,16 @@
     return lax.div(index, size), lax.rem(index, size)
 
 
-def send_orders(sizes, me_ref, pos, cust_slot, prod_slot, live_ref):
+def send_orders(sizes, index_ref):
     nr, nz, nc = sizes
-    rows = pos.shape[1]
+    rows = index_ref.shape[1]
     cs, ps = rows // (nr * nz), rows // (nz * nc)
-    mr, mz, mc = me_ref[0], me_ref[1], me_ref[2]
+    mr, mz, mc = lax.axis_index("rev"), lax.axis_index("cust"), lax.axis_index("prod")
+    pos, cust_slot, prod_slot = (index_ref[n:n + 1, :] for n in range(3))
     block, k = split(iota((1, rows), 1), cs)
     r, z = split(block, nz)
-    live = jnp.zeros((1, rows), jnp.int32)
-    for b in range(nr * nz):
-        live = jnp.where(block == b, live_ref[0, b], live)
+    counts = index_ref[3:4, :LANES].astype(F32).astype(BF)
+    live = dot(counts, one_hot(LANES, 0, block)).astype(jnp.int32)
     cust = mz ^ z, mr ^ r, k, jnp.where(k < live, cust_slot + 1, 0)
     prod_id = jnp.where(k < live, prod_slot + 1, 0)
     block, k = split(pos, ps)
@@ -116,11 +116,10 @@
 
 
 def encode_kernel(sizes, rows, *refs):
-    x_hbm, w_qkv_hbm, w_out_hbm, w_msg_hbm, me_ref = refs[:5]
-    index_hbm, (h_ref, order_ref) = refs[5:9], refs[9:11]
-    x_ref, w_qkv, w_out, w_msg, pos_ref, cust_slot_ref, prod_slot_ref, live_ref, sem = refs[-9:]
+    x_hbm, w_qkv_hbm, w_out_hbm, w_msg_hbm, index_ref, h_ref, order_ref = refs[:7]
+    x_ref, w_qkv, w_out, w_msg, sem = refs[-5:]
     nr, nz, nc = sizes
-    cust_refs, prod_refs = refs[11:11 + nz], refs[11 + nz:-9]
+    cust_refs, prod_refs = refs[7:7 + nz], refs[7 + nz:-5]
     chunks = x_hbm.shape[0] // rows
     copy = pltpu.make_async_copy
     x_copies = [
@@ -133,16 +132,9 @@
     ]
     w_copies.append(copy(w_out_hbm, w_out, sem.at[chunks + 3]))
     last = copy(w_msg_hbm, w_msg, sem.at[chunks + 4])
-    index_refs = (pos_ref, cust_slot_ref, prod_slot_ref, live_ref)
-    index_copies = [
-        copy(source, ref, sem.at[chunks + 5 + n])
-        for n, (source, ref) in enumerate(zip(index_hbm, index_refs))
-    ]
     x_copies[0].start()
     w_copies[0].start()
     w_copies[1].start()
-    for index_copy in index_copies:
-        index_copy.start()
     pair_sum = jnp.where(iota((H, 128), 0) >> 6 == (iota((H, 128), 1) & 7), 1.0, 0.0).astype(BF)
     spread = jnp.where(
         (iota((128, H), 0) < NCOL * HEADS) & ((iota((128, H), 0) & 7) == iota((128, H), 1) >> 6),
@@ -166,11 +158,7 @@
         tokens = [x_ref[at, k * H:(k + 1) * H] for k in range(NCOL)]
         before = first_before if c == 0 else lambda which: None
         h_ref[at, :] = encode_rows(tokens, w_qkv, w_out, pair_sum, spread, before)
-    for index_copy in index_copies:
-        index_copy.wait()
-    (s_of, t_of, k, ids), (ps_of, u_of, pk, prod_ids) = send_orders(
-        sizes, me_ref, pos_ref[...], cust_slot_ref[...], prod_slot_ref[...], live_ref
-    )
+    (s_of, t_of, k, ids), (ps_of, u_of, pk, prod_ids) = send_orders(sizes, index_ref)
     count = h_ref.shape[0]
     cs, ps = count // (nr * nz), count // (nz * nc)
     cust_sent, prod_sent = (s_of * nr + t_of) * cs + k, (u_of * nz + ps_of) * ps + pk
@@ -200,7 +188,7 @@
             ref[size:, :made[s].shape[1]] = made[s].astype(BF)
 
 
-def encode(sizes, me, review_cols, w_qkv, w_out, w_msg, *index):
+def encode(sizes, review_cols, w_qkv, w_out, w_msg, index):
     count = review_cols.shape[0]
     nr, nz, nc = sizes
     rows = min(count, 256)
@@ -208,7 +196,7 @@
     prod_block = jax.ShapeDtypeStruct((count // nc + nz * ID_ROWS, H), BF)
     out = pl.pallas_call(
         functools.partial(encode_kernel, sizes, rows),
-        in_specs=[HBM] * 4 + [SMEM] + [HBM] * 4,
+        in_specs=[HBM] * 4 + [VMEM],
         out_specs=[VMEM] * (2 + nz + nc),
         out_shape=[
             jax.ShapeDtypeStruct((count, H), BF),
@@ -217,12 +205,10 @@
         + [cust_block] * nz
         + [prod_block] * nc,
         scratch_shapes=[pltpu.VMEM(a.shape, BF) for a in (review_cols, w_qkv, w_out, w_msg)]
-        + [pltpu.VMEM(a.shape, jnp.int32) for a in index[:3]]
-        + [pltpu.SMEM(index[3].shape, jnp.int32)]
-        + [pltpu.SemaphoreType.DMA((count // rows + 9,))],
+        + [pltpu.SemaphoreType.DMA((count // rows + 5,))],
         compiler_params=ENCODE_PARAMS,
         name="encode",
-    )(review_cols, w_qkv, w_out, w_msg, me, *index)
+    )(review_cols, w_qkv, w_out, w_msg, index)
     return out[0], out[1], out[2:2 + nz], out[2 + nz:]
 
 
@@ -252,7 +238,8 @@
     for t, ref in enumerate(refs[-groups:]):
         for s in range(parts):
             ref[s * size:(s + 1) * size, :] = refs[s][t * size:(t + 1) * size, :]
-        ref[parts * size:, :] = sum(refs[s][held:, :] for s in range(parts))
+        if held < refs[0].shape[0]:
+            ref[parts * size:, :] = sum(refs[s][held:, :] for s in range(parts))
 
 
 def regroup(size, groups, got, after):
@@ -343,14 +330,14 @@
     )(own, peer, state, weight, *after)
 
 
-def prod_sum_kernel(slabs, parts, me_ref, ids_ref, *refs):
+def prod_sum_kernel(slabs, parts, ids_ref, *refs):
     blocks, pieces = refs[:parts], refs[-slabs:]
     size = pieces[0].shape[0] - ID_ROWS
     rows = jnp.concatenate([ref[:ref.shape[0] - ID_ROWS, :] for ref in blocks], axis=0)
     ones = jnp.ones((ID_ROWS, rows.shape[0]), BF)
     row = iota((ID_ROWS, size), 0)
     for t, ref in enumerate(pieces):
-        owner = me_ref[0] ^ t
+        owner = lax.axis_index("rev") ^ t
         pick = one_hot(size, owner * size, ids_ref[...])
         counts = dot_nt(ones, pick).astype(jnp.int32)
         halves = jnp.where(row == 0, counts >> 5, jnp.where(row == 1, counts & 31, 0))
@@ -359,22 +346,22 @@
         ref[size:, :size] = halves.astype(F32).astype(ref.dtype)
 
 
-def sum_prod(me, ids, blocks, size, slabs, after):
+def sum_prod(ids, blocks, size, slabs, after):
     piece = lambda kind: jax.ShapeDtypeStruct((size // slabs + ID_ROWS, H), kind)
     return pl.pallas_call(
         functools.partial(prod_sum_kernel, slabs, len(blocks)),
-        in_specs=[SMEM] + [VMEM] * (1 + len(blocks)) + [ANY] * len(after),
+        in_specs=[VMEM] * (1 + len(blocks)) + [ANY] * len(after),
         out_specs=[VMEM] * slabs,
         out_shape=[piece(F32)] + [piece(BF)] * (slabs - 1),
         compiler_params=PARAMS,
         name="sum_prod",
-    )(me, ids, *blocks, *after)
-
-
-def prod_update_kernel(slabs, me_ref, state_ref, w_ref, *rest):
+    )(ids, *blocks, *after)
+
+
+def prod_update_kernel(slabs, state_ref, w_ref, *rest):
     new_ref = rest[-1]
     size = new_ref.shape[0]
-    first = pl.multiple_of(me_ref[0] * size, size)
+    first = pl.multiple_of(lax.axis_index("rev") * size, size)
     totals = sum(ref[:size, :].astype(F32) for ref in rest[:slabs])
     halves = sum(ref[size:, :size].astype(F32) for ref in rest[:slabs])
     count_row = halves[0:1, :] * 32.0 + halves[1:2, :]
@@ -383,24 +370,24 @@
     new_ref[...] = refresh(totals, counts, state_ref[pl.ds(first, size), :], w_ref[...])
 
 
-def update_prod(me, state, weight, pieces, after):
+def update_prod(state, weight, pieces, after):
     slabs = len(pieces)
     return pl.pallas_call(
         functools.partial(prod_update_kernel, slabs),
-        in_specs=[SMEM] + [VMEM] * (2 + slabs) + [ANY] * len(after),
+        in_specs=[VMEM] * (2 + slabs) + [ANY] * len(after),
         out_specs=VMEM,
         out_shape=jax.ShapeDtypeStruct((state.shape[0] // slabs, H), BF),
         compiler_params=PARAMS,
         name="update_prod",
-    )(me, state, weight, *pieces, *after)
-
-
-def prod_reply_kernel(slabs, parts, me_ref, ids_ref, *rest):
+    )(state, weight, *pieces, *after)
+
+
+def prod_reply_kernel(slabs, parts, ids_ref, *rest):
     pieces, new_ref, reply_refs = rest[:slabs], rest[-1 - parts], rest[-parts:]
     size = pieces[0].shape[0]
     reply = None
     for t, ref in enumerate(pieces):
-        first = pl.multiple_of((me_ref[0] ^ t) * size, size)
+        first = pl.multiple_of((lax.axis_index("rev") ^ t) * size, size)
         new_ref[pl.ds(first, size), :] = ref[...]
         term = dot_t(one_hot(size, first, ids_ref[...]), ref[...])
         reply = term if reply is None else reply + term
@@ -409,18 +396,18 @@
         ref[...] = reply[s * rows:(s + 1) * rows].astype(BF)
 
 
-def reply_prod(me, ids, pieces, parts, after):
+def reply_prod(ids, pieces, parts, after):
     slabs = len(pieces)
     size, rows = pieces[0].shape[0] * slabs, ids.shape[1]
     out = pl.pallas_call(
         functools.partial(prod_reply_kernel, slabs, parts),
-        in_specs=[SMEM] + [VMEM] * (1 + slabs) + [ANY] * len(after),
+        in_specs=[VMEM] * (1 + slabs) + [ANY] * len(after),
         out_specs=[VMEM] * (1 + parts),
         out_shape=[jax.ShapeDtypeStruct((size, H), BF)]
         + [jax.ShapeDtypeStruct((rows // parts, H), BF)] * parts,
         compiler_params=PARAMS,
         name="reply_prod",
-    )(me, ids, *pieces, *after)
+    )(ids, *pieces, *after)
     return out[0], out[1:]
 
 
@@ -507,23 +494,20 @@
 ):
     rows = review_cols.shape[0]
     nr, nz, nc = lax.axis_size("rev"), lax.axis_size("cust"), lax.axis_size("prod")
-    mr, mz, mc = lax.axis_index("rev"), lax.axis_index("cust"), lax.axis_index("prod")
     cs = rows // (nr * nz)
     ps = rows // (nz * nc)
     wide = rows // nz
-    me = jnp.stack([mr, mz, mc])
-    flat = lambda ids: ids.reshape(1, rows)
+    index = jnp.concatenate(
+        [
+            prod_pos,
+            cust_slot.reshape(1, rows),
+            prod_slot.reshape(1, rows),
+            jnp.pad(live_count, ((0, 0), (0, rows - nr * nz))),
+        ],
+        axis=0,
+    )
     review_h, order, cust_blocks, prod_blocks = encode(
-        (nr, nz, nc),
-        me,
-        review_cols,
-        w_qkv,
-        w_out,
-        w_msg,
-        flat(prod_pos),
-        flat(cust_slot),
-        flat(prod_slot),
-        live_count,
+        (nr, nz, nc), review_cols, w_qkv, w_out, w_msg, index
     )
 
     prod_peer = swap(prod_blocks[1], "prod", 1)
@@ -537,18 +521,18 @@
     peer = swap(own, "prod", 1)
 
     prod_in = jnp.concatenate([ids_in(block[wide:, :wide]) for block in prod_got], axis=1)
-    pieces = sum_prod(me, prod_in, prod_got, prod_state.shape[0], nr, [])
+    pieces = sum_prod(prod_in, prod_got, prod_state.shape[0], nr, [])
     new_cust, reply = update_cust(nr, own, peer, cust_state, w_cust_up, [])
     pieces = [swap(pieces[t], "rev", t) for t in range(nr)]
     blocks = reply.reshape(nr, nz, cs, H)
     cust_got = [swap(blocks[:, s].reshape(wide, H), "cust", s) for s in range(nz)]
 
-    cust_back = [swap(rows_of(cust_got, t * cs, cs), "rev", t) for t in range(nr)]
-
-    new_piece = update_prod(me, prod_state, w_prod_up, pieces, cust_got[1:3])
+    new_piece = update_prod(prod_state, w_prod_up, pieces, cust_got[1:2])
     new_pieces = [swap(new_piece, "rev", t) for t in range(nr)]
-    new_prod, replies = reply_prod(me, prod_in, new_pieces, nz, cust_got[3:])
-    replies = [swap(replies[s], "cust", s) for s in range(nz)]
+    new_prod, made = reply_prod(prod_in, new_pieces, nz, cust_got[2:])
+    replies = [swap(made[s], "cust", s) for s in range(nz)]
+    cust_back = regroup(cs, nr, cust_got, made[:1])
+    cust_back = [swap(cust_back[t], "rev", t) for t in range(nr)]
     part = finish_cust(order, review_h, w_back, cust_back)
     own_replies, peer_replies = halve(replies, [part])
     prod_back = [own_replies, swap(peer_replies, "prod", 1)]

time: 94.8 us -> 87.8 us (0.926)
  Pallas kernels: 22.2 us -> 18.7 us
  local copies, waits for them, and re-layouts: 1.99 us -> 0.06 us
  waiting for transfers between devices: 32.6 us -> 31.4 us
    unnamed x20 -> x10, local copies, waits for them, and re-layouts: 1.92 us -> 0.03 us
    pallas_call x1, Pallas kernels: 13.2 us -> 11.3 us  [encode(): pl.pallas_call(functools.partial(encode_kernel, sizes, rows), in_specs=[H...]
    ppermute x27, waiting for transfers between devices: 32.6 us -> 31.4 us  [swap(): lax.ppermute(value, axis, [(i, i ^ by) for i in range(lax.axis_size(axis))])]
  transfers between devices with their start and end apart: 27 -> 27, of which waited for: 12 -> 13; matrix products, arithmetic and copies ran while one was open for 0% -> 0% of each run, Pallas kernels for 8% -> 5%
where the time goes in v4:
time: 87.8 us; the launch traced here: 87.6 us
  starting transfers between devices  35.8 us (41%)
  waiting for transfers between devices  31.4 us (36%)
  Pallas kernels  18.7 us (21%)
    ppermute x27, starting transfers between devices, swap(): lax.ppermute(value, axis, [(i, i ^ by) for i in range(lax.axis_size(axis))])  35.8 us
    ppermute x27, waiting for transfers between devices, swap(): lax.ppermute(value, axis, [(i, i ^ by) for i in range(lax.axis_size(axis))])  31.4 us
    pallas_call x1, Pallas kernels, encode(): pl.pallas_call(functools.partial(encode_kernel, sizes, rows), in_specs=[H...  11.3 us
    pallas_call x1, Pallas kernels, update_cust(): pl.pallas_call(functools.partial(cust_kernel, groups), in_specs=[VMEM] *...  2.29 us
  transfers between devices with their start and end apart: 27, of which 13 were waited for; matrix products, arithmetic and copies ran while one was open for 0% of the time, Pallas kernels for 5%

profile of v4, /device:TPU:0, one launch (start us, length us, event | category | flops | bytes accessed | tf_op | source)
XLA Modules:
  0.0 87.6 jit_solution(10402481573451058807)
XLA Ops:
  0.6 0.7 pad_add_fusion.refs_4_
  1.4 11.3 %encode.1 = (bf16[512,512]{1,0:T(8,128)(2,1)S(1)}, s32[2,512]{1,0:T(2,128)S(1)}, bf16[144,512]{1,0:T(8,128)(2,1)S(1)}, bf16[144,512]{1,0:T(8,128)(2,1)S(1)}, bf1...) custom-call(bf16[512,2048]{1,0:T(8,128)(2,1)} %refs_0_.1, ...), custom_call_target="tpu_custom_call" | custom-call | tf_op jit(solution)/shard_map/encode/pallas_call | solution.py:197
  12.7 0.5 collective-permute-start.3
  13.2 2.7 %collective-permute-start = (bf16[144,512]{1,0:T(8,128)(2,1)S(1)}, bf16[144,512]{1,0:T(8,128)(2,1)S(1)}, u32[]{:S(2)}, u32[]{:S(2)}) collective-permute-start(bf16[144,512]{1,0:T(8,128)(2,1)S(1)} %get-tuple-element.39), channel_id=1, source_target_pairs={{0,2},{2,0},{4,6},{6,4},{1,3},{3,1},{5,7},{7,5},{8,10},{10,8},{12,... | collective-permute-start | bytes 442376 | tf_op jit(solution)/shard_map/ppermute | solution.py:473
  15.9 2.6 %collective-permute-start.1 = (bf16[144,512]{1,0:T(8,128)(2,1)S(1)}, bf16[144,512]{1,0:T(8,128)(2,1)S(1)}, u32[]{:S(2)}, u32[]{:S(2)}) collective-permute-start(bf16[144,512]{1,0:T(8,128)(2,1)S(1)} %get-tuple-element.40), channel_id=1, source_target_pairs={{0,4},{2,6},{4,0},{6,2},{1,5},{3,7},{5,1},{7,3},{8,12},{10,14},{12... | collective-permute-start | bytes 442376 | tf_op jit(solution)/shard_map/ppermute | solution.py:473
  18.5 4.5 %collective-permute-done.refs_0_.refs_1_ = bf16[144,512]{1,0:T(8,128)(2,1)S(1)} collective-permute-done((bf16[144,512]{1,0:T(8,128)(2,1)S(1)}, bf16[144,512]{1,0:T(8,128)(2,1)S(1)}, u32[]{:S(2)}, u32[]{:S(2)}) %collective-permute-start) | collective-permute-done | bytes 147488 | tf_op jit(solution)/shard_map/ppermute | solution.py:473
  23.0 6.9 %collective-permute-done.1.refs_1_.refs_2_ = bf16[144,512]{1,0:T(8,128)(2,1)S(1)} collective-permute-done((bf16[144,512]{1,0:T(8,128)(2,1)S(1)}, bf16[144,512]{1,0:T(8,128)(2,1)S(1)}, u32[]{:S(2)}, u32[]{:S(2)}) %collective-permute-start.1) | collective-permute-done | bytes 147488 | tf_op jit(solution)/shard_map/ppermute | solution.py:473
  29.8 0.0 collective-permute-done.2.refs_2_.refs_3_
  29.8 0.0 collective-permute-done.3.peer_ref
  29.8 0.0 copy-start.2
  29.9 0.1 pair_product_blocks.1
  29.9 3.0 %collective-permute-start.7 = (bf16[144,512]{1,0:T(8,128)(2,1)S(1)}, bf16[144,512]{1,0:T(8,128)(2,1)S(1)}, u32[]{:S(2)}, u32[]{:S(2)}) collective-permute-start(bf16[144,512]{1,0:T(8,128)(2,1)S(1)} %get-tuple-element.44.refs_4_), channel_id=1, source_target_pairs={{0,2},{2,0},{4,6},{6,4},{1,3},{3,1},{5,7},{7,5},{8,10},{10,8},{12,... | collective-permute-start | bytes 442376 | tf_op jit(solution)/shard_map/ppermute | solution.py:473
  32.9 1.1 %collective-permute-start.8 = (bf16[144,512]{1,0:T(8,128)(2,1)S(1)}, bf16[144,512]{1,0:T(8,128)(2,1)S(1)}, u32[]{:S(2)}, u32[]{:S(2)}) collective-permute-start(bf16[144,512]{1,0:T(8,128)(2,1)S(1)} %get-tuple-element.45.refs_5_), channel_id=1, source_target_pairs={{0,4},{2,6},{4,0},{6,2},{1,5},{3,7},{5,1},{7,3},{8,12},{10,14},{12... | collective-permute-start | bytes 442376 | tf_op jit(solution)/shard_map/ppermute | solution.py:473
  34.0 1.4 %collective-permute-start.13 = (bf16[144,512]{1,0:T(8,128)(2,1)S(1)}, bf16[144,512]{1,0:T(8,128)(2,1)S(1)}, u32[]{:S(2)}, u32[]{:S(2)}) collective-permute-start(bf16[144,512]{1,0:T(8,128)(2,1)S(1)} %get-tuple-element.46.refs_6_), channel_id=1, source_target_pairs={{0,6},{2,4},{4,2},{6,0},{1,7},{3,5},{5,3},{7,1},{8,14},{10,12},{12... | collective-permute-start | bytes 442376 | tf_op jit(solution)/shard_map/ppermute | solution.py:473
  35.4 1.6 %collective-permute-start.4 = (bf16[144,512]{1,0:T(8,128)(2,1)S(1)}, bf16[144,512]{1,0:T(8,128)(2,1)S(1)}, u32[]{:S(2)}, u32[]{:S(2)}) collective-permute-start(bf16[144,512]{1,0:T(8,128)(2,1)S(1)} %get-tuple-element.48), channel_id=1, source_target_pairs={{0,8},{8,0},{16,24},{24,16},{1,9},{9,1},{17,25},{25,17},{2,10},{10... | collective-permute-start | bytes 442376 | tf_op jit(solution)/shard_map/ppermute | solution.py:473
  37.0 1.5 %collective-permute-start.5 = (bf16[144,512]{1,0:T(8,128)(2,1)S(1)}, bf16[144,512]{1,0:T(8,128)(2,1)S(1)}, u32[]{:S(2)}, u32[]{:S(2)}) collective-permute-start(bf16[144,512]{1,0:T(8,128)(2,1)S(1)} %get-tuple-element.49), channel_id=1, source_target_pairs={{0,16},{8,24},{16,0},{24,8},{1,17},{9,25},{17,1},{25,9},{2,18},{10... | collective-permute-start | bytes 442376 | tf_op jit(solution)/shard_map/ppermute | solution.py:473
  38.5 0.0 collective-permute-done.7.refs_4_.refs_1_
  38.5 1.9 %collective-permute-start.6 = (bf16[144,512]{1,0:T(8,128)(2,1)S(1)}, bf16[144,512]{1,0:T(8,128)(2,1)S(1)}, u32[]{:S(2)}, u32[]{:S(2)}) collective-permute-start(bf16[144,512]{1,0:T(8,128)(2,1)S(1)} %get-tuple-element.50), channel_id=1, source_target_pairs={{0,24},{8,16},{16,8},{24,0},{1,25},{9,17},{17,9},{25,1},{2,26},{10... | collective-permute-start | bytes 442376 | tf_op jit(solution)/shard_map/ppermute | solution.py:473
  40.4 1.5 %collective-permute-done.4.refs_1_ = bf16[144,512]{1,0:T(8,128)(2,1)S(1)} collective-permute-done((bf16[144,512]{1,0:T(8,128)(2,1)S(1)}, bf16[144,512]{1,0:T(8,128)(2,1)S(1)}, u32[]{:S(2)}, u32[]{:S(2)}) %collective-permute-start.4) | collective-permute-done | bytes 147488 | tf_op jit(solution)/shard_map/ppermute | solution.py:473
  42.0 3.2 %collective-permute-done.5.refs_2_ = bf16[144,512]{1,0:T(8,128)(2,1)S(1)} collective-permute-done((bf16[144,512]{1,0:T(8,128)(2,1)S(1)}, bf16[144,512]{1,0:T(8,128)(2,1)S(1)}, u32[]{:S(2)}, u32[]{:S(2)}) %collective-permute-start.5) | collective-permute-done | bytes 147488 | tf_op jit(solution)/shard_map/ppermute | solution.py:473
  45.2 0.0 collective-permute-done.6.refs_3_
  45.2 1.4 %collective-permute-done.8.refs_5_.refs_2_ = bf16[144,512]{1,0:T(8,128)(2,1)S(1)} collective-permute-done((bf16[144,512]{1,0:T(8,128)(2,1)S(1)}, bf16[144,512]{1,0:T(8,128)(2,1)S(1)}, u32[]{:S(2)}, u32[]{:S(2)}) %collective-permute-start.8) | collective-permute-done | bytes 147488 | tf_op jit(solution)/shard_map/ppermute | solution.py:473
  46.6 0.0 copy-start.3
  46.6 0.0 copy-start.4
  46.6 0.1 collective-permute-start.9
  46.7 0.0 collective-permute-done.13.refs_3_
  46.8 0.6 sum_prod.1
  47.4 1.6 %collective-permute-start.14 = (bf16[144,512]{1,0:T(8,128)(2,1)S(1)}, bf16[144,512]{1,0:T(8,128)(2,1)S(1)}, u32[]{:S(2)}, u32[]{:S(2)}) collective-permute-start(bf16[144,512]{1,0:T(8,128)(2,1)S(1)} %get-tuple-element.54), channel_id=1, source_target_pairs={{0,8},{8,0},{16,24},{24,16},{1,9},{9,1},{17,25},{25,17},{2,10},{10... | collective-permute-start | bytes 442376 | tf_op jit(solution)/shard_map/ppermute | solution.py:473
  48.9 1.5 %collective-permute-start.15 = (bf16[144,512]{1,0:T(8,128)(2,1)S(1)}, bf16[144,512]{1,0:T(8,128)(2,1)S(1)}, u32[]{:S(2)}, u32[]{:S(2)}) collective-permute-start(bf16[144,512]{1,0:T(8,128)(2,1)S(1)} %get-tuple-element.55), channel_id=1, source_target_pairs={{0,16},{8,24},{16,0},{24,8},{1,17},{9,25},{17,1},{25,9},{2,18},{10... | collective-permute-start | bytes 442376 | tf_op jit(solution)/shard_map/ppermute | solution.py:473
  50.5 0.5 collective-permute-start.16
  50.9 0.0 collective-permute-done.9.peer_ref
  51.0 2.3 %update_cust.1 = (bf16[512,512]{1,0:T(8,128)(2,1)}, bf16[512,512]{1,0:T(8,128)(2,1)S(1)}) custom-call(bf16[576,512]{1,0:T(8,128)(2,1)S(1)} %join.1.own_ref, bf16[576,512]{1,0:T(8,128)(2,1)S(1)} %collective-permute-done.9.peer_ref, bf16[512,512]{1,0:T(8,128)(2,1)S(1)} %copy-done.1, bf16[512,512]{1,0:T(8,128)(2,1)S(1)} %copy-done.2), custom_call_target="tpu_custom_call" | custom-call | tf_op jit(solution)/shard_map/update_cust/pallas_call | solution.py:320
  53.3 2.0 %collective-permute-start.10 = (bf16[128,512]{1,0:T(8,128)(2,1)S(1)}, bf16[128,512]{1,0:T(8,128)(2,1)S(1)}, u32[]{:S(2)}, u32[]{:S(2)}) collective-permute-start(bf16[128,512]{1,0:T(8,128)(2,1)S(1)} %bitcast.19), channel_id=1, source_target_pairs={{0,2},{2,0},{4,6},{6,4},{1,3},{3,1},{5,7},{7,5},{8,10},{10,8},{12,... | collective-permute-start | bytes 393224 | tf_op jit(solution)/shard_map/ppermute | solution.py:473
  55.3 1.0 %collective-permute-start.11 = (bf16[128,512]{1,0:T(8,128)(2,1)S(1)}, bf16[128,512]{1,0:T(8,128)(2,1)S(1)}, u32[]{:S(2)}, u32[]{:S(2)}) collective-permute-start(bf16[128,512]{1,0:T(8,128)(2,1)S(1)} %bitcast.18), channel_id=1, source_target_pairs={{0,4},{2,6},{4,0},{6,2},{1,5},{3,7},{5,1},{7,3},{8,12},{10,14},{12... | collective-permute-start | bytes 393224 | tf_op jit(solution)/shard_map/ppermute | solution.py:473
  56.3 1.4 %collective-permute-start.12 = (bf16[128,512]{1,0:T(8,128)(2,1)S(1)}, bf16[128,512]{1,0:T(8,128)(2,1)S(1)}, u32[]{:S(2)}, u32[]{:S(2)}) collective-permute-start(bf16[128,512]{1,0:T(8,128)(2,1)S(1)} %bitcast.17), channel_id=1, source_target_pairs={{0,6},{2,4},{4,2},{6,0},{1,7},{3,5},{5,3},{7,1},{8,14},{10,12},{12... | collective-permute-start | bytes 393224 | tf_op jit(solution)/shard_map/ppermute | solution.py:473
  57.7 0.3 collective-permute-done.15.rest_2_
  58.1 0.0 collective-permute-done.16.rest_3_
  58.1 2.5 %collective-permute-done.10.rest_4_.refs_1_ = bf16[128,512]{1,0:T(8,128)(2,1)S(1)} collective-permute-done((bf16[128,512]{1,0:T(8,128)(2,1)S(1)}, bf16[128,512]{1,0:T(8,128)(2,1)S(1)}, u32[]{:S(2)}, u32[]{:S(2)}) %collective-permute-start.10) | collective-permute-done | bytes 131104 | tf_op jit(solution)/shard_map/ppermute | solution.py:473
  60.6 0.4 update_prod.1.rest_0_
  61.1 2.5 %collective-permute-start.19 = (bf16[128,512]{1,0:T(8,128)(2,1)S(1)}, bf16[128,512]{1,0:T(8,128)(2,1)S(1)}, u32[]{:S(2)}, u32[]{:S(2)}) collective-permute-start(bf16[128,512]{1,0:T(8,128)(2,1)S(1)} %update_prod.1.rest_0_), channel_id=1, source_target_pairs={{0,24},{8,16},{16,8},{24,0},{1,25},{9,17},{17,9},{25,1},{2,26},{10... | collective-permute-start | bytes 393224 | tf_op jit(solution)/shard_map/ppermute | solution.py:473
  63.6 0.5 collective-permute-start.18
  64.1 0.5 collective-permute-start.17
  64.6 1.8 %collective-permute-done.11.rest_4_.refs_2_ = bf16[128,512]{1,0:T(8,128)(2,1)S(1)} collective-permute-done((bf16[128,512]{1,0:T(8,128)(2,1)S(1)}, bf16[128,512]{1,0:T(8,128)(2,1)S(1)}, u32[]{:S(2)}, u32[]{:S(2)}) %collective-permute-start.11) | collective-permute-done | bytes 131104 | tf_op jit(solution)/shard_map/ppermute | solution.py:473
  66.4 0.0 collective-permute-done.12.rest_5_.refs_3_
  66.4 1.7 %collective-permute-done.19.rest_3_ = bf16[128,512]{1,0:T(8,128)(2,1)S(1)} collective-permute-done((bf16[128,512]{1,0:T(8,128)(2,1)S(1)}, bf16[128,512]{1,0:T(8,128)(2,1)S(1)}, u32[]{:S(2)}, u32[]{:S(2)}) %collective-permute-start.19) | collective-permute-done | bytes 131104 | tf_op jit(solution)/shard_map/ppermute | solution.py:473
  68.1 1.0 %collective-permute-done.18.rest_2_ = bf16[128,512]{1,0:T(8,128)(2,1)S(1)} collective-permute-done((bf16[128,512]{1,0:T(8,128)(2,1)S(1)}, bf16[128,512]{1,0:T(8,128)(2,1)S(1)}, u32[]{:S(2)}, u32[]{:S(2)}) %collective-permute-start.18) | collective-permute-done | bytes 131104 | tf_op jit(solution)/shard_map/ppermute | solution.py:473
  69.1 0.0 collective-permute-done.17.rest_1_
  69.1 1.5 %reply_prod.1 = (bf16[512,512]{1,0:T(8,128)(2,1)}, bf16[128,512]{1,0:T(8,128)(2,1)S(1)}, bf16[128,512]{1,0:T(8,128)(2,1)S(1)}, bf16[128,512]{1,0:T(8,128)(2,1)S(1)}, bf16[128,512]{1,0:T(8,128)(2,1)S(1)}) custom-call(s32[1,512]{1,0:T(1,128)S(1)} %pad_add_fusion.1.ids_ref, bf16[128,512]{1,0:T(8,128)(2,1)S(1)} %update_prod.1.rest_0_, ...), custom_call_target="tpu_custom_call" | custom-call | tf_op jit(solution)/shard_map/reply_prod/pallas_call | solution.py:402
  70.7 0.9 %collective-permute-start.20 = (bf16[128,512]{1,0:T(8,128)(2,1)S(1)}, bf16[128,512]{1,0:T(8,128)(2,1)S(1)}, u32[]{:S(2)}, u32[]{:S(2)}) collective-permute-start(bf16[128,512]{1,0:T(8,128)(2,1)S(1)} %get-tuple-element.59), channel_id=1, source_target_pairs={{0,8},{8,0},{16,24},{24,16},{1,9},{9,1},{17,25},{25,17},{2,10},{10... | collective-permute-start | bytes 393224 | tf_op jit(solution)/shard_map/ppermute | solution.py:473
  71.6 1.1 %collective-permute-start.21 = (bf16[128,512]{1,0:T(8,128)(2,1)S(1)}, bf16[128,512]{1,0:T(8,128)(2,1)S(1)}, u32[]{:S(2)}, u32[]{:S(2)}) collective-permute-start(bf16[128,512]{1,0:T(8,128)(2,1)S(1)} %get-tuple-element.60), channel_id=1, source_target_pairs={{0,16},{8,24},{16,0},{24,8},{1,17},{9,25},{17,1},{25,9},{2,18},{10... | collective-permute-start | bytes 393224 | tf_op jit(solution)/shard_map/ppermute | solution.py:473
  72.7 1.5 %collective-permute-start.22 = (bf16[128,512]{1,0:T(8,128)(2,1)S(1)}, bf16[128,512]{1,0:T(8,128)(2,1)S(1)}, u32[]{:S(2)}, u32[]{:S(2)}) collective-permute-start(bf16[128,512]{1,0:T(8,128)(2,1)S(1)} %get-tuple-element.61), channel_id=1, source_target_pairs={{0,24},{8,16},{16,8},{24,0},{1,25},{9,17},{17,9},{25,1},{2,26},{10... | collective-permute-start | bytes 393224 | tf_op jit(solution)/shard_map/ppermute | solution.py:473
  74.2 1.0 %collective-permute-start.23 = (bf16[128,512]{1,0:T(8,128)(2,1)S(1)}, bf16[128,512]{1,0:T(8,128)(2,1)S(1)}, u32[]{:S(2)}, u32[]{:S(2)}) collective-permute-start(bf16[128,512]{1,0:T(8,128)(2,1)S(1)} %get-tuple-element.62), channel_id=1, source_target_pairs={{0,2},{2,0},{4,6},{6,4},{1,3},{3,1},{5,7},{7,5},{8,10},{10,8},{12,... | collective-permute-start | bytes 393224 | tf_op jit(solution)/shard_map/ppermute | solution.py:473
  75.2 1.0 %collective-permute-start.24 = (bf16[128,512]{1,0:T(8,128)(2,1)S(1)}, bf16[128,512]{1,0:T(8,128)(2,1)S(1)}, u32[]{:S(2)}, u32[]{:S(2)}) collective-permute-start(bf16[128,512]{1,0:T(8,128)(2,1)S(1)} %get-tuple-element.63), channel_id=1, source_target_pairs={{0,4},{2,6},{4,0},{6,2},{1,5},{3,7},{5,1},{7,3},{8,12},{10,14},{12... | collective-permute-start | bytes 393224 | tf_op jit(solution)/shard_map/ppermute | solution.py:473
  76.2 0.0 collective-permute-done.20.rest_1_
  76.2 2.4 %collective-permute-start.25 = (bf16[128,512]{1,0:T(8,128)(2,1)S(1)}, bf16[128,512]{1,0:T(8,128)(2,1)S(1)}, u32[]{:S(2)}, u32[]{:S(2)}) collective-permute-start(bf16[128,512]{1,0:T(8,128)(2,1)S(1)} %get-tuple-element.64), channel_id=1, source_target_pairs={{0,6},{2,4},{4,2},{6,0},{1,7},{3,5},{5,3},{7,1},{8,14},{10,12},{12... | collective-permute-start | bytes 393224 | tf_op jit(solution)/shard_map/ppermute | solution.py:473
  78.6 0.0 collective-permute-done.21.rest_2_
  78.6 0.0 collective-permute-done.22.rest_3_
  78.6 0.7 finish_cust.1.refs_4_.part_ref
  79.4 1.2 %collective-permute-done.23.refs_1_ = bf16[128,512]{1,0:T(8,128)(2,1)S(1)} collective-permute-done((bf16[128,512]{1,0:T(8,128)(2,1)S(1)}, bf16[128,512]{1,0:T(8,128)(2,1)S(1)}, u32[]{:S(2)}, u32[]{:S(2)}) %collective-permute-start.23) | collective-permute-done | bytes 131104 | tf_op jit(solution)/shard_map/ppermute | solution.py:473
  80.6 3.7 %collective-permute-done.24.refs_2_ = bf16[128,512]{1,0:T(8,128)(2,1)S(1)} collective-permute-done((bf16[128,512]{1,0:T(8,128)(2,1)S(1)}, bf16[128,512]{1,0:T(8,128)(2,1)S(1)}, u32[]{:S(2)}, u32[]{:S(2)}) %collective-permute-start.24) | collective-permute-done | bytes 131104 | tf_op jit(solution)/shard_map/ppermute | solution.py:473
  84.3 0.0 collective-permute-done.25.refs_3_
  84.4 0.1 collective-permute-start.26
  84.4 1.5 %collective-permute-done.26.rest_1_ = bf16[256,512]{1,0:T(8,128)(2,1)S(1)} collective-permute-done((bf16[256,512]{1,0:T(8,128)(2,1)S(1)}, bf16[256,512]{1,0:T(8,128)(2,1)S(1)}, u32[]{:S(2)}, u32[]{:S(2)}) %collective-permute-start.26) | collective-permute-done | bytes 262176 | tf_op jit(solution)/shard_map/ppermute | solution.py:473
  86.0 1.6 %finish.1 = bf16[512,512]{1,0:T(8,128)(2,1)} custom-call(s32[2,512]{1,0:T(2,128)S(1)} %get-tuple-element.36.order_ref, f32[512,512]{1,0:T(8,128)S(1)} %finish_cust.1.refs_4_.part_ref, bf16[1024,512]{1,0:T(8,128)(2,1)S(1)} %copy-done, bf16[256,512]{1,0:T(8,128)(2,1)S(1)} %get-tuple-element.65.rest_0_, bf16[256,512]{1,0:T(8,128)(2,1)S(1)} %collective-permute-done.26.rest_1_), custom_call_target="tpu_custom_call" | custom-call | tf_op jit(solution)/shard_map/finish/pallas_call | solution.py:441
  (23 shorter events, 0.3 us)
Async XLA Ops:
  12.7 17.1 %collective-permute-start.3 = (bf16[320,512]{1,0:T(8,128)(2,1)S(1)}, bf16[320,512]{1,0:T(8,128)(2,1)S(1)}, u32[]{:S(2)}, u32[]{:S(2)}) collective-permute-start(bf16[320,512]{1,0:T(8,128)(2,1)S(1)} %get-tuple-element.43), channel_id=1, source_target_pairs={{0,1},{1,0},{2,3},{3,2},{4,5},{5,4},{6,7},{7,6},{8,9},{9,8},{10,11... | collective-permute-start | bytes 983048 | tf_op jit(solution)/shard_map/ppermute | solution.py:473
  13.2 9.8 %collective-permute-start = (bf16[144,512]{1,0:T(8,128)(2,1)S(1)}, bf16[144,512]{1,0:T(8,128)(2,1)S(1)}, u32[]{:S(2)}, u32[]{:S(2)}) collective-permute-start(bf16[144,512]{1,0:T(8,128)(2,1)S(1)} %get-tuple-element.39), channel_id=1, source_target_pairs={{0,2},{2,0},{4,6},{6,4},{1,3},{3,1},{5,7},{7,5},{8,10},{10,8},{12,... | collective-permute-start | bytes 442376 | tf_op jit(solution)/shard_map/ppermute | solution.py:473
  15.9 14.0 %collective-permute-start.1 = (bf16[144,512]{1,0:T(8,128)(2,1)S(1)}, bf16[144,512]{1,0:T(8,128)(2,1)S(1)}, u32[]{:S(2)}, u32[]{:S(2)}) collective-permute-start(bf16[144,512]{1,0:T(8,128)(2,1)S(1)} %get-tuple-element.40), channel_id=1, source_target_pairs={{0,4},{2,6},{4,0},{6,2},{1,5},{3,7},{5,1},{7,3},{8,12},{10,14},{12... | collective-permute-start | bytes 442376 | tf_op jit(solution)/shard_map/ppermute | solution.py:473
  18.5 11.4 %collective-permute-start.2 = (bf16[144,512]{1,0:T(8,128)(2,1)S(1)}, bf16[144,512]{1,0:T(8,128)(2,1)S(1)}, u32[]{:S(2)}, u32[]{:S(2)}) collective-permute-start(bf16[144,512]{1,0:T(8,128)(2,1)S(1)} %get-tuple-element.41), channel_id=1, source_target_pairs={{0,6},{2,4},{4,2},{6,0},{1,7},{3,5},{5,3},{7,1},{8,14},{10,12},{12... | collective-permute-start | bytes 442376 | tf_op jit(solution)/shard_map/ppermute | solution.py:473
  29.8 21.1 %copy-start.1 = (bf16[512,512]{1,0:T(8,128)(2,1)S(1)}, bf16[512,512]{1,0:T(8,128)(2,1)}, u32[]{:S(2)}) copy-start(bf16[512,512]{1,0:T(8,128)(2,1)} %state_ref.2) | copy-start | bytes 1572868
  29.8 21.1 %copy-start.2 = (bf16[512,512]{1,0:T(8,128)(2,1)S(1)}, bf16[512,512]{1,0:T(8,128)(2,1)}, u32[]{:S(2)}) copy-start(bf16[512,512]{1,0:T(8,128)(2,1)} %w_ref.4) | copy-start | bytes 1572868
  29.9 8.6 %collective-permute-start.7 = (bf16[144,512]{1,0:T(8,128)(2,1)S(1)}, bf16[144,512]{1,0:T(8,128)(2,1)S(1)}, u32[]{:S(2)}, u32[]{:S(2)}) collective-permute-start(bf16[144,512]{1,0:T(8,128)(2,1)S(1)} %get-tuple-element.44.refs_4_), channel_id=1, source_target_pairs={{0,2},{2,0},{4,6},{6,4},{1,3},{3,1},{5,7},{7,5},{8,10},{10,8},{12,... | collective-permute-start | bytes 442376 | tf_op jit(solution)/shard_map/ppermute | solution.py:473
  32.9 13.7 %collective-permute-start.8 = (bf16[144,512]{1,0:T(8,128)(2,1)S(1)}, bf16[144,512]{1,0:T(8,128)(2,1)S(1)}, u32[]{:S(2)}, u32[]{:S(2)}) collective-permute-start(bf16[144,512]{1,0:T(8,128)(2,1)S(1)} %get-tuple-element.45.refs_5_), channel_id=1, source_target_pairs={{0,4},{2,6},{4,0},{6,2},{1,5},{3,7},{5,1},{7,3},{8,12},{10,14},{12... | collective-permute-start | bytes 442376 | tf_op jit(solution)/shard_map/ppermute | solution.py:473
  34.0 12.7 %collective-permute-start.13 = (bf16[144,512]{1,0:T(8,128)(2,1)S(1)}, bf16[144,512]{1,0:T(8,128)(2,1)S(1)}, u32[]{:S(2)}, u32[]{:S(2)}) collective-permute-start(bf16[144,512]{1,0:T(8,128)(2,1)S(1)} %get-tuple-element.46.refs_6_), channel_id=1, source_target_pairs={{0,6},{2,4},{4,2},{6,0},{1,7},{3,5},{5,3},{7,1},{8,14},{10,12},{12... | collective-permute-start | bytes 442376 | tf_op jit(solution)/shard_map/ppermute | solution.py:473
  35.4 6.5 %collective-permute-start.4 = (bf16[144,512]{1,0:T(8,128)(2,1)S(1)}, bf16[144,512]{1,0:T(8,128)(2,1)S(1)}, u32[]{:S(2)}, u32[]{:S(2)}) collective-permute-start(bf16[144,512]{1,0:T(8,128)(2,1)S(1)} %get-tuple-element.48), channel_id=1, source_target_pairs={{0,8},{8,0},{16,24},{24,16},{1,9},{9,1},{17,25},{25,17},{2,10},{10... | collective-permute-start | bytes 442376 | tf_op jit(solution)/shard_map/ppermute | solution.py:473
  37.0 8.2 %collective-permute-start.5 = (bf16[144,512]{1,0:T(8,128)(2,1)S(1)}, bf16[144,512]{1,0:T(8,128)(2,1)S(1)}, u32[]{:S(2)}, u32[]{:S(2)}) collective-permute-start(bf16[144,512]{1,0:T(8,128)(2,1)S(1)} %get-tuple-element.49), channel_id=1, source_target_pairs={{0,16},{8,24},{16,0},{24,8},{1,17},{9,25},{17,1},{25,9},{2,18},{10... | collective-permute-start | bytes 442376 | tf_op jit(solution)/shard_map/ppermute | solution.py:473
  38.5 6.6 %collective-permute-start.6 = (bf16[144,512]{1,0:T(8,128)(2,1)S(1)}, bf16[144,512]{1,0:T(8,128)(2,1)S(1)}, u32[]{:S(2)}, u32[]{:S(2)}) collective-permute-start(bf16[144,512]{1,0:T(8,128)(2,1)S(1)} %get-tuple-element.50), channel_id=1, source_target_pairs={{0,24},{8,16},{16,8},{24,0},{1,25},{9,17},{17,9},{25,1},{2,26},{10... | collective-permute-start | bytes 442376 | tf_op jit(solution)/shard_map/ppermute | solution.py:473
  46.6 14.0 %copy-start.3 = (bf16[512,512]{1,0:T(8,128)(2,1)S(1)}, bf16[512,512]{1,0:T(8,128)(2,1)}, u32[]{:S(2)}) copy-start(bf16[512,512]{1,0:T(8,128)(2,1)} %state_ref.3) | copy-start | bytes 1572868
  46.6 14.0 %copy-start.4 = (bf16[512,512]{1,0:T(8,128)(2,1)S(1)}, bf16[512,512]{1,0:T(8,128)(2,1)}, u32[]{:S(2)}) copy-start(bf16[512,512]{1,0:T(8,128)(2,1)} %w_ref.5) | copy-start | bytes 1572868
  46.6 4.3 %collective-permute-start.9 = (bf16[576,512]{1,0:T(8,128)(2,1)S(1)}, bf16[576,512]{1,0:T(8,128)(2,1)S(1)}, u32[]{:S(2)}, u32[]{:S(2)}) collective-permute-start(bf16[576,512]{1,0:T(8,128)(2,1)S(1)} %join.1.own_ref), channel_id=1, source_target_pairs={{0,1},{1,0},{2,3},{3,2},{4,5},{5,4},{6,7},{7,6},{8,9},{9,8},{10,11... | collective-permute-start | bytes 1769480 | tf_op jit(solution)/shard_map/ppermute | solution.py:473
  47.4 9.0 %collective-permute-start.14 = (bf16[144,512]{1,0:T(8,128)(2,1)S(1)}, bf16[144,512]{1,0:T(8,128)(2,1)S(1)}, u32[]{:S(2)}, u32[]{:S(2)}) collective-permute-start(bf16[144,512]{1,0:T(8,128)(2,1)S(1)} %get-tuple-element.54), channel_id=1, source_target_pairs={{0,8},{8,0},{16,24},{24,16},{1,9},{9,1},{17,25},{25,17},{2,10},{10... | collective-permute-start | bytes 442376 | tf_op jit(solution)/shard_map/ppermute | solution.py:473
  48.9 9.1 %collective-permute-start.15 = (bf16[144,512]{1,0:T(8,128)(2,1)S(1)}, bf16[144,512]{1,0:T(8,128)(2,1)S(1)}, u32[]{:S(2)}, u32[]{:S(2)}) collective-permute-start(bf16[144,512]{1,0:T(8,128)(2,1)S(1)} %get-tuple-element.55), channel_id=1, source_target_pairs={{0,16},{8,24},{16,0},{24,8},{1,17},{9,25},{17,1},{25,9},{2,18},{10... | collective-permute-start | bytes 442376 | tf_op jit(solution)/shard_map/ppermute | solution.py:473
  50.5 7.6 %collective-permute-start.16 = (bf16[144,512]{1,0:T(8,128)(2,1)S(1)}, bf16[144,512]{1,0:T(8,128)(2,1)S(1)}, u32[]{:S(2)}, u32[]{:S(2)}) collective-permute-start(bf16[144,512]{1,0:T(8,128)(2,1)S(1)} %get-tuple-element.56), channel_id=1, source_target_pairs={{0,24},{8,16},{16,8},{24,0},{1,25},{9,17},{17,9},{25,1},{2,26},{10... | collective-permute-start | bytes 442376 | tf_op jit(solution)/shard_map/ppermute | solution.py:473
  53.2 25.4 %copy-start = (bf16[1024,512]{1,0:T(8,128)(2,1)S(1)}, bf16[1024,512]{1,0:T(8,128)(2,1)}, u32[]{:S(2)}) copy-start(bf16[1024,512]{1,0:T(8,128)(2,1)} %w_ref.7) | copy-start | bytes 3145732
  53.3 7.3 %collective-permute-start.10 = (bf16[128,512]{1,0:T(8,128)(2,1)S(1)}, bf16[128,512]{1,0:T(8,128)(2,1)S(1)}, u32[]{:S(2)}, u32[]{:S(2)}) collective-permute-start(bf16[128,512]{1,0:T(8,128)(2,1)S(1)} %bitcast.19), channel_id=1, source_target_pairs={{0,2},{2,0},{4,6},{6,4},{1,3},{3,1},{5,7},{7,5},{8,10},{10,8},{12,... | collective-permute-start | bytes 393224 | tf_op jit(solution)/shard_map/ppermute | solution.py:473
  55.3 11.1 %collective-permute-start.11 = (bf16[128,512]{1,0:T(8,128)(2,1)S(1)}, bf16[128,512]{1,0:T(8,128)(2,1)S(1)}, u32[]{:S(2)}, u32[]{:S(2)}) collective-permute-start(bf16[128,512]{1,0:T(8,128)(2,1)S(1)} %bitcast.18), channel_id=1, source_target_pairs={{0,4},{2,6},{4,0},{6,2},{1,5},{3,7},{5,1},{7,3},{8,12},{10,14},{12... | collective-permute-start | bytes 393224 | tf_op jit(solution)/shard_map/ppermute | solution.py:473
  56.3 10.1 %collective-permute-start.12 = (bf16[128,512]{1,0:T(8,128)(2,1)S(1)}, bf16[128,512]{1,0:T(8,128)(2,1)S(1)}, u32[]{:S(2)}, u32[]{:S(2)}) collective-permute-start(bf16[128,512]{1,0:T(8,128)(2,1)S(1)} %bitcast.17), channel_id=1, source_target_pairs={{0,6},{2,4},{4,2},{6,0},{1,7},{3,5},{5,3},{7,1},{8,14},{10,12},{12... | collective-permute-start | bytes 393224 | tf_op jit(solution)/shard_map/ppermute | solution.py:473
  61.1 7.1 %collective-permute-start.19 = (bf16[128,512]{1,0:T(8,128)(2,1)S(1)}, bf16[128,512]{1,0:T(8,128)(2,1)S(1)}, u32[]{:S(2)}, u32[]{:S(2)}) collective-permute-start(bf16[128,512]{1,0:T(8,128)(2,1)S(1)} %update_prod.1.rest_0_), channel_id=1, source_target_pairs={{0,24},{8,16},{16,8},{24,0},{1,25},{9,17},{17,9},{25,1},{2,26},{10... | collective-permute-start | bytes 393224 | tf_op jit(solution)/shard_map/ppermute | solution.py:473
  63.6 5.6 %collective-permute-start.18 = (bf16[128,512]{1,0:T(8,128)(2,1)S(1)}, bf16[128,512]{1,0:T(8,128)(2,1)S(1)}, u32[]{:S(2)}, u32[]{:S(2)}) collective-permute-start(bf16[128,512]{1,0:T(8,128)(2,1)S(1)} %update_prod.1.rest_0_), channel_id=1, source_target_pairs={{0,16},{8,24},{16,0},{24,8},{1,17},{9,25},{17,1},{25,9},{2,18},{10... | collective-permute-start | bytes 393224 | tf_op jit(solution)/shard_map/ppermute | solution.py:473
  64.1 5.1 %collective-permute-start.17 = (bf16[128,512]{1,0:T(8,128)(2,1)S(1)}, bf16[128,512]{1,0:T(8,128)(2,1)S(1)}, u32[]{:S(2)}, u32[]{:S(2)}) collective-permute-start(bf16[128,512]{1,0:T(8,128)(2,1)S(1)} %update_prod.1.rest_0_), channel_id=1, source_target_pairs={{0,8},{8,0},{16,24},{24,16},{1,9},{9,1},{17,25},{25,17},{2,10},{10... | collective-permute-start | bytes 393224 | tf_op jit(solution)/shard_map/ppermute | solution.py:473
  70.7 5.6 %collective-permute-start.20 = (bf16[128,512]{1,0:T(8,128)(2,1)S(1)}, bf16[128,512]{1,0:T(8,128)(2,1)S(1)}, u32[]{:S(2)}, u32[]{:S(2)}) collective-permute-start(bf16[128,512]{1,0:T(8,128)(2,1)S(1)} %get-tuple-element.59), channel_id=1, source_target_pairs={{0,8},{8,0},{16,24},{24,16},{1,9},{9,1},{17,25},{25,17},{2,10},{10... | collective-permute-start | bytes 393224 | tf_op jit(solution)/shard_map/ppermute | solution.py:473
  71.6 7.0 %collective-permute-start.21 = (bf16[128,512]{1,0:T(8,128)(2,1)S(1)}, bf16[128,512]{1,0:T(8,128)(2,1)S(1)}, u32[]{:S(2)}, u32[]{:S(2)}) collective-permute-start(bf16[128,512]{1,0:T(8,128)(2,1)S(1)} %get-tuple-element.60), channel_id=1, source_target_pairs={{0,16},{8,24},{16,0},{24,8},{1,17},{9,25},{17,1},{25,9},{2,18},{10... | collective-permute-start | bytes 393224 | tf_op jit(solution)/shard_map/ppermute | solution.py:473
  72.7 5.9 %collective-permute-start.22 = (bf16[128,512]{1,0:T(8,128)(2,1)S(1)}, bf16[128,512]{1,0:T(8,128)(2,1)S(1)}, u32[]{:S(2)}, u32[]{:S(2)}) collective-permute-start(bf16[128,512]{1,0:T(8,128)(2,1)S(1)} %get-tuple-element.61), channel_id=1, source_target_pairs={{0,24},{8,16},{16,8},{24,0},{1,25},{9,17},{17,9},{25,1},{2,26},{10... | collective-permute-start | bytes 393224 | tf_op jit(solution)/shard_map/ppermute | solution.py:473
  74.2 6.4 %collective-permute-start.23 = (bf16[128,512]{1,0:T(8,128)(2,1)S(1)}, bf16[128,512]{1,0:T(8,128)(2,1)S(1)}, u32[]{:S(2)}, u32[]{:S(2)}) collective-permute-start(bf16[128,512]{1,0:T(8,128)(2,1)S(1)} %get-tuple-element.62), channel_id=1, source_target_pairs={{0,2},{2,0},{4,6},{6,4},{1,3},{3,1},{5,7},{7,5},{8,10},{10,8},{12,... | collective-permute-start | bytes 393224 | tf_op jit(solution)/shard_map/ppermute | solution.py:473
  75.2 9.1 %collective-permute-start.24 = (bf16[128,512]{1,0:T(8,128)(2,1)S(1)}, bf16[128,512]{1,0:T(8,128)(2,1)S(1)}, u32[]{:S(2)}, u32[]{:S(2)}) collective-permute-start(bf16[128,512]{1,0:T(8,128)(2,1)S(1)} %get-tuple-element.63), channel_id=1, source_target_pairs={{0,4},{2,6},{4,0},{6,2},{1,5},{3,7},{5,1},{7,3},{8,12},{10,14},{12... | collective-permute-start | bytes 393224 | tf_op jit(solution)/shard_map/ppermute | solution.py:473
  76.2 8.1 %collective-permute-start.25 = (bf16[128,512]{1,0:T(8,128)(2,1)S(1)}, bf16[128,512]{1,0:T(8,128)(2,1)S(1)}, u32[]{:S(2)}, u32[]{:S(2)}) collective-permute-start(bf16[128,512]{1,0:T(8,128)(2,1)S(1)} %get-tuple-element.64), channel_id=1, source_target_pairs={{0,6},{2,4},{4,2},{6,0},{1,7},{3,5},{5,3},{7,1},{8,14},{10,12},{12... | collective-permute-start | bytes 393224 | tf_op jit(solution)/shard_map/ppermute | solution.py:473
  84.4 1.6 %collective-permute-start.26 = (bf16[256,512]{1,0:T(8,128)(2,1)S(1)}, bf16[256,512]{1,0:T(8,128)(2,1)S(1)}, u32[]{:S(2)}, u32[]{:S(2)}) collective-permute-start(bf16[256,512]{1,0:T(8,128)(2,1)S(1)} %get-tuple-element.66), channel_id=1, source_target_pairs={{0,1},{1,0},{2,3},{3,2},{4,5},{5,4},{6,7},{7,6},{8,9},{9,8},{10,11... | collective-permute-start | bytes 786440 | tf_op jit(solution)/shard_map/ppermute | solution.py:473

commit v5 on v4

--- a/solution.py
+++ b/solution.py
@@ -382,23 +382,20 @@
     )(state, weight, *pieces, *after)
 
 
-def prod_reply_kernel(slabs, parts, ids_ref, *rest):
+def prod_reply_kernel(slabs, parts, pick_ref, *rest):
     pieces, new_ref, reply_refs = rest[:slabs], rest[-1 - parts], rest[-parts:]
     size = pieces[0].shape[0]
-    reply = None
     for t, ref in enumerate(pieces):
         first = pl.multiple_of((lax.axis_index("rev") ^ t) * size, size)
         new_ref[pl.ds(first, size), :] = ref[...]
-        term = dot_t(one_hot(size, first, ids_ref[...]), ref[...])
-        reply = term if reply is None else reply + term
     rows = reply_refs[0].shape[0]
     for s, ref in enumerate(reply_refs):
-        ref[...] = reply[s * rows:(s + 1) * rows].astype(BF)
-
-
-def reply_prod(ids, pieces, parts, after):
+        ref[...] = dot(pick_ref[s * rows:(s + 1) * rows, :], new_ref[...]).astype(BF)
+
+
+def reply_prod(pick, pieces, parts, after):
     slabs = len(pieces)
-    size, rows = pieces[0].shape[0] * slabs, ids.shape[1]
+    size, rows = pieces[0].shape[0] * slabs, pick.shape[0]
     out = pl.pallas_call(
         functools.partial(prod_reply_kernel, slabs, parts),
         in_specs=[VMEM] * (1 + slabs) + [ANY] * len(after),
@@ -407,45 +404,47 @@
         + [jax.ShapeDtypeStruct((rows // parts, H), BF)] * parts,
         compiler_params=PARAMS,
         name="reply_prod",
-    )(ids, *pieces, *after)
+    )(pick, *pieces, *after)
     return out[0], out[1:]
 
 
-def pick_rows(order, refs):
-    rows = jnp.concatenate([ref[...] for ref in refs], axis=0)
-    return dot_t(one_hot(rows.shape[0], 0, order), rows).astype(BF)
-
-
-def finish_cust_kernel(order_ref, h_ref, w_ref, *rest):
-    back = pick_rows(order_ref[0:1, :], rest[:-1])
-    rest[-1][...] = h_ref[...].astype(F32) + dot(back, w_ref[:H, :])
-
-
-def finish_cust(order, review_h, w_back, cust_back):
-    return pl.pallas_call(
-        finish_cust_kernel,
-        in_specs=[VMEM] * (3 + len(cust_back)),
+def turned_kernel(ids_ref, *refs):
+    for n, ref in enumerate(refs):
+        rows = iota((ref.shape[1], ref.shape[0]), 0)
+        ref[...] = jnp.where(rows == ids_ref[n:n + 1, :], 1.0, 0.0).T.astype(BF)
+
+
+def turned_picks(ids, size):
+    pick = jax.ShapeDtypeStruct((ids.shape[1], size), BF)
+    return pl.pallas_call(
+        turned_kernel,
+        in_specs=[VMEM],
+        out_specs=[VMEM] * ids.shape[0],
+        out_shape=[pick] * ids.shape[0],
+        compiler_params=PARAMS,
+        name="turned_picks",
+    )(ids)
+
+
+def finish_part_kernel(start, pick_ref, sum_ref, w_ref, *rest):
+    rows = jnp.concatenate([ref[...] for ref in rest[:-1]], axis=0)
+    at, wide = start
+    back = dot(pick_ref[:, at:at + rows.shape[0]], rows).astype(BF)
+    total = sum_ref[...].astype(F32) + dot(back, w_ref[wide:wide + H, :])
+    if rest[-1].dtype == BF:
+        total = rms_norm(total)
+    rest[-1][...] = total.astype(rest[-1].dtype)
+
+
+def finish_part(start, picks, total, w_back, rows, kind, name):
+    return pl.pallas_call(
+        functools.partial(finish_part_kernel, start),
+        in_specs=[VMEM] * (3 + len(rows)),
         out_specs=VMEM,
-        out_shape=jax.ShapeDtypeStruct(review_h.shape, F32),
-        compiler_params=PARAMS,
-        name="finish_cust",
-    )(order, review_h, w_back, *cust_back)
-
-
-def finish_kernel(order_ref, part_ref, w_ref, *rest):
-    back = pick_rows(order_ref[1:2, :], rest[:-1])
-    rest[-1][...] = rms_norm(part_ref[...] + dot(back, w_ref[H:, :])).astype(BF)
-
-
-def finish(order, part, w_back, prod_back):
-    return pl.pallas_call(
-        finish_kernel,
-        in_specs=[VMEM] * (3 + len(prod_back)),
-        out_specs=VMEM,
-        out_shape=jax.ShapeDtypeStruct(part.shape, BF),
-        compiler_params=PARAMS,
-        name="finish",
-    )(order, part, w_back, *prod_back)
+        out_shape=jax.ShapeDtypeStruct(total.shape, kind),
+        compiler_params=PARAMS,
+        name=name,
+    )(picks, total, w_back, *rows)
 
 
 def halve_kernel(parts, *refs):
@@ -510,9 +509,11 @@
         (nr, nz, nc), review_cols, w_qkv, w_out, w_msg, index
     )
 
+    cust_pick, prod_pick = turned_picks(order, rows)
+
     prod_peer = swap(prod_blocks[1], "prod", 1)
     got = [swap(cust_blocks[s], "cust", s) for s in range(nz)]
-    prod_blocks = pair(nz, prod_blocks[0], prod_peer, got[1:])
+    prod_blocks = pair(nz, prod_blocks[0], prod_peer, got[1:3])
     prod_got = [swap(prod_blocks[s], "cust", s) for s in range(nz)]
 
     groups = regroup(cs, nr, got, prod_blocks[1:])
@@ -529,15 +530,15 @@
 
     new_piece = update_prod(prod_state, w_prod_up, pieces, cust_got[1:2])
     new_pieces = [swap(new_piece, "rev", t) for t in range(nr)]
-    new_prod, made = reply_prod(prod_in, new_pieces, nz, cust_got[2:])
+    new_prod, made = reply_prod(turned_picks(prod_in, prod_state.shape[0])[0], new_pieces, nz, cust_got[2:])
     replies = [swap(made[s], "cust", s) for s in range(nz)]
     cust_back = regroup(cs, nr, cust_got, made[:1])
     cust_back = [swap(cust_back[t], "rev", t) for t in range(nr)]
-    part = finish_cust(order, review_h, w_back, cust_back)
+    part = finish_part((0, 0), cust_pick, review_h, w_back, cust_back, F32, "finish_cust")
     own_replies, peer_replies = halve(replies, [part])
-    prod_back = [own_replies, swap(peer_replies, "prod", 1)]
-
-    review_out = finish(order, part, w_back, prod_back)
+    peer_replies = swap(peer_replies, "prod", 1)
+    part = finish_part((0, H), prod_pick, part, w_back, [own_replies], F32, "finish_own")
+    review_out = finish_part((rows // nc, H), prod_pick, part, w_back, [peer_replies], BF, "finish")
     return (review_out, new_cust, new_prod)
 
 

time: 87.8 us -> 84.8 us (0.966)
  waiting for transfers between devices: 31.4 us -> 29.4 us
  starting transfers between devices: 35.8 us -> 34.1 us
    ppermute x27, waiting for transfers between devices: 31.4 us -> 29.4 us  [swap(): lax.ppermute(value, axis, [(i, i ^ by) for i in range(lax.axis_size(axis))])]
    ppermute x27, starting transfers between devices: 35.8 us -> 34.1 us  [swap(): lax.ppermute(value, axis, [(i, i ^ by) for i in range(lax.axis_size(axis))])]
    pallas_call x2 -> x5, Pallas kernels: 2.39 us -> 3.34 us  [the longest x3 2.75 us: finish_part(): pl.pallas_call(functools.partial(finish_part_kernel, start), in_specs=[VM...]
  transfers between devices with their start and end apart: 27 -> 27, of which waited for: 13 -> 11; matrix products, arithmetic and copies ran while one was open for 0% -> 0% of each run, Pallas kernels for 5% -> 6%
where the time goes in v5:
time: 84.8 us; the launch traced here: 84.6 us
  starting transfers between devices  34.1 us (40%)
  waiting for transfers between devices  29.4 us (35%)
  Pallas kernels  19.3 us (23%)
  between operations  0.87 us (1%)
    ppermute x27, starting transfers between devices, swap(): lax.ppermute(value, axis, [(i, i ^ by) for i in range(lax.axis_size(axis))])  34.1 us
    ppermute x27, waiting for transfers between devices, swap(): lax.ppermute(value, axis, [(i, i ^ by) for i in range(lax.axis_size(axis))])  29.4 us
    pallas_call x1, Pallas kernels, encode(): pl.pallas_call(functools.partial(encode_kernel, sizes, rows), in_specs=[H...  11.3 us
    pallas_call x3, Pallas kernels, finish_part(): pl.pallas_call(functools.partial(finish_part_kernel, start), in_specs=[VM...  2.75 us
    pallas_call x1, Pallas kernels, update_cust(): pl.pallas_call(functools.partial(cust_kernel, groups), in_specs=[VMEM] *...  2.3 us
  transfers between devices with their start and end apart: 27, of which 11 were waited for; matrix products, arithmetic and copies ran while one was open for 0% of the time, Pallas kernels for 6%

profile of v5, /device:TPU:0, one launch (start us, length us, event | category | flops | bytes accessed | tf_op | source)
XLA Modules:
  0.0 84.6 jit_solution(16722853694692583190)
XLA Ops:
  0.6 0.7 pad_add_fusion.refs_4_
  1.4 11.3 %encode.1 = (bf16[512,512]{1,0:T(8,128)(2,1)S(1)}, s32[2,512]{1,0:T(2,128)S(1)}, bf16[144,512]{1,0:T(8,128)(2,1)S(1)}, bf16[144,512]{1,0:T(8,128)(2,1)S(1)}, bf1...) custom-call(bf16[512,2048]{1,0:T(8,128)(2,1)} %refs_0_.1, ...), custom_call_target="tpu_custom_call" | custom-call | tf_op jit(solution)/shard_map/encode/pallas_call | solution.py:197
  12.7 0.0 copy-start.1
  12.7 0.0 copy-start.2
  12.7 0.5 collective-permute-start.3
  13.2 2.7 %collective-permute-start = (bf16[144,512]{1,0:T(8,128)(2,1)S(1)}, bf16[144,512]{1,0:T(8,128)(2,1)S(1)}, u32[]{:S(2)}, u32[]{:S(2)}) collective-permute-start(bf16[144,512]{1,0:T(8,128)(2,1)S(1)} %get-tuple-element.43), channel_id=1, source_target_pairs={{0,2},{2,0},{4,6},{6,4},{1,3},{3,1},{5,7},{7,5},{8,10},{10,8},{12,... | collective-permute-start | bytes 442376 | tf_op jit(solution)/shard_map/ppermute | solution.py:472
  15.9 2.6 %collective-permute-start.1 = (bf16[144,512]{1,0:T(8,128)(2,1)S(1)}, bf16[144,512]{1,0:T(8,128)(2,1)S(1)}, u32[]{:S(2)}, u32[]{:S(2)}) collective-permute-start(bf16[144,512]{1,0:T(8,128)(2,1)S(1)} %get-tuple-element.44), channel_id=1, source_target_pairs={{0,4},{2,6},{4,0},{6,2},{1,5},{3,7},{5,1},{7,3},{8,12},{10,14},{12... | collective-permute-start | bytes 442376 | tf_op jit(solution)/shard_map/ppermute | solution.py:472
  18.5 0.0 collective-permute-start.2
  18.5 4.5 %collective-permute-done.refs_0_.refs_1_ = bf16[144,512]{1,0:T(8,128)(2,1)S(1)} collective-permute-done((bf16[144,512]{1,0:T(8,128)(2,1)S(1)}, bf16[144,512]{1,0:T(8,128)(2,1)S(1)}, u32[]{:S(2)}, u32[]{:S(2)}) %collective-permute-start) | collective-permute-done | bytes 147488 | tf_op jit(solution)/shard_map/ppermute | solution.py:472
  23.0 6.9 %collective-permute-done.1.refs_1_.refs_2_ = bf16[144,512]{1,0:T(8,128)(2,1)S(1)} collective-permute-done((bf16[144,512]{1,0:T(8,128)(2,1)S(1)}, bf16[144,512]{1,0:T(8,128)(2,1)S(1)}, u32[]{:S(2)}, u32[]{:S(2)}) %collective-permute-start.1) | collective-permute-done | bytes 147488 | tf_op jit(solution)/shard_map/ppermute | solution.py:472
  29.9 0.0 collective-permute-done.3.peer_ref
  29.9 0.1 collective-permute-start.7
  30.0 3.0 %collective-permute-start.8 = (bf16[144,512]{1,0:T(8,128)(2,1)S(1)}, bf16[144,512]{1,0:T(8,128)(2,1)S(1)}, u32[]{:S(2)}, u32[]{:S(2)}) collective-permute-start(bf16[144,512]{1,0:T(8,128)(2,1)S(1)} %get-tuple-element.49.refs_5_), channel_id=1, source_target_pairs={{0,4},{2,6},{4,0},{6,2},{1,5},{3,7},{5,1},{7,3},{8,12},{10,14},{12... | collective-permute-start | bytes 442376 | tf_op jit(solution)/shard_map/ppermute | solution.py:472
  33.0 1.4 %collective-permute-start.13 = (bf16[144,512]{1,0:T(8,128)(2,1)S(1)}, bf16[144,512]{1,0:T(8,128)(2,1)S(1)}, u32[]{:S(2)}, u32[]{:S(2)}) collective-permute-start(bf16[144,512]{1,0:T(8,128)(2,1)S(1)} %get-tuple-element.50.refs_6_), channel_id=1, source_target_pairs={{0,6},{2,4},{4,2},{6,0},{1,7},{3,5},{5,3},{7,1},{8,14},{10,12},{12... | collective-permute-start | bytes 442376 | tf_op jit(solution)/shard_map/ppermute | solution.py:472
  34.4 0.0 collective-permute-done.2.refs_3_
  34.4 1.6 %collective-permute-start.4 = (bf16[144,512]{1,0:T(8,128)(2,1)S(1)}, bf16[144,512]{1,0:T(8,128)(2,1)S(1)}, u32[]{:S(2)}, u32[]{:S(2)}) collective-permute-start(bf16[144,512]{1,0:T(8,128)(2,1)S(1)} %get-tuple-element.52), channel_id=1, source_target_pairs={{0,8},{8,0},{16,24},{24,16},{1,9},{9,1},{17,25},{25,17},{2,10},{10... | collective-permute-start | bytes 442376 | tf_op jit(solution)/shard_map/ppermute | solution.py:472
  36.0 1.5 %collective-permute-start.5 = (bf16[144,512]{1,0:T(8,128)(2,1)S(1)}, bf16[144,512]{1,0:T(8,128)(2,1)S(1)}, u32[]{:S(2)}, u32[]{:S(2)}) collective-permute-start(bf16[144,512]{1,0:T(8,128)(2,1)S(1)} %get-tuple-element.53), channel_id=1, source_target_pairs={{0,16},{8,24},{16,0},{24,8},{1,17},{9,25},{17,1},{25,9},{2,18},{10... | collective-permute-start | bytes 442376 | tf_op jit(solution)/shard_map/ppermute | solution.py:472
  37.5 0.0 collective-permute-done.7.refs_4_.refs_1_
  37.5 0.6 collective-permute-start.6
  38.1 1.5 %collective-permute-done.4.refs_1_ = bf16[144,512]{1,0:T(8,128)(2,1)S(1)} collective-permute-done((bf16[144,512]{1,0:T(8,128)(2,1)S(1)}, bf16[144,512]{1,0:T(8,128)(2,1)S(1)}, u32[]{:S(2)}, u32[]{:S(2)}) %collective-permute-start.4) | collective-permute-done | bytes 147488 | tf_op jit(solution)/shard_map/ppermute | solution.py:472
  39.6 1.5 %collective-permute-done.5.refs_2_ = bf16[144,512]{1,0:T(8,128)(2,1)S(1)} collective-permute-done((bf16[144,512]{1,0:T(8,128)(2,1)S(1)}, bf16[144,512]{1,0:T(8,128)(2,1)S(1)}, u32[]{:S(2)}, u32[]{:S(2)}) %collective-permute-start.5) | collective-permute-done | bytes 147488 | tf_op jit(solution)/shard_map/ppermute | solution.py:472
  41.1 2.5 %collective-permute-done.6.refs_3_ = bf16[144,512]{1,0:T(8,128)(2,1)S(1)} collective-permute-done((bf16[144,512]{1,0:T(8,128)(2,1)S(1)}, bf16[144,512]{1,0:T(8,128)(2,1)S(1)}, u32[]{:S(2)}, u32[]{:S(2)}) %collective-permute-start.6) | collective-permute-done | bytes 147488 | tf_op jit(solution)/shard_map/ppermute | solution.py:472
  43.6 0.0 collective-permute-done.8.refs_5_.refs_2_
  43.7 0.0 copy-start.3
  43.7 0.0 copy-start.4
  43.7 0.1 collective-permute-start.9
  43.8 0.0 collective-permute-done.13.refs_3_
  43.8 0.6 sum_prod.1
  44.4 1.2 %collective-permute-start.14 = (bf16[144,512]{1,0:T(8,128)(2,1)S(1)}, bf16[144,512]{1,0:T(8,128)(2,1)S(1)}, u32[]{:S(2)}, u32[]{:S(2)}) collective-permute-start(bf16[144,512]{1,0:T(8,128)(2,1)S(1)} %get-tuple-element.58), channel_id=1, source_target_pairs={{0,8},{8,0},{16,24},{24,16},{1,9},{9,1},{17,25},{25,17},{2,10},{10... | collective-permute-start | bytes 442376 | tf_op jit(solution)/shard_map/ppermute | solution.py:472
  45.6 1.5 %collective-permute-start.15 = (bf16[144,512]{1,0:T(8,128)(2,1)S(1)}, bf16[144,512]{1,0:T(8,128)(2,1)S(1)}, u32[]{:S(2)}, u32[]{:S(2)}) collective-permute-start(bf16[144,512]{1,0:T(8,128)(2,1)S(1)} %get-tuple-element.59), channel_id=1, source_target_pairs={{0,16},{8,24},{16,0},{24,8},{1,17},{9,25},{17,1},{25,9},{2,18},{10... | collective-permute-start | bytes 442376 | tf_op jit(solution)/shard_map/ppermute | solution.py:472
  47.1 0.9 %collective-permute-start.16 = (bf16[144,512]{1,0:T(8,128)(2,1)S(1)}, bf16[144,512]{1,0:T(8,128)(2,1)S(1)}, u32[]{:S(2)}, u32[]{:S(2)}) collective-permute-start(bf16[144,512]{1,0:T(8,128)(2,1)S(1)} %get-tuple-element.60), channel_id=1, source_target_pairs={{0,24},{8,16},{16,8},{24,0},{1,25},{9,17},{17,9},{25,1},{2,26},{10... | collective-permute-start | bytes 442376 | tf_op jit(solution)/shard_map/ppermute | solution.py:472
  48.0 0.0 collective-permute-done.9.peer_ref
  48.0 2.3 %update_cust.1 = (bf16[512,512]{1,0:T(8,128)(2,1)}, bf16[512,512]{1,0:T(8,128)(2,1)S(1)}) custom-call(bf16[576,512]{1,0:T(8,128)(2,1)S(1)} %join.1.own_ref, bf16[576,512]{1,0:T(8,128)(2,1)S(1)} %collective-permute-done.9.peer_ref, bf16[512,512]{1,0:T(8,128)(2,1)S(1)} %copy-done.1, bf16[512,512]{1,0:T(8,128)(2,1)S(1)} %copy-done.2), custom_call_target="tpu_custom_call" | custom-call | tf_op jit(solution)/shard_map/update_cust/pallas_call | solution.py:320
  50.3 1.7 %collective-permute-start.10 = (bf16[128,512]{1,0:T(8,128)(2,1)S(1)}, bf16[128,512]{1,0:T(8,128)(2,1)S(1)}, u32[]{:S(2)}, u32[]{:S(2)}) collective-permute-start(bf16[128,512]{1,0:T(8,128)(2,1)S(1)} %bitcast.19), channel_id=1, source_target_pairs={{0,2},{2,0},{4,6},{6,4},{1,3},{3,1},{5,7},{7,5},{8,10},{10,8},{12,... | collective-permute-start | bytes 393224 | tf_op jit(solution)/shard_map/ppermute | solution.py:472
  52.0 1.4 %collective-permute-start.11 = (bf16[128,512]{1,0:T(8,128)(2,1)S(1)}, bf16[128,512]{1,0:T(8,128)(2,1)S(1)}, u32[]{:S(2)}, u32[]{:S(2)}) collective-permute-start(bf16[128,512]{1,0:T(8,128)(2,1)S(1)} %bitcast.18), channel_id=1, source_target_pairs={{0,4},{2,6},{4,0},{6,2},{1,5},{3,7},{5,1},{7,3},{8,12},{10,14},{12... | collective-permute-start | bytes 393224 | tf_op jit(solution)/shard_map/ppermute | solution.py:472
  53.4 1.3 %collective-permute-start.12 = (bf16[128,512]{1,0:T(8,128)(2,1)S(1)}, bf16[128,512]{1,0:T(8,128)(2,1)S(1)}, u32[]{:S(2)}, u32[]{:S(2)}) collective-permute-start(bf16[128,512]{1,0:T(8,128)(2,1)S(1)} %bitcast.17), channel_id=1, source_target_pairs={{0,6},{2,4},{4,2},{6,0},{1,7},{3,5},{5,3},{7,1},{8,14},{10,12},{12... | collective-permute-start | bytes 393224 | tf_op jit(solution)/shard_map/ppermute | solution.py:472
  54.8 0.0 collective-permute-done.16.rest_3_
  54.8 2.6 %collective-permute-done.10.rest_4_.refs_1_ = bf16[128,512]{1,0:T(8,128)(2,1)S(1)} collective-permute-done((bf16[128,512]{1,0:T(8,128)(2,1)S(1)}, bf16[128,512]{1,0:T(8,128)(2,1)S(1)}, u32[]{:S(2)}, u32[]{:S(2)}) %collective-permute-start.10) | collective-permute-done | bytes 131104 | tf_op jit(solution)/shard_map/ppermute | solution.py:472
  57.4 0.4 update_prod.1.rest_0_
  57.8 1.6 %collective-permute-start.19 = (bf16[128,512]{1,0:T(8,128)(2,1)S(1)}, bf16[128,512]{1,0:T(8,128)(2,1)S(1)}, u32[]{:S(2)}, u32[]{:S(2)}) collective-permute-start(bf16[128,512]{1,0:T(8,128)(2,1)S(1)} %update_prod.1.rest_0_), channel_id=1, source_target_pairs={{0,24},{8,16},{16,8},{24,0},{1,25},{9,17},{17,9},{25,1},{2,26},{10... | collective-permute-start | bytes 393224 | tf_op jit(solution)/shard_map/ppermute | solution.py:472
  59.4 0.5 collective-permute-start.18
  59.9 1.4 %collective-permute-start.17 = (bf16[128,512]{1,0:T(8,128)(2,1)S(1)}, bf16[128,512]{1,0:T(8,128)(2,1)S(1)}, u32[]{:S(2)}, u32[]{:S(2)}) collective-permute-start(bf16[128,512]{1,0:T(8,128)(2,1)S(1)} %update_prod.1.rest_0_), channel_id=1, source_target_pairs={{0,8},{8,0},{16,24},{24,16},{1,9},{9,1},{17,25},{25,17},{2,10},{10... | collective-permute-start | bytes 393224 | tf_op jit(solution)/shard_map/ppermute | solution.py:472
  61.4 0.2 turned_picks.3.pick_ref
  61.6 2.0 %collective-permute-done.11.rest_4_.refs_2_ = bf16[128,512]{1,0:T(8,128)(2,1)S(1)} collective-permute-done((bf16[128,512]{1,0:T(8,128)(2,1)S(1)}, bf16[128,512]{1,0:T(8,128)(2,1)S(1)}, u32[]{:S(2)}, u32[]{:S(2)}) %collective-permute-start.11) | collective-permute-done | bytes 131104 | tf_op jit(solution)/shard_map/ppermute | solution.py:472
  63.5 0.0 collective-permute-done.12.rest_5_.refs_3_
  63.5 0.9 %collective-permute-done.19.rest_3_ = bf16[128,512]{1,0:T(8,128)(2,1)S(1)} collective-permute-done((bf16[128,512]{1,0:T(8,128)(2,1)S(1)}, bf16[128,512]{1,0:T(8,128)(2,1)S(1)}, u32[]{:S(2)}, u32[]{:S(2)}) %collective-permute-start.19) | collective-permute-done | bytes 131104 | tf_op jit(solution)/shard_map/ppermute | solution.py:472
  64.5 1.0 %collective-permute-done.18.rest_2_ = bf16[128,512]{1,0:T(8,128)(2,1)S(1)} collective-permute-done((bf16[128,512]{1,0:T(8,128)(2,1)S(1)}, bf16[128,512]{1,0:T(8,128)(2,1)S(1)}, u32[]{:S(2)}, u32[]{:S(2)}) %collective-permute-start.18) | collective-permute-done | bytes 131104 | tf_op jit(solution)/shard_map/ppermute | solution.py:472
  65.5 1.1 %reply_prod.1 = (bf16[512,512]{1,0:T(8,128)(2,1)}, bf16[128,512]{1,0:T(8,128)(2,1)S(1)}, bf16[128,512]{1,0:T(8,128)(2,1)S(1)}, bf16[128,512]{1,0:T(8,128)(2,1)S(1)}, bf16[128,512]{1,0:T(8,128)(2,1)S(1)}) custom-call(bf16[512,512]{1,0:T(8,128)(2,1)S(1)} %turned_picks.3.pick_ref, bf16[128,512]{1,0:T(8,128)(2,1)S(1)} %update_prod.1.rest_0_, ...), custom_call_target="tpu_custom_call" | custom-call | tf_op jit(solution)/shard_map/reply_prod/pallas_call | solution.py:399
  66.6 1.0 %collective-permute-start.20 = (bf16[128,512]{1,0:T(8,128)(2,1)S(1)}, bf16[128,512]{1,0:T(8,128)(2,1)S(1)}, u32[]{:S(2)}, u32[]{:S(2)}) collective-permute-start(bf16[128,512]{1,0:T(8,128)(2,1)S(1)} %get-tuple-element.63), channel_id=1, source_target_pairs={{0,8},{8,0},{16,24},{24,16},{1,9},{9,1},{17,25},{25,17},{2,10},{10... | collective-permute-start | bytes 393224 | tf_op jit(solution)/shard_map/ppermute | solution.py:472
  67.6 1.2 %collective-permute-start.21 = (bf16[128,512]{1,0:T(8,128)(2,1)S(1)}, bf16[128,512]{1,0:T(8,128)(2,1)S(1)}, u32[]{:S(2)}, u32[]{:S(2)}) collective-permute-start(bf16[128,512]{1,0:T(8,128)(2,1)S(1)} %get-tuple-element.64), channel_id=1, source_target_pairs={{0,16},{8,24},{16,0},{24,8},{1,17},{9,25},{17,1},{25,9},{2,18},{10... | collective-permute-start | bytes 393224 | tf_op jit(solution)/shard_map/ppermute | solution.py:472
  68.8 1.4 %collective-permute-start.22 = (bf16[128,512]{1,0:T(8,128)(2,1)S(1)}, bf16[128,512]{1,0:T(8,128)(2,1)S(1)}, u32[]{:S(2)}, u32[]{:S(2)}) collective-permute-start(bf16[128,512]{1,0:T(8,128)(2,1)S(1)} %get-tuple-element.65), channel_id=1, source_target_pairs={{0,24},{8,16},{16,8},{24,0},{1,25},{9,17},{17,9},{25,1},{2,26},{10... | collective-permute-start | bytes 393224 | tf_op jit(solution)/shard_map/ppermute | solution.py:472
  70.2 1.3 %collective-permute-start.23 = (bf16[128,512]{1,0:T(8,128)(2,1)S(1)}, bf16[128,512]{1,0:T(8,128)(2,1)S(1)}, u32[]{:S(2)}, u32[]{:S(2)}) collective-permute-start(bf16[128,512]{1,0:T(8,128)(2,1)S(1)} %get-tuple-element.66), channel_id=1, source_target_pairs={{0,2},{2,0},{4,6},{6,4},{1,3},{3,1},{5,7},{7,5},{8,10},{10,8},{12,... | collective-permute-start | bytes 393224 | tf_op jit(solution)/shard_map/ppermute | solution.py:472
  71.5 1.8 %collective-permute-start.24 = (bf16[128,512]{1,0:T(8,128)(2,1)S(1)}, bf16[128,512]{1,0:T(8,128)(2,1)S(1)}, u32[]{:S(2)}, u32[]{:S(2)}) collective-permute-start(bf16[128,512]{1,0:T(8,128)(2,1)S(1)} %get-tuple-element.67), channel_id=1, source_target_pairs={{0,4},{2,6},{4,0},{6,2},{1,5},{3,7},{5,1},{7,3},{8,12},{10,14},{12... | collective-permute-start | bytes 393224 | tf_op jit(solution)/shard_map/ppermute | solution.py:472
  73.3 1.9 %collective-permute-start.25 = (bf16[128,512]{1,0:T(8,128)(2,1)S(1)}, bf16[128,512]{1,0:T(8,128)(2,1)S(1)}, u32[]{:S(2)}, u32[]{:S(2)}) collective-permute-start(bf16[128,512]{1,0:T(8,128)(2,1)S(1)} %get-tuple-element.68), channel_id=1, source_target_pairs={{0,6},{2,4},{4,2},{6,0},{1,7},{3,5},{5,3},{7,1},{8,14},{10,12},{12... | collective-permute-start | bytes 393224 | tf_op jit(solution)/shard_map/ppermute | solution.py:472
  75.2 0.4 turned_picks.2
  75.6 0.0 collective-permute-done.21.rest_2_
  75.6 0.7 finish_cust.1.refs_4_.sum_ref
  76.3 0.0 collective-permute-done.23.refs_1_
  76.3 5.2 %collective-permute-done.24.refs_2_ = bf16[128,512]{1,0:T(8,128)(2,1)S(1)} collective-permute-done((bf16[128,512]{1,0:T(8,128)(2,1)S(1)}, bf16[128,512]{1,0:T(8,128)(2,1)S(1)}, u32[]{:S(2)}, u32[]{:S(2)}) %collective-permute-start.24) | collective-permute-done | bytes 131104 | tf_op jit(solution)/shard_map/ppermute | solution.py:472
  81.5 0.0 collective-permute-done.25.refs_3_
  81.5 0.1 collective-permute-start.26
  81.6 0.6 finish_own.1.sum_ref
  82.2 0.9 %collective-permute-done.26.rest_0_ = bf16[256,512]{1,0:T(8,128)(2,1)S(1)} collective-permute-done((bf16[256,512]{1,0:T(8,128)(2,1)S(1)}, bf16[256,512]{1,0:T(8,128)(2,1)S(1)}, u32[]{:S(2)}, u32[]{:S(2)}) %collective-permute-start.26) | collective-permute-done | bytes 262176 | tf_op jit(solution)/shard_map/ppermute | solution.py:472
  83.1 1.5 %finish.1 = bf16[512,512]{1,0:T(8,128)(2,1)} custom-call(bf16[512,512]{1,0:T(8,128)(2,1)S(1)} %get-tuple-element.39.pick_ref, f32[512,512]{1,0:T(8,128)S(1)} %finish_own.1.sum_ref, bf16[1024,512]{1,0:T(8,128)(2,1)S(1)} %copy-done, bf16[256,512]{1,0:T(8,128)(2,1)S(1)} %collective-permute-done.26.rest_0_), custom_call_target="tpu_custom_call" | custom-call | tf_op jit(solution)/shard_map/finish/pallas_call | solution.py:440
  (26 shorter events, 0.3 us)
Async XLA Ops:
  12.7 35.3 %copy-start.1 = (bf16[512,512]{1,0:T(8,128)(2,1)S(1)}, bf16[512,512]{1,0:T(8,128)(2,1)}, u32[]{:S(2)}) copy-start(bf16[512,512]{1,0:T(8,128)(2,1)} %state_ref.2) | copy-start | bytes 1572868
  12.7 35.3 %copy-start.2 = (bf16[512,512]{1,0:T(8,128)(2,1)S(1)}, bf16[512,512]{1,0:T(8,128)(2,1)}, u32[]{:S(2)}) copy-start(bf16[512,512]{1,0:T(8,128)(2,1)} %w_ref.5) | copy-start | bytes 1572868
  12.7 17.1 %collective-permute-start.3 = (bf16[320,512]{1,0:T(8,128)(2,1)S(1)}, bf16[320,512]{1,0:T(8,128)(2,1)S(1)}, u32[]{:S(2)}, u32[]{:S(2)}) collective-permute-start(bf16[320,512]{1,0:T(8,128)(2,1)S(1)} %get-tuple-element.47), channel_id=1, source_target_pairs={{0,1},{1,0},{2,3},{3,2},{4,5},{5,4},{6,7},{7,6},{8,9},{9,8},{10,11... | collective-permute-start | bytes 983048 | tf_op jit(solution)/shard_map/ppermute | solution.py:472
  13.2 9.8 %collective-permute-start = (bf16[144,512]{1,0:T(8,128)(2,1)S(1)}, bf16[144,512]{1,0:T(8,128)(2,1)S(1)}, u32[]{:S(2)}, u32[]{:S(2)}) collective-permute-start(bf16[144,512]{1,0:T(8,128)(2,1)S(1)} %get-tuple-element.43), channel_id=1, source_target_pairs={{0,2},{2,0},{4,6},{6,4},{1,3},{3,1},{5,7},{7,5},{8,10},{10,8},{12,... | collective-permute-start | bytes 442376 | tf_op jit(solution)/shard_map/ppermute | solution.py:472
  15.9 14.0 %collective-permute-start.1 = (bf16[144,512]{1,0:T(8,128)(2,1)S(1)}, bf16[144,512]{1,0:T(8,128)(2,1)S(1)}, u32[]{:S(2)}, u32[]{:S(2)}) collective-permute-start(bf16[144,512]{1,0:T(8,128)(2,1)S(1)} %get-tuple-element.44), channel_id=1, source_target_pairs={{0,4},{2,6},{4,0},{6,2},{1,5},{3,7},{5,1},{7,3},{8,12},{10,14},{12... | collective-permute-start | bytes 442376 | tf_op jit(solution)/shard_map/ppermute | solution.py:472
  18.5 15.9 %collective-permute-start.2 = (bf16[144,512]{1,0:T(8,128)(2,1)S(1)}, bf16[144,512]{1,0:T(8,128)(2,1)S(1)}, u32[]{:S(2)}, u32[]{:S(2)}) collective-permute-start(bf16[144,512]{1,0:T(8,128)(2,1)S(1)} %get-tuple-element.45), channel_id=1, source_target_pairs={{0,6},{2,4},{4,2},{6,0},{1,7},{3,5},{5,3},{7,1},{8,14},{10,12},{12... | collective-permute-start | bytes 442376 | tf_op jit(solution)/shard_map/ppermute | solution.py:472
  29.9 7.6 %collective-permute-start.7 = (bf16[144,512]{1,0:T(8,128)(2,1)S(1)}, bf16[144,512]{1,0:T(8,128)(2,1)S(1)}, u32[]{:S(2)}, u32[]{:S(2)}) collective-permute-start(bf16[144,512]{1,0:T(8,128)(2,1)S(1)} %get-tuple-element.48.refs_4_), channel_id=1, source_target_pairs={{0,2},{2,0},{4,6},{6,4},{1,3},{3,1},{5,7},{7,5},{8,10},{10,8},{12,... | collective-permute-start | bytes 442376 | tf_op jit(solution)/shard_map/ppermute | solution.py:472
  30.0 13.6 %collective-permute-start.8 = (bf16[144,512]{1,0:T(8,128)(2,1)S(1)}, bf16[144,512]{1,0:T(8,128)(2,1)S(1)}, u32[]{:S(2)}, u32[]{:S(2)}) collective-permute-start(bf16[144,512]{1,0:T(8,128)(2,1)S(1)} %get-tuple-element.49.refs_5_), channel_id=1, source_target_pairs={{0,4},{2,6},{4,0},{6,2},{1,5},{3,7},{5,1},{7,3},{8,12},{10,14},{12... | collective-permute-start | bytes 442376 | tf_op jit(solution)/shard_map/ppermute | solution.py:472
  33.0 10.8 %collective-permute-start.13 = (bf16[144,512]{1,0:T(8,128)(2,1)S(1)}, bf16[144,512]{1,0:T(8,128)(2,1)S(1)}, u32[]{:S(2)}, u32[]{:S(2)}) collective-permute-start(bf16[144,512]{1,0:T(8,128)(2,1)S(1)} %get-tuple-element.50.refs_6_), channel_id=1, source_target_pairs={{0,6},{2,4},{4,2},{6,0},{1,7},{3,5},{5,3},{7,1},{8,14},{10,12},{12... | collective-permute-start | bytes 442376 | tf_op jit(solution)/shard_map/ppermute | solution.py:472
  34.4 5.2 %collective-permute-start.4 = (bf16[144,512]{1,0:T(8,128)(2,1)S(1)}, bf16[144,512]{1,0:T(8,128)(2,1)S(1)}, u32[]{:S(2)}, u32[]{:S(2)}) collective-permute-start(bf16[144,512]{1,0:T(8,128)(2,1)S(1)} %get-tuple-element.52), channel_id=1, source_target_pairs={{0,8},{8,0},{16,24},{24,16},{1,9},{9,1},{17,25},{25,17},{2,10},{10... | collective-permute-start | bytes 442376 | tf_op jit(solution)/shard_map/ppermute | solution.py:472
  36.0 5.1 %collective-permute-start.5 = (bf16[144,512]{1,0:T(8,128)(2,1)S(1)}, bf16[144,512]{1,0:T(8,128)(2,1)S(1)}, u32[]{:S(2)}, u32[]{:S(2)}) collective-permute-start(bf16[144,512]{1,0:T(8,128)(2,1)S(1)} %get-tuple-element.53), channel_id=1, source_target_pairs={{0,16},{8,24},{16,0},{24,8},{1,17},{9,25},{17,1},{25,9},{2,18},{10... | collective-permute-start | bytes 442376 | tf_op jit(solution)/shard_map/ppermute | solution.py:472
  37.5 6.1 %collective-permute-start.6 = (bf16[144,512]{1,0:T(8,128)(2,1)S(1)}, bf16[144,512]{1,0:T(8,128)(2,1)S(1)}, u32[]{:S(2)}, u32[]{:S(2)}) collective-permute-start(bf16[144,512]{1,0:T(8,128)(2,1)S(1)} %get-tuple-element.54), channel_id=1, source_target_pairs={{0,24},{8,16},{16,8},{24,0},{1,25},{9,17},{17,9},{25,1},{2,26},{10... | collective-permute-start | bytes 442376 | tf_op jit(solution)/shard_map/ppermute | solution.py:472
  43.7 13.7 %copy-start.3 = (bf16[512,512]{1,0:T(8,128)(2,1)S(1)}, bf16[512,512]{1,0:T(8,128)(2,1)}, u32[]{:S(2)}) copy-start(bf16[512,512]{1,0:T(8,128)(2,1)} %state_ref.3) | copy-start | bytes 1572868
  43.7 13.7 %copy-start.4 = (bf16[512,512]{1,0:T(8,128)(2,1)S(1)}, bf16[512,512]{1,0:T(8,128)(2,1)}, u32[]{:S(2)}) copy-start(bf16[512,512]{1,0:T(8,128)(2,1)} %w_ref.6) | copy-start | bytes 1572868
  43.7 4.3 %collective-permute-start.9 = (bf16[576,512]{1,0:T(8,128)(2,1)S(1)}, bf16[576,512]{1,0:T(8,128)(2,1)S(1)}, u32[]{:S(2)}, u32[]{:S(2)}) collective-permute-start(bf16[576,512]{1,0:T(8,128)(2,1)S(1)} %join.1.own_ref), channel_id=1, source_target_pairs={{0,1},{1,0},{2,3},{3,2},{4,5},{5,4},{6,7},{7,6},{8,9},{9,8},{10,11... | collective-permute-start | bytes 1769480 | tf_op jit(solution)/shard_map/ppermute | solution.py:472
  44.4 9.0 %collective-permute-start.14 = (bf16[144,512]{1,0:T(8,128)(2,1)S(1)}, bf16[144,512]{1,0:T(8,128)(2,1)S(1)}, u32[]{:S(2)}, u32[]{:S(2)}) collective-permute-start(bf16[144,512]{1,0:T(8,128)(2,1)S(1)} %get-tuple-element.58), channel_id=1, source_target_pairs={{0,8},{8,0},{16,24},{24,16},{1,9},{9,1},{17,25},{25,17},{2,10},{10... | collective-permute-start | bytes 442376 | tf_op jit(solution)/shard_map/ppermute | solution.py:472
  45.6 9.2 %collective-permute-start.15 = (bf16[144,512]{1,0:T(8,128)(2,1)S(1)}, bf16[144,512]{1,0:T(8,128)(2,1)S(1)}, u32[]{:S(2)}, u32[]{:S(2)}) collective-permute-start(bf16[144,512]{1,0:T(8,128)(2,1)S(1)} %get-tuple-element.59), channel_id=1, source_target_pairs={{0,16},{8,24},{16,0},{24,8},{1,17},{9,25},{17,1},{25,9},{2,18},{10... | collective-permute-start | bytes 442376 | tf_op jit(solution)/shard_map/ppermute | solution.py:472
  47.1 7.7 %collective-permute-start.16 = (bf16[144,512]{1,0:T(8,128)(2,1)S(1)}, bf16[144,512]{1,0:T(8,128)(2,1)S(1)}, u32[]{:S(2)}, u32[]{:S(2)}) collective-permute-start(bf16[144,512]{1,0:T(8,128)(2,1)S(1)} %get-tuple-element.60), channel_id=1, source_target_pairs={{0,24},{8,16},{16,8},{24,0},{1,25},{9,17},{17,9},{25,1},{2,26},{10... | collective-permute-start | bytes 442376 | tf_op jit(solution)/shard_map/ppermute | solution.py:472
  50.3 7.0 %collective-permute-start.10 = (bf16[128,512]{1,0:T(8,128)(2,1)S(1)}, bf16[128,512]{1,0:T(8,128)(2,1)S(1)}, u32[]{:S(2)}, u32[]{:S(2)}) collective-permute-start(bf16[128,512]{1,0:T(8,128)(2,1)S(1)} %bitcast.19), channel_id=1, source_target_pairs={{0,2},{2,0},{4,6},{6,4},{1,3},{3,1},{5,7},{7,5},{8,10},{10,8},{12,... | collective-permute-start | bytes 393224 | tf_op jit(solution)/shard_map/ppermute | solution.py:472
  52.0 11.5 %collective-permute-start.11 = (bf16[128,512]{1,0:T(8,128)(2,1)S(1)}, bf16[128,512]{1,0:T(8,128)(2,1)S(1)}, u32[]{:S(2)}, u32[]{:S(2)}) collective-permute-start(bf16[128,512]{1,0:T(8,128)(2,1)S(1)} %bitcast.18), channel_id=1, source_target_pairs={{0,4},{2,6},{4,0},{6,2},{1,5},{3,7},{5,1},{7,3},{8,12},{10,14},{12... | collective-permute-start | bytes 393224 | tf_op jit(solution)/shard_map/ppermute | solution.py:472
  53.4 10.1 %collective-permute-start.12 = (bf16[128,512]{1,0:T(8,128)(2,1)S(1)}, bf16[128,512]{1,0:T(8,128)(2,1)S(1)}, u32[]{:S(2)}, u32[]{:S(2)}) collective-permute-start(bf16[128,512]{1,0:T(8,128)(2,1)S(1)} %bitcast.17), channel_id=1, source_target_pairs={{0,6},{2,4},{4,2},{6,0},{1,7},{3,5},{5,3},{7,1},{8,14},{10,12},{12... | collective-permute-start | bytes 393224 | tf_op jit(solution)/shard_map/ppermute | solution.py:472
  57.3 18.2 %copy-start = (bf16[1024,512]{1,0:T(8,128)(2,1)S(1)}, bf16[1024,512]{1,0:T(8,128)(2,1)}, u32[]{:S(2)}) copy-start(bf16[1024,512]{1,0:T(8,128)(2,1)} %w_ref.9) | copy-start | bytes 3145732
  57.8 6.7 %collective-permute-start.19 = (bf16[128,512]{1,0:T(8,128)(2,1)S(1)}, bf16[128,512]{1,0:T(8,128)(2,1)S(1)}, u32[]{:S(2)}, u32[]{:S(2)}) collective-permute-start(bf16[128,512]{1,0:T(8,128)(2,1)S(1)} %update_prod.1.rest_0_), channel_id=1, source_target_pairs={{0,24},{8,16},{16,8},{24,0},{1,25},{9,17},{17,9},{25,1},{2,26},{10... | collective-permute-start | bytes 393224 | tf_op jit(solution)/shard_map/ppermute | solution.py:472
  59.4 6.0 %collective-permute-start.18 = (bf16[128,512]{1,0:T(8,128)(2,1)S(1)}, bf16[128,512]{1,0:T(8,128)(2,1)S(1)}, u32[]{:S(2)}, u32[]{:S(2)}) collective-permute-start(bf16[128,512]{1,0:T(8,128)(2,1)S(1)} %update_prod.1.rest_0_), channel_id=1, source_target_pairs={{0,16},{8,24},{16,0},{24,8},{1,17},{9,25},{17,1},{25,9},{2,18},{10... | collective-permute-start | bytes 393224 | tf_op jit(solution)/shard_map/ppermute | solution.py:472
  59.9 5.5 %collective-permute-start.17 = (bf16[128,512]{1,0:T(8,128)(2,1)S(1)}, bf16[128,512]{1,0:T(8,128)(2,1)S(1)}, u32[]{:S(2)}, u32[]{:S(2)}) collective-permute-start(bf16[128,512]{1,0:T(8,128)(2,1)S(1)} %update_prod.1.rest_0_), channel_id=1, source_target_pairs={{0,8},{8,0},{16,24},{24,16},{1,9},{9,1},{17,25},{25,17},{2,10},{10... | collective-permute-start | bytes 393224 | tf_op jit(solution)/shard_map/ppermute | solution.py:472
  66.6 6.7 %collective-permute-start.20 = (bf16[128,512]{1,0:T(8,128)(2,1)S(1)}, bf16[128,512]{1,0:T(8,128)(2,1)S(1)}, u32[]{:S(2)}, u32[]{:S(2)}) collective-permute-start(bf16[128,512]{1,0:T(8,128)(2,1)S(1)} %get-tuple-element.63), channel_id=1, source_target_pairs={{0,8},{8,0},{16,24},{24,16},{1,9},{9,1},{17,25},{25,17},{2,10},{10... | collective-permute-start | bytes 393224 | tf_op jit(solution)/shard_map/ppermute | solution.py:472
  67.6 8.0 %collective-permute-start.21 = (bf16[128,512]{1,0:T(8,128)(2,1)S(1)}, bf16[128,512]{1,0:T(8,128)(2,1)S(1)}, u32[]{:S(2)}, u32[]{:S(2)}) collective-permute-start(bf16[128,512]{1,0:T(8,128)(2,1)S(1)} %get-tuple-element.64), channel_id=1, source_target_pairs={{0,16},{8,24},{16,0},{24,8},{1,17},{9,25},{17,1},{25,9},{2,18},{10... | collective-permute-start | bytes 393224 | tf_op jit(solution)/shard_map/ppermute | solution.py:472
  68.8 6.8 %collective-permute-start.22 = (bf16[128,512]{1,0:T(8,128)(2,1)S(1)}, bf16[128,512]{1,0:T(8,128)(2,1)S(1)}, u32[]{:S(2)}, u32[]{:S(2)}) collective-permute-start(bf16[128,512]{1,0:T(8,128)(2,1)S(1)} %get-tuple-element.65), channel_id=1, source_target_pairs={{0,24},{8,16},{16,8},{24,0},{1,25},{9,17},{17,9},{25,1},{2,26},{10... | collective-permute-start | bytes 393224 | tf_op jit(solution)/shard_map/ppermute | solution.py:472
  70.2 6.1 %collective-permute-start.23 = (bf16[128,512]{1,0:T(8,128)(2,1)S(1)}, bf16[128,512]{1,0:T(8,128)(2,1)S(1)}, u32[]{:S(2)}, u32[]{:S(2)}) collective-permute-start(bf16[128,512]{1,0:T(8,128)(2,1)S(1)} %get-tuple-element.66), channel_id=1, source_target_pairs={{0,2},{2,0},{4,6},{6,4},{1,3},{3,1},{5,7},{7,5},{8,10},{10,8},{12,... | collective-permute-start | bytes 393224 | tf_op jit(solution)/shard_map/ppermute | solution.py:472
  71.5 10.0 %collective-permute-start.24 = (bf16[128,512]{1,0:T(8,128)(2,1)S(1)}, bf16[128,512]{1,0:T(8,128)(2,1)S(1)}, u32[]{:S(2)}, u32[]{:S(2)}) collective-permute-start(bf16[128,512]{1,0:T(8,128)(2,1)S(1)} %get-tuple-element.67), channel_id=1, source_target_pairs={{0,4},{2,6},{4,0},{6,2},{1,5},{3,7},{5,1},{7,3},{8,12},{10,14},{12... | collective-permute-start | bytes 393224 | tf_op jit(solution)/shard_map/ppermute | solution.py:472
  73.3 8.2 %collective-permute-start.25 = (bf16[128,512]{1,0:T(8,128)(2,1)S(1)}, bf16[128,512]{1,0:T(8,128)(2,1)S(1)}, u32[]{:S(2)}, u32[]{:S(2)}) collective-permute-start(bf16[128,512]{1,0:T(8,128)(2,1)S(1)} %get-tuple-element.68), channel_id=1, source_target_pairs={{0,6},{2,4},{4,2},{6,0},{1,7},{3,5},{5,3},{7,1},{8,14},{10,12},{12... | collective-permute-start | bytes 393224 | tf_op jit(solution)/shard_map/ppermute | solution.py:472
  81.5 1.6 %collective-permute-start.26 = (bf16[256,512]{1,0:T(8,128)(2,1)S(1)}, bf16[256,512]{1,0:T(8,128)(2,1)S(1)}, u32[]{:S(2)}, u32[]{:S(2)}) collective-permute-start(bf16[256,512]{1,0:T(8,128)(2,1)S(1)} %get-tuple-element.70), channel_id=1, source_target_pairs={{0,1},{1,0},{2,3},{3,2},{4,5},{5,4},{6,7},{7,6},{8,9},{9,8},{10,11... | collective-permute-start | bytes 786440 | tf_op jit(solution)/shard_map/ppermute | solution.py:472

commit v6 on v5

--- a/solution.py
+++ b/solution.py
@@ -383,7 +383,7 @@
 
 
 def prod_reply_kernel(slabs, parts, pick_ref, *rest):
-    pieces, new_ref, reply_refs = rest[:slabs], rest[-1 - parts], rest[-parts:]
+    pieces, new_ref, reply_refs = rest[:slabs], rest[-1], rest[-1 - parts:-1]
     size = pieces[0].shape[0]
     for t, ref in enumerate(pieces):
         first = pl.multiple_of((lax.axis_index("rev") ^ t) * size, size)
@@ -395,17 +395,37 @@
 
 def reply_prod(pick, pieces, parts, after):
     slabs = len(pieces)
-    size, rows = pieces[0].shape[0] * slabs, pick.shape[0]
-    out = pl.pallas_call(
+    rows = pick.shape[0]
+    return pl.pallas_call(
         functools.partial(prod_reply_kernel, slabs, parts),
         in_specs=[VMEM] * (1 + slabs) + [ANY] * len(after),
-        out_specs=[VMEM] * (1 + parts),
-        out_shape=[jax.ShapeDtypeStruct((size, H), BF)]
-        + [jax.ShapeDtypeStruct((rows // parts, H), BF)] * parts,
+        out_specs=[VMEM] * parts,
+        out_shape=[jax.ShapeDtypeStruct((rows // parts, H), BF)] * parts,
+        scratch_shapes=[pltpu.VMEM((pieces[0].shape[0] * slabs, H), BF)],
         compiler_params=PARAMS,
         name="reply_prod",
     )(pick, *pieces, *after)
-    return out[0], out[1:]
+
+
+def states_kernel(cust_ref, *refs):
+    pieces, (cust_out, prod_out) = refs[:-2], refs[-2:]
+    size = pieces[0].shape[0]
+    cust_out[...] = cust_ref[...]
+    for t, ref in enumerate(pieces):
+        first = pl.multiple_of((lax.axis_index("rev") ^ t) * size, size)
+        prod_out[pl.ds(first, size), :] = ref[...]
+
+
+def states(new_cust, pieces):
+    rows = pieces[0].shape[0] * len(pieces)
+    return pl.pallas_call(
+        states_kernel,
+        in_specs=[VMEM] * (1 + len(pieces)),
+        out_specs=[VMEM] * 2,
+        out_shape=[jax.ShapeDtypeStruct(new_cust.shape, BF), jax.ShapeDtypeStruct((rows, H), BF)],
+        compiler_params=PARAMS,
+        name="states",
+    )(new_cust, *pieces)
 
 
 def turned_kernel(ids_ref, *refs):
@@ -530,12 +550,13 @@
 
     new_piece = update_prod(prod_state, w_prod_up, pieces, cust_got[1:2])
     new_pieces = [swap(new_piece, "rev", t) for t in range(nr)]
-    new_prod, made = reply_prod(turned_picks(prod_in, prod_state.shape[0])[0], new_pieces, nz, cust_got[2:])
+    made = reply_prod(turned_picks(prod_in, prod_state.shape[0])[0], new_pieces, nz, cust_got[2:])
+    new_cust, new_prod = states(new_cust, new_pieces)
     replies = [swap(made[s], "cust", s) for s in range(nz)]
     cust_back = regroup(cs, nr, cust_got, made[:1])
     cust_back = [swap(cust_back[t], "rev", t) for t in range(nr)]
     part = finish_part((0, 0), cust_pick, review_h, w_back, cust_back, F32, "finish_cust")
-    own_replies, peer_replies = halve(replies, [part])
+    own_replies, peer_replies = halve(replies, [part, new_prod])
     peer_replies = swap(peer_replies, "prod", 1)
     part = finish_part((0, H), prod_pick, part, w_back, [own_replies], F32, "finish_own")
     review_out = finish_part((rows // nc, H), prod_pick, part, w_back, [peer_replies], BF, "finish")

time: 84.8 us -> 83.8 us (0.988)
  waiting for transfers between devices: 29.4 us -> 28.5 us
    pallas_call x0 -> x1, Pallas kernels: none -> 1.05 us  [states(): pl.pallas_call(states_kernel, in_specs=[VMEM] * (1 + len(pieces)), out_sp...]
    ppermute x27, waiting for transfers between devices: 29.4 us -> 28.5 us  [swap(): lax.ppermute(value, axis, [(i, i ^ by) for i in range(lax.axis_size(axis))])]
  transfers between devices with their start and end apart: 27 -> 27, of which waited for: 11 -> 12; matrix products, arithmetic and copies ran while one was open for 0% -> 0% of each run, Pallas kernels for 6% -> 7%
where the time goes in v6:
time: 83.8 us; the launch traced here: 83.6 us
  starting transfers between devices  34.1 us (41%)
  waiting for transfers between devices  28.5 us (34%)
  Pallas kernels  19.3 us (23%)
  between operations  0.88 us (1%)
    ppermute x27, starting transfers between devices, swap(): lax.ppermute(value, axis, [(i, i ^ by) for i in range(lax.axis_size(axis))])  34.1 us
    ppermute x27, waiting for transfers between devices, swap(): lax.ppermute(value, axis, [(i, i ^ by) for i in range(lax.axis_size(axis))])  28.5 us
    pallas_call x1, Pallas kernels, encode(): pl.pallas_call(functools.partial(encode_kernel, sizes, rows), in_specs=[H...  11.3 us
    pallas_call x3, Pallas kernels, finish_part(): pl.pallas_call(functools.partial(finish_part_kernel, start), in_specs=[VM...  2.75 us
    pallas_call x1, Pallas kernels, update_cust(): pl.pallas_call(functools.partial(cust_kernel, groups), in_specs=[VMEM] *...  1.75 us
  transfers between devices with their start and end apart: 27, of which 12 were waited for; matrix products, arithmetic and copies ran while one was open for 0% of the time, Pallas kernels for 7%

profile of v6, /device:TPU:0, one launch (start us, length us, event | category | flops | bytes accessed | tf_op | source)
XLA Modules:
  0.0 83.6 jit_solution(5234639364453969750)
XLA Ops:
  0.6 0.7 pad_add_fusion.refs_4_
  1.4 11.3 %encode.1 = (bf16[512,512]{1,0:T(8,128)(2,1)S(1)}, s32[2,512]{1,0:T(2,128)S(1)}, bf16[144,512]{1,0:T(8,128)(2,1)S(1)}, bf16[144,512]{1,0:T(8,128)(2,1)S(1)}, bf1...) custom-call(bf16[512,2048]{1,0:T(8,128)(2,1)} %refs_0_.1, ...), custom_call_target="tpu_custom_call" | custom-call | tf_op jit(solution)/shard_map/encode/pallas_call | solution.py:197
  12.7 0.0 copy-start.1
  12.7 0.0 copy-start.2
  12.7 0.5 collective-permute-start.3
  13.3 2.6 %collective-permute-start = (bf16[144,512]{1,0:T(8,128)(2,1)S(1)}, bf16[144,512]{1,0:T(8,128)(2,1)S(1)}, u32[]{:S(2)}, u32[]{:S(2)}) collective-permute-start(bf16[144,512]{1,0:T(8,128)(2,1)S(1)} %get-tuple-element.44), channel_id=1, source_target_pairs={{0,2},{2,0},{4,6},{6,4},{1,3},{3,1},{5,7},{7,5},{8,10},{10,8},{12,... | collective-permute-start | bytes 442376 | tf_op jit(solution)/shard_map/ppermute | solution.py:492
  15.9 2.6 %collective-permute-start.1 = (bf16[144,512]{1,0:T(8,128)(2,1)S(1)}, bf16[144,512]{1,0:T(8,128)(2,1)S(1)}, u32[]{:S(2)}, u32[]{:S(2)}) collective-permute-start(bf16[144,512]{1,0:T(8,128)(2,1)S(1)} %get-tuple-element.45), channel_id=1, source_target_pairs={{0,4},{2,6},{4,0},{6,2},{1,5},{3,7},{5,1},{7,3},{8,12},{10,14},{12... | collective-permute-start | bytes 442376 | tf_op jit(solution)/shard_map/ppermute | solution.py:492
  18.5 0.0 collective-permute-start.2
  18.5 4.5 %collective-permute-done.refs_0_.refs_1_ = bf16[144,512]{1,0:T(8,128)(2,1)S(1)} collective-permute-done((bf16[144,512]{1,0:T(8,128)(2,1)S(1)}, bf16[144,512]{1,0:T(8,128)(2,1)S(1)}, u32[]{:S(2)}, u32[]{:S(2)}) %collective-permute-start) | collective-permute-done | bytes 147488 | tf_op jit(solution)/shard_map/ppermute | solution.py:492
  23.0 6.9 %collective-permute-done.1.refs_1_.refs_2_ = bf16[144,512]{1,0:T(8,128)(2,1)S(1)} collective-permute-done((bf16[144,512]{1,0:T(8,128)(2,1)S(1)}, bf16[144,512]{1,0:T(8,128)(2,1)S(1)}, u32[]{:S(2)}, u32[]{:S(2)}) %collective-permute-start.1) | collective-permute-done | bytes 147488 | tf_op jit(solution)/shard_map/ppermute | solution.py:492
  29.9 0.1 collective-permute-start.7
  30.0 3.0 %collective-permute-start.8 = (bf16[144,512]{1,0:T(8,128)(2,1)S(1)}, bf16[144,512]{1,0:T(8,128)(2,1)S(1)}, u32[]{:S(2)}, u32[]{:S(2)}) collective-permute-start(bf16[144,512]{1,0:T(8,128)(2,1)S(1)} %get-tuple-element.50.refs_5_), channel_id=1, source_target_pairs={{0,4},{2,6},{4,0},{6,2},{1,5},{3,7},{5,1},{7,3},{8,12},{10,14},{12... | collective-permute-start | bytes 442376 | tf_op jit(solution)/shard_map/ppermute | solution.py:492
  33.0 1.4 %collective-permute-start.13 = (bf16[144,512]{1,0:T(8,128)(2,1)S(1)}, bf16[144,512]{1,0:T(8,128)(2,1)S(1)}, u32[]{:S(2)}, u32[]{:S(2)}) collective-permute-start(bf16[144,512]{1,0:T(8,128)(2,1)S(1)} %get-tuple-element.51.refs_6_), channel_id=1, source_target_pairs={{0,6},{2,4},{4,2},{6,0},{1,7},{3,5},{5,3},{7,1},{8,14},{10,12},{12... | collective-permute-start | bytes 442376 | tf_op jit(solution)/shard_map/ppermute | solution.py:492
  34.4 0.0 collective-permute-done.2.refs_3_
  34.4 1.6 %collective-permute-start.4 = (bf16[144,512]{1,0:T(8,128)(2,1)S(1)}, bf16[144,512]{1,0:T(8,128)(2,1)S(1)}, u32[]{:S(2)}, u32[]{:S(2)}) collective-permute-start(bf16[144,512]{1,0:T(8,128)(2,1)S(1)} %get-tuple-element.53), channel_id=1, source_target_pairs={{0,8},{8,0},{16,24},{24,16},{1,9},{9,1},{17,25},{25,17},{2,10},{10... | collective-permute-start | bytes 442376 | tf_op jit(solution)/shard_map/ppermute | solution.py:492
  36.0 1.5 %collective-permute-start.5 = (bf16[144,512]{1,0:T(8,128)(2,1)S(1)}, bf16[144,512]{1,0:T(8,128)(2,1)S(1)}, u32[]{:S(2)}, u32[]{:S(2)}) collective-permute-start(bf16[144,512]{1,0:T(8,128)(2,1)S(1)} %get-tuple-element.54), channel_id=1, source_target_pairs={{0,16},{8,24},{16,0},{24,8},{1,17},{9,25},{17,1},{25,9},{2,18},{10... | collective-permute-start | bytes 442376 | tf_op jit(solution)/shard_map/ppermute | solution.py:492
  37.5 0.0 collective-permute-done.7.refs_4_.refs_1_
  37.5 0.6 collective-permute-start.6
  38.1 1.5 %collective-permute-done.4.refs_1_ = bf16[144,512]{1,0:T(8,128)(2,1)S(1)} collective-permute-done((bf16[144,512]{1,0:T(8,128)(2,1)S(1)}, bf16[144,512]{1,0:T(8,128)(2,1)S(1)}, u32[]{:S(2)}, u32[]{:S(2)}) %collective-permute-start.4) | collective-permute-done | bytes 147488 | tf_op jit(solution)/shard_map/ppermute | solution.py:492
  39.6 1.5 %collective-permute-done.5.refs_2_ = bf16[144,512]{1,0:T(8,128)(2,1)S(1)} collective-permute-done((bf16[144,512]{1,0:T(8,128)(2,1)S(1)}, bf16[144,512]{1,0:T(8,128)(2,1)S(1)}, u32[]{:S(2)}, u32[]{:S(2)}) %collective-permute-start.5) | collective-permute-done | bytes 147488 | tf_op jit(solution)/shard_map/ppermute | solution.py:492
  41.1 2.5 %collective-permute-done.6.refs_3_ = bf16[144,512]{1,0:T(8,128)(2,1)S(1)} collective-permute-done((bf16[144,512]{1,0:T(8,128)(2,1)S(1)}, bf16[144,512]{1,0:T(8,128)(2,1)S(1)}, u32[]{:S(2)}, u32[]{:S(2)}) %collective-permute-start.6) | collective-permute-done | bytes 147488 | tf_op jit(solution)/shard_map/ppermute | solution.py:492
  43.6 0.0 collective-permute-done.8.refs_5_.refs_2_
  43.7 0.0 copy-start.3
  43.7 0.0 copy-start.4
  43.7 0.1 collective-permute-start.9
  43.8 0.6 sum_prod.1
  44.4 1.2 %collective-permute-start.14 = (bf16[144,512]{1,0:T(8,128)(2,1)S(1)}, bf16[144,512]{1,0:T(8,128)(2,1)S(1)}, u32[]{:S(2)}, u32[]{:S(2)}) collective-permute-start(bf16[144,512]{1,0:T(8,128)(2,1)S(1)} %get-tuple-element.59), channel_id=1, source_target_pairs={{0,8},{8,0},{16,24},{24,16},{1,9},{9,1},{17,25},{25,17},{2,10},{10... | collective-permute-start | bytes 442376 | tf_op jit(solution)/shard_map/ppermute | solution.py:492
  45.6 1.5 %collective-permute-start.15 = (bf16[144,512]{1,0:T(8,128)(2,1)S(1)}, bf16[144,512]{1,0:T(8,128)(2,1)S(1)}, u32[]{:S(2)}, u32[]{:S(2)}) collective-permute-start(bf16[144,512]{1,0:T(8,128)(2,1)S(1)} %get-tuple-element.60), channel_id=1, source_target_pairs={{0,16},{8,24},{16,0},{24,8},{1,17},{9,25},{17,1},{25,9},{2,18},{10... | collective-permute-start | bytes 442376 | tf_op jit(solution)/shard_map/ppermute | solution.py:492
  47.1 0.9 %collective-permute-start.16 = (bf16[144,512]{1,0:T(8,128)(2,1)S(1)}, bf16[144,512]{1,0:T(8,128)(2,1)S(1)}, u32[]{:S(2)}, u32[]{:S(2)}) collective-permute-start(bf16[144,512]{1,0:T(8,128)(2,1)S(1)} %get-tuple-element.61), channel_id=1, source_target_pairs={{0,24},{8,16},{16,8},{24,0},{1,25},{9,17},{17,9},{25,1},{2,26},{10... | collective-permute-start | bytes 442376 | tf_op jit(solution)/shard_map/ppermute | solution.py:492
  48.0 0.0 collective-permute-done.9.peer_ref
  48.0 1.7 %update_cust.1 = (bf16[512,512]{1,0:T(8,128)(2,1)S(1)}, bf16[512,512]{1,0:T(8,128)(2,1)S(1)}) custom-call(bf16[576,512]{1,0:T(8,128)(2,1)S(1)} %join.1.own_ref, bf16[576,512]{1,0:T(8,128)(2,1)S(1)} %collective-permute-done.9.peer_ref, bf16[512,512]{1,0:T(8,128)(2,1)S(1)} %copy-done.1, bf16[512,512]{1,0:T(8,128)(2,1)S(1)} %copy-done.2), custom_call_target="tpu_custom_call" | custom-call | tf_op jit(solution)/shard_map/update_cust/pallas_call | solution.py:320
  49.8 1.7 %collective-permute-start.10 = (bf16[128,512]{1,0:T(8,128)(2,1)S(1)}, bf16[128,512]{1,0:T(8,128)(2,1)S(1)}, u32[]{:S(2)}, u32[]{:S(2)}) collective-permute-start(bf16[128,512]{1,0:T(8,128)(2,1)S(1)} %bitcast.19), channel_id=1, source_target_pairs={{0,2},{2,0},{4,6},{6,4},{1,3},{3,1},{5,7},{7,5},{8,10},{10,8},{12,... | collective-permute-start | bytes 393224 | tf_op jit(solution)/shard_map/ppermute | solution.py:492
  51.5 1.4 %collective-permute-start.11 = (bf16[128,512]{1,0:T(8,128)(2,1)S(1)}, bf16[128,512]{1,0:T(8,128)(2,1)S(1)}, u32[]{:S(2)}, u32[]{:S(2)}) collective-permute-start(bf16[128,512]{1,0:T(8,128)(2,1)S(1)} %bitcast.18), channel_id=1, source_target_pairs={{0,4},{2,6},{4,0},{6,2},{1,5},{3,7},{5,1},{7,3},{8,12},{10,14},{12... | collective-permute-start | bytes 393224 | tf_op jit(solution)/shard_map/ppermute | solution.py:492
  52.9 1.4 %collective-permute-start.12 = (bf16[128,512]{1,0:T(8,128)(2,1)S(1)}, bf16[128,512]{1,0:T(8,128)(2,1)S(1)}, u32[]{:S(2)}, u32[]{:S(2)}) collective-permute-start(bf16[128,512]{1,0:T(8,128)(2,1)S(1)} %bitcast.17), channel_id=1, source_target_pairs={{0,6},{2,4},{4,2},{6,0},{1,7},{3,5},{5,3},{7,1},{8,14},{10,12},{12... | collective-permute-start | bytes 393224 | tf_op jit(solution)/shard_map/ppermute | solution.py:492
  54.2 0.5 collective-permute-done.15.rest_2_
  54.7 2.1 %collective-permute-done.10.rest_4_.refs_1_ = bf16[128,512]{1,0:T(8,128)(2,1)S(1)} collective-permute-done((bf16[128,512]{1,0:T(8,128)(2,1)S(1)}, bf16[128,512]{1,0:T(8,128)(2,1)S(1)}, u32[]{:S(2)}, u32[]{:S(2)}) %collective-permute-start.10) | collective-permute-done | bytes 131104 | tf_op jit(solution)/shard_map/ppermute | solution.py:492
  56.8 0.4 update_prod.1.rest_0_.refs_0_
  57.3 0.0 copy-start
  57.3 1.6 %collective-permute-start.19 = (bf16[128,512]{1,0:T(8,128)(2,1)S(1)}, bf16[128,512]{1,0:T(8,128)(2,1)S(1)}, u32[]{:S(2)}, u32[]{:S(2)}) collective-permute-start(bf16[128,512]{1,0:T(8,128)(2,1)S(1)} %update_prod.1.rest_0_.refs_0_), channel_id=1, source_target_pairs={{0,24},{8,16},{16,8},{24,0},{1,25},{9,17},{17,9},{25,1},{2,26},{10... | collective-permute-start | bytes 393224 | tf_op jit(solution)/shard_map/ppermute | solution.py:492
  58.9 0.5 collective-permute-start.18
  59.4 1.4 %collective-permute-start.17 = (bf16[128,512]{1,0:T(8,128)(2,1)S(1)}, bf16[128,512]{1,0:T(8,128)(2,1)S(1)}, u32[]{:S(2)}, u32[]{:S(2)}) collective-permute-start(bf16[128,512]{1,0:T(8,128)(2,1)S(1)} %update_prod.1.rest_0_.refs_0_), channel_id=1, source_target_pairs={{0,8},{8,0},{16,24},{24,16},{1,9},{9,1},{17,25},{25,17},{2,10},{10... | collective-permute-start | bytes 393224 | tf_op jit(solution)/shard_map/ppermute | solution.py:492
  60.8 0.2 turned_picks.3.pick_ref
  61.0 1.9 %collective-permute-done.11.rest_4_.refs_2_ = bf16[128,512]{1,0:T(8,128)(2,1)S(1)} collective-permute-done((bf16[128,512]{1,0:T(8,128)(2,1)S(1)}, bf16[128,512]{1,0:T(8,128)(2,1)S(1)}, u32[]{:S(2)}, u32[]{:S(2)}) %collective-permute-start.11) | collective-permute-done | bytes 131104 | tf_op jit(solution)/shard_map/ppermute | solution.py:492
  63.0 1.0 %collective-permute-done.19.rest_3_.refs_3_ = bf16[128,512]{1,0:T(8,128)(2,1)S(1)} collective-permute-done((bf16[128,512]{1,0:T(8,128)(2,1)S(1)}, bf16[128,512]{1,0:T(8,128)(2,1)S(1)}, u32[]{:S(2)}, u32[]{:S(2)}) %collective-permute-start.19) | collective-permute-done | bytes 131104 | tf_op jit(solution)/shard_map/ppermute | solution.py:492
  63.9 1.0 %collective-permute-done.18.rest_2_.refs_2_ = bf16[128,512]{1,0:T(8,128)(2,1)S(1)} collective-permute-done((bf16[128,512]{1,0:T(8,128)(2,1)S(1)}, bf16[128,512]{1,0:T(8,128)(2,1)S(1)}, u32[]{:S(2)}, u32[]{:S(2)}) %collective-permute-start.18) | collective-permute-done | bytes 131104 | tf_op jit(solution)/shard_map/ppermute | solution.py:492
  64.9 0.0 collective-permute-done.17.rest_1_.refs_1_
  64.9 0.6 reply_prod.1
  65.6 1.0 %collective-permute-start.20 = (bf16[128,512]{1,0:T(8,128)(2,1)S(1)}, bf16[128,512]{1,0:T(8,128)(2,1)S(1)}, u32[]{:S(2)}, u32[]{:S(2)}) collective-permute-start(bf16[128,512]{1,0:T(8,128)(2,1)S(1)} %get-tuple-element.64), channel_id=1, source_target_pairs={{0,8},{8,0},{16,24},{24,16},{1,9},{9,1},{17,25},{25,17},{2,10},{10... | collective-permute-start | bytes 393224 | tf_op jit(solution)/shard_map/ppermute | solution.py:492
  66.5 1.2 %collective-permute-start.21 = (bf16[128,512]{1,0:T(8,128)(2,1)S(1)}, bf16[128,512]{1,0:T(8,128)(2,1)S(1)}, u32[]{:S(2)}, u32[]{:S(2)}) collective-permute-start(bf16[128,512]{1,0:T(8,128)(2,1)S(1)} %get-tuple-element.65), channel_id=1, source_target_pairs={{0,16},{8,24},{16,0},{24,8},{1,17},{9,25},{17,1},{25,9},{2,18},{10... | collective-permute-start | bytes 393224 | tf_op jit(solution)/shard_map/ppermute | solution.py:492
  67.7 1.4 %collective-permute-start.22 = (bf16[128,512]{1,0:T(8,128)(2,1)S(1)}, bf16[128,512]{1,0:T(8,128)(2,1)S(1)}, u32[]{:S(2)}, u32[]{:S(2)}) collective-permute-start(bf16[128,512]{1,0:T(8,128)(2,1)S(1)} %get-tuple-element.66), channel_id=1, source_target_pairs={{0,24},{8,16},{16,8},{24,0},{1,25},{9,17},{17,9},{25,1},{2,26},{10... | collective-permute-start | bytes 393224 | tf_op jit(solution)/shard_map/ppermute | solution.py:492
  69.1 1.3 %collective-permute-start.23 = (bf16[128,512]{1,0:T(8,128)(2,1)S(1)}, bf16[128,512]{1,0:T(8,128)(2,1)S(1)}, u32[]{:S(2)}, u32[]{:S(2)}) collective-permute-start(bf16[128,512]{1,0:T(8,128)(2,1)S(1)} %get-tuple-element.67), channel_id=1, source_target_pairs={{0,2},{2,0},{4,6},{6,4},{1,3},{3,1},{5,7},{7,5},{8,10},{10,8},{12,... | collective-permute-start | bytes 393224 | tf_op jit(solution)/shard_map/ppermute | solution.py:492
  70.4 1.8 %collective-permute-start.24 = (bf16[128,512]{1,0:T(8,128)(2,1)S(1)}, bf16[128,512]{1,0:T(8,128)(2,1)S(1)}, u32[]{:S(2)}, u32[]{:S(2)}) collective-permute-start(bf16[128,512]{1,0:T(8,128)(2,1)S(1)} %get-tuple-element.68), channel_id=1, source_target_pairs={{0,4},{2,6},{4,0},{6,2},{1,5},{3,7},{5,1},{7,3},{8,12},{10,14},{12... | collective-permute-start | bytes 393224 | tf_op jit(solution)/shard_map/ppermute | solution.py:492
  72.2 0.0 collective-permute-done.20.rest_1_
  72.2 1.9 %collective-permute-start.25 = (bf16[128,512]{1,0:T(8,128)(2,1)S(1)}, bf16[128,512]{1,0:T(8,128)(2,1)S(1)}, u32[]{:S(2)}, u32[]{:S(2)}) collective-permute-start(bf16[128,512]{1,0:T(8,128)(2,1)S(1)} %get-tuple-element.69), channel_id=1, source_target_pairs={{0,6},{2,4},{4,2},{6,0},{1,7},{3,5},{5,3},{7,1},{8,14},{10,12},{12... | collective-permute-start | bytes 393224 | tf_op jit(solution)/shard_map/ppermute | solution.py:492
  74.1 0.4 turned_picks.2
  74.5 1.0 %states.1 = (bf16[512,512]{1,0:T(8,128)(2,1)}, bf16[512,512]{1,0:T(8,128)(2,1)}) custom-call(bf16[512,512]{1,0:T(8,128)(2,1)S(1)} %get-tuple-element.70.cust_ref, bf16[128,512]{1,0:T(8,128)(2,1)S(1)} %update_prod.1.rest_0_.refs_0_, bf16[128,512]{1,0:T(8,128)(2,1)S(1)} %collective-permute-done.17.rest_1_.refs_1_, ...), custom_call_target="tpu_custom_call" | custom-call | tf_op jit(solution)/shard_map/states/pallas_call | solution.py:421
  75.6 0.0 collective-permute-done.21.rest_2_
  75.6 0.7 finish_cust.1.refs_4_.sum_ref
  76.3 0.0 collective-permute-done.23.refs_1_
  76.3 4.2 %collective-permute-done.24.refs_2_ = bf16[128,512]{1,0:T(8,128)(2,1)S(1)} collective-permute-done((bf16[128,512]{1,0:T(8,128)(2,1)S(1)}, bf16[128,512]{1,0:T(8,128)(2,1)S(1)}, u32[]{:S(2)}, u32[]{:S(2)}) %collective-permute-start.24) | collective-permute-done | bytes 131104 | tf_op jit(solution)/shard_map/ppermute | solution.py:492
  80.5 0.1 collective-permute-start.26
  80.6 0.6 finish_own.1.sum_ref
  81.2 0.9 %collective-permute-done.26.rest_0_ = bf16[256,512]{1,0:T(8,128)(2,1)S(1)} collective-permute-done((bf16[256,512]{1,0:T(8,128)(2,1)S(1)}, bf16[256,512]{1,0:T(8,128)(2,1)S(1)}, u32[]{:S(2)}, u32[]{:S(2)}) %collective-permute-start.26) | collective-permute-done | bytes 262176 | tf_op jit(solution)/shard_map/ppermute | solution.py:492
  82.1 1.5 %finish.1 = bf16[512,512]{1,0:T(8,128)(2,1)} custom-call(bf16[512,512]{1,0:T(8,128)(2,1)S(1)} %get-tuple-element.40.pick_ref, f32[512,512]{1,0:T(8,128)S(1)} %finish_own.1.sum_ref, bf16[1024,512]{1,0:T(8,128)(2,1)S(1)} %copy-done, bf16[256,512]{1,0:T(8,128)(2,1)S(1)} %collective-permute-done.26.rest_0_), custom_call_target="tpu_custom_call" | custom-call | tf_op jit(solution)/shard_map/finish/pallas_call | solution.py:460
  (29 shorter events, 0.3 us)
Async XLA Ops:
  12.7 35.3 %copy-start.1 = (bf16[512,512]{1,0:T(8,128)(2,1)S(1)}, bf16[512,512]{1,0:T(8,128)(2,1)}, u32[]{:S(2)}) copy-start(bf16[512,512]{1,0:T(8,128)(2,1)} %state_ref.2) | copy-start | bytes 1572868
  12.7 35.3 %copy-start.2 = (bf16[512,512]{1,0:T(8,128)(2,1)S(1)}, bf16[512,512]{1,0:T(8,128)(2,1)}, u32[]{:S(2)}) copy-start(bf16[512,512]{1,0:T(8,128)(2,1)} %w_ref.5) | copy-start | bytes 1572868
  12.7 17.1 %collective-permute-start.3 = (bf16[320,512]{1,0:T(8,128)(2,1)S(1)}, bf16[320,512]{1,0:T(8,128)(2,1)S(1)}, u32[]{:S(2)}, u32[]{:S(2)}) collective-permute-start(bf16[320,512]{1,0:T(8,128)(2,1)S(1)} %get-tuple-element.48), channel_id=1, source_target_pairs={{0,1},{1,0},{2,3},{3,2},{4,5},{5,4},{6,7},{7,6},{8,9},{9,8},{10,11... | collective-permute-start | bytes 983048 | tf_op jit(solution)/shard_map/ppermute | solution.py:492
  13.3 9.8 %collective-permute-start = (bf16[144,512]{1,0:T(8,128)(2,1)S(1)}, bf16[144,512]{1,0:T(8,128)(2,1)S(1)}, u32[]{:S(2)}, u32[]{:S(2)}) collective-permute-start(bf16[144,512]{1,0:T(8,128)(2,1)S(1)} %get-tuple-element.44), channel_id=1, source_target_pairs={{0,2},{2,0},{4,6},{6,4},{1,3},{3,1},{5,7},{7,5},{8,10},{10,8},{12,... | collective-permute-start | bytes 442376 | tf_op jit(solution)/shard_map/ppermute | solution.py:492
  15.9 14.0 %collective-permute-start.1 = (bf16[144,512]{1,0:T(8,128)(2,1)S(1)}, bf16[144,512]{1,0:T(8,128)(2,1)S(1)}, u32[]{:S(2)}, u32[]{:S(2)}) collective-permute-start(bf16[144,512]{1,0:T(8,128)(2,1)S(1)} %get-tuple-element.45), channel_id=1, source_target_pairs={{0,4},{2,6},{4,0},{6,2},{1,5},{3,7},{5,1},{7,3},{8,12},{10,14},{12... | collective-permute-start | bytes 442376 | tf_op jit(solution)/shard_map/ppermute | solution.py:492
  18.5 15.9 %collective-permute-start.2 = (bf16[144,512]{1,0:T(8,128)(2,1)S(1)}, bf16[144,512]{1,0:T(8,128)(2,1)S(1)}, u32[]{:S(2)}, u32[]{:S(2)}) collective-permute-start(bf16[144,512]{1,0:T(8,128)(2,1)S(1)} %get-tuple-element.46), channel_id=1, source_target_pairs={{0,6},{2,4},{4,2},{6,0},{1,7},{3,5},{5,3},{7,1},{8,14},{10,12},{12... | collective-permute-start | bytes 442376 | tf_op jit(solution)/shard_map/ppermute | solution.py:492
  29.9 7.6 %collective-permute-start.7 = (bf16[144,512]{1,0:T(8,128)(2,1)S(1)}, bf16[144,512]{1,0:T(8,128)(2,1)S(1)}, u32[]{:S(2)}, u32[]{:S(2)}) collective-permute-start(bf16[144,512]{1,0:T(8,128)(2,1)S(1)} %get-tuple-element.49.refs_4_), channel_id=1, source_target_pairs={{0,2},{2,0},{4,6},{6,4},{1,3},{3,1},{5,7},{7,5},{8,10},{10,8},{12,... | collective-permute-start | bytes 442376 | tf_op jit(solution)/shard_map/ppermute | solution.py:492
  30.0 13.6 %collective-permute-start.8 = (bf16[144,512]{1,0:T(8,128)(2,1)S(1)}, bf16[144,512]{1,0:T(8,128)(2,1)S(1)}, u32[]{:S(2)}, u32[]{:S(2)}) collective-permute-start(bf16[144,512]{1,0:T(8,128)(2,1)S(1)} %get-tuple-element.50.refs_5_), channel_id=1, source_target_pairs={{0,4},{2,6},{4,0},{6,2},{1,5},{3,7},{5,1},{7,3},{8,12},{10,14},{12... | collective-permute-start | bytes 442376 | tf_op jit(solution)/shard_map/ppermute | solution.py:492
  33.0 10.8 %collective-permute-start.13 = (bf16[144,512]{1,0:T(8,128)(2,1)S(1)}, bf16[144,512]{1,0:T(8,128)(2,1)S(1)}, u32[]{:S(2)}, u32[]{:S(2)}) collective-permute-start(bf16[144,512]{1,0:T(8,128)(2,1)S(1)} %get-tuple-element.51.refs_6_), channel_id=1, source_target_pairs={{0,6},{2,4},{4,2},{6,0},{1,7},{3,5},{5,3},{7,1},{8,14},{10,12},{12... | collective-permute-start | bytes 442376 | tf_op jit(solution)/shard_map/ppermute | solution.py:492
  34.4 5.2 %collective-permute-start.4 = (bf16[144,512]{1,0:T(8,128)(2,1)S(1)}, bf16[144,512]{1,0:T(8,128)(2,1)S(1)}, u32[]{:S(2)}, u32[]{:S(2)}) collective-permute-start(bf16[144,512]{1,0:T(8,128)(2,1)S(1)} %get-tuple-element.53), channel_id=1, source_target_pairs={{0,8},{8,0},{16,24},{24,16},{1,9},{9,1},{17,25},{25,17},{2,10},{10... | collective-permute-start | bytes 442376 | tf_op jit(solution)/shard_map/ppermute | solution.py:492
  36.0 5.1 %collective-permute-start.5 = (bf16[144,512]{1,0:T(8,128)(2,1)S(1)}, bf16[144,512]{1,0:T(8,128)(2,1)S(1)}, u32[]{:S(2)}, u32[]{:S(2)}) collective-permute-start(bf16[144,512]{1,0:T(8,128)(2,1)S(1)} %get-tuple-element.54), channel_id=1, source_target_pairs={{0,16},{8,24},{16,0},{24,8},{1,17},{9,25},{17,1},{25,9},{2,18},{10... | collective-permute-start | bytes 442376 | tf_op jit(solution)/shard_map/ppermute | solution.py:492
  37.5 6.1 %collective-permute-start.6 = (bf16[144,512]{1,0:T(8,128)(2,1)S(1)}, bf16[144,512]{1,0:T(8,128)(2,1)S(1)}, u32[]{:S(2)}, u32[]{:S(2)}) collective-permute-start(bf16[144,512]{1,0:T(8,128)(2,1)S(1)} %get-tuple-element.55), channel_id=1, source_target_pairs={{0,24},{8,16},{16,8},{24,0},{1,25},{9,17},{17,9},{25,1},{2,26},{10... | collective-permute-start | bytes 442376 | tf_op jit(solution)/shard_map/ppermute | solution.py:492
  43.7 13.2 %copy-start.3 = (bf16[512,512]{1,0:T(8,128)(2,1)S(1)}, bf16[512,512]{1,0:T(8,128)(2,1)}, u32[]{:S(2)}) copy-start(bf16[512,512]{1,0:T(8,128)(2,1)} %state_ref.3) | copy-start | bytes 1572868
  43.7 13.1 %copy-start.4 = (bf16[512,512]{1,0:T(8,128)(2,1)S(1)}, bf16[512,512]{1,0:T(8,128)(2,1)}, u32[]{:S(2)}) copy-start(bf16[512,512]{1,0:T(8,128)(2,1)} %w_ref.6) | copy-start | bytes 1572868
  43.7 4.3 %collective-permute-start.9 = (bf16[576,512]{1,0:T(8,128)(2,1)S(1)}, bf16[576,512]{1,0:T(8,128)(2,1)S(1)}, u32[]{:S(2)}, u32[]{:S(2)}) collective-permute-start(bf16[576,512]{1,0:T(8,128)(2,1)S(1)} %join.1.own_ref), channel_id=1, source_target_pairs={{0,1},{1,0},{2,3},{3,2},{4,5},{5,4},{6,7},{7,6},{8,9},{9,8},{10,11... | collective-permute-start | bytes 1769480 | tf_op jit(solution)/shard_map/ppermute | solution.py:492
  44.4 8.5 %collective-permute-start.14 = (bf16[144,512]{1,0:T(8,128)(2,1)S(1)}, bf16[144,512]{1,0:T(8,128)(2,1)S(1)}, u32[]{:S(2)}, u32[]{:S(2)}) collective-permute-start(bf16[144,512]{1,0:T(8,128)(2,1)S(1)} %get-tuple-element.59), channel_id=1, source_target_pairs={{0,8},{8,0},{16,24},{24,16},{1,9},{9,1},{17,25},{25,17},{2,10},{10... | collective-permute-start | bytes 442376 | tf_op jit(solution)/shard_map/ppermute | solution.py:492
  45.6 9.1 %collective-permute-start.15 = (bf16[144,512]{1,0:T(8,128)(2,1)S(1)}, bf16[144,512]{1,0:T(8,128)(2,1)S(1)}, u32[]{:S(2)}, u32[]{:S(2)}) collective-permute-start(bf16[144,512]{1,0:T(8,128)(2,1)S(1)} %get-tuple-element.60), channel_id=1, source_target_pairs={{0,16},{8,24},{16,0},{24,8},{1,17},{9,25},{17,1},{25,9},{2,18},{10... | collective-permute-start | bytes 442376 | tf_op jit(solution)/shard_map/ppermute | solution.py:492
  47.1 7.6 %collective-permute-start.16 = (bf16[144,512]{1,0:T(8,128)(2,1)S(1)}, bf16[144,512]{1,0:T(8,128)(2,1)S(1)}, u32[]{:S(2)}, u32[]{:S(2)}) collective-permute-start(bf16[144,512]{1,0:T(8,128)(2,1)S(1)} %get-tuple-element.61), channel_id=1, source_target_pairs={{0,24},{8,16},{16,8},{24,0},{1,25},{9,17},{17,9},{25,1},{2,26},{10... | collective-permute-start | bytes 442376 | tf_op jit(solution)/shard_map/ppermute | solution.py:492
  49.8 7.0 %collective-permute-start.10 = (bf16[128,512]{1,0:T(8,128)(2,1)S(1)}, bf16[128,512]{1,0:T(8,128)(2,1)S(1)}, u32[]{:S(2)}, u32[]{:S(2)}) collective-permute-start(bf16[128,512]{1,0:T(8,128)(2,1)S(1)} %bitcast.19), channel_id=1, source_target_pairs={{0,2},{2,0},{4,6},{6,4},{1,3},{3,1},{5,7},{7,5},{8,10},{10,8},{12,... | collective-permute-start | bytes 393224 | tf_op jit(solution)/shard_map/ppermute | solution.py:492
  51.5 11.5 %collective-permute-start.11 = (bf16[128,512]{1,0:T(8,128)(2,1)S(1)}, bf16[128,512]{1,0:T(8,128)(2,1)S(1)}, u32[]{:S(2)}, u32[]{:S(2)}) collective-permute-start(bf16[128,512]{1,0:T(8,128)(2,1)S(1)} %bitcast.18), channel_id=1, source_target_pairs={{0,4},{2,6},{4,0},{6,2},{1,5},{3,7},{5,1},{7,3},{8,12},{10,14},{12... | collective-permute-start | bytes 393224 | tf_op jit(solution)/shard_map/ppermute | solution.py:492
  52.9 10.1 %collective-permute-start.12 = (bf16[128,512]{1,0:T(8,128)(2,1)S(1)}, bf16[128,512]{1,0:T(8,128)(2,1)S(1)}, u32[]{:S(2)}, u32[]{:S(2)}) collective-permute-start(bf16[128,512]{1,0:T(8,128)(2,1)S(1)} %bitcast.17), channel_id=1, source_target_pairs={{0,6},{2,4},{4,2},{6,0},{1,7},{3,5},{5,3},{7,1},{8,14},{10,12},{12... | collective-permute-start | bytes 393224 | tf_op jit(solution)/shard_map/ppermute | solution.py:492
  57.3 18.3 %copy-start = (bf16[1024,512]{1,0:T(8,128)(2,1)S(1)}, bf16[1024,512]{1,0:T(8,128)(2,1)}, u32[]{:S(2)}) copy-start(bf16[1024,512]{1,0:T(8,128)(2,1)} %w_ref.9) | copy-start | bytes 3145732
  57.3 6.7 %collective-permute-start.19 = (bf16[128,512]{1,0:T(8,128)(2,1)S(1)}, bf16[128,512]{1,0:T(8,128)(2,1)S(1)}, u32[]{:S(2)}, u32[]{:S(2)}) collective-permute-start(bf16[128,512]{1,0:T(8,128)(2,1)S(1)} %update_prod.1.rest_0_.refs_0_), channel_id=1, source_target_pairs={{0,24},{8,16},{16,8},{24,0},{1,25},{9,17},{17,9},{25,1},{2,26},{10... | collective-permute-start | bytes 393224 | tf_op jit(solution)/shard_map/ppermute | solution.py:492
  58.9 6.0 %collective-permute-start.18 = (bf16[128,512]{1,0:T(8,128)(2,1)S(1)}, bf16[128,512]{1,0:T(8,128)(2,1)S(1)}, u32[]{:S(2)}, u32[]{:S(2)}) collective-permute-start(bf16[128,512]{1,0:T(8,128)(2,1)S(1)} %update_prod.1.rest_0_.refs_0_), channel_id=1, source_target_pairs={{0,16},{8,24},{16,0},{24,8},{1,17},{9,25},{17,1},{25,9},{2,18},{10... | collective-permute-start | bytes 393224 | tf_op jit(solution)/shard_map/ppermute | solution.py:492
  59.4 5.5 %collective-permute-start.17 = (bf16[128,512]{1,0:T(8,128)(2,1)S(1)}, bf16[128,512]{1,0:T(8,128)(2,1)S(1)}, u32[]{:S(2)}, u32[]{:S(2)}) collective-permute-start(bf16[128,512]{1,0:T(8,128)(2,1)S(1)} %update_prod.1.rest_0_.refs_0_), channel_id=1, source_target_pairs={{0,8},{8,0},{16,24},{24,16},{1,9},{9,1},{17,25},{25,17},{2,10},{10... | collective-permute-start | bytes 393224 | tf_op jit(solution)/shard_map/ppermute | solution.py:492
  65.6 6.6 %collective-permute-start.20 = (bf16[128,512]{1,0:T(8,128)(2,1)S(1)}, bf16[128,512]{1,0:T(8,128)(2,1)S(1)}, u32[]{:S(2)}, u32[]{:S(2)}) collective-permute-start(bf16[128,512]{1,0:T(8,128)(2,1)S(1)} %get-tuple-element.64), channel_id=1, source_target_pairs={{0,8},{8,0},{16,24},{24,16},{1,9},{9,1},{17,25},{25,17},{2,10},{10... | collective-permute-start | bytes 393224 | tf_op jit(solution)/shard_map/ppermute | solution.py:492
  66.5 9.0 %collective-permute-start.21 = (bf16[128,512]{1,0:T(8,128)(2,1)S(1)}, bf16[128,512]{1,0:T(8,128)(2,1)S(1)}, u32[]{:S(2)}, u32[]{:S(2)}) collective-permute-start(bf16[128,512]{1,0:T(8,128)(2,1)S(1)} %get-tuple-element.65), channel_id=1, source_target_pairs={{0,16},{8,24},{16,0},{24,8},{1,17},{9,25},{17,1},{25,9},{2,18},{10... | collective-permute-start | bytes 393224 | tf_op jit(solution)/shard_map/ppermute | solution.py:492
  67.7 7.8 %collective-permute-start.22 = (bf16[128,512]{1,0:T(8,128)(2,1)S(1)}, bf16[128,512]{1,0:T(8,128)(2,1)S(1)}, u32[]{:S(2)}, u32[]{:S(2)}) collective-permute-start(bf16[128,512]{1,0:T(8,128)(2,1)S(1)} %get-tuple-element.66), channel_id=1, source_target_pairs={{0,24},{8,16},{16,8},{24,0},{1,25},{9,17},{17,9},{25,1},{2,26},{10... | collective-permute-start | bytes 393224 | tf_op jit(solution)/shard_map/ppermute | solution.py:492
  69.1 7.2 %collective-permute-start.23 = (bf16[128,512]{1,0:T(8,128)(2,1)S(1)}, bf16[128,512]{1,0:T(8,128)(2,1)S(1)}, u32[]{:S(2)}, u32[]{:S(2)}) collective-permute-start(bf16[128,512]{1,0:T(8,128)(2,1)S(1)} %get-tuple-element.67), channel_id=1, source_target_pairs={{0,2},{2,0},{4,6},{6,4},{1,3},{3,1},{5,7},{7,5},{8,10},{10,8},{12,... | collective-permute-start | bytes 393224 | tf_op jit(solution)/shard_map/ppermute | solution.py:492
  70.4 10.0 %collective-permute-start.24 = (bf16[128,512]{1,0:T(8,128)(2,1)S(1)}, bf16[128,512]{1,0:T(8,128)(2,1)S(1)}, u32[]{:S(2)}, u32[]{:S(2)}) collective-permute-start(bf16[128,512]{1,0:T(8,128)(2,1)S(1)} %get-tuple-element.68), channel_id=1, source_target_pairs={{0,4},{2,6},{4,0},{6,2},{1,5},{3,7},{5,1},{7,3},{8,12},{10,14},{12... | collective-permute-start | bytes 393224 | tf_op jit(solution)/shard_map/ppermute | solution.py:492
  72.2 8.3 %collective-permute-start.25 = (bf16[128,512]{1,0:T(8,128)(2,1)S(1)}, bf16[128,512]{1,0:T(8,128)(2,1)S(1)}, u32[]{:S(2)}, u32[]{:S(2)}) collective-permute-start(bf16[128,512]{1,0:T(8,128)(2,1)S(1)} %get-tuple-element.69), channel_id=1, source_target_pairs={{0,6},{2,4},{4,2},{6,0},{1,7},{3,5},{5,3},{7,1},{8,14},{10,12},{12... | collective-permute-start | bytes 393224 | tf_op jit(solution)/shard_map/ppermute | solution.py:492
  75.6 4.9 %copy-start.5 = (bf16[512,512]{1,0:T(8,128)(2,1)S(1)}, bf16[512,512]{1,0:T(8,128)(2,1)}, u32[]{:S(2)}) copy-start(bf16[512,512]{1,0:T(8,128)(2,1)} %get-tuple-element.38.refs_5_) | copy-start | bytes 1572868
  80.5 1.6 %collective-permute-start.26 = (bf16[256,512]{1,0:T(8,128)(2,1)S(1)}, bf16[256,512]{1,0:T(8,128)(2,1)S(1)}, u32[]{:S(2)}, u32[]{:S(2)}) collective-permute-start(bf16[256,512]{1,0:T(8,128)(2,1)S(1)} %get-tuple-element.73), channel_id=1, source_target_pairs={{0,1},{1,0},{2,3},{3,2},{4,5},{5,4},{6,7},{7,6},{8,9},{9,8},{10,11... | collective-permute-start | bytes 786440 | tf_op jit(solution)/shard_map/ppermute | solution.py:492

commit v7 on v6

--- a/solution.py
+++ b/solution.py
@@ -117,9 +117,9 @@
 
 def encode_kernel(sizes, rows, *refs):
     x_hbm, w_qkv_hbm, w_out_hbm, w_msg_hbm, index_ref, h_ref, order_ref = refs[:7]
-    x_ref, w_qkv, w_out, w_msg, sem = refs[-5:]
+    x_ref, w_qkv, w_out, w_msg, cust_rows, sem = refs[-6:]
     nr, nz, nc = sizes
-    cust_refs, prod_refs = refs[7:7 + nz], refs[7 + nz:-5]
+    cust_refs, prod_refs = refs[7:7 + nz], refs[7 + nz:-6]
     chunks = x_hbm.shape[0] // rows
     copy = pltpu.make_async_copy
     x_copies = [
@@ -176,14 +176,21 @@
     ]
     last.wait()
     message = dot(h_ref[...], w_msg[...]).astype(BF)
+    cust_rows[...] = message[:, :H]
     for sent, made, refs, which in (
         (cust_sent, cust_ids, cust_refs, 0),
         (prod_sent, prod_ids, prod_refs, 1),
     ):
         size = count // len(refs)
         for s, ref in enumerate(refs):
-            pick = one_hot(size, s * size, sent)
-            ref[:size, :] = dot(pick, message[:, which * H:(which + 1) * H]).astype(BF)
+            if which == 0 and cs % 16 == 0:
+                z = lax.axis_index("cust") ^ s
+                for t in range(nr):
+                    first = pl.multiple_of(((lax.axis_index("rev") ^ t) * nz + z) * cs, cs)
+                    ref[t * cs:(t + 1) * cs, :] = cust_rows[pl.ds(first, cs), :]
+            else:
+                pick = one_hot(size, s * size, sent)
+                ref[:size, :] = dot(pick, message[:, which * H:(which + 1) * H]).astype(BF)
             ref[size:, :] = jnp.zeros((ref.shape[0] - size, H), BF)
             ref[size:, :made[s].shape[1]] = made[s].astype(BF)
 
@@ -205,6 +212,7 @@
         + [cust_block] * nz
         + [prod_block] * nc,
         scratch_shapes=[pltpu.VMEM(a.shape, BF) for a in (review_cols, w_qkv, w_out, w_msg)]
+        + [pltpu.VMEM((count, H), BF)]
         + [pltpu.SemaphoreType.DMA((count // rows + 5,))],
         compiler_params=ENCODE_PARAMS,
         name="encode",
@@ -556,10 +564,10 @@
     cust_back = regroup(cs, nr, cust_got, made[:1])
     cust_back = [swap(cust_back[t], "rev", t) for t in range(nr)]
     part = finish_part((0, 0), cust_pick, review_h, w_back, cust_back, F32, "finish_cust")
-    own_replies, peer_replies = halve(replies, [part, new_prod])
-    peer_replies = swap(peer_replies, "prod", 1)
-    part = finish_part((0, H), prod_pick, part, w_back, [own_replies], F32, "finish_own")
-    review_out = finish_part((rows // nc, H), prod_pick, part, w_back, [peer_replies], BF, "finish")
+    early, late = halve(replies[:nz // 2], []), halve(replies[nz // 2:], [part, new_prod])
+    peers = [swap(early[1], "prod", 1), swap(late[1], "prod", 1)]
+    part = finish_part((0, H), prod_pick, part, w_back, [early[0], late[0]], F32, "finish_own")
+    review_out = finish_part((rows // nc, H), prod_pick, part, w_back, peers, BF, "finish")
     return (review_out, new_cust, new_prod)
 
 

time: 83.8 us -> 83.2 us (level)
    ppermute x27 -> x28, starting transfers between devices: 34.1 us -> 33.7 us  [swap(): lax.ppermute(value, axis, [(i, i ^ by) for i in range(lax.axis_size(axis))])]
    ppermute x27 -> x28, waiting for transfers between devices: 28.5 us -> 28.6 us  [swap(): lax.ppermute(value, axis, [(i, i ^ by) for i in range(lax.axis_size(axis))])]
  transfers between devices with their start and end apart: 27 -> 28, of which waited for: 12 -> 12; matrix products, arithmetic and copies ran while one was open for 0% -> 0% of each run, Pallas kernels for 7% -> 7%
where the time goes in v7:
time: 83.2 us; the launch traced here: 83.1 us
  starting transfers between devices  33.7 us (41%)
  waiting for transfers between devices  28.6 us (34%)
  Pallas kernels  19 us (23%)
  between operations  0.91 us (1%)
    ppermute x28, starting transfers between devices, swap(): lax.ppermute(value, axis, [(i, i ^ by) for i in range(lax.axis_size(axis))])  33.7 us
    ppermute x28, waiting for transfers between devices, swap(): lax.ppermute(value, axis, [(i, i ^ by) for i in range(lax.axis_size(axis))])  28.6 us
    pallas_call x1, Pallas kernels, encode(): pl.pallas_call(functools.partial(encode_kernel, sizes, rows), in_specs=[H...  11.1 us
    pallas_call x3, Pallas kernels, finish_part(): pl.pallas_call(functools.partial(finish_part_kernel, start), in_specs=[VM...  2.75 us
    pallas_call x1, Pallas kernels, update_cust(): pl.pallas_call(functools.partial(cust_kernel, groups), in_specs=[VMEM] *...  1.75 us
  transfers between devices with their start and end apart: 28, of which 12 were waited for; matrix products, arithmetic and copies ran while one was open for 0% of the time, Pallas kernels for 7%

profile of v7, /device:TPU:0, one launch (start us, length us, event | category | flops | bytes accessed | tf_op | source)
XLA Modules:
  0.0 83.1 jit_solution(8502708148616482700)
XLA Ops:
  0.6 0.7 pad_add_fusion.refs_4_
  1.4 11.1 %encode.1 = (bf16[512,512]{1,0:T(8,128)(2,1)S(1)}, s32[2,512]{1,0:T(2,128)S(1)}, bf16[144,512]{1,0:T(8,128)(2,1)S(1)}, bf16[144,512]{1,0:T(8,128)(2,1)S(1)}, bf1...) custom-call(bf16[512,2048]{1,0:T(8,128)(2,1)} %refs_0_.1, ...), custom_call_target="tpu_custom_call" | custom-call | tf_op jit(solution)/shard_map/encode/pallas_call | solution.py:204
  12.5 0.0 copy-start.1
  12.5 0.0 copy-start.2
  12.5 0.5 collective-permute-start.3
  13.1 2.7 %collective-permute-start = (bf16[144,512]{1,0:T(8,128)(2,1)S(1)}, bf16[144,512]{1,0:T(8,128)(2,1)S(1)}, u32[]{:S(2)}, u32[]{:S(2)}) collective-permute-start(bf16[144,512]{1,0:T(8,128)(2,1)S(1)} %get-tuple-element.46), channel_id=1, source_target_pairs={{0,2},{2,0},{4,6},{6,4},{1,3},{3,1},{5,7},{7,5},{8,10},{10,8},{12,... | collective-permute-start | bytes 442376 | tf_op jit(solution)/shard_map/ppermute | solution.py:500
  15.7 2.6 %collective-permute-start.1 = (bf16[144,512]{1,0:T(8,128)(2,1)S(1)}, bf16[144,512]{1,0:T(8,128)(2,1)S(1)}, u32[]{:S(2)}, u32[]{:S(2)}) collective-permute-start(bf16[144,512]{1,0:T(8,128)(2,1)S(1)} %get-tuple-element.47), channel_id=1, source_target_pairs={{0,4},{2,6},{4,0},{6,2},{1,5},{3,7},{5,1},{7,3},{8,12},{10,14},{12... | collective-permute-start | bytes 442376 | tf_op jit(solution)/shard_map/ppermute | solution.py:500
  18.3 4.5 %collective-permute-done.refs_0_.refs_1_ = bf16[144,512]{1,0:T(8,128)(2,1)S(1)} collective-permute-done((bf16[144,512]{1,0:T(8,128)(2,1)S(1)}, bf16[144,512]{1,0:T(8,128)(2,1)S(1)}, u32[]{:S(2)}, u32[]{:S(2)}) %collective-permute-start) | collective-permute-done | bytes 147488 | tf_op jit(solution)/shard_map/ppermute | solution.py:500
  22.8 6.9 %collective-permute-done.1.refs_1_.refs_2_ = bf16[144,512]{1,0:T(8,128)(2,1)S(1)} collective-permute-done((bf16[144,512]{1,0:T(8,128)(2,1)S(1)}, bf16[144,512]{1,0:T(8,128)(2,1)S(1)}, u32[]{:S(2)}, u32[]{:S(2)}) %collective-permute-start.1) | collective-permute-done | bytes 147488 | tf_op jit(solution)/shard_map/ppermute | solution.py:500
  29.7 0.0 collective-permute-done.3.peer_ref
  29.7 0.1 collective-permute-start.7
  29.8 3.0 %collective-permute-start.8 = (bf16[144,512]{1,0:T(8,128)(2,1)S(1)}, bf16[144,512]{1,0:T(8,128)(2,1)S(1)}, u32[]{:S(2)}, u32[]{:S(2)}) collective-permute-start(bf16[144,512]{1,0:T(8,128)(2,1)S(1)} %get-tuple-element.52.refs_5_), channel_id=1, source_target_pairs={{0,4},{2,6},{4,0},{6,2},{1,5},{3,7},{5,1},{7,3},{8,12},{10,14},{12... | collective-permute-start | bytes 442376 | tf_op jit(solution)/shard_map/ppermute | solution.py:500
  32.8 1.4 %collective-permute-start.13 = (bf16[144,512]{1,0:T(8,128)(2,1)S(1)}, bf16[144,512]{1,0:T(8,128)(2,1)S(1)}, u32[]{:S(2)}, u32[]{:S(2)}) collective-permute-start(bf16[144,512]{1,0:T(8,128)(2,1)S(1)} %get-tuple-element.53.refs_6_), channel_id=1, source_target_pairs={{0,6},{2,4},{4,2},{6,0},{1,7},{3,5},{5,3},{7,1},{8,14},{10,12},{12... | collective-permute-start | bytes 442376 | tf_op jit(solution)/shard_map/ppermute | solution.py:500
  34.2 0.0 collective-permute-done.2.refs_3_
  34.2 1.6 %collective-permute-start.4 = (bf16[144,512]{1,0:T(8,128)(2,1)S(1)}, bf16[144,512]{1,0:T(8,128)(2,1)S(1)}, u32[]{:S(2)}, u32[]{:S(2)}) collective-permute-start(bf16[144,512]{1,0:T(8,128)(2,1)S(1)} %get-tuple-element.55), channel_id=1, source_target_pairs={{0,8},{8,0},{16,24},{24,16},{1,9},{9,1},{17,25},{25,17},{2,10},{10... | collective-permute-start | bytes 442376 | tf_op jit(solution)/shard_map/ppermute | solution.py:500
  35.8 1.5 %collective-permute-start.5 = (bf16[144,512]{1,0:T(8,128)(2,1)S(1)}, bf16[144,512]{1,0:T(8,128)(2,1)S(1)}, u32[]{:S(2)}, u32[]{:S(2)}) collective-permute-start(bf16[144,512]{1,0:T(8,128)(2,1)S(1)} %get-tuple-element.56), channel_id=1, source_target_pairs={{0,16},{8,24},{16,0},{24,8},{1,17},{9,25},{17,1},{25,9},{2,18},{10... | collective-permute-start | bytes 442376 | tf_op jit(solution)/shard_map/ppermute | solution.py:500
  37.3 0.0 collective-permute-done.7.refs_4_.refs_1_
  37.3 0.6 collective-permute-start.6
  37.9 1.5 %collective-permute-done.4.refs_1_ = bf16[144,512]{1,0:T(8,128)(2,1)S(1)} collective-permute-done((bf16[144,512]{1,0:T(8,128)(2,1)S(1)}, bf16[144,512]{1,0:T(8,128)(2,1)S(1)}, u32[]{:S(2)}, u32[]{:S(2)}) %collective-permute-start.4) | collective-permute-done | bytes 147488 | tf_op jit(solution)/shard_map/ppermute | solution.py:500
  39.4 1.5 %collective-permute-done.5.refs_2_ = bf16[144,512]{1,0:T(8,128)(2,1)S(1)} collective-permute-done((bf16[144,512]{1,0:T(8,128)(2,1)S(1)}, bf16[144,512]{1,0:T(8,128)(2,1)S(1)}, u32[]{:S(2)}, u32[]{:S(2)}) %collective-permute-start.5) | collective-permute-done | bytes 147488 | tf_op jit(solution)/shard_map/ppermute | solution.py:500
  40.9 2.5 %collective-permute-done.6.refs_3_ = bf16[144,512]{1,0:T(8,128)(2,1)S(1)} collective-permute-done((bf16[144,512]{1,0:T(8,128)(2,1)S(1)}, bf16[144,512]{1,0:T(8,128)(2,1)S(1)}, u32[]{:S(2)}, u32[]{:S(2)}) %collective-permute-start.6) | collective-permute-done | bytes 147488 | tf_op jit(solution)/shard_map/ppermute | solution.py:500
  43.4 0.0 collective-permute-done.8.refs_5_.refs_2_
  43.5 0.0 copy-start.4
  43.5 0.0 copy-start.5
  43.5 0.1 collective-permute-start.9
  43.6 0.0 collective-permute-done.13.refs_3_
  43.6 0.6 sum_prod.1
  44.2 1.2 %collective-permute-start.14 = (bf16[144,512]{1,0:T(8,128)(2,1)S(1)}, bf16[144,512]{1,0:T(8,128)(2,1)S(1)}, u32[]{:S(2)}, u32[]{:S(2)}) collective-permute-start(bf16[144,512]{1,0:T(8,128)(2,1)S(1)} %get-tuple-element.61), channel_id=1, source_target_pairs={{0,8},{8,0},{16,24},{24,16},{1,9},{9,1},{17,25},{25,17},{2,10},{10... | collective-permute-start | bytes 442376 | tf_op jit(solution)/shard_map/ppermute | solution.py:500
  45.4 1.5 %collective-permute-start.15 = (bf16[144,512]{1,0:T(8,128)(2,1)S(1)}, bf16[144,512]{1,0:T(8,128)(2,1)S(1)}, u32[]{:S(2)}, u32[]{:S(2)}) collective-permute-start(bf16[144,512]{1,0:T(8,128)(2,1)S(1)} %get-tuple-element.62), channel_id=1, source_target_pairs={{0,16},{8,24},{16,0},{24,8},{1,17},{9,25},{17,1},{25,9},{2,18},{10... | collective-permute-start | bytes 442376 | tf_op jit(solution)/shard_map/ppermute | solution.py:500
  46.9 0.9 %collective-permute-start.16 = (bf16[144,512]{1,0:T(8,128)(2,1)S(1)}, bf16[144,512]{1,0:T(8,128)(2,1)S(1)}, u32[]{:S(2)}, u32[]{:S(2)}) collective-permute-start(bf16[144,512]{1,0:T(8,128)(2,1)S(1)} %get-tuple-element.63), channel_id=1, source_target_pairs={{0,24},{8,16},{16,8},{24,0},{1,25},{9,17},{17,9},{25,1},{2,26},{10... | collective-permute-start | bytes 442376 | tf_op jit(solution)/shard_map/ppermute | solution.py:500
  47.8 1.7 %update_cust.1 = (bf16[512,512]{1,0:T(8,128)(2,1)S(1)}, bf16[512,512]{1,0:T(8,128)(2,1)S(1)}) custom-call(bf16[576,512]{1,0:T(8,128)(2,1)S(1)} %join.1.own_ref, bf16[576,512]{1,0:T(8,128)(2,1)S(1)} %collective-permute-done.9.peer_ref, bf16[512,512]{1,0:T(8,128)(2,1)S(1)} %copy-done.1, bf16[512,512]{1,0:T(8,128)(2,1)S(1)} %copy-done.2), custom_call_target="tpu_custom_call" | custom-call | tf_op jit(solution)/shard_map/update_cust/pallas_call | solution.py:328
  49.6 1.7 %collective-permute-start.10 = (bf16[128,512]{1,0:T(8,128)(2,1)S(1)}, bf16[128,512]{1,0:T(8,128)(2,1)S(1)}, u32[]{:S(2)}, u32[]{:S(2)}) collective-permute-start(bf16[128,512]{1,0:T(8,128)(2,1)S(1)} %bitcast.19), channel_id=1, source_target_pairs={{0,2},{2,0},{4,6},{6,4},{1,3},{3,1},{5,7},{7,5},{8,10},{10,8},{12,... | collective-permute-start | bytes 393224 | tf_op jit(solution)/shard_map/ppermute | solution.py:500
  51.3 1.4 %collective-permute-start.11 = (bf16[128,512]{1,0:T(8,128)(2,1)S(1)}, bf16[128,512]{1,0:T(8,128)(2,1)S(1)}, u32[]{:S(2)}, u32[]{:S(2)}) collective-permute-start(bf16[128,512]{1,0:T(8,128)(2,1)S(1)} %bitcast.18), channel_id=1, source_target_pairs={{0,4},{2,6},{4,0},{6,2},{1,5},{3,7},{5,1},{7,3},{8,12},{10,14},{12... | collective-permute-start | bytes 393224 | tf_op jit(solution)/shard_map/ppermute | solution.py:500
  52.7 0.0 collective-permute-done.14.rest_1_
  52.7 1.3 %collective-permute-start.12 = (bf16[128,512]{1,0:T(8,128)(2,1)S(1)}, bf16[128,512]{1,0:T(8,128)(2,1)S(1)}, u32[]{:S(2)}, u32[]{:S(2)}) collective-permute-start(bf16[128,512]{1,0:T(8,128)(2,1)S(1)} %bitcast.17), channel_id=1, source_target_pairs={{0,6},{2,4},{4,2},{6,0},{1,7},{3,5},{5,3},{7,1},{8,14},{10,12},{12... | collective-permute-start | bytes 393224 | tf_op jit(solution)/shard_map/ppermute | solution.py:500
  54.1 0.5 collective-permute-done.15.rest_2_
  54.5 2.2 %collective-permute-done.10.rest_4_.refs_1_ = bf16[128,512]{1,0:T(8,128)(2,1)S(1)} collective-permute-done((bf16[128,512]{1,0:T(8,128)(2,1)S(1)}, bf16[128,512]{1,0:T(8,128)(2,1)S(1)}, u32[]{:S(2)}, u32[]{:S(2)}) %collective-permute-start.10) | collective-permute-done | bytes 131104 | tf_op jit(solution)/shard_map/ppermute | solution.py:500
  56.7 0.4 update_prod.1.rest_0_.refs_0_
  57.1 0.0 copy-start
  57.2 1.5 %collective-permute-start.19 = (bf16[128,512]{1,0:T(8,128)(2,1)S(1)}, bf16[128,512]{1,0:T(8,128)(2,1)S(1)}, u32[]{:S(2)}, u32[]{:S(2)}) collective-permute-start(bf16[128,512]{1,0:T(8,128)(2,1)S(1)} %update_prod.1.rest_0_.refs_0_), channel_id=1, source_target_pairs={{0,24},{8,16},{16,8},{24,0},{1,25},{9,17},{17,9},{25,1},{2,26},{10... | collective-permute-start | bytes 393224 | tf_op jit(solution)/shard_map/ppermute | solution.py:500
  58.7 0.5 collective-permute-start.18
  59.2 1.5 %collective-permute-start.17 = (bf16[128,512]{1,0:T(8,128)(2,1)S(1)}, bf16[128,512]{1,0:T(8,128)(2,1)S(1)}, u32[]{:S(2)}, u32[]{:S(2)}) collective-permute-start(bf16[128,512]{1,0:T(8,128)(2,1)S(1)} %update_prod.1.rest_0_.refs_0_), channel_id=1, source_target_pairs={{0,8},{8,0},{16,24},{24,16},{1,9},{9,1},{17,25},{25,17},{2,10},{10... | collective-permute-start | bytes 393224 | tf_op jit(solution)/shard_map/ppermute | solution.py:500
  60.7 0.2 turned_picks.3.pick_ref
  60.9 1.9 %collective-permute-done.11.rest_4_.refs_2_ = bf16[128,512]{1,0:T(8,128)(2,1)S(1)} collective-permute-done((bf16[128,512]{1,0:T(8,128)(2,1)S(1)}, bf16[128,512]{1,0:T(8,128)(2,1)S(1)}, u32[]{:S(2)}, u32[]{:S(2)}) %collective-permute-start.11) | collective-permute-done | bytes 131104 | tf_op jit(solution)/shard_map/ppermute | solution.py:500
  62.8 0.0 collective-permute-done.12.rest_5_.refs_3_
  62.8 0.9 %collective-permute-done.19.rest_3_.refs_3_ = bf16[128,512]{1,0:T(8,128)(2,1)S(1)} collective-permute-done((bf16[128,512]{1,0:T(8,128)(2,1)S(1)}, bf16[128,512]{1,0:T(8,128)(2,1)S(1)}, u32[]{:S(2)}, u32[]{:S(2)}) %collective-permute-start.19) | collective-permute-done | bytes 131104 | tf_op jit(solution)/shard_map/ppermute | solution.py:500
  63.7 1.0 %collective-permute-done.18.rest_2_.refs_2_ = bf16[128,512]{1,0:T(8,128)(2,1)S(1)} collective-permute-done((bf16[128,512]{1,0:T(8,128)(2,1)S(1)}, bf16[128,512]{1,0:T(8,128)(2,1)S(1)}, u32[]{:S(2)}, u32[]{:S(2)}) %collective-permute-start.18) | collective-permute-done | bytes 131104 | tf_op jit(solution)/shard_map/ppermute | solution.py:500
  64.8 0.5 reply_prod.1
  65.3 1.3 %collective-permute-start.23 = (bf16[128,512]{1,0:T(8,128)(2,1)S(1)}, bf16[128,512]{1,0:T(8,128)(2,1)S(1)}, u32[]{:S(2)}, u32[]{:S(2)}) collective-permute-start(bf16[128,512]{1,0:T(8,128)(2,1)S(1)} %get-tuple-element.69), channel_id=1, source_target_pairs={{0,2},{2,0},{4,6},{6,4},{1,3},{3,1},{5,7},{7,5},{8,10},{10,8},{12,... | collective-permute-start | bytes 393224 | tf_op jit(solution)/shard_map/ppermute | solution.py:500
  66.6 1.0 %collective-permute-start.20 = (bf16[128,512]{1,0:T(8,128)(2,1)S(1)}, bf16[128,512]{1,0:T(8,128)(2,1)S(1)}, u32[]{:S(2)}, u32[]{:S(2)}) collective-permute-start(bf16[128,512]{1,0:T(8,128)(2,1)S(1)} %get-tuple-element.66), channel_id=1, source_target_pairs={{0,8},{8,0},{16,24},{24,16},{1,9},{9,1},{17,25},{25,17},{2,10},{10... | collective-permute-start | bytes 393224 | tf_op jit(solution)/shard_map/ppermute | solution.py:500
  67.6 1.2 %collective-permute-start.21 = (bf16[128,512]{1,0:T(8,128)(2,1)S(1)}, bf16[128,512]{1,0:T(8,128)(2,1)S(1)}, u32[]{:S(2)}, u32[]{:S(2)}) collective-permute-start(bf16[128,512]{1,0:T(8,128)(2,1)S(1)} %get-tuple-element.67), channel_id=1, source_target_pairs={{0,16},{8,24},{16,0},{24,8},{1,17},{9,25},{17,1},{25,9},{2,18},{10... | collective-permute-start | bytes 393224 | tf_op jit(solution)/shard_map/ppermute | solution.py:500
  68.9 1.3 %collective-permute-start.22 = (bf16[128,512]{1,0:T(8,128)(2,1)S(1)}, bf16[128,512]{1,0:T(8,128)(2,1)S(1)}, u32[]{:S(2)}, u32[]{:S(2)}) collective-permute-start(bf16[128,512]{1,0:T(8,128)(2,1)S(1)} %get-tuple-element.68), channel_id=1, source_target_pairs={{0,24},{8,16},{16,8},{24,0},{1,25},{9,17},{17,9},{25,1},{2,26},{10... | collective-permute-start | bytes 393224 | tf_op jit(solution)/shard_map/ppermute | solution.py:500
  70.2 1.8 %collective-permute-start.24 = (bf16[128,512]{1,0:T(8,128)(2,1)S(1)}, bf16[128,512]{1,0:T(8,128)(2,1)S(1)}, u32[]{:S(2)}, u32[]{:S(2)}) collective-permute-start(bf16[128,512]{1,0:T(8,128)(2,1)S(1)} %get-tuple-element.71), channel_id=1, source_target_pairs={{0,4},{2,6},{4,0},{6,2},{1,5},{3,7},{5,1},{7,3},{8,12},{10,14},{12... | collective-permute-start | bytes 393224 | tf_op jit(solution)/shard_map/ppermute | solution.py:500
  72.0 0.0 collective-permute-done.23.refs_1_
  72.0 1.3 %collective-permute-start.25 = (bf16[128,512]{1,0:T(8,128)(2,1)S(1)}, bf16[128,512]{1,0:T(8,128)(2,1)S(1)}, u32[]{:S(2)}, u32[]{:S(2)}) collective-permute-start(bf16[128,512]{1,0:T(8,128)(2,1)S(1)} %get-tuple-element.72), channel_id=1, source_target_pairs={{0,6},{2,4},{4,2},{6,0},{1,7},{3,5},{5,3},{7,1},{8,14},{10,12},{12... | collective-permute-start | bytes 393224 | tf_op jit(solution)/shard_map/ppermute | solution.py:500
  73.3 0.4 turned_picks.2
  73.7 1.0 %states.1 = (bf16[512,512]{1,0:T(8,128)(2,1)}, bf16[512,512]{1,0:T(8,128)(2,1)}) custom-call(bf16[512,512]{1,0:T(8,128)(2,1)S(1)} %get-tuple-element.73.cust_ref, bf16[128,512]{1,0:T(8,128)(2,1)S(1)} %update_prod.1.rest_0_.refs_0_, bf16[128,512]{1,0:T(8,128)(2,1)S(1)} %collective-permute-done.17.rest_1_.refs_1_, ...), custom_call_target="tpu_custom_call" | custom-call | tf_op jit(solution)/shard_map/states/pallas_call | solution.py:429
  74.8 0.1 collective-permute-start.26
  74.9 0.7 finish_cust.1.refs_2_.sum_ref
  75.6 4.5 %collective-permute-done.24.refs_0_ = bf16[128,512]{1,0:T(8,128)(2,1)S(1)} collective-permute-done((bf16[128,512]{1,0:T(8,128)(2,1)S(1)}, bf16[128,512]{1,0:T(8,128)(2,1)S(1)}, u32[]{:S(2)}, u32[]{:S(2)}) %collective-permute-start.24) | collective-permute-done | bytes 131104 | tf_op jit(solution)/shard_map/ppermute | solution.py:500
  80.2 0.1 collective-permute-start.27
  80.3 0.6 finish_own.1.sum_ref
  80.8 0.7 collective-permute-done.27.rest_1_
  81.6 1.5 %finish.1 = bf16[512,512]{1,0:T(8,128)(2,1)} custom-call(bf16[512,512]{1,0:T(8,128)(2,1)S(1)} %get-tuple-element.42.pick_ref, f32[512,512]{1,0:T(8,128)S(1)} %finish_own.1.sum_ref, bf16[1024,512]{1,0:T(8,128)(2,1)S(1)} %copy-done, bf16[128,512]{1,0:T(8,128)(2,1)S(1)} %collective-permute-done.26.rest_0_, bf16[128,512]{1,0:T(8,128)(2,1)S(1)} %collective-permute-done.27.rest_1_), custom_call_target="tpu_custom_call" | custom-call | tf_op jit(solution)/shard_map/finish/pallas_call | solution.py:468
  (32 shorter events, 0.3 us)
Async XLA Ops:
  12.5 35.3 %copy-start.1 = (bf16[512,512]{1,0:T(8,128)(2,1)S(1)}, bf16[512,512]{1,0:T(8,128)(2,1)}, u32[]{:S(2)}) copy-start(bf16[512,512]{1,0:T(8,128)(2,1)} %state_ref.2) | copy-start | bytes 1572868
  12.5 35.3 %copy-start.2 = (bf16[512,512]{1,0:T(8,128)(2,1)S(1)}, bf16[512,512]{1,0:T(8,128)(2,1)}, u32[]{:S(2)}) copy-start(bf16[512,512]{1,0:T(8,128)(2,1)} %w_ref.5) | copy-start | bytes 1572868
  12.5 17.1 %collective-permute-start.3 = (bf16[320,512]{1,0:T(8,128)(2,1)S(1)}, bf16[320,512]{1,0:T(8,128)(2,1)S(1)}, u32[]{:S(2)}, u32[]{:S(2)}) collective-permute-start(bf16[320,512]{1,0:T(8,128)(2,1)S(1)} %get-tuple-element.50), channel_id=1, source_target_pairs={{0,1},{1,0},{2,3},{3,2},{4,5},{5,4},{6,7},{7,6},{8,9},{9,8},{10,11... | collective-permute-start | bytes 983048 | tf_op jit(solution)/shard_map/ppermute | solution.py:500
  13.1 9.8 %collective-permute-start = (bf16[144,512]{1,0:T(8,128)(2,1)S(1)}, bf16[144,512]{1,0:T(8,128)(2,1)S(1)}, u32[]{:S(2)}, u32[]{:S(2)}) collective-permute-start(bf16[144,512]{1,0:T(8,128)(2,1)S(1)} %get-tuple-element.46), channel_id=1, source_target_pairs={{0,2},{2,0},{4,6},{6,4},{1,3},{3,1},{5,7},{7,5},{8,10},{10,8},{12,... | collective-permute-start | bytes 442376 | tf_op jit(solution)/shard_map/ppermute | solution.py:500
  15.7 14.0 %collective-permute-start.1 = (bf16[144,512]{1,0:T(8,128)(2,1)S(1)}, bf16[144,512]{1,0:T(8,128)(2,1)S(1)}, u32[]{:S(2)}, u32[]{:S(2)}) collective-permute-start(bf16[144,512]{1,0:T(8,128)(2,1)S(1)} %get-tuple-element.47), channel_id=1, source_target_pairs={{0,4},{2,6},{4,0},{6,2},{1,5},{3,7},{5,1},{7,3},{8,12},{10,14},{12... | collective-permute-start | bytes 442376 | tf_op jit(solution)/shard_map/ppermute | solution.py:500
  18.3 15.9 %collective-permute-start.2 = (bf16[144,512]{1,0:T(8,128)(2,1)S(1)}, bf16[144,512]{1,0:T(8,128)(2,1)S(1)}, u32[]{:S(2)}, u32[]{:S(2)}) collective-permute-start(bf16[144,512]{1,0:T(8,128)(2,1)S(1)} %get-tuple-element.48), channel_id=1, source_target_pairs={{0,6},{2,4},{4,2},{6,0},{1,7},{3,5},{5,3},{7,1},{8,14},{10,12},{12... | collective-permute-start | bytes 442376 | tf_op jit(solution)/shard_map/ppermute | solution.py:500
  29.7 7.6 %collective-permute-start.7 = (bf16[144,512]{1,0:T(8,128)(2,1)S(1)}, bf16[144,512]{1,0:T(8,128)(2,1)S(1)}, u32[]{:S(2)}, u32[]{:S(2)}) collective-permute-start(bf16[144,512]{1,0:T(8,128)(2,1)S(1)} %get-tuple-element.51.refs_4_), channel_id=1, source_target_pairs={{0,2},{2,0},{4,6},{6,4},{1,3},{3,1},{5,7},{7,5},{8,10},{10,8},{12,... | collective-permute-start | bytes 442376 | tf_op jit(solution)/shard_map/ppermute | solution.py:500
  29.8 13.6 %collective-permute-start.8 = (bf16[144,512]{1,0:T(8,128)(2,1)S(1)}, bf16[144,512]{1,0:T(8,128)(2,1)S(1)}, u32[]{:S(2)}, u32[]{:S(2)}) collective-permute-start(bf16[144,512]{1,0:T(8,128)(2,1)S(1)} %get-tuple-element.52.refs_5_), channel_id=1, source_target_pairs={{0,4},{2,6},{4,0},{6,2},{1,5},{3,7},{5,1},{7,3},{8,12},{10,14},{12... | collective-permute-start | bytes 442376 | tf_op jit(solution)/shard_map/ppermute | solution.py:500
  32.8 10.8 %collective-permute-start.13 = (bf16[144,512]{1,0:T(8,128)(2,1)S(1)}, bf16[144,512]{1,0:T(8,128)(2,1)S(1)}, u32[]{:S(2)}, u32[]{:S(2)}) collective-permute-start(bf16[144,512]{1,0:T(8,128)(2,1)S(1)} %get-tuple-element.53.refs_6_), channel_id=1, source_target_pairs={{0,6},{2,4},{4,2},{6,0},{1,7},{3,5},{5,3},{7,1},{8,14},{10,12},{12... | collective-permute-start | bytes 442376 | tf_op jit(solution)/shard_map/ppermute | solution.py:500
  34.2 5.2 %collective-permute-start.4 = (bf16[144,512]{1,0:T(8,128)(2,1)S(1)}, bf16[144,512]{1,0:T(8,128)(2,1)S(1)}, u32[]{:S(2)}, u32[]{:S(2)}) collective-permute-start(bf16[144,512]{1,0:T(8,128)(2,1)S(1)} %get-tuple-element.55), channel_id=1, source_target_pairs={{0,8},{8,0},{16,24},{24,16},{1,9},{9,1},{17,25},{25,17},{2,10},{10... | collective-permute-start | bytes 442376 | tf_op jit(solution)/shard_map/ppermute | solution.py:500
  35.8 5.1 %collective-permute-start.5 = (bf16[144,512]{1,0:T(8,128)(2,1)S(1)}, bf16[144,512]{1,0:T(8,128)(2,1)S(1)}, u32[]{:S(2)}, u32[]{:S(2)}) collective-permute-start(bf16[144,512]{1,0:T(8,128)(2,1)S(1)} %get-tuple-element.56), channel_id=1, source_target_pairs={{0,16},{8,24},{16,0},{24,8},{1,17},{9,25},{17,1},{25,9},{2,18},{10... | collective-permute-start | bytes 442376 | tf_op jit(solution)/shard_map/ppermute | solution.py:500
  37.3 6.1 %collective-permute-start.6 = (bf16[144,512]{1,0:T(8,128)(2,1)S(1)}, bf16[144,512]{1,0:T(8,128)(2,1)S(1)}, u32[]{:S(2)}, u32[]{:S(2)}) collective-permute-start(bf16[144,512]{1,0:T(8,128)(2,1)S(1)} %get-tuple-element.57), channel_id=1, source_target_pairs={{0,24},{8,16},{16,8},{24,0},{1,25},{9,17},{17,9},{25,1},{2,26},{10... | collective-permute-start | bytes 442376 | tf_op jit(solution)/shard_map/ppermute | solution.py:500
  43.5 13.2 %copy-start.4 = (bf16[512,512]{1,0:T(8,128)(2,1)S(1)}, bf16[512,512]{1,0:T(8,128)(2,1)}, u32[]{:S(2)}) copy-start(bf16[512,512]{1,0:T(8,128)(2,1)} %state_ref.3) | copy-start | bytes 1572868
  43.5 13.2 %copy-start.5 = (bf16[512,512]{1,0:T(8,128)(2,1)S(1)}, bf16[512,512]{1,0:T(8,128)(2,1)}, u32[]{:S(2)}) copy-start(bf16[512,512]{1,0:T(8,128)(2,1)} %w_ref.6) | copy-start | bytes 1572868
  43.5 4.3 %collective-permute-start.9 = (bf16[576,512]{1,0:T(8,128)(2,1)S(1)}, bf16[576,512]{1,0:T(8,128)(2,1)S(1)}, u32[]{:S(2)}, u32[]{:S(2)}) collective-permute-start(bf16[576,512]{1,0:T(8,128)(2,1)S(1)} %join.1.own_ref), channel_id=1, source_target_pairs={{0,1},{1,0},{2,3},{3,2},{4,5},{5,4},{6,7},{7,6},{8,9},{9,8},{10,11... | collective-permute-start | bytes 1769480 | tf_op jit(solution)/shard_map/ppermute | solution.py:500
  44.2 8.5 %collective-permute-start.14 = (bf16[144,512]{1,0:T(8,128)(2,1)S(1)}, bf16[144,512]{1,0:T(8,128)(2,1)S(1)}, u32[]{:S(2)}, u32[]{:S(2)}) collective-permute-start(bf16[144,512]{1,0:T(8,128)(2,1)S(1)} %get-tuple-element.61), channel_id=1, source_target_pairs={{0,8},{8,0},{16,24},{24,16},{1,9},{9,1},{17,25},{25,17},{2,10},{10... | collective-permute-start | bytes 442376 | tf_op jit(solution)/shard_map/ppermute | solution.py:500
  45.4 9.1 %collective-permute-start.15 = (bf16[144,512]{1,0:T(8,128)(2,1)S(1)}, bf16[144,512]{1,0:T(8,128)(2,1)S(1)}, u32[]{:S(2)}, u32[]{:S(2)}) collective-permute-start(bf16[144,512]{1,0:T(8,128)(2,1)S(1)} %get-tuple-element.62), channel_id=1, source_target_pairs={{0,16},{8,24},{16,0},{24,8},{1,17},{9,25},{17,1},{25,9},{2,18},{10... | collective-permute-start | bytes 442376 | tf_op jit(solution)/shard_map/ppermute | solution.py:500
  46.9 7.6 %collective-permute-start.16 = (bf16[144,512]{1,0:T(8,128)(2,1)S(1)}, bf16[144,512]{1,0:T(8,128)(2,1)S(1)}, u32[]{:S(2)}, u32[]{:S(2)}) collective-permute-start(bf16[144,512]{1,0:T(8,128)(2,1)S(1)} %get-tuple-element.63), channel_id=1, source_target_pairs={{0,24},{8,16},{16,8},{24,0},{1,25},{9,17},{17,9},{25,1},{2,26},{10... | collective-permute-start | bytes 442376 | tf_op jit(solution)/shard_map/ppermute | solution.py:500
  49.6 7.1 %collective-permute-start.10 = (bf16[128,512]{1,0:T(8,128)(2,1)S(1)}, bf16[128,512]{1,0:T(8,128)(2,1)S(1)}, u32[]{:S(2)}, u32[]{:S(2)}) collective-permute-start(bf16[128,512]{1,0:T(8,128)(2,1)S(1)} %bitcast.19), channel_id=1, source_target_pairs={{0,2},{2,0},{4,6},{6,4},{1,3},{3,1},{5,7},{7,5},{8,10},{10,8},{12,... | collective-permute-start | bytes 393224 | tf_op jit(solution)/shard_map/ppermute | solution.py:500
  51.3 11.5 %collective-permute-start.11 = (bf16[128,512]{1,0:T(8,128)(2,1)S(1)}, bf16[128,512]{1,0:T(8,128)(2,1)S(1)}, u32[]{:S(2)}, u32[]{:S(2)}) collective-permute-start(bf16[128,512]{1,0:T(8,128)(2,1)S(1)} %bitcast.18), channel_id=1, source_target_pairs={{0,4},{2,6},{4,0},{6,2},{1,5},{3,7},{5,1},{7,3},{8,12},{10,14},{12... | collective-permute-start | bytes 393224 | tf_op jit(solution)/shard_map/ppermute | solution.py:500
  52.7 10.1 %collective-permute-start.12 = (bf16[128,512]{1,0:T(8,128)(2,1)S(1)}, bf16[128,512]{1,0:T(8,128)(2,1)S(1)}, u32[]{:S(2)}, u32[]{:S(2)}) collective-permute-start(bf16[128,512]{1,0:T(8,128)(2,1)S(1)} %bitcast.17), channel_id=1, source_target_pairs={{0,6},{2,4},{4,2},{6,0},{1,7},{3,5},{5,3},{7,1},{8,14},{10,12},{12... | collective-permute-start | bytes 393224 | tf_op jit(solution)/shard_map/ppermute | solution.py:500
  57.1 17.8 %copy-start = (bf16[1024,512]{1,0:T(8,128)(2,1)S(1)}, bf16[1024,512]{1,0:T(8,128)(2,1)}, u32[]{:S(2)}) copy-start(bf16[1024,512]{1,0:T(8,128)(2,1)} %w_ref.9) | copy-start | bytes 3145732
  57.2 6.6 %collective-permute-start.19 = (bf16[128,512]{1,0:T(8,128)(2,1)S(1)}, bf16[128,512]{1,0:T(8,128)(2,1)S(1)}, u32[]{:S(2)}, u32[]{:S(2)}) collective-permute-start(bf16[128,512]{1,0:T(8,128)(2,1)S(1)} %update_prod.1.rest_0_.refs_0_), channel_id=1, source_target_pairs={{0,24},{8,16},{16,8},{24,0},{1,25},{9,17},{17,9},{25,1},{2,26},{10... | collective-permute-start | bytes 393224 | tf_op jit(solution)/shard_map/ppermute | solution.py:500
  58.7 6.1 %collective-permute-start.18 = (bf16[128,512]{1,0:T(8,128)(2,1)S(1)}, bf16[128,512]{1,0:T(8,128)(2,1)S(1)}, u32[]{:S(2)}, u32[]{:S(2)}) collective-permute-start(bf16[128,512]{1,0:T(8,128)(2,1)S(1)} %update_prod.1.rest_0_.refs_0_), channel_id=1, source_target_pairs={{0,16},{8,24},{16,0},{24,8},{1,17},{9,25},{17,1},{25,9},{2,18},{10... | collective-permute-start | bytes 393224 | tf_op jit(solution)/shard_map/ppermute | solution.py:500
  59.2 5.6 %collective-permute-start.17 = (bf16[128,512]{1,0:T(8,128)(2,1)S(1)}, bf16[128,512]{1,0:T(8,128)(2,1)S(1)}, u32[]{:S(2)}, u32[]{:S(2)}) collective-permute-start(bf16[128,512]{1,0:T(8,128)(2,1)S(1)} %update_prod.1.rest_0_.refs_0_), channel_id=1, source_target_pairs={{0,8},{8,0},{16,24},{24,16},{1,9},{9,1},{17,25},{25,17},{2,10},{10... | collective-permute-start | bytes 393224 | tf_op jit(solution)/shard_map/ppermute | solution.py:500
  65.3 6.7 %collective-permute-start.23 = (bf16[128,512]{1,0:T(8,128)(2,1)S(1)}, bf16[128,512]{1,0:T(8,128)(2,1)S(1)}, u32[]{:S(2)}, u32[]{:S(2)}) collective-permute-start(bf16[128,512]{1,0:T(8,128)(2,1)S(1)} %get-tuple-element.69), channel_id=1, source_target_pairs={{0,2},{2,0},{4,6},{6,4},{1,3},{3,1},{5,7},{7,5},{8,10},{10,8},{12,... | collective-permute-start | bytes 393224 | tf_op jit(solution)/shard_map/ppermute | solution.py:500
  66.6 8.2 %collective-permute-start.20 = (bf16[128,512]{1,0:T(8,128)(2,1)S(1)}, bf16[128,512]{1,0:T(8,128)(2,1)S(1)}, u32[]{:S(2)}, u32[]{:S(2)}) collective-permute-start(bf16[128,512]{1,0:T(8,128)(2,1)S(1)} %get-tuple-element.66), channel_id=1, source_target_pairs={{0,8},{8,0},{16,24},{24,16},{1,9},{9,1},{17,25},{25,17},{2,10},{10... | collective-permute-start | bytes 393224 | tf_op jit(solution)/shard_map/ppermute | solution.py:500
  67.6 7.2 %collective-permute-start.21 = (bf16[128,512]{1,0:T(8,128)(2,1)S(1)}, bf16[128,512]{1,0:T(8,128)(2,1)S(1)}, u32[]{:S(2)}, u32[]{:S(2)}) collective-permute-start(bf16[128,512]{1,0:T(8,128)(2,1)S(1)} %get-tuple-element.67), channel_id=1, source_target_pairs={{0,16},{8,24},{16,0},{24,8},{1,17},{9,25},{17,1},{25,9},{2,18},{10... | collective-permute-start | bytes 393224 | tf_op jit(solution)/shard_map/ppermute | solution.py:500
  68.9 6.0 %collective-permute-start.22 = (bf16[128,512]{1,0:T(8,128)(2,1)S(1)}, bf16[128,512]{1,0:T(8,128)(2,1)S(1)}, u32[]{:S(2)}, u32[]{:S(2)}) collective-permute-start(bf16[128,512]{1,0:T(8,128)(2,1)S(1)} %get-tuple-element.68), channel_id=1, source_target_pairs={{0,24},{8,16},{16,8},{24,0},{1,25},{9,17},{17,9},{25,1},{2,26},{10... | collective-permute-start | bytes 393224 | tf_op jit(solution)/shard_map/ppermute | solution.py:500
  70.2 10.0 %collective-permute-start.24 = (bf16[128,512]{1,0:T(8,128)(2,1)S(1)}, bf16[128,512]{1,0:T(8,128)(2,1)S(1)}, u32[]{:S(2)}, u32[]{:S(2)}) collective-permute-start(bf16[128,512]{1,0:T(8,128)(2,1)S(1)} %get-tuple-element.71), channel_id=1, source_target_pairs={{0,4},{2,6},{4,0},{6,2},{1,5},{3,7},{5,1},{7,3},{8,12},{10,14},{12... | collective-permute-start | bytes 393224 | tf_op jit(solution)/shard_map/ppermute | solution.py:500
  72.0 8.2 %collective-permute-start.25 = (bf16[128,512]{1,0:T(8,128)(2,1)S(1)}, bf16[128,512]{1,0:T(8,128)(2,1)S(1)}, u32[]{:S(2)}, u32[]{:S(2)}) collective-permute-start(bf16[128,512]{1,0:T(8,128)(2,1)S(1)} %get-tuple-element.72), channel_id=1, source_target_pairs={{0,6},{2,4},{4,2},{6,0},{1,7},{3,5},{5,3},{7,1},{8,14},{10,12},{12... | collective-permute-start | bytes 393224 | tf_op jit(solution)/shard_map/ppermute | solution.py:500
  74.8 5.4 %copy-start.3 = (bf16[512,512]{1,0:T(8,128)(2,1)S(1)}, bf16[512,512]{1,0:T(8,128)(2,1)}, u32[]{:S(2)}) copy-start(bf16[512,512]{1,0:T(8,128)(2,1)} %get-tuple-element.40.refs_3_) | copy-start | bytes 1572868
  74.8 6.0 %collective-permute-start.26 = (bf16[128,512]{1,0:T(8,128)(2,1)S(1)}, bf16[128,512]{1,0:T(8,128)(2,1)S(1)}, u32[]{:S(2)}, u32[]{:S(2)}) collective-permute-start(bf16[128,512]{1,0:T(8,128)(2,1)S(1)} %get-tuple-element.76), channel_id=1, source_target_pairs={{0,1},{1,0},{2,3},{3,2},{4,5},{5,4},{6,7},{7,6},{8,9},{9,8},{10,11... | collective-permute-start | bytes 393224 | tf_op jit(solution)/shard_map/ppermute | solution.py:500
  80.2 1.4 %collective-permute-start.27 = (bf16[128,512]{1,0:T(8,128)(2,1)S(1)}, bf16[128,512]{1,0:T(8,128)(2,1)S(1)}, u32[]{:S(2)}, u32[]{:S(2)}) collective-permute-start(bf16[128,512]{1,0:T(8,128)(2,1)S(1)} %get-tuple-element.77), channel_id=1, source_target_pairs={{0,1},{1,0},{2,3},{3,2},{4,5},{5,4},{6,7},{7,6},{8,9},{9,8},{10,11... | collective-permute-start | bytes 393224 | tf_op jit(solution)/shard_map/ppermute | solution.py:500
